TPU v7x, 32 devices: a whole 2x2x4 slice. The times are simulated.
32 devices in a mesh: dp: 8 (over z, x), tensor: 4 (over y, core).
Axes of the slice: x: 2, y: 2, z: 4, core: 2. Of those that a mesh axis runs over, the one named last changes fastest.
Arguments:
- frames: bfloat16 [16, 1500, 768], P('dp', 'tensor'), may hold values from -6 to 6
- cotangent: bfloat16 [16, 1500, 768], P('dp', 'tensor'), may hold values from -6 to 6
- qkv_weight: bfloat16 [2, 768, 3, 768], P(None, 'dp', None, 'tensor'), may hold values from -0.21875 to 0.21875
- out_weight: bfloat16 [2, 768, 768], P(None, 'tensor', 'dp'), may hold values from -6 to 6
- up_weight: bfloat16 [2, 768, 3072], P(None, 'dp', 'tensor'), may hold values from -0.21875 to 0.21875
- down_weight: bfloat16 [2, 3072, 768], P(None, 'tensor', 'dp'), may hold values from -0.109375 to 0.109375
- qv_bias: float32 [2, 2, 768], P(None, None, ('tensor', 'dp')), may hold values from -0.3 to 0.3
- up_bias: float32 [2, 3072], P(None, ('tensor', 'dp')), may hold values from -3 to 3
- norm_gains: float32 [2, 2, 768], P(None, None, ('dp', 'tensor')), may hold values from 0.5 to 1.5
- norm_shifts: float32 [2, 2, 768], P(None, None, ('dp', 'tensor')), may hold values from -0.3 to 0.3
- out_biases: float32 [2, 2, 768], P(None, None, ('dp', 'tensor')), may hold values from -2 to 2
Outputs:
- encoded: float32 [16, 1500, 768], P('dp', 'tensor')
- frames_grad: float32 [16, 1500, 768], P('dp', 'tensor')
- qkv_grad: float32 [2, 768, 3, 768], P(None, 'dp', None, 'tensor')
- out_grad: float32 [2, 768, 768], P(None, 'tensor', 'dp')
- up_grad: float32 [2, 768, 3072], P(None, 'dp', 'tensor')
- down_grad: float32 [2, 3072, 768], P(None, 'tensor', 'dp')
- qv_bias_grad: float32 [2, 2, 768], P(None, None, ('tensor', 'dp'))
- up_bias_grad: float32 [2, 3072], P(None, ('tensor', 'dp'))
- gains_grad: float32 [2, 2, 768], P(None, None, ('dp', 'tensor'))
- shifts_grad: float32 [2, 2, 768], P(None, None, ('dp', 'tensor'))
- out_biases_grad: float32 [2, 2, 768], P(None, None, ('dp', 'tensor'))
All inputs are finite; a program needn't handle non-finite values.
Results may differ from a plain program's by a relative error of at most 0.023.
Values may be sent and summed in bfloat16 or wider, within the bound.
No kernel may reach another device: no remote copies, remote signals or barrier semaphores. Data moves between devices by JAX's collectives and lax.ppermute only.
A program may use at most 320 MiB of HBM per device.

v0:
```python
import jax
import jax.numpy as jnp
from jax import lax
from jax.sharding import PartitionSpec as P

HD = 64


eps = 1e-05


def as_sent(value):
    return jax.tree.map(lambda a: a.astype(jnp.bfloat16) if a.dtype == jnp.float32 else a, value)


def layer_norm(value, gain, shift):
    centre = jnp.mean(value, axis=-1, keepdims=True)
    centred = value - centre
    spread = jnp.mean(centred * centred, axis=-1, keepdims=True)
    return centred * lax.rsqrt(spread + eps) * gain + shift


def gelu_exact(value):
    return jax.nn.gelu(value, approximate=False)


def lead_split(value, dim, count):
    shape = value.shape
    split = value.reshape(shape[:dim] + (count, shape[dim] // count) + shape[dim + 1 :])
    return jnp.moveaxis(split, dim, 0)


def tensor_share(partial_sum, count_tensor):
    return lax.psum_scatter(
        lead_split(partial_sum, 1, count_tensor).astype(jnp.bfloat16),
        "tensor",
        scatter_dimension=0,
        tiled=True,
    ).astype(jnp.float32)[0]


def attend_clip(operands):
    queries, key_rows, value_rows = operands
    score_scale = queries.shape[-1] ** (-0.5)
    scores = (
        jnp.einsum("qhd,khd->hqk", queries, key_rows, preferred_element_type=jnp.float32)
        * score_scale
    )
    row_max = jnp.max(scores, axis=-1, keepdims=True)
    exponent = jnp.exp(scores - row_max)
    row_total = jnp.sum(exponent, axis=-1, keepdims=True)
    weights_low = (exponent / row_total).astype(jnp.bfloat16)
    attended = jnp.einsum(
        "hqk,khd->qhd", weights_low, value_rows, preferred_element_type=jnp.float32
    )
    return (attended.astype(jnp.bfloat16), (row_max + jnp.log(row_total))[..., 0])


def attend_back(operands):
    queries, key_rows, value_rows, grad_out, logsum = operands
    score_scale = queries.shape[-1] ** (-0.5)
    scores = (
        jnp.einsum("qhd,khd->hqk", queries, key_rows, preferred_element_type=jnp.float32)
        * score_scale
    )
    probs = jnp.exp(scores - logsum[..., None])
    weights_low = probs.astype(jnp.bfloat16)
    grad_values = jnp.einsum(
        "hqk,qhd->khd", weights_low, grad_out, preferred_element_type=jnp.float32
    )
    grad_probs = jnp.einsum(
        "qhd,khd->hqk", grad_out, value_rows, preferred_element_type=jnp.float32
    )
    inner = jnp.sum(probs * grad_probs, axis=-1, keepdims=True)
    grad_scores = (probs * (grad_probs - inner)).astype(jnp.bfloat16)
    grad_queries = (
        jnp.einsum("hqk,khd->qhd", grad_scores, key_rows, preferred_element_type=jnp.float32)
        * score_scale
    )
    grad_keys = (
        jnp.einsum("hqk,qhd->khd", grad_scores, queries, preferred_element_type=jnp.float32)
        * score_scale
    )
    return jnp.stack([grad_queries, grad_keys, grad_values], axis=1).astype(jnp.bfloat16)


def fetch(layer_at, qkv_weight, out_weight, up_weight, down_weight, qv_bias, up_bias):
    fetched = (
        lax.all_gather(qkv_weight[layer_at], "dp", axis=0, tiled=True),
        lax.all_gather(out_weight[layer_at], "dp", axis=1, tiled=True),
        lax.all_gather(up_weight[layer_at], "dp", axis=0, tiled=True),
        lax.all_gather(down_weight[layer_at], "dp", axis=1, tiled=True),
        lax.all_gather(qv_bias[layer_at].astype(jnp.bfloat16), "dp", axis=1, tiled=True).astype(
            jnp.float32
        ),
        lax.all_gather(up_bias[layer_at].astype(jnp.bfloat16), "dp", axis=0, tiled=True).astype(
            jnp.float32
        ),
    )
    widened = (
        lax.all_gather(fetched[2], "tensor", axis=1, tiled=True),
        lax.all_gather(fetched[3], "tensor", axis=0, tiled=True),
        lax.all_gather(as_sent(fetched[5]), "tensor", axis=0, tiled=True),
    )
    fetched = (fetched[0], fetched[1], widened[0], widened[1], fetched[4], widened[2])
    return fetched


def local(
    frames,
    cotangent,
    qkv_weight,
    out_weight,
    up_weight,
    down_weight,
    qv_bias,
    up_bias,
    norm_gains,
    norm_shifts,
    out_biases,
):
    layer_count = qkv_weight.shape[0]
    clip_count = frames.shape[0]
    count_tensor = lax.axis_size("tensor")
    count_dp = lax.axis_size("dp")
    count_all = lax.axis_size(("dp", "tensor"))
    gain_all, shift_all, obias_all = (
        lax.all_gather(norm_gains, ("dp", "tensor"), axis=2, tiled=True),
        lax.all_gather(norm_shifts, ("dp", "tensor"), axis=2, tiled=True),
        lax.all_gather(out_biases, ("dp", "tensor"), axis=2, tiled=True),
    )
    weight_args = (qkv_weight, out_weight, up_weight, down_weight, qv_bias, up_bias)

    def by_heads(tensor_in):
        return tensor_in.reshape(clip_count, tensor_in.shape[1], -1, HD)

    current = frames.astype(jnp.float32)
    saved = []
    kept = []
    for layer_at in range(layer_count):
        w_qkv, w_out, w_up, w_down, b_qv, b_up = fetch(layer_at, *weight_args)
        kept.append((w_qkv, w_out, w_up, w_down, b_qv, b_up))
        normed_one = layer_norm(current, gain_all[layer_at, 0], shift_all[layer_at, 0]).astype(
            jnp.bfloat16
        )

        def project_qkv(rows_in, first_row, w_qkv=w_qkv):
            return (
                rows_in,
                jnp.einsum("cfd,dkh->cfkh", rows_in, w_qkv, preferred_element_type=jnp.float32),
            )

        normed_full, projected = project_qkv(
            lax.all_gather(normed_one, "tensor", axis=1, tiled=True), jnp.int32(0)
        )
        queries = (projected[:, :, 0] + b_qv[0]).astype(jnp.bfloat16)
        key_rows = projected[:, :, 1].astype(jnp.bfloat16)
        value_rows = (projected[:, :, 2] + b_qv[1]).astype(jnp.bfloat16)
        attended, logsum = lax.map(
            attend_clip, (by_heads(queries), by_heads(key_rows), by_heads(value_rows))
        )
        attended = attended.reshape(queries.shape)
        partial_sum = jnp.einsum("cfh,hd->cfd", attended, w_out, preferred_element_type=jnp.float32)
        branch = tensor_share(partial_sum, count_tensor) + obias_all[layer_at, 0]
        middle = current + branch
        normed_two = layer_norm(middle, gain_all[layer_at, 1], shift_all[layer_at, 1]).astype(
            jnp.bfloat16
        )
        ff_input = normed_two
        upward = (
            jnp.einsum("cfd,dk->cfk", normed_two, w_up, preferred_element_type=jnp.float32) + b_up
        )
        activated = gelu_exact(upward).astype(jnp.bfloat16)
        feed_out = (
            jnp.einsum("cfk,kd->cfd", activated, w_down, preferred_element_type=jnp.float32)
            + obias_all[layer_at, 1]
        )
        saved.append(
            (
                current,
                normed_full,
                queries,
                key_rows,
                value_rows,
                attended,
                logsum,
                middle,
                ff_input,
                upward,
                activated,
            )
        )
        current = middle + feed_out
    gradient = cotangent.astype(jnp.float32)
    weight_grads = [None] * layer_count
    gain_grads = [None] * layer_count
    shift_grads = [None] * layer_count
    obias_grads = [None] * layer_count
    for layer_at in reversed(range(layer_count)):
        (
            layer_in,
            normed_full,
            queries,
            key_rows,
            value_rows,
            attended,
            logsum,
            middle,
            ff_input,
            upward,
            activated,
        ) = saved[layer_at]
        w_qkv, w_out, w_up, w_down, b_qv, b_up = fetch(layer_at, *weight_args)
        grad_feed = gradient.astype(jnp.bfloat16)
        grad_obias_two = jnp.sum(grad_feed, axis=(0, 1), dtype=jnp.float32)
        grad_act = jnp.einsum("cfd,kd->cfk", grad_feed, w_down, preferred_element_type=jnp.float32)
        grad_wdown = jnp.einsum(
            "cfk,cfd->kd", activated, grad_feed, preferred_element_type=jnp.float32
        )
        grad_upward = jax.vjp(gelu_exact, upward)[1](grad_act)[0].astype(jnp.bfloat16)
        grad_bup = jnp.sum(grad_upward, axis=(0, 1), dtype=jnp.float32)
        grad_wup = jnp.einsum(
            "cfd,cfk->dk", ff_input, grad_upward, preferred_element_type=jnp.float32
        )
        partial_sum = jnp.einsum(
            "cfk,dk->cfd", grad_upward, w_up, preferred_element_type=jnp.float32
        )
        grad_normed_two = partial_sum
        summed_ff = (
            lax.psum_scatter(
                lead_split(grad_wup, 1, count_tensor).astype(jnp.bfloat16),
                "tensor",
                scatter_dimension=0,
                tiled=True,
            ).astype(jnp.float32),
            lax.psum_scatter(
                lead_split(grad_wdown, 0, count_tensor).astype(jnp.bfloat16),
                "tensor",
                scatter_dimension=0,
                tiled=True,
            ).astype(jnp.float32),
            lax.psum_scatter(
                lead_split(grad_bup, 0, count_tensor).astype(jnp.bfloat16),
                "tensor",
                scatter_dimension=0,
                tiled=True,
            ).astype(jnp.float32),
        )
        grad_wup, grad_wdown, grad_bup = (summed_ff[0][0], summed_ff[1][0], summed_ff[2][0])
        norm_back = jax.vjp(layer_norm, middle, gain_all[layer_at, 1], shift_all[layer_at, 1])[1]
        grad_middle, grad_gain_two, grad_shift_two = norm_back(grad_normed_two)
        gradient = gradient + grad_middle
        grad_branch = gradient.astype(jnp.bfloat16)
        grad_obias_one = jnp.sum(grad_branch, axis=(0, 1), dtype=jnp.float32)

        def out_back(rows_in, first_row, w_out=w_out):
            return (
                rows_in,
                jnp.einsum("cfd,hd->cfh", rows_in, w_out, preferred_element_type=jnp.float32),
            )

        grad_attn_full, grad_attended = out_back(
            lax.all_gather(grad_branch, "tensor", axis=1, tiled=True), jnp.int32(0)
        )
        grad_wout = jnp.einsum(
            "cfh,cfd->hd", attended, grad_attn_full, preferred_element_type=jnp.float32
        )
        grad_attended = grad_attended.astype(jnp.bfloat16)
        grads_qkv = lax.map(
            attend_back,
            (
                by_heads(queries),
                by_heads(key_rows),
                by_heads(value_rows),
                by_heads(grad_attended),
                logsum,
            ),
        )
        grads_qkv = grads_qkv.reshape(clip_count, queries.shape[1], 3, queries.shape[2])
        grad_wqkv = jnp.einsum(
            "cfd,cfkh->dkh", normed_full, grads_qkv, preferred_element_type=jnp.float32
        )
        grad_bqv = jnp.sum(grads_qkv[:, :, 0::2], axis=(0, 1), dtype=jnp.float32)
        partial_sum = jnp.einsum(
            "cfkh,dkh->cfd", grads_qkv, w_qkv, preferred_element_type=jnp.float32
        )
        grad_normed_one = lax.psum_scatter(
            lead_split(partial_sum, 1, count_tensor).astype(jnp.bfloat16),
            "tensor",
            scatter_dimension=0,
            tiled=True,
        ).astype(jnp.float32)[0]
        norm_back = jax.vjp(layer_norm, layer_in, gain_all[layer_at, 0], shift_all[layer_at, 0])[1]
        grad_input, grad_gain_one, grad_shift_one = norm_back(grad_normed_one)
        gradient = gradient + grad_input
        summed_w = (
            lax.psum_scatter(
                lead_split(grad_wqkv, 0, count_dp), "dp", scatter_dimension=0, tiled=True
            ),
            lax.psum_scatter(
                lead_split(grad_wout, 1, count_dp), "dp", scatter_dimension=0, tiled=True
            ),
            lax.psum_scatter(
                lead_split(grad_wup, 0, count_dp), "dp", scatter_dimension=0, tiled=True
            ),
            lax.psum_scatter(
                lead_split(grad_wdown, 1, count_dp), "dp", scatter_dimension=0, tiled=True
            ),
            lax.psum_scatter(
                lead_split(grad_bqv, 1, count_dp), "dp", scatter_dimension=0, tiled=True
            ),
            lax.psum_scatter(
                lead_split(grad_bup, 0, count_dp), "dp", scatter_dimension=0, tiled=True
            ),
        )
        weight_grads[layer_at] = [member[0] for member in summed_w]
        gain_grads[layer_at] = jnp.stack([grad_gain_one, grad_gain_two])
        shift_grads[layer_at] = jnp.stack([grad_shift_one, grad_shift_two])
        obias_grads[layer_at] = jnp.stack([grad_obias_one, grad_obias_two])
    summed_v = (
        lax.psum_scatter(
            lead_split(jnp.stack(gain_grads), 2, count_all),
            ("dp", "tensor"),
            scatter_dimension=0,
            tiled=True,
        ),
        lax.psum_scatter(
            lead_split(jnp.stack(shift_grads), 2, count_all),
            ("dp", "tensor"),
            scatter_dimension=0,
            tiled=True,
        ),
        lax.psum_scatter(
            lead_split(jnp.stack(obias_grads), 2, count_all),
            ("dp", "tensor"),
            scatter_dimension=0,
            tiled=True,
        ),
    )
    gains_grad, shifts_grad, out_biases_grad = (summed_v[0][0], summed_v[1][0], summed_v[2][0])
    stacked = [
        jnp.stack([weight_grads[index_at][member] for index_at in range(layer_count)])
        for member in range(6)
    ]
    return (
        current,
        gradient,
        stacked[0],
        stacked[1],
        stacked[2],
        stacked[3],
        stacked[4],
        stacked[5],
        gains_grad,
        shifts_grad,
        out_biases_grad,
    )


def solution(mesh):
    in_specs = (
        P("dp", "tensor", None),
        P("dp", "tensor", None),
        P(None, "dp", None, "tensor"),
        P(None, "tensor", "dp"),
        P(None, "dp", "tensor"),
        P(None, "tensor", "dp"),
        P(None, None, ("tensor", "dp")),
        P(None, ("tensor", "dp")),
        P(None, None, ("dp", "tensor")),
        P(None, None, ("dp", "tensor")),
        P(None, None, ("dp", "tensor")),
    )
    out_specs = (
        P("dp", "tensor", None),
        P("dp", "tensor", None),
        P(None, "dp", None, "tensor"),
        P(None, "tensor", "dp"),
        P(None, "dp", "tensor"),
        P(None, "tensor", "dp"),
        P(None, None, ("tensor", "dp")),
        P(None, ("tensor", "dp")),
        P(None, None, ("dp", "tensor")),
        P(None, None, ("dp", "tensor")),
        P(None, None, ("dp", "tensor")),
    )
    return jax.shard_map(local, mesh=mesh, in_specs=in_specs, out_specs=out_specs, check_vma=False)
```

profile of v0, /device:TPU:0, one launch (start us, length us, event | category | flops | bytes accessed | tf_op | source)
XLA Modules:
  0.0 2206.8 jit_solution(15830780841428648586)
XLA Ops:
  12.6 45.5 %all_gather.88 = f32[2,2,768]{1,0,2:T(2,128)S(1)} all-gather(f32[2,2,24]{1,0,2:T(2,128)S(1)} %copy.550), channel_id=1, replica_groups=mesh['dp'=8,'tensor'=4] {'dp','tensor'}, dimensions={2}, use_global_device_ids=true | all-gather | bytes 12672 | tf_op jit(solution)/shard_map/all_gather | solution.py:129
  67.8 39.0 %all_gather.87 = f32[2,2,768]{1,0,2:T(2,128)S(1)} all-gather(f32[2,2,24]{1,0,2:T(2,128)S(1)} %copy.549), channel_id=1, replica_groups=mesh['dp'=8,'tensor'=4] {'dp','tensor'}, dimensions={2}, use_global_device_ids=true | all-gather | bytes 12672 | tf_op jit(solution)/shard_map/all_gather | solution.py:128
  121.4 30.5 %all-gather.1 = bf16[1,2,192]{1,0,2:T(2,128)(2,1)S(1)} all-gather(bf16[1,2,24]{1,0,2:T(2,128)(2,1)S(1)} %get-tuple-element.397), channel_id=3, replica_groups=mesh['dp'=8,'tensor'=4] {'dp'}, dimensions={2}, use_global_device_ids=true | all-gather | bytes 864 | tf_op jit(solution)/shard_map/all_gather | solution.py:93
  156.7 34.0 %all-gather.2 = bf16[1,192,768]{1,0,2:T(2,128)(2,1)S(1)} all-gather(bf16[1,192,96]{1,0,2:T(2,128)(2,1)S(1)} %copy.641), channel_id=4, replica_groups=mesh['dp'=8,'tensor'=4] {'dp'}, dimensions={2}, use_global_device_ids=true | all-gather | bytes 331776 | tf_op jit(solution)/shard_map/all_gather | solution.py:90
  192.3 37.0 %all-gather = bf16[1,768,3,192]{3,2,0,1:T(4,128)(2,1)S(1)} all-gather(bf16[1,96,3,192]{3,2,0,1:T(4,128)(2,1)S(1)} %copy.640), channel_id=2, replica_groups=mesh['dp'=8,'tensor'=4] {'dp'}, dimensions={1}, use_global_device_ids=true | all-gather | bytes 995328 | tf_op jit(solution)/shard_map/all_gather | solution.py:89
  239.1 71.3 %while.44 = (s32[]{:T(128)}, bf16[2,1500,3,64]{1,3,2,0:T(8,128)(2,1)S(1)}, f32[2,3,1500]{2,1,0:T(4,128)}, bf16[2,1500,3,64]{1,3,2,0:T(8,128)(2,1)}, bf16[2,1500,...) while((s32[]{:T(128)}, bf16[2,1500,3,64]{1,3,2,0:T(8,128)(2,1)S(1)}, ...), condition=%wide.region_5.6_spmd, body=%wide.region_2.5_spmd.sunk | while | flops 1789033472 | bytes 84548088 | solution.py:159
  239.1 11.2 multiply_reduce_fusion.15
  250.3 11.8 fusion.280
  262.1 12.0 fusion.281
  285.9 11.8 fusion.280
  297.7 12.0 fusion.281
  329.9 19.7 all-reduce.17
  355.2 40.4 %all_gather.93 = f32[2,2,768]{1,0,2:T(2,128)S(1)} all-gather(f32[2,2,24]{1,0,2:T(2,128)S(1)} %copy.561), channel_id=1, replica_groups=mesh['dp'=8,'tensor'=4] {'dp','tensor'}, dimensions={2}, use_global_device_ids=true | all-gather | bytes 12672 | tf_op jit(solution)/shard_map/all_gather | solution.py:130
  408.1 16.1 all-reduce.24.cloned.1.call-done
  428.5 34.3 %all-gather.41.cloned.1.call-done = bf16[1,768,3072]{2,1,0:T(8,128)(2,1)} async-done(((bf16[1,768,768]{2,1,0:T(8,128)(2,1)}), bf16[1,768,3072]{2,1,0:T(8,128)(2,1)}) %all-gather.41.cloned.1.call-update) | async-done | bytes 4718608 | tf_op jit(solution)/shard_map/all_gather | solution.py:101
  476.0 23.2 %multiply_convert_fusion.3 = (bf16[2,375,3072]{2,1,0:T(8,128)(2,1)}, f32[2,375,3072]{2,1,0:T(8,128)}) fusion(f32[2,375,3072]{2,1,0:T(8,128)S(1)} %get-tuple-element.402, f32[3072]{0:T(1024)S(1)} %bitcast.557, u8[375,3072]{1,0:T(8,128)(4,1)S(1)} %get-tuple-element.270, u8[375,3072]{1,0:T(8,128)(4,1)S(1)} %get-tuple-element.269), kind=kLoop, calls=%fused_computation.140 | loop fusion | flops 163584000 | bytes 25356288 | tf_op jit(solution)/shard_map/convert_element_type | solution.py:173
  514.6 30.6 %all-gather.10 = bf16[1,2,192]{1,0,2:T(2,128)(2,1)S(1)} all-gather(bf16[1,2,24]{1,0,2:T(2,128)(2,1)S(1)} %copy-done.82), channel_id=12, replica_groups=mesh['dp'=8,'tensor'=4] {'dp'}, dimensions={2}, use_global_device_ids=true | all-gather | bytes 864 | tf_op jit(solution)/shard_map/all_gather | solution.py:93
  548.7 32.2 %all-gather.11 = bf16[1,192,768]{1,0,2:T(2,128)(2,1)S(1)} all-gather(bf16[1,192,96]{1,0,2:T(2,128)(2,1)S(1)} %copy.643), channel_id=13, replica_groups=mesh['dp'=8,'tensor'=4] {'dp'}, dimensions={2}, use_global_device_ids=true | all-gather | bytes 331776 | tf_op jit(solution)/shard_map/all_gather | solution.py:90
  582.4 40.8 %all-gather.9 = bf16[1,768,3,192]{3,2,0,1:T(4,128)(2,1)S(1)} all-gather(bf16[1,96,3,192]{3,2,0,1:T(4,128)(2,1)S(1)} %copy.642), channel_id=11, replica_groups=mesh['dp'=8,'tensor'=4] {'dp'}, dimensions={1}, use_global_device_ids=true | all-gather | bytes 995328 | tf_op jit(solution)/shard_map/all_gather | solution.py:89
  633.2 71.7 %while.45 = (s32[]{:T(128)}, bf16[2,1500,3,64]{1,3,2,0:T(8,128)(2,1)S(1)}, f32[2,3,1500]{2,1,0:T(4,128)}, bf16[2,1500,3,64]{1,3,2,0:T(8,128)(2,1)}, bf16[2,1500,...) while((s32[]{:T(128)}, bf16[2,1500,3,64]{1,3,2,0:T(8,128)(2,1)S(1)}, ...), condition=%wide.region_14.15_spmd, body=%wide.region_11.14_spmd.sunk | while | flops 1789033472 | bytes 84548088 | solution.py:159
  633.2 11.4 multiply_reduce_fusion.16
  644.6 11.8 fusion.283
  656.4 12.0 fusion.284
  669.1 11.3 multiply_reduce_fusion.16
  680.4 11.8 fusion.283
  692.2 12.0 fusion.284
  730.7 81.2 %all-reduce.26.cloned.1.call-done = bf16[4,2,375,768]{3,1,2,0:T(2,128)(2,1)} async-done(((bf16[4,2,375,768]{3,1,2,0:T(2,128)(2,1)}), bf16[4,2,375,768]{3,1,2,0:T(2,128)(2,1)}) %all-reduce.26.cloned.1.call-update) | async-done | bytes 4608016
  818.4 32.5 %all-gather.49.cloned.1.call-done = bf16[1,768,3072]{2,1,0:T(8,128)(2,1)} async-done(((bf16[1,768,768]{2,1,0:T(8,128)(2,1)}), bf16[1,768,3072]{2,1,0:T(8,128)(2,1)}) %all-gather.49.cloned.1.call-update) | async-done | bytes 4718608 | tf_op jit(solution)/shard_map/all_gather | solution.py:101
  864.4 23.2 %multiply_convert_fusion.2 = (bf16[2,375,3072]{2,1,0:T(8,128)(2,1)}, f32[2,375,3072]{2,1,0:T(8,128)}) fusion(f32[2,375,3072]{2,1,0:T(8,128)S(1)} %get-tuple-element.405, f32[3072]{0:T(1024)S(1)} %bitcast.560, u8[375,3072]{1,0:T(8,128)(4,1)S(1)} %get-tuple-element.268, u8[375,3072]{1,0:T(8,128)(4,1)S(1)} %get-tuple-element.267), kind=kLoop, calls=%fused_computation.127 | loop fusion | flops 163584000 | bytes 25356288 | tf_op jit(solution)/shard_map/convert_element_type | solution.py:173
  889.9 12.2 fusion.229
  916.2 36.9 %all-gather.35.cloned.1.call-done = bf16[2,1500,768]{2,0,1:T(2,128)(2,1)} async-done(((bf16[2,375,768]{2,0,1:T(2,128)(2,1)}), bf16[2,1500,768]{2,0,1:T(2,128)(2,1)}) %all-gather.35.cloned.1.call-update) | async-done | bytes 4608016 | tf_op jit(solution)/shard_map/all_gather | solution.py:263
  953.1 12.5 copy.596
  972.4 183.1 %while.46 = (s32[]{:T(128)}, bf16[2,1500,3,3,64]{1,4,3,2,0:T(8,128)(2,1)}, bf16[2,1500,3,64]{1,3,2,0:T(8,128)(2,1)S(1)}, bf16[2,1500,3,64]{1,3,2,0:T(8,128)(2,1)...) while((s32[]{:T(128)}, ...), condition=%wide.region_22.23_spmd, body=%wide.region_20.22_spmd.sunk | while | flops 4380619264 | bytes 240364208 | solution.py:269
  972.6 14.2 fusion.293
  986.7 21.6 multiply_reduce_fusion.17
  1008.4 23.6 %multiply_convert_fusion.6 = bf16[3,1500,1500]{1,2,0:T(8,128)(2,1)} fusion(f32[3,1500,1500]{1,2,0:T(8,128)} %get-tuple-element.581, f32[3,1500,1500]{1,2,0:T(8,128)} %fusion.293, f32[3,1500]{1,0:T(4,128)S(1)} %get-tuple-element.582), kind=kLoop, calls=%fused_computation.38.clone.1 | loop fusion | flops 20250000 | bytes 67518000 | tf_op jit(solution)/shard_map/while/body/eval_jaxpr/convert_element_type | solution.py:75
  1032.0 13.2 fusion.294
  1063.9 14.2 fusion.293
  1078.1 21.6 multiply_reduce_fusion.17
  1099.7 23.6 %multiply_convert_fusion.6 = bf16[3,1500,1500]{1,2,0:T(8,128)(2,1)} fusion(f32[3,1500,1500]{1,2,0:T(8,128)} %get-tuple-element.581, f32[3,1500,1500]{1,2,0:T(8,128)} %fusion.293, f32[3,1500]{1,0:T(4,128)S(1)} %get-tuple-element.582), kind=kLoop, calls=%fused_computation.38.clone.1 | loop fusion | flops 20250000 | bytes 67518000 | tf_op jit(solution)/shard_map/while/body/eval_jaxpr/convert_element_type | solution.py:75
  1123.3 13.2 fusion.294
  1180.0 92.4 %all-reduce.28.cloned.1.call-done = bf16[4,2,375,768]{3,1,2,0:T(2,128)(2,1)} async-done(((bf16[4,2,375,768]{3,1,2,0:T(2,128)(2,1)}), bf16[4,2,375,768]{3,1,2,0:T(2,128)(2,1)}) %all-reduce.28.cloned.1.call-update) | async-done | bytes 4608016
  1280.0 13.0 fusion.230
  1348.5 12.7 copy.594
  1371.5 189.0 %while.47 = (s32[]{:T(128)}, bf16[2,1500,3,3,64]{1,4,3,2,0:T(8,128)(2,1)}, bf16[2,1500,3,64]{1,3,2,0:T(8,128)(2,1)S(1)}, bf16[2,1500,3,64]{1,3,2,0:T(8,128)(2,1)...) while((s32[]{:T(128)}, ...), condition=%wide.region_30.31_spmd, body=%wide.region_28.30_spmd.sunk | while | flops 4380619264 | bytes 240364208 | solution.py:269
  1371.9 14.4 fusion.305
  1386.4 22.1 %multiply_reduce_fusion.18 = (f32[3,1500]{1,0:T(4,128)S(1)}, f32[3,1500,1500]{1,2,0:T(8,128)}) fusion(f32[3,1500,1500]{1,2,0:T(8,128)} %fusion.305, f32[3,1500]{1,0:T(4,128)S(1)} %dynamic-slice_bitcast_fusion.5, bf16[2,1500,3,64]{1,3,2,0:T(8,128)(2,1)S(1)} %get-tuple-element.676, s32[]{:T(128)S(6)} %copy.815, ...), kind=kOutput, calls=%fused_computation.74.clone.1 | convolution fusion | flops 890995520 | bytes 55223248 | tf_op jit(solution)/shard_map/while/body/eval_jaxpr/qhd,khd->hqk/dot_general | solution.py:63
  1408.5 24.4 %multiply_convert_fusion.7 = bf16[3,1500,1500]{1,2,0:T(8,128)(2,1)} fusion(f32[3,1500,1500]{1,2,0:T(8,128)} %get-tuple-element.590, f32[3,1500,1500]{1,2,0:T(8,128)} %fusion.305, f32[3,1500]{1,0:T(4,128)S(1)} %get-tuple-element.591), kind=kLoop, calls=%fused_computation.73.clone.1 | loop fusion | flops 20250000 | bytes 67518000 | tf_op jit(solution)/shard_map/while/body/eval_jaxpr/convert_element_type | solution.py:75
  1432.8 13.4 fusion.306
  1465.9 14.4 fusion.305
  1480.3 23.1 %multiply_reduce_fusion.18 = (f32[3,1500]{1,0:T(4,128)S(1)}, f32[3,1500,1500]{1,2,0:T(8,128)}) fusion(f32[3,1500,1500]{1,2,0:T(8,128)} %fusion.305, f32[3,1500]{1,0:T(4,128)S(1)} %dynamic-slice_bitcast_fusion.5, bf16[2,1500,3,64]{1,3,2,0:T(8,128)(2,1)S(1)} %get-tuple-element.676, s32[]{:T(128)S(6)} %copy.815, ...), kind=kOutput, calls=%fused_computation.74.clone.1 | convolution fusion | flops 890995520 | bytes 55223248 | tf_op jit(solution)/shard_map/while/body/eval_jaxpr/qhd,khd->hqk/dot_general | solution.py:63
  1503.4 24.8 %multiply_convert_fusion.7 = bf16[3,1500,1500]{1,2,0:T(8,128)(2,1)} fusion(f32[3,1500,1500]{1,2,0:T(8,128)} %get-tuple-element.590, f32[3,1500,1500]{1,2,0:T(8,128)} %fusion.305, f32[3,1500]{1,0:T(4,128)S(1)} %get-tuple-element.591), kind=kLoop, calls=%fused_computation.73.clone.1 | loop fusion | flops 20250000 | bytes 67518000 | tf_op jit(solution)/shard_map/while/body/eval_jaxpr/convert_element_type | solution.py:75
  1528.2 13.4 fusion.306
  1585.2 12.9 copy.591
  1605.8 12.7 copy.588
  1664.6 36.9 %all-reduce.16 = (f32[8,2,24]{2,1,0:T(2,128)S(1)}, f32[8,2,24]{2,1,0:T(2,128)S(1)}, f32[8,96]{1,0:T(8,128)S(1)}, f32[8,96]{1,0:T(8,128)S(1)}) all-reduce(f32[8,2,24]{2,1,0:T(2,128)S(1)} %copy.604, f32[8,2,24]{2,1,0:T(2,128)S(1)} %copy.603, f32[8,96]{1,0:T(8,128)S(1)} %reshape.442, ...), channel_id=37, replica_groups=mesh['dp'=8,'tensor'=4] {'dp'}, use_global_device_ids=true, to_apply=%region_49.50.clone | all-reduce | flops 2304 | bytes 18432
  1707.0 59.9 %all-reduce.30.cloned.1.call-done = bf16[4,2,375,768]{3,1,2,0:T(2,128)(2,1)} async-done(((bf16[4,2,375,768]{3,1,2,0:T(2,128)(2,1)}), bf16[4,2,375,768]{3,1,2,0:T(2,128)(2,1)}) %all-reduce.30.cloned.1.call-update) | async-done | bytes 4608016
  1776.9 43.4 %all-reduce.15 = (f32[32,2,2,24]{3,2,1,0:T(2,128)S(1)}, f32[32,2,2,24]{3,2,1,0:T(2,128)S(1)}, f32[32,2,2,24]{3,2,1,0:T(2,128)S(1)}) all-reduce(f32[32,2,2,24]{3,2,1,0:T(2,128)S(1)} %copy.605, f32[32,2,2,24]{3,2,1,0:T(2,128)S(1)} %copy.606, f32[32,2,2,24]{3,2,1,0:T(2,128)S(1)} %copy.607), channel_id=42, replica_groups=mesh['dp'=8,'tensor'=4] {'dp','tensor'}, use_global_device_ids=true, to_apply=%region_60.61.clone | all-reduce | flops 9216 | bytes 73728
  1821.4 18.5 reduce-scatter.15.cloned.1.call-done
  1839.9 71.6 %reduce-scatter.13.cloned.1.call-done = f32[1,96,3,192]{3,1,2,0:T(8,128)} async-done(((f32[8,96,3,192]{3,1,2,0:T(8,128)}), f32[1,96,3,192]{3,1,2,0:T(8,128)}) %reduce-scatter.13.cloned.1.call-update) | async-done | bytes 221200 | tf_op jit(solution)/shard_map/reduce_scatter | solution.py:297
  1913.4 69.8 %reduce-scatter.27.cloned.1.call-done = f32[1,96,768]{2,1,0:T(8,128)} async-done(((f32[8,96,768]{2,1,0:T(8,128)}), f32[1,96,768]{2,1,0:T(8,128)}) %reduce-scatter.27.cloned.1.call-update) | async-done | bytes 294928 | tf_op jit(solution)/shard_map/reduce_scatter | solution.py:303
  1983.2 71.4 %reduce-scatter.23.cloned.1.call-done = f32[1,96,768]{2,1,0:T(8,128)} async-done(((f32[8,96,768]{2,1,0:T(8,128)}), f32[1,96,768]{2,1,0:T(8,128)}) %reduce-scatter.23.cloned.1.call-update) | async-done | bytes 294928 | tf_op jit(solution)/shard_map/reduce_scatter | solution.py:303
  2056.5 69.5 %reduce-scatter.35.cloned.1.call-done = f32[1,768,96]{1,2,0:T(8,128)} async-done(((f32[8,768,96]{1,2,0:T(8,128)}), f32[1,768,96]{1,2,0:T(8,128)}) %reduce-scatter.35.cloned.1.call-update) | async-done | bytes 294928 | tf_op jit(solution)/shard_map/reduce_scatter | solution.py:306
  2126.0 71.5 %reduce-scatter.31.cloned.1.call-done = f32[1,768,96]{1,2,0:T(8,128)} async-done(((f32[8,768,96]{1,2,0:T(8,128)}), f32[1,768,96]{1,2,0:T(8,128)}) %reduce-scatter.31.cloned.1.call-update) | async-done | bytes 294928 | tf_op jit(solution)/shard_map/reduce_scatter | solution.py:306
  (553 shorter events, 485.7 us)
Async XLA Ops:
  7.2 223.1 %all-gather.31.cloned.1.call-start = ((), (), s32[]{:S(2)}) async-start(), calls=%async_computation.12 | async-start | bytes 5760000 | tf_op jit(solution)/shard_map/all_gather | solution.py:154
  8.7 107.7 %copy-start.60 = (f32[2,375]{1,0:T(2,128)}, f32[2,375]{1,0:T(2,128)S(1)}, u32[]{:S(2)}) copy-start(f32[2,375]{1,0:T(2,128)S(1)} %broadcast_multiply_fusion.3) | copy-start | bytes 9004
  11.0 105.4 %copy-start.83 = (f32[2,375]{1,0:T(2,128)}, f32[2,375]{1,0:T(2,128)S(1)}, u32[]{:S(2)}) copy-start(f32[2,375]{1,0:T(2,128)S(1)} %fusion.203) | copy-start | bytes 9004
  12.6 103.9 %copy-start = (bf16[2,375,768]{2,0,1:T(2,128)(2,1)S(1)}, bf16[2,375,768]{2,0,1:T(2,128)(2,1)}, u32[]{:S(2)}) copy-start(bf16[2,375,768]{2,0,1:T(2,128)(2,1)} %param.19) | copy-start | bytes 3456004
  117.0 38.1 %copy-start.66 = (bf16[2,192,96]{2,1,0:T(8,128)(2,1)S(1)}, bf16[2,192,96]{2,1,0:T(8,128)(2,1)}, u32[]{:S(2)}) copy-start(bf16[2,192,96]{2,1,0:T(8,128)(2,1)} %param.22) | copy-start | bytes 221188
  118.9 37.0 %copy-start.53 = (bf16[2,96,3,192]{3,1,2,0:T(8,128)(2,1)S(1)}, bf16[2,96,3,192]{3,1,2,0:T(8,128)(2,1)}, u32[]{:S(2)}) copy-start(bf16[2,96,3,192]{3,1,2,0:T(8,128)(2,1)} %param.21) | copy-start | bytes 663556
  118.9 208.0 %all-gather.39.cloned.1.call-start = ((), (), s32[]{:S(2)}) async-start(), calls=%async_computation.28 | async-start | bytes 1327104 | tf_op jit(solution)/shard_map/all_gather | solution.py:91
  119.7 285.6 %all-gather.43.cloned.1.call-start = ((), (), s32[]{:S(2)}) async-start(), calls=%async_computation.30 | async-start | bytes 1327104 | tf_op jit(solution)/shard_map/all_gather | solution.py:92
  120.6 303.6 %all-reduce.24.cloned.1.call-start = ((), (), s32[]{:S(2)}) async-start(), calls=%async_computation.36 | async-start | bytes 9216000
  326.9 28.2 %copy-start.122 = (f32[2,2,24]{2,1,0:T(2,128)S(1)}, f32[2,2,24]{2,1,0:T(2,128)}, u32[]{:S(2)}) copy-start(f32[2,2,24]{2,1,0:T(2,128)} %param.29) | copy-start | bytes 1156
  326.9 135.9 %all-gather.41.cloned.1.call-start = ((), (), s32[]{:S(2)}) async-start(), calls=%async_computation.29 | async-start | bytes 5898240 | tf_op jit(solution)/shard_map/all_gather | solution.py:101
  327.5 174.9 %all-gather.45.cloned.1.call-start = ((), (), s32[]{:S(2)}) async-start(), calls=%async_computation.31 | async-start | bytes 5898240 | tf_op jit(solution)/shard_map/all_gather | solution.py:102
  355.1 116.9 %copy-start.80 = (f32[1,3072]{1,0:T(1,128)}, f32[1,3072]{1,0:T(1,128)S(1)}, u32[]{:S(2)}) copy-start(f32[1,3072]{1,0:T(1,128)S(1)} %convert_element_type.301) | copy-start | bytes 36868
  405.3 97.1 %copy-start.55 = (f32[768]{0:T(1024)}, f32[768]{0:T(1024)S(1)}, u32[]{:S(2)}) copy-start(f32[768]{0:T(1024)S(1)} %get-tuple-element.285) | copy-start | bytes 9220
  405.3 21.6 copy-start.1
  407.8 216.5 %all-gather.33.cloned.1.call-start = ((), (), s32[]{:S(2)}) async-start(), calls=%async_computation.13 | async-start | bytes 5760000 | tf_op jit(solution)/shard_map/all_gather | solution.py:154
  426.9 75.5 %copy-start.10 = (bf16[1,2,375,768]{3,1,2,0:T(2,128)(2,1)}, bf16[1,2,375,768]{3,1,2,0:T(2,128)(2,1)S(1)}, u32[]{:S(2)}) copy-start(bf16[1,2,375,768]{3,1,2,0:T(2,128)(2,1)S(1)} %constant_dynamic-slice_fusion.12) | copy-start | bytes 3456004
  426.9 35.9 %copy-start.70 = (f32[768]{0:T(1024)S(1)}, f32[768]{0:T(1024)}, u32[]{:S(2)}) copy-start(f32[768]{0:T(1024)} %get-tuple-element.288) | copy-start | bytes 9220
  426.9 35.9 %copy-start.111 = (f32[768]{0:T(1024)S(1)}, f32[768]{0:T(1024)}, u32[]{:S(2)}) copy-start(f32[768]{0:T(1024)} %get-tuple-element.292) | copy-start | bytes 9220
  427.4 44.6 %copy-start.67 = (f32[2,375]{1,0:T(2,128)}, f32[2,375]{1,0:T(2,128)S(1)}, u32[]{:S(2)}) copy-start(f32[2,375]{1,0:T(2,128)S(1)} %broadcast_multiply_fusion.2) | copy-start | bytes 9004
  428.5 43.5 %copy-start.73 = (f32[2,375]{1,0:T(2,128)}, f32[2,375]{1,0:T(2,128)S(1)}, u32[]{:S(2)}) copy-start(f32[2,375]{1,0:T(2,128)S(1)} %fusion.204) | copy-start | bytes 9004
  511.1 37.3 %copy-start.54 = (bf16[1,192,96]{2,1,0:T(8,128)(2,1)S(1)}, bf16[1,192,96]{2,1,0:T(8,128)(2,1)}, u32[]{:S(2)}) copy-start(bf16[1,192,96]{2,1,0:T(8,128)(2,1)} %get-tuple-element.394) | copy-start | bytes 110596
  511.1 37.5 %copy-start.50 = (bf16[1,96,3,192]{3,1,2,0:T(8,128)(2,1)S(1)}, bf16[1,96,3,192]{3,1,2,0:T(8,128)(2,1)}, u32[]{:S(2)}) copy-start(bf16[1,96,3,192]{3,1,2,0:T(8,128)(2,1)} %get-tuple-element.392) | copy-start | bytes 331780
  513.0 209.0 %all-gather.47.cloned.1.call-start = ((), (), s32[]{:S(2)}) async-start(), calls=%async_computation.32 | async-start | bytes 1327104 | tf_op jit(solution)/shard_map/all_gather | solution.py:91
  513.8 214.2 %all-gather.51.cloned.1.call-start = ((), (), s32[]{:S(2)}) async-start(), calls=%async_computation.34 | async-start | bytes 1327104 | tf_op jit(solution)/shard_map/all_gather | solution.py:92
  514.5 297.3 %all-reduce.26.cloned.1.call-start = ((), (), s32[]{:S(2)}) async-start(), calls=%async_computation.37 | async-start | bytes 9216000
  721.9 129.1 %all-gather.49.cloned.1.call-start = ((), (), s32[]{:S(2)}) async-start(), calls=%async_computation.33 | async-start | bytes 5898240 | tf_op jit(solution)/shard_map/all_gather | solution.py:101
  722.7 167.2 %all-gather.53.cloned.1.call-start = ((), (), s32[]{:S(2)}) async-start(), calls=%async_computation.35 | async-start | bytes 5898240 | tf_op jit(solution)/shard_map/all_gather | solution.py:102
  727.9 86.6 %copy-start.98 = (f32[768]{0:T(1024)S(1)}, f32[768]{0:T(1024)}, u32[]{:S(2)}) copy-start(f32[768]{0:T(1024)} %get-tuple-element.283) | copy-start | bytes 9220
  730.4 222.7 %all-gather.35.cloned.1.call-start = ((), (), s32[]{:S(2)}) async-start(), calls=%async_computation.14 | async-start | bytes 5760000 | tf_op jit(solution)/shard_map/all_gather | solution.py:263
  814.5 36.4 %copy-start.103 = (f32[768]{0:T(1024)S(1)}, f32[768]{0:T(1024)}, u32[]{:S(2)}) copy-start(f32[768]{0:T(1024)} %get-tuple-element.286) | copy-start | bytes 9220
  814.5 36.4 %copy-start.114 = (f32[768]{0:T(1024)S(1)}, f32[768]{0:T(1024)}, u32[]{:S(2)}) copy-start(f32[768]{0:T(1024)} %get-tuple-element.290) | copy-start | bytes 9220
  816.6 94.4 %copy-start.95 = (f32[2,375]{1,0:T(2,128)}, f32[2,375]{1,0:T(2,128)S(1)}, u32[]{:S(2)}) copy-start(f32[2,375]{1,0:T(2,128)S(1)} %broadcast_multiply_fusion) | copy-start | bytes 9004
  818.4 92.5 %copy-start.107 = (f32[2,375]{1,0:T(2,128)}, f32[2,375]{1,0:T(2,128)S(1)}, u32[]{:S(2)}) copy-start(f32[2,375]{1,0:T(2,128)S(1)} %fusion.206) | copy-start | bytes 9004
  864.4 25.5 %copy-start.38 = (bf16[2,375,768]{2,0,1:T(2,128)(2,1)S(1)}, bf16[2,375,768]{2,0,1:T(2,128)(2,1)}, u32[]{:S(2)}) copy-start(bf16[2,375,768]{2,0,1:T(2,128)(2,1)} %param.20) | copy-start | bytes 3456004
  916.1 356.3 %all-reduce.28.cloned.1.call-start = ((), (), s32[]{:S(2)}) async-start(), calls=%async_computation.38 | async-start | bytes 9216000
  916.2 49.4 %copy-start.41 = (bf16[1,192,768]{2,1,0:T(8,128)(2,1)S(1)}, bf16[1,192,768]{2,1,0:T(8,128)(2,1)}, u32[]{:S(2)}) copy-start(bf16[1,192,768]{2,1,0:T(8,128)(2,1)} %copy.568) | copy-start | bytes 884740
  1179.9 95.2 %copy-start.9 = (f32[2,375,768]{2,1,0:T(8,128)S(1)}, f32[2,375,768]{2,1,0:T(8,128)}, u32[]{:S(2)}) copy-start(f32[2,375,768]{2,1,0:T(8,128)} %copy-done.8) | copy-start | bytes 6912004
  1179.9 95.2 %copy-start.59 = (f32[2,375]{1,0:T(2,128)S(1)}, f32[2,375]{1,0:T(2,128)}, u32[]{:S(2)}) copy-start(f32[2,375]{1,0:T(2,128)} %copy-done.58) | copy-start | bytes 9004
  1179.9 95.2 %copy-start.65 = (f32[768]{0:T(1024)S(1)}, f32[768]{0:T(1024)}, u32[]{:S(2)}) copy-start(f32[768]{0:T(1024)} %get-tuple-element.287) | copy-start | bytes 9220
  1179.9 95.8 %copy-start.92 = (f32[2,375]{1,0:T(2,128)S(1)}, f32[2,375]{1,0:T(2,128)}, u32[]{:S(2)}) copy-start(f32[2,375]{1,0:T(2,128)} %copy-done.91) | copy-start | bytes 9004
  1179.9 95.8 %copy-start.77 = (f32[2,375]{1,0:T(2,128)S(1)}, f32[2,375]{1,0:T(2,128)}, u32[]{:S(2)}) copy-start(f32[2,375]{1,0:T(2,128)} %copy-done.76) | copy-start | bytes 9004
  1180.0 168.5 %all-gather.37.cloned.1.call-start = ((), (), s32[]{:S(2)}) async-start(), calls=%async_computation.15 | async-start | bytes 5760000 | tf_op jit(solution)/shard_map/all_gather | solution.py:263
  1277.7 15.3 slice-start
  1279.9 19.9 copy-start.28
  1303.6 322.6 %reduce-scatter.25.cloned.1.call-start = ((), (), s32[]{:S(2)}) async-start(), calls=%async_computation.22 | async-start | bytes 5898240 | tf_op jit(solution)/shard_map/reduce_scatter | solution.py:230
  1313.8 315.3 %reduce-scatter.21.cloned.1.call-start = ((), (), s32[]{:S(2)}) async-start(), calls=%async_computation.20 | async-start | bytes 5898240 | tf_op jit(solution)/shard_map/reduce_scatter | solution.py:230
  1324.0 308.1 %reduce-scatter.33.cloned.1.call-start = ((), (), s32[]{:S(2)}) async-start(), calls=%async_computation.26 | async-start | bytes 5898240 | tf_op jit(solution)/shard_map/reduce_scatter | solution.py:236
  1332.3 302.7 %reduce-scatter.29.cloned.1.call-start = ((), (), s32[]{:S(2)}) async-start(), calls=%async_computation.24 | async-start | bytes 5898240 | tf_op jit(solution)/shard_map/reduce_scatter | solution.py:236
  1342.1 363.3 %reduce-scatter.19.cloned.1.call-start = ((), (), s32[]{:S(2)}) async-start(), calls=%async_computation.19 | async-start | bytes 884736 | tf_op jit(solution)/shard_map/reduce_scatter | solution.py:300
  1348.4 356.9 %reduce-scatter.17.cloned.1.call-start = ((), (), s32[]{:S(2)}) async-start(), calls=%async_computation.18 | async-start | bytes 884736 | tf_op jit(solution)/shard_map/reduce_scatter | solution.py:300
  1369.3 397.6 %all-reduce.30.cloned.1.call-start = ((), (), s32[]{:S(2)}) async-start(), calls=%async_computation.39 | async-start | bytes 9216000
  1585.1 254.8 %reduce-scatter.15.cloned.1.call-start = ((), (), s32[]{:S(2)}) async-start(), calls=%async_computation.17 | async-start | bytes 2654208 | tf_op jit(solution)/shard_map/reduce_scatter | solution.py:297
  1605.7 305.8 %reduce-scatter.13.cloned.1.call-start = ((), (), s32[]{:S(2)}) async-start(), calls=%async_computation.16 | async-start | bytes 2654208 | tf_op jit(solution)/shard_map/reduce_scatter | solution.py:297
  1626.1 357.2 %reduce-scatter.27.cloned.1.call-start = ((), (), s32[]{:S(2)}) async-start(), calls=%async_computation.23 | async-start | bytes 2654208 | tf_op jit(solution)/shard_map/reduce_scatter | solution.py:303
  1629.0 425.6 %reduce-scatter.23.cloned.1.call-start = ((), (), s32[]{:S(2)}) async-start(), calls=%async_computation.21 | async-start | bytes 2654208 | tf_op jit(solution)/shard_map/reduce_scatter | solution.py:303
  1632.0 494.0 %reduce-scatter.35.cloned.1.call-start = ((), (), s32[]{:S(2)}) async-start(), calls=%async_computation.27 | async-start | bytes 2654208 | tf_op jit(solution)/shard_map/reduce_scatter | solution.py:306
  1634.9 562.7 %reduce-scatter.31.cloned.1.call-start = ((), (), s32[]{:S(2)}) async-start(), calls=%async_computation.25 | async-start | bytes 2654208 | tf_op jit(solution)/shard_map/reduce_scatter | solution.py:306
  1648.0 14.2 copy-start.102
  1662.4 107.4 %copy-start.3 = (bf16[2,375,768]{2,0,1:T(2,128)(2,1)S(1)}, bf16[2,375,768]{2,0,1:T(2,128)(2,1)}, u32[]{:S(2)}) copy-start(bf16[2,375,768]{2,0,1:T(2,128)(2,1)} %param.19) | copy-start | bytes 3456004
  1662.4 107.4 %copy-start.61 = (f32[2,375]{1,0:T(2,128)S(1)}, f32[2,375]{1,0:T(2,128)}, u32[]{:S(2)}) copy-start(f32[2,375]{1,0:T(2,128)} %copy-done.60) | copy-start | bytes 9004
  1662.4 107.4 %copy-start.63 = (f32[768]{0:T(1024)S(1)}, f32[768]{0:T(1024)}, u32[]{:S(2)}) copy-start(f32[768]{0:T(1024)} %copy-done.62) | copy-start | bytes 9220
  1707.0 63.5 %copy-start.90 = (f32[2,375]{1,0:T(2,128)S(1)}, f32[2,375]{1,0:T(2,128)}, u32[]{:S(2)}) copy-start(f32[2,375]{1,0:T(2,128)} %copy-done.89) | copy-start | bytes 9004
  1707.0 63.6 %copy-start.84 = (f32[2,375]{1,0:T(2,128)S(1)}, f32[2,375]{1,0:T(2,128)}, u32[]{:S(2)}) copy-start(f32[2,375]{1,0:T(2,128)} %copy-done.83) | copy-start | bytes 9004
  (101 other events, 503.3 us)
Sparse Core Ops, SparseCore 0:
  119.1 34.3 all-gather.30
  156.2 54.4 all-gather.38
  212.9 41.9 all-gather.42
  327.0 97.1 all-reduce.23
  425.7 37.0 all-gather.40
  464.9 37.4 all-gather.44
  513.1 36.8 all-gather.32
  553.0 53.5 all-gather.46
  609.0 41.7 all-gather.50
  722.0 89.7 all-reduce.25
  813.4 37.5 all-gather.48
  852.4 37.4 all-gather.52
  916.2 36.8 all-gather.34
  1180.1 92.3 all-reduce.27
  1303.7 36.9 all-gather.36
  1343.2 47.8 reduce-scatter.24
  1393.4 47.8 reduce-scatter.20
  1443.8 47.8 reduce-scatter.32
  1494.2 47.8 reduce-scatter.28
  1545.6 62.5 reduce-scatter.18
  1611.5 61.5 reduce-scatter.16
  1675.6 91.2 all-reduce.29
  1770.4 69.4 reduce-scatter.14
  1843.3 68.1 reduce-scatter.12
  1915.0 68.2 reduce-scatter.26
  1986.6 68.0 reduce-scatter.22
  2058.0 68.0 reduce-scatter.34
  2129.5 68.0 reduce-scatter.30
where the time goes:
time: 2220 us; the launch traced here: 2210 us
  waiting for transfers between devices  734 us (33%)
  matrix products  523 us (24%)
  blocking collectives  451 us (20%)
  local copies, waits for them, and re-layouts  242 us (11%)
  other arithmetic  236 us (11%)
    unnamed x32, waiting for transfers between devices  252 us
    reduce_scatter x2, waiting for transfers between devices, local(): lax.psum_scatter(lead_split(grad_wup, 0, count_dp), 'dp', scatter_dimensi...  141 us
    reduce_scatter x2, waiting for transfers between devices, local(): lax.psum_scatter(lead_split(grad_wdown, 1, count_dp), 'dp', scatter_dimen...  141 us
    unnamed x4, blocking collectives  110 us
    convert_element_type x4, other arithmetic, attend_back(): grad_scores = (probs * (grad_probs - inner)).astype(jnp.bfloat16)  96.4 us
    reduce_scatter x2, waiting for transfers between devices, local(): lax.psum_scatter(lead_split(grad_wqkv, 0, count_dp), 'dp', scatter_dimens...  90.1 us
    dot_general x4, matrix products, attend_back(): jnp.einsum('qhd,khd->hqk', queries, key_rows, preferred_element_type=jnp....  88.4 us
    all_gather x2, blocking collectives, fetch(): lax.all_gather(qkv_weight[layer_at], 'dp', axis=0, tiled=True)  77.8 us
  transfers between devices with their start and end apart: 28, of which 15 were waited for; matrix products, arithmetic and copies ran while one was open for 30% of the time, Pallas kernels for 0%

commit v1 on v0

v1 whole, which is shorter than its diff:
```python
import functools
import math

import jax
import jax.numpy as jnp
from jax import lax
from jax.experimental import pallas as pl
from jax.experimental.pallas import tpu as pltpu
from jax.sharding import PartitionSpec as P

HD = 64
WIDE = 128
eps = 1e-05
LOG2E = 1.0 / math.log(2.0)
LN2 = math.log(2.0)
MASKED = -1e30
bf16 = jnp.bfloat16
f32 = jnp.float32


def exchange(value, axis, mask):
    count = lax.axis_size(axis)
    return lax.ppermute(value, axis, [(i, i ^ mask) for i in range(count)])


def dp_masks():
    count = lax.axis_size("dp")
    masks = []
    while count > 1:
        count //= 2
        masks.append(count)
    return masks


def relative_mask(position):
    result = 0
    for at, mask in enumerate(dp_masks()):
        result = result + ((position >> at) & 1) * mask
    return result


def spread(block, y_last):
    masks = dp_masks()
    early = masks if y_last else masks[:-1]
    for mask in early:
        block = jnp.concatenate([block, exchange(block, "dp", mask)], axis=0)
    other = exchange(block, "tensor", 2)
    if y_last:
        return [block, other]
    return [
        jnp.concatenate([part, exchange(part, "dp", masks[-1])], axis=0) for part in (block, other)
    ]


def add_low(kept, received):
    return (kept.astype(f32) + received.astype(f32)).astype(bf16)


def halve(value, mask):
    half = value.shape[0] // 2
    return add_low(value[:half], exchange(value[half:], "dp", mask))


def fold(own, other, y_first):
    masks = dp_masks()
    if not y_first:
        own, other = halve(own, masks[-1]), halve(other, masks[-1])
    own = add_low(own, exchange(other, "tensor", 2))
    for mask in reversed(masks if y_first else masks[:-1]):
        own = halve(own, mask)
    return own


def split_low(value):
    high = value.astype(bf16)
    rest = value - high.astype(f32)
    mid = rest.astype(bf16)
    return high, mid, (rest - mid.astype(f32)).astype(bf16)


def lane_at(rows):
    return lax.broadcasted_iota(jnp.int32, (rows, WIDE - HD), 1)


def key_extra(rows, row_count, quarter, ones):
    lane = lane_at(rows)
    row = lax.broadcasted_iota(jnp.int32, (rows, WIDE - HD), 0)
    masked = lax.rem(row, quarter) >= row_count
    bias = jnp.where(masked, MASKED, 0.0).astype(f32)
    value = jnp.where(lane == 0, bias, jnp.where(lane <= ones, 1.0, 0.0))
    return value.astype(bf16)


def ones_extra(rows, ones):
    return jnp.where(lane_at(rows) < ones, 1.0, 0.0).astype(bf16)


def widen(part, extra):
    return jnp.concatenate([part, extra], axis=1)


def nt_dot(left, right):
    return lax.dot_general(left, right, (((1,), (1,)), ((), ())), preferred_element_type=f32)


def nn_dot(left, right):
    return lax.dot_general(left, right, (((1,), (0,)), ((), ())), preferred_element_type=f32)


def tn_dot(left, right):
    return lax.dot_general(left, right, (((0,), (0,)), ((), ())), preferred_element_type=f32)


def attend_kernel(row_count, quarter, step, qk_a, v_a, qk_b, v_b, o_a, o_b, lse, q_s, k_s, v_s, o_s):
    rows = qk_a.shape[1]
    wide = v_a.shape[2]
    heads = wide // HD
    k_more = key_extra(rows, row_count, quarter, 0)
    one = ones_extra(rows, 1)
    for half, (qk, v) in enumerate(((qk_a, v_a), (qk_b, v_b))):
        at = pl.ds(half * rows, rows)
        for h in range(heads):
            low, high = h * HD, (h + 1) * HD
            q_s[h, at, :] = widen(qk[0, :, low:high], one)
            k_s[h, at, :] = widen(qk[0, :, wide + low : wide + high], k_more)
            v_s[h, at, :] = widen(v[0, :, low:high], one)

    for h in range(heads):

        def work(i, carry, h=h):
            for part in range(2):
                at = pl.ds(pl.multiple_of((2 * i + part) * step, step), step)
                scores = nt_dot(q_s[h, at, :], k_s[h])
                top = jnp.max(scores, axis=-1, keepdims=True)
                weights = jnp.exp2(scores - top).astype(bf16)
                summed = nn_dot(weights, v_s[h])
                total = summed[:, HD : HD + 1]
                o_s[at, h * HD : (h + 1) * HD] = (summed[:, :HD] / total).astype(bf16)
                lse[0, at, h : h + 1] = top + jnp.log2(total)
            return carry

        lax.fori_loop(0, rows // step, work, 0)
    o_a[0] = o_s[pl.ds(0, rows), :]
    o_b[0] = o_s[pl.ds(rows, rows), :]


def block_of(shape):
    return pl.BlockSpec((1,) + shape, lambda t: (t, 0, 0))


def attend(row_count, quarter, qk_a, v_a, qk_b, v_b):
    groups, rows, wide = v_a.shape
    heads = wide // HD
    return pl.pallas_call(
        functools.partial(attend_kernel, row_count, quarter, min(256, rows)),
        grid=(groups,),
        in_specs=[block_of((rows, 2 * wide)), block_of((rows, wide))] * 2,
        out_specs=[block_of((rows, wide))] * 2 + [block_of((2 * rows, 8))],
        out_shape=[jax.ShapeDtypeStruct((groups, rows, wide), bf16)] * 2
        + [jax.ShapeDtypeStruct((groups, 2 * rows, 8), f32)],
        scratch_shapes=[pltpu.VMEM((heads, 2 * rows, WIDE), bf16)] * 3
        + [pltpu.VMEM((2 * rows, wide), bf16)],
        compiler_params=pltpu.CompilerParams(vmem_limit_bytes=48 * 2**20),
    )(qk_a, v_a, qk_b, v_b)


def attend_back_kernel(
    row_count, quarter, step,
    qk_a, v_a, qk_b, v_b, o_a, o_b, do_a, do_b, lse,
    dqk_a, dv_a, dqk_b, dv_b,
    q_s, k_s, kt_s, v_s, do_s, dq_s, dk_s, dv_s,
):
    rows = qk_a.shape[1]
    wide = v_a.shape[2]
    heads = wide // HD
    k_more = key_extra(rows, row_count, quarter, 3)
    three = ones_extra(rows, 3)
    lane = lane_at(rows)

    def spread_lanes(first, parts):
        value = jnp.where(lane < first, 1.0, 0.0).astype(f32)
        for at, part in enumerate(parts):
            value = jnp.where(lane == first + at, part.astype(f32), value)
        return value.astype(bf16)

    for half, (qk, v, o, do) in enumerate(((qk_a, v_a, o_a, do_a), (qk_b, v_b, o_b, do_b))):
        at = pl.ds(half * rows, rows)
        for h in range(heads):
            low, high = h * HD, (h + 1) * HD
            minus_lse = split_low(-lse[0, at, h : h + 1])
            q_s[h, at, :] = widen(qk[0, :, low:high], spread_lanes(1, minus_lse))
            keys = widen(qk[0, :, wide + low : wide + high], k_more)
            k_s[h, at, :] = keys
            kt_s[h, :, at] = jnp.transpose(keys.astype(f32)).astype(bf16)
            v_s[h, at, :] = widen(v[0, :, low:high], three)
            grad = do[0, :, low:high]
            inner = jnp.sum(grad.astype(f32) * o[0, :, low:high].astype(f32), axis=1, keepdims=True)
            do_s[h, at, :] = widen(grad, spread_lanes(0, split_low(-inner)))

    dk_s[...] = jnp.zeros_like(dk_s)
    dv_s[...] = jnp.zeros_like(dv_s)
    chunks = 2 * rows // step

    def work(i, carry):
        h = i // chunks
        at = pl.ds(pl.multiple_of(lax.rem(i, chunks) * step, step), step)
        queries = q_s[h, at, :]
        grad_out = do_s[h, at, :]
        probs = jnp.exp2(nt_dot(k_s[h], queries))
        grad_scores = (probs * nt_dot(v_s[h], grad_out)).astype(bf16)
        dv_s[h] += nn_dot(probs.astype(bf16), grad_out)
        dk_s[h] += nn_dot(grad_scores, queries)
        dq_s[h, at, :] = jnp.transpose(nn_dot(kt_s[h], grad_scores))
        return carry

    lax.fori_loop(0, heads * chunks, work, 0)
    for half, (dqk, dv) in enumerate(((dqk_a, dv_a), (dqk_b, dv_b))):
        at = pl.ds(half * rows, rows)
        for h in range(heads):
            low, high = h * HD, (h + 1) * HD
            dqk[0, :, low:high] = (dq_s[h, at, :][:, :HD] * HD**-0.5).astype(bf16)
            dqk[0, :, wide + low : wide + high] = (dk_s[h, at, :][:, :HD] * LN2).astype(bf16)
            dv[0, :, low:high] = dv_s[h, at, :][:, :HD].astype(bf16)


def attend_back(row_count, quarter, qk_a, v_a, qk_b, v_b, o_a, o_b, do_a, do_b, lse):
    groups, rows, wide = v_a.shape
    heads = wide // HD
    return pl.pallas_call(
        functools.partial(attend_back_kernel, row_count, quarter, min(256, rows)),
        grid=(groups,),
        in_specs=[block_of((rows, 2 * wide)), block_of((rows, wide))] * 2
        + [block_of((rows, wide))] * 4
        + [block_of((2 * rows, 8))],
        out_specs=[block_of((rows, 2 * wide)), block_of((rows, wide))] * 2,
        out_shape=[
            jax.ShapeDtypeStruct((groups, rows, 2 * wide), bf16),
            jax.ShapeDtypeStruct((groups, rows, wide), bf16),
        ]
        * 2,
        scratch_shapes=[
            pltpu.VMEM((heads, 2 * rows, WIDE), bf16),
            pltpu.VMEM((heads, 2 * rows, WIDE), bf16),
            pltpu.VMEM((heads, WIDE, 2 * rows), bf16),
            pltpu.VMEM((heads, 2 * rows, WIDE), bf16),
            pltpu.VMEM((heads, 2 * rows, WIDE), bf16),
            pltpu.VMEM((heads, 2 * rows, WIDE), f32),
            pltpu.VMEM((heads, 2 * rows, WIDE), f32),
            pltpu.VMEM((heads, 2 * rows, WIDE), f32),
        ],
        compiler_params=pltpu.CompilerParams(vmem_limit_bytes=56 * 2**20),
    )(qk_a, v_a, qk_b, v_b, o_a, o_b, do_a, do_b, lse)


def normalized(value):
    centred = value - jnp.mean(value, axis=-1, keepdims=True)
    scale = lax.rsqrt(jnp.mean(centred * centred, axis=-1, keepdims=True) + eps)
    return centred * scale, scale


def norm_back(value, gain, grad):
    unit, scale = normalized(value)
    scaled = grad * gain
    result = scale * (
        scaled
        - jnp.mean(scaled, axis=-1, keepdims=True)
        - unit * jnp.mean(scaled * unit, axis=-1, keepdims=True)
    )
    return result, jnp.sum(grad * unit, axis=0), jnp.sum(grad, axis=0)


def gelu_both(value):
    share = 0.5 * (1.0 + lax.erf(value * math.sqrt(0.5)))
    density = jnp.exp(-0.5 * value * value) * (1.0 / math.sqrt(2.0 * math.pi))
    return (value * share).astype(bf16), (share + value * density).astype(bf16)


def local(
    frames,
    cotangent,
    qkv_weight,
    out_weight,
    up_weight,
    down_weight,
    qv_bias,
    up_bias,
    norm_gains,
    norm_shifts,
    out_biases,
):
    layers, block = qkv_weight.shape[:2]
    wide = qkv_weight.shape[3]
    row_count, width = frames.shape[1:]
    hidden = up_weight.shape[2]
    quarter = -(-row_count // 128) * 128
    rows = 2 * quarter
    count_dp = lax.axis_size("dp")
    me = lax.axis_index("dp")
    t_me = lax.axis_index("tensor")
    y_me = t_me // 2
    t_order = jnp.arange(4) ^ t_me
    positions = jnp.arange(count_dp)
    block_at = relative_mask(positions) ^ me
    place_of = jnp.argmax(block_at[None, :] == positions[:, None], axis=1)

    small_parts = (norm_gains, norm_shifts, out_biases, qv_bias, up_bias)
    small_sizes = [part.size for part in small_parts]
    small = jnp.concatenate([part.reshape(1, -1) for part in small_parts], axis=1)
    for mask in dp_masks():
        small = jnp.concatenate([small, exchange(small, "dp", mask)], axis=0)
    small = jnp.stack([small, exchange(small, "tensor", 1)])
    small = jnp.stack([small, exchange(small, "tensor", 2)])
    small = small.reshape(4, count_dp, -1)
    by_part = jnp.split(small, [sum(small_sizes[: i + 1]) for i in range(4)], axis=2)

    def by_width(part):
        part = jnp.take(part, t_order, axis=0).reshape(4, count_dp, layers, 2, -1)
        return part.transpose(2, 3, 1, 0, 4).reshape(layers, 2, width)

    gain_all, shift_all, obias_all = [by_width(part) for part in by_part[:3]]
    qv_all = jnp.take(by_part[3][0::2], place_of, axis=1).reshape(2, count_dp, layers, 2, -1)
    qv_all = qv_all.transpose(2, 3, 0, 1, 4).reshape(layers, 2, 2, wide)
    up_all = jnp.take(by_part[4], place_of, axis=1).reshape(4, count_dp, layers, -1)
    up_all = up_all.transpose(2, 0, 1, 3).reshape(layers, 4, hidden)

    source = jnp.repeat(block_at, block) * block + jnp.tile(jnp.arange(block), count_dp)
    to_relative = (jnp.arange(width)[:, None] == source[None, :]).astype(bf16)

    def take_clip(value):
        mine = lax.dynamic_index_in_dim(value, y_me, 0, keepdims=False)
        theirs = exchange(lax.dynamic_index_in_dim(value, 1 - y_me, 0, keepdims=False), "tensor", 2)
        padding = ((0, 0), (0, quarter - row_count), (0, 0))
        both = jnp.pad(jnp.stack([mine, theirs]), padding).reshape(rows, width)
        return nn_dot(both, to_relative)

    def give_clip(value):
        mine, theirs = value[:quarter], value[quarter:].astype(bf16)
        theirs = nt_dot(exchange(theirs, "tensor", 2), to_relative)[:row_count]
        high = mine.astype(bf16)
        low = (mine - high.astype(f32)).astype(bf16)
        mine = (nt_dot(high, to_relative) + nt_dot(low, to_relative))[:row_count]
        first = y_me == 0
        return jnp.stack([jnp.where(first, mine, theirs), jnp.where(first, theirs, mine)])

    current = take_clip(frames)
    gradient = take_clip(cotangent)

    weights = []
    for at in range(layers):
        qk = jnp.concatenate([qkv_weight[at, :, 0], qkv_weight[at, :, 1]], axis=1)
        vo = jnp.concatenate([qkv_weight[at, :, 2], out_weight[at].T], axis=1)
        w_qk = jnp.stack(spread(qk, True))
        w_vo = jnp.stack(spread(vo, False))
        w_up = spread(up_weight[at], True)
        w_down = spread(down_weight[at].T, False)
        w_up = [
            w_up[0], exchange(w_up[0], "tensor", 1), w_up[1], exchange(w_up[1], "tensor", 1)
        ]
        w_down = [
            w_down[0], exchange(w_down[0], "tensor", 1), w_down[1], exchange(w_down[1], "tensor", 1)
        ]
        weights.append((w_qk, w_vo[:, :, :wide], w_vo[:, :, wide:], w_up, w_down))

    def project(value, weight):
        return jnp.einsum("fd,tdk->tfk", value, weight, preferred_element_type=f32)

    saved = []
    q_scale = HD**-0.5 * LOG2E
    for at in range(layers):
        w_qk, w_v, w_o, w_up, w_down = weights[at]
        unit, _ = normalized(current)
        normed_a = (unit * gain_all[at, 0] + shift_all[at, 0]).astype(bf16)
        normed_b = exchange(normed_a, "tensor", 1)
        qk_scale = jnp.where(jnp.arange(2 * wide) < wide, q_scale, 1.0)
        qk_bias = jnp.concatenate([qv_all[at, 0], jnp.zeros_like(qv_all[at, 0])], axis=1)

        def heads_of(normed):
            qk = ((project(normed, w_qk) + qk_bias[:, None]) * qk_scale).astype(bf16)
            v = (project(normed, w_v) + qv_all[at, 1][:, None]).astype(bf16)
            return qk, v

        qk_a, v_a = heads_of(normed_a)
        qk_b, v_b = heads_of(normed_b)
        o_a, o_b, lse = attend(row_count, quarter, qk_a, v_a, qk_b, v_b)
        share_b = nt_dot(o_b[0], w_o[0]) + nt_dot(o_b[1], w_o[1])
        share_b = exchange(share_b.astype(bf16), "tensor", 1)
        share_a = nt_dot(o_a[0], w_o[0]) + nt_dot(o_a[1], w_o[1])
        middle = current + (share_a + share_b.astype(f32) + obias_all[at, 0])
        unit, _ = normalized(middle)
        normed_two = (unit * gain_all[at, 1] + shift_all[at, 1]).astype(bf16)
        activated = [gelu_both(nn_dot(normed_two, w_up[t]) + up_all[at, t]) for t in range(4)]
        feed = obias_all[at, 1]
        for t in range(4):
            feed = feed + nt_dot(activated[t][0], w_down[t])
        saved.append(
            (current, normed_a, normed_b, qk_a, v_a, qk_b, v_b, o_a, o_b, lse, middle, normed_two, activated)
        )
        current = middle + feed
    encoded = give_clip(current)

    small_grads = [None] * layers
    weight_grads = [None] * layers
    for at in reversed(range(layers)):
        w_qk, w_v, w_o, w_up, w_down = weights[at]
        (layer_in, normed_a, normed_b, qk_a, v_a, qk_b, v_b, o_a, o_b, lse, middle, normed_two, activated) = saved[at]
        grad_feed = gradient.astype(bf16)
        obias_two = jnp.sum(grad_feed, axis=0, dtype=f32)
        grad_up = [
            (nn_dot(grad_feed, w_down[t]) * activated[t][1].astype(f32)).astype(bf16)
            for t in range(4)
        ]
        grad_normed = sum(nt_dot(grad_up[t], w_up[t]) for t in range(4))
        bup = jnp.stack([jnp.sum(part, axis=0, dtype=f32) for part in grad_up])
        dw_up = [tn_dot(normed_two, grad_up[t]).astype(bf16) for t in range(4)]
        dw_down = [tn_dot(grad_feed, activated[t][0]).astype(bf16) for t in range(4)]
        for dw in (dw_up, dw_down):
            for t in (0, 2):
                dw[t] = add_low(dw[t], exchange(dw[t + 1], "tensor", 1))
        dw_up = fold(dw_up[0], dw_up[2], True)
        dw_down = fold(dw_down[0], dw_down[2], False)

        grad_middle, gain_two, shift_two = norm_back(middle, gain_all[at, 1], grad_normed)
        gradient = gradient + grad_middle
        branch_a = gradient.astype(bf16)
        branch_b = exchange(branch_a, "tensor", 1)
        obias_one = jnp.sum(branch_a, axis=0, dtype=f32)
        do_a = project(branch_a, w_o).astype(bf16)
        do_b = project(branch_b, w_o).astype(bf16)
        dqk_a, dv_a, dqk_b, dv_b = attend_back(
            row_count, quarter, qk_a, v_a, qk_b, v_b, o_a, o_b, do_a, do_b, lse
        )

        def back_normed(dqk, dv):
            return sum(nt_dot(dqk[t], w_qk[t]) + nt_dot(dv[t], w_v[t]) for t in range(2))

        share_b = exchange(back_normed(dqk_b, dv_b).astype(bf16), "tensor", 1)
        grad_normed = back_normed(dqk_a, dv_a) + share_b.astype(f32)
        dw_qk = [
            (tn_dot(normed_a, dqk_a[t]) + tn_dot(normed_b, dqk_b[t])).astype(bf16) for t in range(2)
        ]
        dw_vo = [
            jnp.concatenate(
                [
                    (tn_dot(normed_a, dv_a[t]) + tn_dot(normed_b, dv_b[t])).astype(bf16),
                    (tn_dot(branch_a, o_a[t]) + tn_dot(branch_b, o_b[t])).astype(bf16),
                ],
                axis=1,
            )
            for t in range(2)
        ]
        dw_qk = fold(dw_qk[0], dw_qk[1], True)
        dw_vo = fold(dw_vo[0], dw_vo[1], False)
        weight_grads[at] = [part.astype(f32) for part in (dw_qk, dw_vo, dw_up, dw_down)]
        bq = jnp.sum(dqk_a[:, :, :wide], axis=1, dtype=f32)
        bq = bq + jnp.sum(dqk_b[:, :, :wide], axis=1, dtype=f32)
        bv = jnp.sum(dv_a, axis=1, dtype=f32) + jnp.sum(dv_b, axis=1, dtype=f32)
        grad_in, gain_one, shift_one = norm_back(layer_in, gain_all[at, 0], grad_normed)
        gradient = gradient + grad_in
        small_grads[at] = (
            jnp.stack([gain_one, gain_two]),
            jnp.stack([shift_one, shift_two]),
            jnp.stack([obias_one, obias_two]),
            jnp.stack([bq, bv]),
            bup,
        )
    frames_grad = give_clip(gradient)

    gains, shifts, obiases, bqv, bups = [
        jnp.stack([small_grads[at][i] for at in range(layers)]) for i in range(5)
    ]

    def from_width(part):
        part = part.reshape(layers, 2, count_dp, 4, -1).transpose(3, 2, 0, 1, 4)
        return jnp.take(part.reshape(4, count_dp, -1), t_order, axis=0)

    bqv = bqv.reshape(layers, 2, 2, count_dp, -1).transpose(2, 3, 0, 1, 4)
    bqv = jnp.take(bqv.reshape(2, count_dp, -1), block_at, axis=1)
    bqv = jnp.stack([bqv, jnp.zeros_like(bqv)], axis=1).reshape(4, count_dp, -1)
    bups = bups.reshape(layers, 4, count_dp, -1).transpose(1, 2, 0, 3)
    bups = jnp.take(bups.reshape(4, count_dp, -1), block_at, axis=1)
    small = jnp.concatenate(
        [from_width(gains), from_width(shifts), from_width(obiases), bqv, bups], axis=2
    )
    small = small.reshape(2, 2, count_dp, -1)
    small = small[0] + exchange(small[1], "tensor", 2)
    small = small[0] + exchange(small[1], "tensor", 1)
    for mask in reversed(dp_masks()):
        half = small.shape[0] // 2
        small = small[:half] + exchange(small[half:], "dp", mask)
    pieces = jnp.split(small[0], [sum(small_sizes[: i + 1]) for i in range(4)])
    gains, shifts, obiases, bqv, bups = [
        piece.reshape(part.shape) for piece, part in zip(pieces, small_parts)
    ]

    def stacked(make):
        return jnp.stack([make(*weight_grads[at]) for at in range(layers)])

    return (
        encoded,
        frames_grad,
        stacked(lambda qk, vo, up, down: jnp.stack([qk[:, :wide], qk[:, wide:], vo[:, :wide]], axis=1)),
        stacked(lambda qk, vo, up, down: vo[:, wide:].T),
        stacked(lambda qk, vo, up, down: up),
        stacked(lambda qk, vo, up, down: down.T),
        bqv,
        bups,
        gains,
        shifts,
        obiases,
    )


def solution(mesh):
    in_specs = (
        P("dp", "tensor", None),
        P("dp", "tensor", None),
        P(None, "dp", None, "tensor"),
        P(None, "tensor", "dp"),
        P(None, "dp", "tensor"),
        P(None, "tensor", "dp"),
        P(None, None, ("tensor", "dp")),
        P(None, ("tensor", "dp")),
        P(None, None, ("dp", "tensor")),
        P(None, None, ("dp", "tensor")),
        P(None, None, ("dp", "tensor")),
    )
    out_specs = (
        P("dp", "tensor", None),
        P("dp", "tensor", None),
        P(None, "dp", None, "tensor"),
        P(None, "tensor", "dp"),
        P(None, "dp", "tensor"),
        P(None, "tensor", "dp"),
        P(None, None, ("tensor", "dp")),
        P(None, ("tensor", "dp")),
        P(None, None, ("dp", "tensor")),
        P(None, None, ("dp", "tensor")),
        P(None, None, ("dp", "tensor")),
    )
    return jax.shard_map(local, mesh=mesh, in_specs=in_specs, out_specs=out_specs, check_vma=False)
```

time: 2220 us -> 905 us (0.41)
  waiting for transfers between devices: 734 us -> 220 us
  blocking collectives: 451 us -> 0 us
  matrix products: 523 us -> 206 us
  Pallas kernels: 0 us -> 170 us
  other arithmetic: 236 us -> 83.3 us
  local copies, waits for them, and re-layouts: 242 us -> 112 us
  starting transfers between devices: 1.83 us -> 101 us
    reduce_scatter x12 -> x0, waiting for transfers between devices: 372 us -> none  [the longest x2 141 us: local(): lax.psum_scatter(lead_split(grad_wup, 0, count_dp), 'dp', scatter_dimensi...]
    all_gather x11 -> x0, blocking collectives: 341 us -> none  [the longest x2 77.8 us: fetch(): lax.all_gather(qkv_weight[layer_at], 'dp', axis=0, tiled=True)]
    dot_general x52 -> x116, matrix products: 523 us -> 206 us  [the longest x40 75.2 us: tn_dot(): lax.dot_general(left, right, (((0,), (0,)), ((), ())), preferred_element_...]
    unnamed x32 -> x0, waiting for transfers between devices: 252 us -> none
    ppermute x0 -> x110, waiting for transfers between devices: none -> 220 us  [exchange(): return lax.ppermute(value, axis, [(i, i ^ mask) for i in range(count)])]
    pallas_call x0 -> x4, Pallas kernels: none -> 170 us  [the longest x2 112 us: attend_back(): pl.pallas_call(functools.partial(attend_back_kernel, row_count, quarter,...]
    convert_element_type x16 -> x30, other arithmetic: 147 us -> 18.1 us  [the longest x22 16.5 us: add_low(): return (kept.astype(f32) + received.astype(f32)).astype(bf16)]
    unnamed x4 -> x0, blocking collectives: 110 us -> none
  transfers between devices with their start and end apart: 28 -> 110, of which waited for: 15 -> 36; matrix products, arithmetic and copies ran while one was open for 30% -> 39% of each run, Pallas kernels for 0% -> 19%
where the time goes in v1:
time: 905 us; the launch traced here: 898 us
  waiting for transfers between devices  220 us (24%)
  matrix products  206 us (23%)
  Pallas kernels  170 us (19%)
  local copies, waits for them, and re-layouts  112 us (12%)
  starting transfers between devices  101 us (11%)
  other arithmetic  83.3 us (9%)
    ppermute x110, waiting for transfers between devices, exchange(): return lax.ppermute(value, axis, [(i, i ^ mask) for i in range(count)])  220 us
    pallas_call x2, Pallas kernels, attend_back(): pl.pallas_call(functools.partial(attend_back_kernel, row_count, quarter,...  112 us
    ppermute x110, starting transfers between devices, exchange(): return lax.ppermute(value, axis, [(i, i ^ mask) for i in range(count)])  101 us
    dot_general x40, matrix products, tn_dot(): lax.dot_general(left, right, (((0,), (0,)), ((), ())), preferred_element_...  75.2 us
    dot_general x46, matrix products, nt_dot(): lax.dot_general(left, right, (((1,), (1,)), ((), ())), preferred_element_...  71.5 us
    pallas_call x2, Pallas kernels, attend(): pl.pallas_call(functools.partial(attend_kernel, row_count, quarter, min(2...  57.9 us
    dot_general x18, matrix products, nn_dot(): lax.dot_general(left, right, (((1,), (0,)), ((), ())), preferred_element_...  44.2 us
    unnamed x493, local copies, waits for them, and re-layouts  29 us
  transfers between devices with their start and end apart: 110, of which 36 were waited for; matrix products, arithmetic and copies ran while one was open for 39% of the time, Pallas kernels for 19%

profile of v1, /device:TPU:0, one launch (start us, length us, event | category | flops | bytes accessed | tf_op | source)
XLA Modules:
  0.0 897.6 jit_solution(7528425048844665478)
XLA Ops:
  4.6 4.0 collective-permute-start.5
  12.2 2.9 collective-permute-start.30
  16.8 2.9 collective-permute-start.1
  23.7 7.5 constant_dynamic-slice_fusion.1
  58.7 2.7 collective-permute-start.17
  63.9 2.7 collective-permute-start.20
  69.1 6.5 collective-permute-done.17
  77.8 3.1 collective-permute-done.20
  83.1 10.5 %collective-permute-done.11 = bf16[192,384]{0,1:T(8,128)(2,1)S(1)} collective-permute-done((bf16[192,384]{0,1:T(8,128)(2,1)S(1)}, bf16[192,384]{0,1:T(8,128)(2,1)S(1)}, u32[]{:S(2)}, u32[]{:S(2)}) %collective-permute-start.11) | collective-permute-done | bytes 147488 | tf_op jit(solution)/shard_map/ppermute | solution.py:23
  103.5 6.9 collective-permute-done.21
  117.1 5.9 collective-permute-done.18
  135.4 8.2 collective-permute-done.4
  149.4 28.8 %shard_map.194 = (bf16[2,768,192]{2,1,0:T(8,128)(2,1)S(1)}, bf16[2,768,192]{2,1,0:T(8,128)(2,1)S(1)}, f32[2,1536,8]{2,1,0:T(8,128)}) custom-call(bf16[2,768,384]{2,1,0:T(8,128)(2,1)S(1)} %fusion.52.qk_a, bf16[2,768,192]{2,1,0:T(8,128)(2,1)S(1)} %fusion.66.v_a, bf16[2,768,384]{2,1,0:T(8,128)(2,1)S(1)} %fusion.53.qk_b, bf16[2,768,192]{2,1,0:T(8,128)(2,1)S(1)} %fusion.67.v_b), custom_call_target="tpu_custom_call" | custom-call | tf_op jit(solution)/shard_map/pallas_call | solution.py:154
  188.3 9.0 %collective-permute-done.27 = bf16[384,768]{1,0:T(8,128)(2,1)S(1)} collective-permute-done((bf16[384,768]{1,0:T(8,128)(2,1)S(1)}, bf16[384,768]{1,0:T(8,128)(2,1)S(1)}, u32[]{:S(2)}, u32[]{:S(2)}) %collective-permute-start.27) | collective-permute-done | bytes 589856 | tf_op jit(solution)/shard_map/ppermute | solution.py:23
  202.2 25.4 %collective-permute-done.25 = bf16[768,768]{1,0:T(8,128)(2,1)S(1)} collective-permute-done((bf16[768,768]{1,0:T(8,128)(2,1)S(1)}, bf16[768,768]{1,0:T(8,128)(2,1)S(1)}, u32[]{:S(2)}, u32[]{:S(2)}) %collective-permute-start.25) | collective-permute-done | bytes 1179680 | tf_op jit(solution)/shard_map/ppermute | solution.py:23
  227.6 2.7 multiply_convert_fusion.16
  233.3 3.8 multiply_convert_fusion.17
  237.0 2.6 fusion.277
  241.2 2.7 multiply_convert_fusion.14
  252.8 15.7 %collective-permute-done.38 = bf16[384,384]{0,1:T(8,128)(2,1)S(1)} collective-permute-done((bf16[384,384]{0,1:T(8,128)(2,1)S(1)}, bf16[384,384]{0,1:T(8,128)(2,1)S(1)}, u32[]{:S(2)}, u32[]{:S(2)}) %collective-permute-start.38) | collective-permute-done | bytes 294944 | tf_op jit(solution)/shard_map/ppermute | solution.py:23
  273.3 7.9 collective-permute-done.51
  287.6 29.1 %shard_map.195 = (bf16[2,768,192]{2,1,0:T(8,128)(2,1)S(1)}, bf16[2,768,192]{2,1,0:T(8,128)(2,1)S(1)}, f32[2,1536,8]{2,1,0:T(8,128)}) custom-call(bf16[2,768,384]{2,1,0:T(8,128)(2,1)S(1)} %fusion.54.qk_a, bf16[2,768,192]{2,1,0:T(8,128)(2,1)S(1)} %fusion.68.v_a, bf16[2,768,384]{2,1,0:T(8,128)(2,1)S(1)} %fusion.55.qk_b, bf16[2,768,192]{2,1,0:T(8,128)(2,1)S(1)} %fusion.69.v_b), custom_call_target="tpu_custom_call" | custom-call | tf_op jit(solution)/shard_map/pallas_call | solution.py:154
  320.8 2.9 convert_reduce_fusion.8
  324.4 3.1 copy.466
  337.0 2.6 convert_reduce_fusion
  350.1 2.6 convert_reduce_fusion.1
  355.7 2.6 fusion.274
  371.4 2.7 convert_reduce_fusion.3
  393.3 3.5 convolution_convert_fusion.10
  396.8 6.3 collective-permute-done.54
  405.2 2.6 copy.514
  410.9 56.3 %shard_map.196 = (bf16[2,768,384]{2,1,0:T(8,128)(2,1)}, bf16[2,768,192]{2,1,0:T(8,128)(2,1)}, bf16[2,768,384]{2,1,0:T(8,128)(2,1)}, bf16[2,768,192]{2,1,0:T(8,128)(2,1)}) custom-call(bf16[2,768,384]{2,1,0:T(8,128)(2,1)} %copy-done.9, bf16[2,768,192]{2,1,0:T(8,128)(2,1)} %copy-done.13, bf16[2,768,384]{2,1,0:T(8,128)(2,1)} %copy-done.10, ...), custom_call_target="tpu_custom_call" | custom-call | tf_op jit(solution)/shard_map/pallas_call | solution.py:229
  473.6 2.5 add_convert_fusion
  482.9 3.5 add_convert_fusion.5
  504.7 3.6 add_convert_fusion.6
  519.6 14.2 %collective-permute-done.76 = bf16[384,384]{0,1:T(8,128)(2,1)} collective-permute-done((bf16[384,384]{0,1:T(8,128)(2,1)}, bf16[384,384]{0,1:T(8,128)(2,1)}, u32[]{:S(2)}, u32[]{:S(2)}) %collective-permute-start.76) | collective-permute-done | bytes 294944 | tf_op jit(solution)/shard_map/ppermute | solution.py:23
  543.1 4.0 collective-permute-done.71
  547.1 3.7 collective-permute-start.78
  551.0 4.4 collective-permute-done.78
  555.4 6.7 collective-permute-done.72
  562.5 6.5 collective-permute-done.73
  573.5 2.8 convert_reduce_fusion.5
  576.4 2.8 convert_reduce_fusion.4
  579.3 2.8 convert_reduce_fusion.6
  582.1 3.6 convert_reduce_fusion.7
  591.1 2.6 multiply_reduce_fusion.2
  593.7 3.1 convert_reduce_fusion.11
  627.3 3.9 convolution_convert_fusion.12
  645.3 4.5 collective-permute-done.89
  650.9 8.2 collective-permute-done.104
  659.8 7.2 collective-permute-done.90
  670.8 56.1 %shard_map.197 = (bf16[2,768,384]{2,1,0:T(8,128)(2,1)}, bf16[2,768,192]{2,1,0:T(8,128)(2,1)}, bf16[2,768,384]{2,1,0:T(8,128)(2,1)}, bf16[2,768,192]{2,1,0:T(8,128)(2,1)}) custom-call(bf16[2,768,384]{2,1,0:T(8,128)(2,1)} %copy-done.7, bf16[2,768,192]{2,1,0:T(8,128)(2,1)} %copy-done.11, bf16[2,768,384]{2,1,0:T(8,128)(2,1)} %copy-done.8, ...), custom_call_target="tpu_custom_call" | custom-call | tf_op jit(solution)/shard_map/pallas_call | solution.py:229
  761.3 3.4 add_convert_fusion.8
  765.9 3.0 add_convert_fusion.2
  777.7 3.4 add_convert_fusion.9
  787.7 19.8 %collective-permute-done.67 = bf16[384,384]{0,1:T(8,128)(2,1)S(1)} collective-permute-done((bf16[384,384]{0,1:T(8,128)(2,1)S(1)}, bf16[384,384]{0,1:T(8,128)(2,1)S(1)}, u32[]{:S(2)}, u32[]{:S(2)}) %collective-permute-start.67) | collective-permute-done | bytes 294944 | tf_op jit(solution)/shard_map/ppermute | solution.py:23
  808.6 6.5 collective-permute-done.68
  818.6 4.7 collective-permute-done.69
  824.6 5.9 collective-permute-done.63
  832.7 4.3 collective-permute-done.64
  840.3 6.2 multiply_reduce_fusion.3
  850.8 3.2 multiply_add_fusion
  885.8 4.4 collective-permute-done.83
  892.2 2.6 copy.515
  (1058 shorter events, 402.2 us)
Async XLA Ops:
  4.6 27.1 %collective-permute-start.5 = (f32[1,576]{1,0:T(1,128)S(1)}, f32[1,576]{1,0:T(1,128)S(1)}, u32[]{:S(2)}, u32[]{:S(2)}) collective-permute-start(f32[1,576]{1,0:T(1,128)S(1)} %concatenate.166), channel_id=1, source_target_pairs={{0,16},{4,20},{8,24},{12,28},{16,0},{20,4},{24,8},{28,12},{1,17},{... | collective-permute-start | bytes 6920 | tf_op jit(solution)/shard_map/ppermute | solution.py:23
  11.3 56.3 %collective-permute-start.34 = (bf16[96,384]{0,1:T(8,128)(2,1)}, bf16[96,384]{0,1:T(8,128)(2,1)}, u32[]{:S(2)}, u32[]{:S(2)}) collective-permute-start(bf16[96,384]{0,1:T(8,128)(2,1)} %pad_maximum_fusion.41), channel_id=1, source_target_pairs={{0,16},{4,20},{8,24},{12,28},{16,0},{20,4},{24,8},{28,12},{1,17},{... | collective-permute-start | bytes 221192 | tf_op jit(solution)/shard_map/ppermute | solution.py:23
  12.2 51.6 %collective-permute-start.30 = (bf16[96,384]{0,1:T(8,128)(2,1)}, bf16[96,384]{0,1:T(8,128)(2,1)}, u32[]{:S(2)}, u32[]{:S(2)}) collective-permute-start(bf16[96,384]{0,1:T(8,128)(2,1)} %pad_maximum_fusion.40), channel_id=1, source_target_pairs={{0,16},{4,20},{8,24},{12,28},{16,0},{20,4},{24,8},{28,12},{1,17},{... | collective-permute-start | bytes 221192 | tf_op jit(solution)/shard_map/ppermute | solution.py:23
  15.9 46.5 %collective-permute-start.10 = (bf16[96,384]{0,1:T(8,128)(2,1)}, bf16[96,384]{0,1:T(8,128)(2,1)}, u32[]{:S(2)}, u32[]{:S(2)}) collective-permute-start(bf16[96,384]{0,1:T(8,128)(2,1)} %pad_maximum_fusion.39), channel_id=1, source_target_pairs={{0,16},{4,20},{8,24},{12,28},{16,0},{20,4},{24,8},{28,12},{1,17},{... | collective-permute-start | bytes 221192 | tf_op jit(solution)/shard_map/ppermute | solution.py:23
  16.8 41.9 %collective-permute-start.1 = (bf16[96,384]{0,1:T(8,128)(2,1)}, bf16[96,384]{0,1:T(8,128)(2,1)}, u32[]{:S(2)}, u32[]{:S(2)}) collective-permute-start(bf16[96,384]{0,1:T(8,128)(2,1)} %pad_maximum_fusion.38), channel_id=1, source_target_pairs={{0,16},{4,20},{8,24},{12,28},{16,0},{20,4},{24,8},{28,12},{1,17},{... | collective-permute-start | bytes 221192 | tf_op jit(solution)/shard_map/ppermute | solution.py:23
  49.3 26.4 %collective-permute-start.41 = (bf16[96,768]{1,0:T(8,128)(2,1)S(1)}, bf16[96,768]{1,0:T(8,128)(2,1)S(1)}, u32[]{:S(2)}, u32[]{:S(2)}) collective-permute-start(bf16[96,768]{1,0:T(8,128)(2,1)S(1)} %copy-done.75), channel_id=1, source_target_pairs={{0,16},{4,20},{8,24},{12,28},{16,0},{20,4},{24,8},{28,12},{1,17},{... | collective-permute-start | bytes 442376 | tf_op jit(solution)/shard_map/ppermute | solution.py:23
  58.7 17.0 %collective-permute-start.17 = (bf16[96,768]{1,0:T(8,128)(2,1)S(1)}, bf16[96,768]{1,0:T(8,128)(2,1)S(1)}, u32[]{:S(2)}, u32[]{:S(2)}) collective-permute-start(bf16[96,768]{1,0:T(8,128)(2,1)S(1)} %copy-done.71), channel_id=1, source_target_pairs={{0,16},{4,20},{8,24},{12,28},{16,0},{20,4},{24,8},{28,12},{1,17},{... | collective-permute-start | bytes 442376 | tf_op jit(solution)/shard_map/ppermute | solution.py:23
  62.4 19.2 %collective-permute-start.44 = (bf16[96,768]{1,0:T(8,128)(2,1)S(1)}, bf16[96,768]{1,0:T(8,128)(2,1)S(1)}, u32[]{:S(2)}, u32[]{:S(2)}) collective-permute-start(bf16[96,768]{1,0:T(8,128)(2,1)S(1)} %copy-done.76), channel_id=1, source_target_pairs={{0,16},{4,20},{8,24},{12,28},{16,0},{20,4},{24,8},{28,12},{1,17},{... | collective-permute-start | bytes 442376 | tf_op jit(solution)/shard_map/ppermute | solution.py:23
  63.9 17.1 %collective-permute-start.20 = (bf16[96,768]{1,0:T(8,128)(2,1)S(1)}, bf16[96,768]{1,0:T(8,128)(2,1)S(1)}, u32[]{:S(2)}, u32[]{:S(2)}) collective-permute-start(bf16[96,768]{1,0:T(8,128)(2,1)S(1)} %copy-done.73), channel_id=1, source_target_pairs={{0,16},{4,20},{8,24},{12,28},{16,0},{20,4},{24,8},{28,12},{1,17},{... | collective-permute-start | bytes 442376 | tf_op jit(solution)/shard_map/ppermute | solution.py:23
  67.5 45.9 %collective-permute-start = (bf16[375,768]{1,0:T(8,128)(2,1)}, bf16[375,768]{1,0:T(8,128)(2,1)S(1)}, u32[]{:S(2)}, u32[]{:S(2)}) collective-permute-start(bf16[375,768]{1,0:T(8,128)(2,1)} %bitcast.544), channel_id=1, source_target_pairs={{0,2},{1,3},{2,0},{3,1},{4,6},{5,7},{6,4},{7,5},{8,10},{9,11},{10,... | collective-permute-start | bytes 1728008 | tf_op jit(solution)/shard_map/ppermute | solution.py:23
  75.7 19.0 %collective-permute-start.35 = (bf16[192,384]{0,1:T(8,128)(2,1)S(1)}, bf16[192,384]{0,1:T(8,128)(2,1)S(1)}, u32[]{:S(2)}, u32[]{:S(2)}) collective-permute-start(bf16[192,384]{0,1:T(8,128)(2,1)S(1)} %pad_maximum_fusion.36), channel_id=1, source_target_pairs={{0,8},{4,12},{8,0},{12,4},{16,24},{20,28},{24,16},{28,20},{1,9},{5... | collective-permute-start | bytes 442376 | tf_op jit(solution)/shard_map/ppermute | solution.py:23
  75.7 23.9 %collective-permute-start.31 = (bf16[192,384]{0,1:T(8,128)(2,1)S(1)}, bf16[192,384]{0,1:T(8,128)(2,1)S(1)}, u32[]{:S(2)}, u32[]{:S(2)}) collective-permute-start(bf16[192,384]{0,1:T(8,128)(2,1)S(1)} %pad_maximum_fusion.35), channel_id=1, source_target_pairs={{0,8},{4,12},{8,0},{12,4},{16,24},{20,28},{24,16},{28,20},{1,9},{5... | collective-permute-start | bytes 442376 | tf_op jit(solution)/shard_map/ppermute | solution.py:23
  81.6 16.9 %collective-permute-start.2 = (bf16[192,384]{0,1:T(8,128)(2,1)S(1)}, bf16[192,384]{0,1:T(8,128)(2,1)S(1)}, u32[]{:S(2)}, u32[]{:S(2)}) collective-permute-start(bf16[192,384]{0,1:T(8,128)(2,1)S(1)} %pad_maximum_fusion.33), channel_id=1, source_target_pairs={{0,8},{4,12},{8,0},{12,4},{16,24},{20,28},{24,16},{28,20},{1,9},{5... | collective-permute-start | bytes 442376 | tf_op jit(solution)/shard_map/ppermute | solution.py:23
  93.6 17.4 %collective-permute-start.45 = (bf16[192,768]{1,0:T(8,128)(2,1)S(1)}, bf16[192,768]{1,0:T(8,128)(2,1)S(1)}, u32[]{:S(2)}, u32[]{:S(2)}) collective-permute-start(bf16[192,768]{1,0:T(8,128)(2,1)S(1)} %pad_maximum_fusion.32), channel_id=1, source_target_pairs={{0,8},{4,12},{8,0},{12,4},{16,24},{20,28},{24,16},{28,20},{1,9},{5... | collective-permute-start | bytes 884744 | tf_op jit(solution)/shard_map/ppermute | solution.py:23
  98.5 81.1 %collective-permute-start.42 = (bf16[192,768]{1,0:T(8,128)(2,1)S(1)}, bf16[192,768]{1,0:T(8,128)(2,1)S(1)}, u32[]{:S(2)}, u32[]{:S(2)}) collective-permute-start(bf16[192,768]{1,0:T(8,128)(2,1)S(1)} %pad_maximum_fusion.31), channel_id=1, source_target_pairs={{0,8},{4,12},{8,0},{12,4},{16,24},{20,28},{24,16},{28,20},{1,9},{5... | collective-permute-start | bytes 884744 | tf_op jit(solution)/shard_map/ppermute | solution.py:23
  99.6 23.3 %collective-permute-start.18 = (bf16[192,768]{1,0:T(8,128)(2,1)S(1)}, bf16[192,768]{1,0:T(8,128)(2,1)S(1)}, u32[]{:S(2)}, u32[]{:S(2)}) collective-permute-start(bf16[192,768]{1,0:T(8,128)(2,1)S(1)} %pad_maximum_fusion.27), channel_id=1, source_target_pairs={{0,8},{4,12},{8,0},{12,4},{16,24},{20,28},{24,16},{28,20},{1,9},{5... | collective-permute-start | bytes 884744 | tf_op jit(solution)/shard_map/ppermute | solution.py:23
  110.9 19.5 %collective-permute-start.12 = (bf16[384,384]{0,1:T(8,128)(2,1)S(1)}, bf16[384,384]{0,1:T(8,128)(2,1)S(1)}, u32[]{:S(2)}, u32[]{:S(2)}) collective-permute-start(bf16[384,384]{0,1:T(8,128)(2,1)S(1)} %pad_maximum_fusion.26), channel_id=1, source_target_pairs={{0,4},{4,0},{8,12},{12,8},{16,20},{20,16},{24,28},{28,24},{1,5},{5... | collective-permute-start | bytes 884744 | tf_op jit(solution)/shard_map/ppermute | solution.py:23
  123.0 23.3 %collective-permute-start.15 = (bf16[768,768]{0,1:T(8,128)(2,1)S(1)}, bf16[768,768]{0,1:T(8,128)(2,1)S(1)}, u32[]{:S(2)}, u32[]{:S(2)}) collective-permute-start(bf16[768,768]{0,1:T(8,128)(2,1)S(1)} %add_convert_fusion.17), channel_id=1, source_target_pairs={{0,1},{1,0},{2,3},{3,2},{4,5},{5,4},{6,7},{7,6},{8,9},{9,8},{10,11... | collective-permute-start | bytes 3538952 | tf_op jit(solution)/shard_map/ppermute | solution.py:23
  130.5 49.3 %collective-permute-start.32 = (bf16[384,384]{0,1:T(8,128)(2,1)}, bf16[384,384]{0,1:T(8,128)(2,1)S(1)}, u32[]{:S(2)}, u32[]{:S(2)}) collective-permute-start(bf16[384,384]{0,1:T(8,128)(2,1)} %pad_maximum_fusion.29), channel_id=1, source_target_pairs={{0,4},{4,0},{8,12},{12,8},{16,20},{20,16},{24,28},{28,24},{1,5},{5... | collective-permute-start | bytes 884744 | tf_op jit(solution)/shard_map/ppermute | solution.py:23
  133.1 48.8 %collective-permute-start.26 = (bf16[384,768]{1,0:T(8,128)(2,1)S(1)}, bf16[384,768]{1,0:T(8,128)(2,1)S(1)}, u32[]{:S(2)}, u32[]{:S(2)}) collective-permute-start(bf16[384,768]{1,0:T(8,128)(2,1)S(1)} %pad_maximum_fusion.16), channel_id=1, source_target_pairs={{0,2},{1,3},{2,0},{3,1},{4,6},{5,7},{6,4},{7,5},{8,10},{9,11},{10,... | collective-permute-start | bytes 1769480 | tf_op jit(solution)/shard_map/ppermute | solution.py:23
  143.6 43.5 %collective-permute-start.22 = (bf16[384,768]{1,0:T(8,128)(2,1)S(1)}, bf16[384,768]{1,0:T(8,128)(2,1)}, u32[]{:S(2)}, u32[]{:S(2)}) collective-permute-start(bf16[384,768]{1,0:T(8,128)(2,1)S(1)} %pad_maximum_fusion.16), channel_id=1, source_target_pairs={{0,4},{4,0},{8,12},{12,8},{16,20},{20,16},{24,28},{28,24},{1,5},{5... | collective-permute-start | bytes 1769480 | tf_op jit(solution)/shard_map/ppermute | solution.py:23
  146.3 39.5 %collective-permute-start.19 = (bf16[384,768]{1,0:T(8,128)(2,1)S(1)}, bf16[384,768]{1,0:T(8,128)(2,1)}, u32[]{:S(2)}, u32[]{:S(2)}) collective-permute-start(bf16[384,768]{1,0:T(8,128)(2,1)S(1)} %pad_maximum_fusion.15), channel_id=1, source_target_pairs={{0,4},{4,0},{8,12},{12,8},{16,20},{20,16},{24,28},{28,24},{1,5},{5... | collective-permute-start | bytes 1769480 | tf_op jit(solution)/shard_map/ppermute | solution.py:23
  179.7 18.6 %collective-permute-start.16 = (bf16[768,768]{0,1:T(8,128)(2,1)S(1)}, bf16[768,768]{0,1:T(8,128)(2,1)S(1)}, u32[]{:S(2)}, u32[]{:S(2)}) collective-permute-start(bf16[768,768]{0,1:T(8,128)(2,1)S(1)} %add_convert_fusion.16), channel_id=1, source_target_pairs={{0,1},{1,0},{2,3},{3,2},{4,5},{5,4},{6,7},{7,6},{8,9},{9,8},{10,11... | collective-permute-start | bytes 3538952 | tf_op jit(solution)/shard_map/ppermute | solution.py:23
  179.8 139.8 %collective-permute-start.55 = (bf16[375,768]{1,0:T(8,128)(2,1)}, bf16[375,768]{1,0:T(8,128)(2,1)}, u32[]{:S(2)}, u32[]{:S(2)}) collective-permute-start(bf16[375,768]{1,0:T(8,128)(2,1)} %bitcast.499), channel_id=1, source_target_pairs={{0,2},{1,3},{2,0},{3,1},{4,6},{5,7},{6,4},{7,5},{8,10},{9,11},{10,... | collective-permute-start | bytes 1728008 | tf_op jit(solution)/shard_map/ppermute | solution.py:23
  185.8 58.1 %collective-permute-start.37 = (bf16[384,384]{0,1:T(8,128)(2,1)S(1)}, bf16[384,384]{0,1:T(8,128)(2,1)S(1)}, u32[]{:S(2)}, u32[]{:S(2)}) collective-permute-start(bf16[384,384]{0,1:T(8,128)(2,1)S(1)} %copy-done.148), channel_id=1, source_target_pairs={{0,2},{1,3},{2,0},{3,1},{4,6},{5,7},{6,4},{7,5},{8,10},{9,11},{10,... | collective-permute-start | bytes 884744 | tf_op jit(solution)/shard_map/ppermute | solution.py:23
  197.3 30.3 %collective-permute-start.25 = (bf16[768,768]{1,0:T(8,128)(2,1)S(1)}, bf16[768,768]{1,0:T(8,128)(2,1)S(1)}, u32[]{:S(2)}, u32[]{:S(2)}) collective-permute-start(bf16[768,768]{1,0:T(8,128)(2,1)S(1)} %pad_maximum_fusion.3), channel_id=1, source_target_pairs={{0,2},{1,3},{2,0},{3,1},{4,6},{5,7},{6,4},{7,5},{8,10},{9,11},{10,... | collective-permute-start | bytes 3538952 | tf_op jit(solution)/shard_map/ppermute | solution.py:23
  198.3 33.2 %collective-permute-start.24 = (bf16[768,768]{1,0:T(8,128)(2,1)S(1)}, bf16[768,768]{1,0:T(8,128)(2,1)S(1)}, u32[]{:S(2)}, u32[]{:S(2)}) collective-permute-start(bf16[768,768]{1,0:T(8,128)(2,1)S(1)} %pad_maximum_fusion.4), channel_id=1, source_target_pairs={{0,1},{1,0},{2,3},{3,2},{4,5},{5,4},{6,7},{7,6},{8,9},{9,8},{10,11... | collective-permute-start | bytes 3538952 | tf_op jit(solution)/shard_map/ppermute | solution.py:23
  200.5 44.0 %collective-permute-start.50 = (bf16[384,768]{1,0:T(8,128)(2,1)}, bf16[384,768]{1,0:T(8,128)(2,1)S(1)}, u32[]{:S(2)}, u32[]{:S(2)}) collective-permute-start(bf16[384,768]{1,0:T(8,128)(2,1)} %pad_maximum_fusion.19), channel_id=1, source_target_pairs={{0,2},{1,3},{2,0},{3,1},{4,6},{5,7},{6,4},{7,5},{8,10},{9,11},{10,... | collective-permute-start | bytes 1769480 | tf_op jit(solution)/shard_map/ppermute | solution.py:23
  243.9 26.7 %collective-permute-start.43 = (bf16[384,768]{1,0:T(8,128)(2,1)S(1)}, bf16[384,768]{1,0:T(8,128)(2,1)S(1)}, u32[]{:S(2)}, u32[]{:S(2)}) collective-permute-start(bf16[384,768]{1,0:T(8,128)(2,1)S(1)} %pad_maximum_fusion.18), channel_id=1, source_target_pairs={{0,4},{4,0},{8,12},{12,8},{16,20},{20,16},{24,28},{28,24},{1,5},{5... | collective-permute-start | bytes 1769480 | tf_op jit(solution)/shard_map/ppermute | solution.py:23
  244.6 24.0 %collective-permute-start.38 = (bf16[384,384]{0,1:T(8,128)(2,1)S(1)}, bf16[384,384]{0,1:T(8,128)(2,1)S(1)}, u32[]{:S(2)}, u32[]{:S(2)}) collective-permute-start(bf16[384,384]{0,1:T(8,128)(2,1)S(1)} %collective-permute-done.37), channel_id=1, source_target_pairs={{0,4},{4,0},{8,12},{12,8},{16,20},{20,16},{24,28},{28,24},{1,5},{5... | collective-permute-start | bytes 884744 | tf_op jit(solution)/shard_map/ppermute | solution.py:23
  246.0 35.2 %collective-permute-start.51 = (bf16[384,768]{1,0:T(8,128)(2,1)S(1)}, bf16[384,768]{1,0:T(8,128)(2,1)S(1)}, u32[]{:S(2)}, u32[]{:S(2)}) collective-permute-start(bf16[384,768]{1,0:T(8,128)(2,1)S(1)} %collective-permute-done.50), channel_id=1, source_target_pairs={{0,4},{4,0},{8,12},{12,8},{16,20},{20,16},{24,28},{28,24},{1,5},{5... | collective-permute-start | bytes 1769480 | tf_op jit(solution)/shard_map/ppermute | solution.py:23
  251.2 34.2 %collective-permute-start.39 = (bf16[768,768]{0,1:T(8,128)(2,1)S(1)}, bf16[768,768]{0,1:T(8,128)(2,1)S(1)}, u32[]{:S(2)}, u32[]{:S(2)}) collective-permute-start(bf16[768,768]{0,1:T(8,128)(2,1)S(1)} %add_convert_fusion.14), channel_id=1, source_target_pairs={{0,1},{1,0},{2,3},{3,2},{4,5},{5,4},{6,7},{7,6},{8,9},{9,8},{10,11... | collective-permute-start | bytes 3538952 | tf_op jit(solution)/shard_map/ppermute | solution.py:23
  270.6 56.9 %collective-permute-start.46 = (bf16[384,768]{1,0:T(8,128)(2,1)}, bf16[384,768]{1,0:T(8,128)(2,1)}, u32[]{:S(2)}, u32[]{:S(2)}) collective-permute-start(bf16[384,768]{1,0:T(8,128)(2,1)} %pad_maximum_fusion.19), channel_id=1, source_target_pairs={{0,4},{4,0},{8,12},{12,8},{16,20},{20,16},{24,28},{28,24},{1,5},{5... | collective-permute-start | bytes 1769480 | tf_op jit(solution)/shard_map/ppermute | solution.py:23
  281.2 48.2 %collective-permute-start.49 = (bf16[768,768]{1,0:T(8,128)(2,1)}, bf16[768,768]{1,0:T(8,128)(2,1)}, u32[]{:S(2)}, u32[]{:S(2)}) collective-permute-start(bf16[768,768]{1,0:T(8,128)(2,1)} %pad_maximum_fusion.6), channel_id=1, source_target_pairs={{0,2},{1,3},{2,0},{3,1},{4,6},{5,7},{6,4},{7,5},{8,10},{9,11},{10,... | collective-permute-start | bytes 3538952 | tf_op jit(solution)/shard_map/ppermute | solution.py:23
  284.0 45.4 %collective-permute-start.53 = (bf16[768,768]{1,0:T(8,128)(2,1)S(1)}, bf16[768,768]{1,0:T(8,128)(2,1)}, u32[]{:S(2)}, u32[]{:S(2)}) collective-permute-start(bf16[768,768]{1,0:T(8,128)(2,1)S(1)} %constant_dynamic-update-slice_fusion.2), channel_id=1, source_target_pairs={{0,1},{1,0},{2,3},{3,2},{4,5},{5,4},{6,7},{7,6},{8,9},{9,8},{10,11... | collective-permute-start | bytes 3538952 | tf_op jit(solution)/shard_map/ppermute | solution.py:23
  328.9 23.9 %collective-permute-start.48 = (bf16[768,768]{1,0:T(8,128)(2,1)S(1)}, bf16[768,768]{1,0:T(8,128)(2,1)S(1)}, u32[]{:S(2)}, u32[]{:S(2)}) collective-permute-start(bf16[768,768]{1,0:T(8,128)(2,1)S(1)} %pad_maximum_fusion.7), channel_id=1, source_target_pairs={{0,1},{1,0},{2,3},{3,2},{4,5},{5,4},{6,7},{7,6},{8,9},{9,8},{10,11... | collective-permute-start | bytes 3538952 | tf_op jit(solution)/shard_map/ppermute | solution.py:23
  381.2 26.6 %collective-permute-start.56 = (bf16[768,768]{0,1:T(8,128)(2,1)S(1)}, bf16[768,768]{0,1:T(8,128)(2,1)}, u32[]{:S(2)}, u32[]{:S(2)}) collective-permute-start(bf16[768,768]{0,1:T(8,128)(2,1)S(1)} %get-tuple-element.150), channel_id=1, source_target_pairs={{0,1},{1,0},{2,3},{3,2},{4,5},{5,4},{6,7},{7,6},{8,9},{9,8},{10,11... | collective-permute-start | bytes 3538952 | tf_op jit(solution)/shard_map/ppermute | solution.py:23
  384.6 87.8 %collective-permute-start.100 = (bf16[768,768]{1,0:T(8,128)(2,1)}, bf16[768,768]{1,0:T(8,128)(2,1)}, u32[]{:S(2)}, u32[]{:S(2)}) collective-permute-start(bf16[768,768]{1,0:T(8,128)(2,1)} %convolution_convert_fusion), channel_id=1, source_target_pairs={{0,1},{1,0},{2,3},{3,2},{4,5},{5,4},{6,7},{7,6},{8,9},{9,8},{10,11... | collective-permute-start | bytes 3538952 | tf_op jit(solution)/shard_map/ppermute | solution.py:23
  384.7 98.2 %collective-permute-start.86 = (bf16[768,768]{1,0:T(8,128)(2,1)}, bf16[768,768]{1,0:T(8,128)(2,1)}, u32[]{:S(2)}, u32[]{:S(2)}) collective-permute-start(bf16[768,768]{1,0:T(8,128)(2,1)} %convolution_convert_fusion.8), channel_id=1, source_target_pairs={{0,1},{1,0},{2,3},{3,2},{4,5},{5,4},{6,7},{7,6},{8,9},{9,8},{10,11... | collective-permute-start | bytes 3538952 | tf_op jit(solution)/shard_map/ppermute | solution.py:23
  386.4 112.7 %collective-permute-start.98 = (bf16[768,768]{1,0:T(8,128)(2,1)}, bf16[768,768]{1,0:T(8,128)(2,1)}, u32[]{:S(2)}, u32[]{:S(2)}) collective-permute-start(bf16[768,768]{1,0:T(8,128)(2,1)} %convolution_convert_fusion.2), channel_id=1, source_target_pairs={{0,1},{1,0},{2,3},{3,2},{4,5},{5,4},{6,7},{7,6},{8,9},{9,8},{10,11... | collective-permute-start | bytes 3538952 | tf_op jit(solution)/shard_map/ppermute | solution.py:23
  403.1 99.8 %collective-permute-start.85 = (bf16[768,768]{1,0:T(8,128)(2,1)}, bf16[768,768]{1,0:T(8,128)(2,1)}, u32[]{:S(2)}, u32[]{:S(2)}) collective-permute-start(bf16[768,768]{1,0:T(8,128)(2,1)} %convolution_convert_fusion.10), channel_id=1, source_target_pairs={{0,1},{1,0},{2,3},{3,2},{4,5},{5,4},{6,7},{7,6},{8,9},{9,8},{10,11... | collective-permute-start | bytes 3538952 | tf_op jit(solution)/shard_map/ppermute | solution.py:23
  477.0 60.6 %collective-permute-start.101 = (bf16[384,768]{1,0:T(8,128)(2,1)}, bf16[384,768]{1,0:T(8,128)(2,1)}, u32[]{:S(2)}, u32[]{:S(2)}) collective-permute-start(bf16[384,768]{1,0:T(8,128)(2,1)} %slice.826), channel_id=1, source_target_pairs={{0,4},{4,0},{8,12},{12,8},{16,20},{20,16},{24,28},{28,24},{1,5},{5... | collective-permute-start | bytes 1769480 | tf_op jit(solution)/shard_map/ppermute | solution.py:23
  486.4 119.6 %collective-permute-start.87 = (bf16[768,768]{1,0:T(8,128)(2,1)}, bf16[768,768]{1,0:T(8,128)(2,1)}, u32[]{:S(2)}, u32[]{:S(2)}) collective-permute-start(bf16[768,768]{1,0:T(8,128)(2,1)} %add_convert_fusion.5), channel_id=1, source_target_pairs={{0,2},{1,3},{2,0},{3,1},{4,6},{5,7},{6,4},{7,5},{8,10},{9,11},{10,... | collective-permute-start | bytes 3538952 | tf_op jit(solution)/shard_map/ppermute | solution.py:23
  490.1 28.9 %collective-permute-start.74 = (bf16[384,384]{0,1:T(8,128)(2,1)}, bf16[384,384]{0,1:T(8,128)(2,1)}, u32[]{:S(2)}, u32[]{:S(2)}) collective-permute-start(bf16[384,384]{0,1:T(8,128)(2,1)} %pad_maximum_fusion.22), channel_id=1, source_target_pairs={{0,4},{4,0},{8,12},{12,8},{16,20},{20,16},{24,28},{28,24},{1,5},{5... | collective-permute-start | bytes 884744 | tf_op jit(solution)/shard_map/ppermute | solution.py:23
  503.0 32.2 %collective-permute-start.70 = (bf16[768,384]{0,1:T(8,128)(2,1)}, bf16[768,384]{0,1:T(8,128)(2,1)}, u32[]{:S(2)}, u32[]{:S(2)}) collective-permute-start(bf16[768,384]{0,1:T(8,128)(2,1)} %fusion.65), channel_id=1, source_target_pairs={{0,2},{1,3},{2,0},{3,1},{4,6},{5,7},{6,4},{7,5},{8,10},{9,11},{10,... | collective-permute-start | bytes 1769480 | tf_op jit(solution)/shard_map/ppermute | solution.py:23
  512.8 20.9 %collective-permute-start.76 = (bf16[384,384]{0,1:T(8,128)(2,1)}, bf16[384,384]{0,1:T(8,128)(2,1)}, u32[]{:S(2)}, u32[]{:S(2)}) collective-permute-start(bf16[384,384]{0,1:T(8,128)(2,1)} %add_convert_fusion.35), channel_id=1, source_target_pairs={{0,2},{1,3},{2,0},{3,1},{4,6},{5,7},{6,4},{7,5},{8,10},{9,11},{10,... | collective-permute-start | bytes 884744 | tf_op jit(solution)/shard_map/ppermute | solution.py:23
  519.0 112.2 %collective-permute-start.99 = (bf16[384,768]{1,0:T(8,128)(2,1)}, bf16[384,768]{1,0:T(8,128)(2,1)}, u32[]{:S(2)}, u32[]{:S(2)}) collective-permute-start(bf16[384,768]{1,0:T(8,128)(2,1)} %slice.824), channel_id=1, source_target_pairs={{0,4},{4,0},{8,12},{12,8},{16,20},{20,16},{24,28},{28,24},{1,5},{5... | collective-permute-start | bytes 1769480 | tf_op jit(solution)/shard_map/ppermute | solution.py:23
  533.8 35.4 %collective-permute-start.57 = (bf16[768,768]{0,1:T(8,128)(2,1)}, bf16[768,768]{0,1:T(8,128)(2,1)S(1)}, u32[]{:S(2)}, u32[]{:S(2)}) collective-permute-start(bf16[768,768]{0,1:T(8,128)(2,1)} %add_convert_fusion.11), channel_id=1, source_target_pairs={{0,1},{1,0},{2,3},{3,2},{4,5},{5,4},{6,7},{7,6},{8,9},{9,8},{10,11... | collective-permute-start | bytes 3538952 | tf_op jit(solution)/shard_map/ppermute | solution.py:23
  542.5 89.0 %collective-permute-start.102 = (bf16[384,768]{1,0:T(8,128)(2,1)}, bf16[384,768]{1,0:T(8,128)(2,1)}, u32[]{:S(2)}, u32[]{:S(2)}) collective-permute-start(bf16[384,768]{1,0:T(8,128)(2,1)} %add_convert_fusion.23), channel_id=1, source_target_pairs={{0,2},{1,3},{2,0},{3,1},{4,6},{5,7},{6,4},{7,5},{8,10},{9,11},{10,... | collective-permute-start | bytes 1769480 | tf_op jit(solution)/shard_map/ppermute | solution.py:23
  598.2 69.5 %collective-permute-start.58 = (bf16[768,768]{0,1:T(8,128)(2,1)S(1)}, bf16[768,768]{0,1:T(8,128)(2,1)}, u32[]{:S(2)}, u32[]{:S(2)}) collective-permute-start(bf16[768,768]{0,1:T(8,128)(2,1)S(1)} %get-tuple-element.144), channel_id=1, source_target_pairs={{0,1},{1,0},{2,3},{3,2},{4,5},{5,4},{6,7},{7,6},{8,9},{9,8},{10,11... | collective-permute-start | bytes 3538952 | tf_op jit(solution)/shard_map/ppermute | solution.py:23
  609.5 24.5 %collective-permute-start.88 = (bf16[384,768]{1,0:T(8,128)(2,1)}, bf16[384,768]{1,0:T(8,128)(2,1)}, u32[]{:S(2)}, u32[]{:S(2)}) collective-permute-start(bf16[384,768]{1,0:T(8,128)(2,1)} %slice.810), channel_id=1, source_target_pairs={{0,4},{4,0},{8,12},{12,8},{16,20},{20,16},{24,28},{28,24},{1,5},{5... | collective-permute-start | bytes 1769480 | tf_op jit(solution)/shard_map/ppermute | solution.py:23
  622.1 154.5 %collective-permute-start.79 = (bf16[768,768]{1,0:T(8,128)(2,1)}, bf16[768,768]{1,0:T(8,128)(2,1)}, u32[]{:S(2)}, u32[]{:S(2)}) collective-permute-start(bf16[768,768]{1,0:T(8,128)(2,1)} %convolution_convert_fusion.14), channel_id=1, source_target_pairs={{0,1},{1,0},{2,3},{3,2},{4,5},{5,4},{6,7},{7,6},{8,9},{9,8},{10,11... | collective-permute-start | bytes 3538952 | tf_op jit(solution)/shard_map/ppermute | solution.py:23
  631.2 129.2 %collective-permute-start.80 = (bf16[768,768]{1,0:T(8,128)(2,1)}, bf16[768,768]{1,0:T(8,128)(2,1)}, u32[]{:S(2)}, u32[]{:S(2)}) collective-permute-start(bf16[768,768]{1,0:T(8,128)(2,1)} %convolution_convert_fusion.12), channel_id=1, source_target_pairs={{0,1},{1,0},{2,3},{3,2},{4,5},{5,4},{6,7},{7,6},{8,9},{9,8},{10,11... | collective-permute-start | bytes 3538952 | tf_op jit(solution)/shard_map/ppermute | solution.py:23
  644.1 108.0 %collective-permute-start.91 = (bf16[768,768]{1,0:T(8,128)(2,1)}, bf16[768,768]{1,0:T(8,128)(2,1)}, u32[]{:S(2)}, u32[]{:S(2)}) collective-permute-start(bf16[768,768]{1,0:T(8,128)(2,1)} %convolution_convert_fusion.6), channel_id=1, source_target_pairs={{0,1},{1,0},{2,3},{3,2},{4,5},{5,4},{6,7},{7,6},{8,9},{9,8},{10,11... | collective-permute-start | bytes 3538952 | tf_op jit(solution)/shard_map/ppermute | solution.py:23
  667.0 97.7 %collective-permute-start.93 = (bf16[768,768]{1,0:T(8,128)(2,1)}, bf16[768,768]{1,0:T(8,128)(2,1)}, u32[]{:S(2)}, u32[]{:S(2)}) collective-permute-start(bf16[768,768]{1,0:T(8,128)(2,1)} %convolution_convert_fusion.4), channel_id=1, source_target_pairs={{0,1},{1,0},{2,3},{3,2},{4,5},{5,4},{6,7},{7,6},{8,9},{9,8},{10,11... | collective-permute-start | bytes 3538952 | tf_op jit(solution)/shard_map/ppermute | solution.py:23
  747.9 38.8 %collective-permute-start.65 = (bf16[384,384]{0,1:T(8,128)(2,1)S(1)}, bf16[384,384]{0,1:T(8,128)(2,1)S(1)}, u32[]{:S(2)}, u32[]{:S(2)}) collective-permute-start(bf16[384,384]{0,1:T(8,128)(2,1)S(1)} %pad_maximum_fusion.24), channel_id=1, source_target_pairs={{0,4},{4,0},{8,12},{12,8},{16,20},{20,16},{24,28},{28,24},{1,5},{5... | collective-permute-start | bytes 884744 | tf_op jit(solution)/shard_map/ppermute | solution.py:23
  752.2 32.9 %collective-permute-start.66 = (bf16[384,384]{0,1:T(8,128)(2,1)S(1)}, bf16[384,384]{0,1:T(8,128)(2,1)S(1)}, u32[]{:S(2)}, u32[]{:S(2)}) collective-permute-start(bf16[384,384]{0,1:T(8,128)(2,1)S(1)} %pad_maximum_fusion.23), channel_id=1, source_target_pairs={{0,4},{4,0},{8,12},{12,8},{16,20},{20,16},{24,28},{28,24},{1,5},{5... | collective-permute-start | bytes 884744 | tf_op jit(solution)/shard_map/ppermute | solution.py:23
  760.4 47.4 %collective-permute-start.61 = (bf16[768,384]{0,1:T(8,128)(2,1)S(1)}, bf16[768,384]{0,1:T(8,128)(2,1)S(1)}, u32[]{:S(2)}, u32[]{:S(2)}) collective-permute-start(bf16[768,384]{0,1:T(8,128)(2,1)S(1)} %fusion.60), channel_id=1, source_target_pairs={{0,2},{1,3},{2,0},{3,1},{4,6},{5,7},{6,4},{7,5},{8,10},{9,11},{10,... | collective-permute-start | bytes 1769480 | tf_op jit(solution)/shard_map/ppermute | solution.py:23
  764.7 89.5 %collective-permute-start.81 = (bf16[768,768]{1,0:T(8,128)(2,1)}, bf16[768,768]{1,0:T(8,128)(2,1)}, u32[]{:S(2)}, u32[]{:S(2)}) collective-permute-start(bf16[768,768]{1,0:T(8,128)(2,1)} %add_convert_fusion.8), channel_id=1, source_target_pairs={{0,2},{1,3},{2,0},{3,1},{4,6},{5,7},{6,4},{7,5},{8,10},{9,11},{10,... | collective-permute-start | bytes 3538952 | tf_op jit(solution)/shard_map/ppermute | solution.py:23
  776.6 83.0 %collective-permute-start.92 = (bf16[384,768]{1,0:T(8,128)(2,1)}, bf16[384,768]{1,0:T(8,128)(2,1)}, u32[]{:S(2)}, u32[]{:S(2)}) collective-permute-start(bf16[384,768]{1,0:T(8,128)(2,1)} %slice.816), channel_id=1, source_target_pairs={{0,4},{4,0},{8,12},{12,8},{16,20},{20,16},{24,28},{28,24},{1,5},{5... | collective-permute-start | bytes 1769480 | tf_op jit(solution)/shard_map/ppermute | solution.py:23
  785.1 22.4 %collective-permute-start.67 = (bf16[384,384]{0,1:T(8,128)(2,1)S(1)}, bf16[384,384]{0,1:T(8,128)(2,1)S(1)}, u32[]{:S(2)}, u32[]{:S(2)}) collective-permute-start(bf16[384,384]{0,1:T(8,128)(2,1)S(1)} %add_convert_fusion.39), channel_id=1, source_target_pairs={{0,2},{1,3},{2,0},{3,1},{4,6},{5,7},{6,4},{7,5},{8,10},{9,11},{10,... | collective-permute-start | bytes 884744 | tf_op jit(solution)/shard_map/ppermute | solution.py:23
  786.7 29.4 %collective-permute-start.94 = (bf16[384,768]{1,0:T(8,128)(2,1)S(1)}, bf16[384,768]{1,0:T(8,128)(2,1)S(1)}, u32[]{:S(2)}, u32[]{:S(2)}) collective-permute-start(bf16[384,768]{1,0:T(8,128)(2,1)S(1)} %slice.818), channel_id=1, source_target_pairs={{0,4},{4,0},{8,12},{12,8},{16,20},{20,16},{24,28},{28,24},{1,5},{5... | collective-permute-start | bytes 1769480 | tf_op jit(solution)/shard_map/ppermute | solution.py:23
  807.5 32.7 %collective-permute-start.59 = (bf16[768,768]{0,1:T(8,128)(2,1)}, bf16[768,768]{0,1:T(8,128)(2,1)}, u32[]{:S(2)}, u32[]{:S(2)}) collective-permute-start(bf16[768,768]{0,1:T(8,128)(2,1)} %add_convert_fusion.10), channel_id=1, source_target_pairs={{0,1},{1,0},{2,3},{3,2},{4,5},{5,4},{6,7},{7,6},{8,9},{9,8},{10,11... | collective-permute-start | bytes 3538952 | tf_op jit(solution)/shard_map/ppermute | solution.py:23
  823.3 36.3 %collective-permute-start.95 = (bf16[384,768]{1,0:T(8,128)(2,1)}, bf16[384,768]{1,0:T(8,128)(2,1)}, u32[]{:S(2)}, u32[]{:S(2)}) collective-permute-start(bf16[384,768]{1,0:T(8,128)(2,1)} %add_convert_fusion.26), channel_id=1, source_target_pairs={{0,2},{1,3},{2,0},{3,1},{4,6},{5,7},{6,4},{7,5},{8,10},{9,11},{10,... | collective-permute-start | bytes 1769480 | tf_op jit(solution)/shard_map/ppermute | solution.py:23
  (284 other events, 4145.5 us)

commit v2 on v1

--- a/solution.py
+++ b/solution.py
@@ -39,36 +39,97 @@
     return result
 
 
-def spread(block, y_last):
+def together(*values):
+    return lax.optimization_barrier(values)
+
+
+def spread(first, second, small=None):
     masks = dp_masks()
-    early = masks if y_last else masks[:-1]
-    for mask in early:
-        block = jnp.concatenate([block, exchange(block, "dp", mask)], axis=0)
-    other = exchange(block, "tensor", 2)
-    if y_last:
-        return [block, other]
-    return [
-        jnp.concatenate([part, exchange(part, "dp", masks[-1])], axis=0) for part in (block, other)
-    ]
+    cut = first.shape[1]
+    block = jnp.concatenate([first, second], axis=1)
+    for mask in masks[:-1]:
+        more = exchange(block, "dp", mask)
+        if small is not None:
+            more, small_more = together(more, exchange(small, "dp", mask))
+            small = jnp.concatenate([small, small_more], axis=0)
+        block = jnp.concatenate([block, more], axis=0)
+    if small is not None:
+        small = jnp.concatenate([small, exchange(small, "dp", masks[-1])], axis=0)
+        small = jnp.stack([small, exchange(small, "tensor", 1)])
+        small = jnp.stack([small, exchange(small, "tensor", 2)])
+    first, second = block[:, :cut], block[:, cut:]
+    first, second = together(first, second)
+    first_more, second_other = together(
+        exchange(first, "dp", masks[-1]), exchange(second, "tensor", 2)
+    )
+    first = jnp.concatenate([first, first_more], axis=0)
+    second = jnp.stack([second, second_other])
+    first, second = together(first, second)
+    first_other, second_more = together(
+        exchange(first, "tensor", 2), exchange(second, "dp", masks[-1])
+    )
+    second = [jnp.concatenate([second[i], second_more[i]], axis=0) for i in range(2)]
+    return [first, first_other], second, second_other, small
+
+
+def behind(values, *tokens):
+    return together(*values, *tokens)[: len(values)]
 
 
 def add_low(kept, received):
     return (kept.astype(f32) + received.astype(f32)).astype(bf16)
 
 
-def halve(value, mask):
-    half = value.shape[0] // 2
-    return add_low(value[:half], exchange(value[half:], "dp", mask))
-
-
-def fold(own, other, y_first):
-    masks = dp_masks()
-    if not y_first:
-        own, other = halve(own, masks[-1]), halve(other, masks[-1])
-    own = add_low(own, exchange(other, "tensor", 2))
-    for mask in reversed(masks if y_first else masks[:-1]):
-        own = halve(own, mask)
-    return own
+def near_one(first, second):
+    mask = dp_masks()[-1]
+    half = first.shape[1] // 2
+    return (
+        add_low(first[0], exchange(first[1], "tensor", 2)),
+        add_low(second[:, :half], exchange(second[:, half:], "dp", mask)),
+    )
+
+
+def near_two(first, second):
+    mask = dp_masks()[-1]
+    half = first.shape[0] // 2
+    return (
+        add_low(first[:half], exchange(first[half:], "dp", mask)),
+        add_low(second[0], exchange(second[1], "tensor", 2)),
+    )
+
+
+def far(value, masks):
+    for mask in masks:
+        half = value.shape[0] // 2
+        value = add_low(value[:half], exchange(value[half:], "dp", mask))
+    return value
+
+
+class Folding:
+    def __init__(self, qk, vo, up, down):
+        masks = dp_masks()[-2::-1]
+        self.masks = masks[:-1], masks[-1:]
+        self.attn = together(qk, vo)
+        self.feed = jnp.concatenate([up, down], axis=1)
+        self.step = 0
+
+    def advance(self):
+        step = self.step
+        self.step += 1
+        if step < 2:
+            attn = (near_one, near_two)[step](*self.attn)
+            *attn, self.feed = together(*attn, far(self.feed, self.masks[step]))
+            self.attn = attn if step == 0 else jnp.concatenate(attn, axis=1)
+        else:
+            (self.attn,) = together(far(self.attn, self.masks[step - 2]))
+
+    def token(self):
+        return (self.feed, self.attn) if self.step > 1 else (self.feed, *self.attn)
+
+    def result(self):
+        half, low = self.attn.shape[1] // 2, self.feed.shape[1] // 2
+        parts = self.attn[:, :half], self.attn[:, half:], self.feed[:, :low], self.feed[:, low:]
+        return [part.astype(f32) for part in parts]
 
 
 def split_low(value):
@@ -223,19 +284,26 @@
             dv[0, :, low:high] = dv_s[h, at, :][:, :HD].astype(bf16)
 
 
-def attend_back(row_count, quarter, qk_a, v_a, qk_b, v_b, o_a, o_b, do_a, do_b, lse):
-    groups, rows, wide = v_a.shape
+def attend_back(group, row_count, quarter, qk_a, v_a, qk_b, v_b, o_a, o_b, do_a, do_b, lse):
+    _, rows, wide = v_a.shape
     heads = wide // HD
+
+    def block_of(shape):
+        return pl.BlockSpec((1,) + shape, lambda t: (group, 0, 0))
+
+    def out_block(shape):
+        return pl.BlockSpec((1,) + shape, lambda t: (0, 0, 0))
+
     return pl.pallas_call(
         functools.partial(attend_back_kernel, row_count, quarter, min(256, rows)),
-        grid=(groups,),
+        grid=(1,),
         in_specs=[block_of((rows, 2 * wide)), block_of((rows, wide))] * 2
         + [block_of((rows, wide))] * 4
         + [block_of((2 * rows, 8))],
-        out_specs=[block_of((rows, 2 * wide)), block_of((rows, wide))] * 2,
+        out_specs=[out_block((rows, 2 * wide)), out_block((rows, wide))] * 2,
         out_shape=[
-            jax.ShapeDtypeStruct((groups, rows, 2 * wide), bf16),
-            jax.ShapeDtypeStruct((groups, rows, wide), bf16),
+            jax.ShapeDtypeStruct((1, rows, 2 * wide), bf16),
+            jax.ShapeDtypeStruct((1, rows, wide), bf16),
         ]
         * 2,
         scratch_shapes=[
@@ -273,6 +341,101 @@
     share = 0.5 * (1.0 + lax.erf(value * math.sqrt(0.5)))
     density = jnp.exp(-0.5 * value * value) * (1.0 / math.sqrt(2.0 * math.pi))
     return (value * share).astype(bf16), (share + value * density).astype(bf16)
+
+
+def feed_kernel(normed, base, bias, *refs):
+    ups, downs, activated, slopes, total = refs[:4], refs[4:8], refs[8:12], refs[12:16], refs[16]
+    rows_in = normed[...]
+    for t in range(4):
+        upward = nn_dot(rows_in, ups[t][...]) + bias[t : t + 1, :]
+        activated[t][...], slopes[t][...] = gelu_both(upward)
+    joined = jnp.concatenate([ref[...] for ref in activated], axis=1)
+    down = jnp.concatenate([ref[...] for ref in downs], axis=1)
+    share = nt_dot(joined, down)
+
+    @pl.when(pl.program_id(0) == 0)
+    def _():
+        total[...] = base[...] + share
+
+    @pl.when(pl.program_id(0) > 0)
+    def _():
+        total[...] += share
+
+
+def whole_block(shape):
+    return pl.BlockSpec(shape, lambda j: (0, 0))
+
+
+def column_block(rows, step):
+    return pl.BlockSpec((rows, step), lambda j: (0, j))
+
+
+def feed(normed, base, bias, ups, downs):
+    rows, width = normed.shape
+    hidden = bias.shape[1]
+    step = min(256, hidden)
+    return pl.pallas_call(
+        feed_kernel,
+        grid=(hidden // step,),
+        in_specs=[whole_block((rows, width))] * 2
+        + [column_block(4, step)]
+        + [column_block(width, step)] * 8,
+        out_specs=[column_block(rows, step)] * 8 + [whole_block((rows, width))],
+        out_shape=[jax.ShapeDtypeStruct((rows, hidden), bf16)] * 8
+        + [jax.ShapeDtypeStruct((rows, width), f32)],
+        compiler_params=pltpu.CompilerParams(vmem_limit_bytes=56 * 2**20),
+    )(normed, base, bias, *ups, *downs)
+
+
+def feed_back_kernel(normed, grad, *refs):
+    ups, downs, activated, slopes = refs[:4], refs[4:8], refs[8:12], refs[12:16]
+    own, other, bias_grad, total, normed_t, grad_t = refs[16:]
+
+    @pl.when(pl.program_id(0) == 0)
+    def _():
+        normed_t[...] = jnp.transpose(normed[...].astype(f32)).astype(bf16)
+        grad_t[...] = jnp.transpose(grad[...].astype(f32)).astype(bf16)
+
+    grad_rows = grad[...]
+    grad_ups = []
+    for t in range(4):
+        grad_act = nn_dot(grad_rows, downs[t][...])
+        scaled = grad_act * slopes[t][...].astype(f32)
+        grad_ups.append(scaled.astype(bf16))
+        bias_grad[t : t + 1, :] = jnp.sum(scaled, axis=0, keepdims=True)
+        dest = (own, other)[t % 2]
+        dest[t // 2] = nn_dot(normed_t[...], grad_ups[t]).astype(bf16)
+        dest[2 + t // 2] = nn_dot(grad_t[...], activated[t][...]).astype(bf16)
+    joined = jnp.concatenate(grad_ups, axis=1)
+    up = jnp.concatenate([ref[...] for ref in ups], axis=1)
+    share = nt_dot(joined, up)
+
+    @pl.when(pl.program_id(0) == 0)
+    def _():
+        total[...] = share
+
+    @pl.when(pl.program_id(0) > 0)
+    def _():
+        total[...] += share
+
+
+def feed_back(normed, grad, ups, downs, activated, slopes):
+    rows, width = normed.shape
+    hidden = activated[0].shape[1]
+    step = min(256, hidden)
+    stack = pl.BlockSpec((4, width, step), lambda j: (0, 0, j))
+    return pl.pallas_call(
+        feed_back_kernel,
+        grid=(hidden // step,),
+        in_specs=[whole_block((rows, width))] * 2
+        + [column_block(width, step)] * 8
+        + [column_block(rows, step)] * 8,
+        out_specs=[stack] * 2 + [column_block(4, step), whole_block((rows, width))],
+        out_shape=[jax.ShapeDtypeStruct((4, width, hidden), bf16)] * 2
+        + [jax.ShapeDtypeStruct((4, hidden), f32), jax.ShapeDtypeStruct((rows, width), f32)],
+        scratch_shapes=[pltpu.VMEM((width, rows), bf16)] * 2,
+        compiler_params=pltpu.CompilerParams(vmem_limit_bytes=60 * 2**20),
+    )(normed, grad, *ups, *downs, *activated, *slopes)
 
 
 def local(
@@ -306,22 +469,6 @@
     small_parts = (norm_gains, norm_shifts, out_biases, qv_bias, up_bias)
     small_sizes = [part.size for part in small_parts]
     small = jnp.concatenate([part.reshape(1, -1) for part in small_parts], axis=1)
-    for mask in dp_masks():
-        small = jnp.concatenate([small, exchange(small, "dp", mask)], axis=0)
-    small = jnp.stack([small, exchange(small, "tensor", 1)])
-    small = jnp.stack([small, exchange(small, "tensor", 2)])
-    small = small.reshape(4, count_dp, -1)
-    by_part = jnp.split(small, [sum(small_sizes[: i + 1]) for i in range(4)], axis=2)
-
-    def by_width(part):
-        part = jnp.take(part, t_order, axis=0).reshape(4, count_dp, layers, 2, -1)
-        return part.transpose(2, 3, 1, 0, 4).reshape(layers, 2, width)
-
-    gain_all, shift_all, obias_all = [by_width(part) for part in by_part[:3]]
-    qv_all = jnp.take(by_part[3][0::2], place_of, axis=1).reshape(2, count_dp, layers, 2, -1)
-    qv_all = qv_all.transpose(2, 3, 0, 1, 4).reshape(layers, 2, 2, wide)
-    up_all = jnp.take(by_part[4], place_of, axis=1).reshape(4, count_dp, layers, -1)
-    up_all = up_all.transpose(2, 0, 1, 3).reshape(layers, 4, hidden)
 
     source = jnp.repeat(block_at, block) * block + jnp.tile(jnp.arange(block), count_dp)
     to_relative = (jnp.arange(width)[:, None] == source[None, :]).astype(bf16)
@@ -345,21 +492,51 @@
     current = take_clip(frames)
     gradient = take_clip(cotangent)
 
-    weights = []
-    for at in range(layers):
+    def attn_blocks(at):
         qk = jnp.concatenate([qkv_weight[at, :, 0], qkv_weight[at, :, 1]], axis=1)
-        vo = jnp.concatenate([qkv_weight[at, :, 2], out_weight[at].T], axis=1)
-        w_qk = jnp.stack(spread(qk, True))
-        w_vo = jnp.stack(spread(vo, False))
-        w_up = spread(up_weight[at], True)
-        w_down = spread(down_weight[at].T, False)
-        w_up = [
-            w_up[0], exchange(w_up[0], "tensor", 1), w_up[1], exchange(w_up[1], "tensor", 1)
+        return qk, jnp.concatenate([qkv_weight[at, :, 2], out_weight[at].T], axis=1)
+
+    def feed_blocks(at):
+        return up_weight[at], down_weight[at].T
+
+    def attn_weights(qk, vo):
+        vo = jnp.stack(vo)
+        return jnp.stack(qk), vo[:, :, :wide], vo[:, :, wide:]
+
+    def feed_weights(ups, downs):
+        ups = [ups[0], exchange(ups[0], "tensor", 1), ups[1], exchange(ups[1], "tensor", 1)]
+        downs = [
+            downs[0], exchange(downs[0], "tensor", 1), downs[1], exchange(downs[1], "tensor", 1)
         ]
-        w_down = [
-            w_down[0], exchange(w_down[0], "tensor", 1), w_down[1], exchange(w_down[1], "tensor", 1)
-        ]
-        weights.append((w_qk, w_vo[:, :, :wide], w_vo[:, :, wide:], w_up, w_down))
+        return ups, downs
+
+    qk, vo, token, small = spread(*attn_blocks(0), small)
+    weights = [attn_weights(qk, vo)]
+    ups, downs, token, _ = spread(*behind(feed_blocks(0), token))
+    weights[0] += feed_weights(ups, downs)
+    for at in range(1, layers):
+        (up, down), (qk, vo) = feed_blocks(at), attn_blocks(at)
+        first, second = jnp.concatenate([up, qk], axis=1), jnp.concatenate([down, vo], axis=1)
+        first, second, token, _ = spread(*behind((first, second), token))
+        weights.append(
+            attn_weights([part[:, hidden:] for part in first], [part[:, hidden:] for part in second])
+            + feed_weights(
+                [part[:, :hidden] for part in first], [part[:, :hidden] for part in second]
+            )
+        )
+
+    small = small.reshape(4, count_dp, -1)
+    by_part = jnp.split(small, [sum(small_sizes[: i + 1]) for i in range(4)], axis=2)
+
+    def by_width(part):
+        part = jnp.take(part, t_order, axis=0).reshape(4, count_dp, layers, 2, -1)
+        return part.transpose(2, 3, 1, 0, 4).reshape(layers, 2, width)
+
+    gain_all, shift_all, obias_all = [by_width(part) for part in by_part[:3]]
+    qv_all = jnp.take(by_part[3][0::2], place_of, axis=1).reshape(2, count_dp, layers, 2, -1)
+    qv_all = qv_all.transpose(2, 3, 0, 1, 4).reshape(layers, 2, 2, wide)
+    up_all = jnp.take(by_part[4], place_of, axis=1).reshape(4, count_dp, layers, -1)
+    up_all = up_all.transpose(2, 0, 1, 3).reshape(layers, 4, hidden)
 
     def project(value, weight):
         return jnp.einsum("fd,tdk->tfk", value, weight, preferred_element_type=f32)
@@ -388,36 +565,28 @@
         middle = current + (share_a + share_b.astype(f32) + obias_all[at, 0])
         unit, _ = normalized(middle)
         normed_two = (unit * gain_all[at, 1] + shift_all[at, 1]).astype(bf16)
-        activated = [gelu_both(nn_dot(normed_two, w_up[t]) + up_all[at, t]) for t in range(4)]
-        feed = obias_all[at, 1]
-        for t in range(4):
-            feed = feed + nt_dot(activated[t][0], w_down[t])
+        fed = feed(normed_two, middle + obias_all[at, 1], up_all[at], w_up, w_down)
         saved.append(
-            (current, normed_a, normed_b, qk_a, v_a, qk_b, v_b, o_a, o_b, lse, middle, normed_two, activated)
+            (current, normed_a, normed_b, qk_a, v_a, qk_b, v_b, o_a, o_b, lse, middle, normed_two, fed[:4], fed[4:8])
         )
-        current = middle + feed
+        current = fed[8]
     encoded = give_clip(current)
 
     small_grads = [None] * layers
     weight_grads = [None] * layers
+    folding = None
     for at in reversed(range(layers)):
         w_qk, w_v, w_o, w_up, w_down = weights[at]
-        (layer_in, normed_a, normed_b, qk_a, v_a, qk_b, v_b, o_a, o_b, lse, middle, normed_two, activated) = saved[at]
+        (layer_in, normed_a, normed_b, qk_a, v_a, qk_b, v_b, o_a, o_b, lse, middle, normed_two, activated, slopes) = saved[at]
         grad_feed = gradient.astype(bf16)
         obias_two = jnp.sum(grad_feed, axis=0, dtype=f32)
-        grad_up = [
-            (nn_dot(grad_feed, w_down[t]) * activated[t][1].astype(f32)).astype(bf16)
-            for t in range(4)
-        ]
-        grad_normed = sum(nt_dot(grad_up[t], w_up[t]) for t in range(4))
-        bup = jnp.stack([jnp.sum(part, axis=0, dtype=f32) for part in grad_up])
-        dw_up = [tn_dot(normed_two, grad_up[t]).astype(bf16) for t in range(4)]
-        dw_down = [tn_dot(grad_feed, activated[t][0]).astype(bf16) for t in range(4)]
-        for dw in (dw_up, dw_down):
-            for t in (0, 2):
-                dw[t] = add_low(dw[t], exchange(dw[t + 1], "tensor", 1))
-        dw_up = fold(dw_up[0], dw_up[2], True)
-        dw_down = fold(dw_down[0], dw_down[2], False)
+        if folding is not None:
+            folding.advance()
+            (grad_feed,) = behind((grad_feed,), *folding.token())
+        dw_feed, dw_other, bup, grad_normed = feed_back(
+            normed_two, grad_feed, w_up, w_down, activated, slopes
+        )
+        dw_feed = add_low(dw_feed, exchange(dw_other, "tensor", 1))
 
         grad_middle, gain_two, shift_two = norm_back(middle, gain_all[at, 1], grad_normed)
         gradient = gradient + grad_middle
@@ -426,34 +595,62 @@
         obias_one = jnp.sum(branch_a, axis=0, dtype=f32)
         do_a = project(branch_a, w_o).astype(bf16)
         do_b = project(branch_b, w_o).astype(bf16)
-        dqk_a, dv_a, dqk_b, dv_b = attend_back(
-            row_count, quarter, qk_a, v_a, qk_b, v_b, o_a, o_b, do_a, do_b, lse
-        )
+        parts = []
+        for t in range(2):
+            if folding is not None:
+                folding.advance()
+                do_a, do_b = behind((do_a, do_b), *folding.token())
+            feed_state = (dw_feed,) if t == 0 else dw_feed
+            ready = behind((do_a, do_b), *feed_state, *[part[0] for part in parts])
+            parts.append(
+                attend_back(t, row_count, quarter, qk_a, v_a, qk_b, v_b, o_a, o_b, *ready, lse)
+            )
+            dw_feed = near_two(*dw_feed) if t else near_one(dw_feed[:2], dw_feed[2:])
+        if folding is not None:
+            folding.advance()
+            parts[1] = behind(parts[1], *dw_feed, *folding.token())
+            weight_grads[at + 1] = folding.result()
+        else:
+            parts[1] = behind(parts[1], *dw_feed)
+        dqk_a, dv_a, dqk_b, dv_b = [[parts[t][i][0] for t in range(2)] for i in range(4)]
 
         def back_normed(dqk, dv):
             return sum(nt_dot(dqk[t], w_qk[t]) + nt_dot(dv[t], w_v[t]) for t in range(2))
 
         share_b = exchange(back_normed(dqk_b, dv_b).astype(bf16), "tensor", 1)
         grad_normed = back_normed(dqk_a, dv_a) + share_b.astype(f32)
-        dw_qk = [
-            (tn_dot(normed_a, dqk_a[t]) + tn_dot(normed_b, dqk_b[t])).astype(bf16) for t in range(2)
-        ]
-        dw_vo = [
-            jnp.concatenate(
-                [
-                    (tn_dot(normed_a, dv_a[t]) + tn_dot(normed_b, dv_b[t])).astype(bf16),
-                    (tn_dot(branch_a, o_a[t]) + tn_dot(branch_b, o_b[t])).astype(bf16),
-                ],
-                axis=1,
-            )
-            for t in range(2)
-        ]
-        dw_qk = fold(dw_qk[0], dw_qk[1], True)
-        dw_vo = fold(dw_vo[0], dw_vo[1], False)
-        weight_grads[at] = [part.astype(f32) for part in (dw_qk, dw_vo, dw_up, dw_down)]
-        bq = jnp.sum(dqk_a[:, :, :wide], axis=1, dtype=f32)
-        bq = bq + jnp.sum(dqk_b[:, :, :wide], axis=1, dtype=f32)
-        bv = jnp.sum(dv_a, axis=1, dtype=f32) + jnp.sum(dv_b, axis=1, dtype=f32)
+        dw_qk = jnp.stack(
+            [
+                (tn_dot(normed_a, dqk_a[t]) + tn_dot(normed_b, dqk_b[t])).astype(bf16)
+                for t in range(2)
+            ]
+        )
+        dw_vo = jnp.stack(
+            [
+                jnp.concatenate(
+                    [
+                        (tn_dot(normed_a, dv_a[t]) + tn_dot(normed_b, dv_b[t])).astype(bf16),
+                        (tn_dot(branch_a, o_a[t]) + tn_dot(branch_b, o_b[t])).astype(bf16),
+                    ],
+                    axis=1,
+                )
+                for t in range(2)
+            ]
+        )
+        folding = Folding(dw_qk, dw_vo, *dw_feed)
+        bq = jnp.stack(
+            [
+                jnp.sum(dqk_a[t][:, :wide], axis=0, dtype=f32)
+                + jnp.sum(dqk_b[t][:, :wide], axis=0, dtype=f32)
+                for t in range(2)
+            ]
+        )
+        bv = jnp.stack(
+            [
+                jnp.sum(dv_a[t], axis=0, dtype=f32) + jnp.sum(dv_b[t], axis=0, dtype=f32)
+                for t in range(2)
+            ]
+        )
         grad_in, gain_one, shift_one = norm_back(layer_in, gain_all[at, 0], grad_normed)
         gradient = gradient + grad_in
         small_grads[at] = (
@@ -463,6 +660,11 @@
             jnp.stack([bq, bv]),
             bup,
         )
+    for step in range(4):
+        if step == 2:
+            (folding.attn,) = behind((folding.attn,), gradient)
+        folding.advance()
+    weight_grads[0] = folding.result()
     frames_grad = give_clip(gradient)
 
     gains, shifts, obiases, bqv, bups = [

time: 905 us -> 849 us (0.938)
  matrix products: 206 us -> 108 us
  Pallas kernels: 170 us -> 265 us
  starting transfers between devices: 101 us -> 67.8 us
  waiting for transfers between devices: 220 us -> 188 us
    pallas_call x0 -> x4, Pallas kernels: none -> 87.2 us  [the longest x2 53.7 us: feed_back(): pl.pallas_call(feed_back_kernel, grid=(hidden // step,), in_specs=[whole_...]
    dot_general x40 -> x24, matrix products: 75.2 us -> 25.9 us  [tn_dot(): lax.dot_general(left, right, (((0,), (0,)), ((), ())), preferred_element_...]
    dot_general x18 -> x2, matrix products: 44.2 us -> 7.06 us  [nn_dot(): lax.dot_general(left, right, (((1,), (0,)), ((), ())), preferred_element_...]
    ppermute x110 -> x74, starting transfers between devices: 101 us -> 67.8 us  [exchange(): return lax.ppermute(value, axis, [(i, i ^ mask) for i in range(count)])]
    ppermute x110 -> x74, waiting for transfers between devices: 220 us -> 188 us  [exchange(): return lax.ppermute(value, axis, [(i, i ^ mask) for i in range(count)])]
    concatenate x32 -> x19, other arithmetic: 21.4 us -> 4.42 us  [the longest x3 1.67 us: spread(): first = jnp.concatenate([first, first_more], axis=0)]
    dot_general x46 -> x30, matrix products: 71.5 us -> 57.4 us  [nt_dot(): lax.dot_general(left, right, (((1,), (1,)), ((), ())), preferred_element_...]
    squeeze x1 -> x18, local copies, waits for them, and re-layouts: 0.72 us -> 14 us  [the longest x4 3.15 us: near_one(): first[1]]
  transfers between devices with their start and end apart: 110 -> 74, of which waited for: 36 -> 27; matrix products, arithmetic and copies ran while one was open for 39% -> 28% of each run, Pallas kernels for 19% -> 19%
where the time goes in v2:
time: 849 us; the launch traced here: 840 us
  Pallas kernels  265 us (31%)
  waiting for transfers between devices  188 us (22%)
  local copies, waits for them, and re-layouts  118 us (14%)
  matrix products  108 us (13%)
  other arithmetic  89.1 us (10%)
  starting transfers between devices  67.8 us (8%)
    ppermute x74, waiting for transfers between devices, exchange(): return lax.ppermute(value, axis, [(i, i ^ mask) for i in range(count)])  188 us
    pallas_call x4, Pallas kernels, attend_back(): pl.pallas_call(functools.partial(attend_back_kernel, row_count, quarter,...  119 us
    ppermute x74, starting transfers between devices, exchange(): return lax.ppermute(value, axis, [(i, i ^ mask) for i in range(count)])  67.8 us
    pallas_call x2, Pallas kernels, attend(): pl.pallas_call(functools.partial(attend_kernel, row_count, quarter, min(2...  58.3 us
    dot_general x30, matrix products, nt_dot(): lax.dot_general(left, right, (((1,), (1,)), ((), ())), preferred_element_...  57.4 us
    pallas_call x2, Pallas kernels, feed_back(): pl.pallas_call(feed_back_kernel, grid=(hidden // step,), in_specs=[whole_...  53.7 us
    unnamed x376, local copies, waits for them, and re-layouts  35.6 us
    pallas_call x2, Pallas kernels, feed(): pl.pallas_call(feed_kernel, grid=(hidden // step,), in_specs=[whole_block...  33.6 us
  transfers between devices with their start and end apart: 74, of which 27 were waited for; matrix products, arithmetic and copies ran while one was open for 28% of the time, Pallas kernels for 19%

profile of v2, /device:TPU:0, one launch (start us, length us, event | category | flops | bytes accessed | tf_op | source)
XLA Modules:
  0.0 840.3 jit_solution(8930224020855084413)
XLA Ops:
  0.7 7.3 constant_dynamic-slice_fusion.1
  8.9 3.0 collective-permute-start
  13.5 2.7 collective-permute-start.1
  22.2 3.0 collective-permute-done.2
  28.1 7.4 collective-permute-done.4
  56.7 3.3 fusion.215
  66.2 3.4 collective-permute-start.14
  70.2 11.3 %collective-permute-done.14 = bf16[96,1536]{1,0:T(8,128)(2,1)S(1)} collective-permute-done((bf16[96,1536]{1,0:T(8,128)(2,1)S(1)}, bf16[96,1536]{1,0:T(8,128)(2,1)S(1)}, u32[]{:S(2)}, u32[]{:S(2)}) %collective-permute-start.14) | collective-permute-done | bytes 294944 | tf_op jit(solution)/shard_map/ppermute | solution.py:23
  85.1 10.7 %collective-permute-done.15 = bf16[192,1536]{1,0:T(8,128)(2,1)S(1)} collective-permute-done((bf16[192,1536]{1,0:T(8,128)(2,1)S(1)}, bf16[192,1536]{1,0:T(8,128)(2,1)S(1)}, u32[]{:S(2)}, u32[]{:S(2)}) %collective-permute-start.15) | collective-permute-done | bytes 589856 | tf_op jit(solution)/shard_map/ppermute | solution.py:23
  101.2 29.0 %shard_map.194 = (bf16[2,768,192]{2,1,0:T(8,128)(2,1)S(1)}, bf16[2,768,192]{2,1,0:T(8,128)(2,1)S(1)}, f32[2,1536,8]{2,1,0:T(8,128)}) custom-call(bf16[2,768,384]{2,1,0:T(8,128)(2,1)S(1)} %fusion.14.qk_a, bf16[2,768,192]{2,1,0:T(8,128)(2,1)S(1)} %fusion.20.v_a, bf16[2,768,384]{2,1,0:T(8,128)(2,1)S(1)} %fusion.15.qk_b, bf16[2,768,192]{2,1,0:T(8,128)(2,1)S(1)} %fusion.21.v_b), custom_call_target="tpu_custom_call" | custom-call | tf_op jit(solution)/shard_map/pallas_call | solution.py:215
  132.4 3.4 collective-permute-start.24
  138.1 18.1 %collective-permute-done.24 = bf16[96,2304]{1,0:T(8,128)(2,1)S(1)} collective-permute-done((bf16[96,2304]{1,0:T(8,128)(2,1)S(1)}, bf16[96,2304]{1,0:T(8,128)(2,1)S(1)}, u32[]{:S(2)}, u32[]{:S(2)}) %collective-permute-start.24) | collective-permute-done | bytes 442400 | tf_op jit(solution)/shard_map/ppermute | solution.py:23
  158.4 19.4 %collective-permute-done.25 = bf16[192,2304]{1,0:T(8,128)(2,1)S(1)} collective-permute-done((bf16[192,2304]{1,0:T(8,128)(2,1)S(1)}, bf16[192,2304]{1,0:T(8,128)(2,1)S(1)}, u32[]{:S(2)}, u32[]{:S(2)}) %collective-permute-start.25) | collective-permute-done | bytes 884768 | tf_op jit(solution)/shard_map/ppermute | solution.py:23
  183.6 15.1 %collective-permute-done.26 = bf16[384,1152]{1,0:T(8,128)(2,1)S(1)} collective-permute-done((bf16[384,1152]{1,0:T(8,128)(2,1)S(1)}, bf16[384,1152]{1,0:T(8,128)(2,1)S(1)}, u32[]{:S(2)}, u32[]{:S(2)}) %collective-permute-start.26) | collective-permute-done | bytes 884768 | tf_op jit(solution)/shard_map/ppermute | solution.py:23
  203.5 2.8 slice_bitcast_fusion.5
  209.9 16.9 %shard_map.195 = (bf16[768,768]{1,0:T(8,128)(2,1)}, bf16[768,768]{1,0:T(8,128)(2,1)}, bf16[768,768]{1,0:T(8,128)(2,1)}, bf16[768,768]{1,0:T(8,128)(2,1)}, bf16[7...) custom-call(bf16[768,768]{1,0:T(8,128)(2,1)} %get-tuple-element.360., ...), custom_call_target="tpu_custom_call" | custom-call | tf_op jit(solution)/shard_map/pallas_call | solution.py:377
  231.7 10.5 %collective-permute-done.28 = bf16[768,1152]{1,0:T(8,128)(2,1)} collective-permute-done((bf16[768,1152]{1,0:T(8,128)(2,1)S(1)}, bf16[768,1152]{1,0:T(8,128)(2,1)}, u32[]{:S(2)}, u32[]{:S(2)}) %collective-permute-start.28) | collective-permute-done | bytes 1769504 | tf_op jit(solution)/shard_map/ppermute | solution.py:23
  251.3 29.2 %shard_map.196 = (bf16[2,768,192]{2,1,0:T(8,128)(2,1)S(1)}, bf16[2,768,192]{2,1,0:T(8,128)(2,1)S(1)}, f32[2,1536,8]{2,1,0:T(8,128)}) custom-call(bf16[2,768,384]{2,1,0:T(8,128)(2,1)S(1)} %fusion.16.qk_a, bf16[2,768,192]{2,1,0:T(8,128)(2,1)S(1)} %fusion.22.v_a, bf16[2,768,384]{2,1,0:T(8,128)(2,1)S(1)} %fusion.17.qk_b, bf16[2,768,192]{2,1,0:T(8,128)(2,1)S(1)} %fusion.23.v_b), custom_call_target="tpu_custom_call" | custom-call | tf_op jit(solution)/shard_map/pallas_call | solution.py:215
  285.7 3.7 convert_reduce_fusion
  299.9 2.3 broadcast_add_fusion
  304.4 16.6 %shard_map.197 = (bf16[768,768]{1,0:T(8,128)(2,1)}, bf16[768,768]{1,0:T(8,128)(2,1)}, bf16[768,768]{1,0:T(8,128)(2,1)}, bf16[768,768]{1,0:T(8,128)(2,1)}, bf16[7...) custom-call(bf16[768,768]{1,0:T(8,128)(2,1)} %get-tuple-element.358., ...), custom_call_target="tpu_custom_call" | custom-call | tf_op jit(solution)/shard_map/pallas_call | solution.py:377
  321.1 26.9 %shard_map.198 = (bf16[4,768,768]{2,1,0:T(8,128)(2,1)}, bf16[4,768,768]{2,1,0:T(8,128)(2,1)}, f32[4,768]{1,0:T(4,128)}, f32[768,768]{1,0:T(8,128)}) custom-call(bf16[768,768]{1,0:T(8,128)(2,1)} %get-tuple-element.358.normed, bf16[768,768]{1,0:T(8,128)(2,1)} %get-tuple-element.351.grad, bf16[768,768]{1,0:T(8,128)(2,1)} %copy-done.36, ...), custom_call_target="tpu_custom_call" | custom-call | tf_op jit(solution)/shard_map/pallas_call | solution.py:427
  352.9 3.5 multiply_reduce_fusion
  356.7 3.8 convert_reduce_fusion.1
  360.8 3.1 convolution_convert_fusion.3
  363.9 2.3 copy.301
  374.0 2.6 copy.327
  376.6 3.1 convolution_convert_fusion.2
  385.4 2.4 add_convert_fusion.32
  387.8 2.5 add_convert_fusion.34
  390.3 4.9 add_convert_fusion.1
  397.4 30.0 %shard_map.199 = (bf16[1,768,384]{2,1,0:T(8,128)(2,1)}, bf16[1,768,192]{2,1,0:T(8,128)(2,1)}, bf16[1,768,384]{2,1,0:T(8,128)(2,1)}, bf16[1,768,192]{2,1,0:T(8,128)(2,1)}) custom-call(bf16[2,768,384]{2,1,0:T(8,128)(2,1)} %copy-done.6, bf16[2,768,192]{2,1,0:T(8,128)(2,1)} %copy-done.10, bf16[2,768,384]{2,1,0:T(8,128)(2,1)} %copy-done.7, ...), custom_call_target="tpu_custom_call" | custom-call | tf_op jit(solution)/shard_map/pallas_call | solution.py:297
  427.4 3.1 fusion.90
  439.2 3.3 fusion.66
  442.6 16.6 %collective-permute-done.40 = bf16[768,768]{1,0:T(8,128)(2,1)S(1)} collective-permute-done((bf16[768,768]{1,0:T(8,128)(2,1)}, bf16[768,768]{1,0:T(8,128)(2,1)S(1)}, u32[]{:S(2)}, u32[]{:S(2)}) %collective-permute-start.40) | collective-permute-done | bytes 1179680 | tf_op jit(solution)/shard_map/ppermute | solution.py:23
  466.6 3.3 fusion.68
  469.9 29.8 %shard_map.200 = (bf16[1,768,384]{2,1,0:T(8,128)(2,1)}, bf16[1,768,192]{2,1,0:T(8,128)(2,1)}, bf16[1,768,384]{2,1,0:T(8,128)(2,1)}, bf16[1,768,192]{2,1,0:T(8,128)(2,1)}) custom-call(bf16[2,768,384]{2,1,0:T(8,128)(2,1)} %copy-done.6, bf16[2,768,192]{2,1,0:T(8,128)(2,1)} %copy-done.10, bf16[2,768,384]{2,1,0:T(8,128)(2,1)} %copy-done.7, ...), custom_call_target="tpu_custom_call" | custom-call | tf_op jit(solution)/shard_map/pallas_call | solution.py:297
  504.8 3.0 add_convert_fusion.4
  518.6 10.1 %collective-permute-done.45 = bf16[768,384]{0,1:T(8,128)(2,1)S(1)} collective-permute-done((bf16[768,384]{0,1:T(8,128)(2,1)S(1)}, bf16[768,384]{0,1:T(8,128)(2,1)S(1)}, u32[]{:S(2)}, u32[]{:S(2)}) %collective-permute-start.45) | collective-permute-done | bytes 589856 | tf_op jit(solution)/shard_map/ppermute | solution.py:23
  537.4 3.1 collective-permute-start.51
  542.7 9.4 %collective-permute-done.51 = bf16[96,1536]{1,0:T(8,128)(2,1)S(1)} collective-permute-done((bf16[96,1536]{1,0:T(8,128)(2,1)S(1)}, bf16[96,1536]{1,0:T(8,128)(2,1)S(1)}, u32[]{:S(2)}, u32[]{:S(2)}) %collective-permute-start.51) | collective-permute-done | bytes 294944 | tf_op jit(solution)/shard_map/ppermute | solution.py:23
  553.9 4.9 multiply_reduce_fusion.1
  561.1 26.7 %shard_map.201 = (bf16[4,768,768]{2,1,0:T(8,128)(2,1)}, bf16[4,768,768]{2,1,0:T(8,128)(2,1)}, f32[4,768]{1,0:T(4,128)}, f32[768,768]{1,0:T(8,128)}) custom-call(bf16[768,768]{1,0:T(8,128)(2,1)} %get-tuple-element.360.normed, bf16[768,768]{1,0:T(8,128)(2,1)} %get-tuple-element.205.grad, bf16[768,768]{1,0:T(8,128)(2,1)} %copy-done.33, ...), custom_call_target="tpu_custom_call" | custom-call | tf_op jit(solution)/shard_map/pallas_call | solution.py:427
  589.9 3.4 collective-permute-start.58
  593.2 4.1 multiply_reduce_fusion.2
  597.4 4.3 convert_reduce_fusion.3
  620.5 2.7 convolution_convert_fusion
  631.3 4.9 add_convert_fusion
  638.3 29.8 %shard_map.202 = (bf16[1,768,384]{2,1,0:T(8,128)(2,1)}, bf16[1,768,192]{2,1,0:T(8,128)(2,1)}, bf16[1,768,384]{2,1,0:T(8,128)(2,1)}, bf16[1,768,192]{2,1,0:T(8,128)(2,1)}) custom-call(bf16[2,768,384]{2,1,0:T(8,128)(2,1)} %copy-done.4, bf16[2,768,192]{2,1,0:T(8,128)(2,1)} %copy-done.8, bf16[2,768,384]{2,1,0:T(8,128)(2,1)} %copy-done.5, ...), custom_call_target="tpu_custom_call" | custom-call | tf_op jit(solution)/shard_map/pallas_call | solution.py:297
  680.7 19.5 %collective-permute-done.54 = bf16[768,768]{1,0:T(8,128)(2,1)S(1)} collective-permute-done((bf16[768,768]{1,0:T(8,128)(2,1)S(1)}, bf16[768,768]{1,0:T(8,128)(2,1)S(1)}, u32[]{:S(2)}, u32[]{:S(2)}) %collective-permute-start.54) | collective-permute-done | bytes 1179680 | tf_op jit(solution)/shard_map/ppermute | solution.py:23
  705.5 3.4 fusion.185
  708.9 29.8 %shard_map.203 = (bf16[1,768,384]{2,1,0:T(8,128)(2,1)}, bf16[1,768,192]{2,1,0:T(8,128)(2,1)}, bf16[1,768,384]{2,1,0:T(8,128)(2,1)}, bf16[1,768,192]{2,1,0:T(8,128)(2,1)}) custom-call(bf16[2,768,384]{2,1,0:T(8,128)(2,1)} %copy-done.4, bf16[2,768,192]{2,1,0:T(8,128)(2,1)} %copy-done.8, bf16[2,768,384]{2,1,0:T(8,128)(2,1)} %copy-done.5, ...), custom_call_target="tpu_custom_call" | custom-call | tf_op jit(solution)/shard_map/pallas_call | solution.py:297
  758.5 3.5 fusion.181
  764.8 3.4 collective-permute-done.61
  775.1 6.0 collective-permute-done.64
  782.3 8.1 collective-permute-done.66
  792.5 3.7 multiply_reduce_fusion.3
  799.5 3.0 collective-permute-done.69
  804.7 3.0 multiply_add_fusion
  811.6 2.4 fusion.8
  815.2 4.6 collective-permute-done.73
  820.7 2.7 collective-permute-start.68
  826.8 5.0 collective-permute-done.68
  837.5 2.6 copy.328
  (850 shorter events, 268.6 us)
Async XLA Ops:
  8.9 46.7 %collective-permute-start = (bf16[375,768]{1,0:T(8,128)(2,1)}, bf16[375,768]{1,0:T(8,128)(2,1)}, u32[]{:S(2)}, u32[]{:S(2)}) collective-permute-start(bf16[375,768]{1,0:T(8,128)(2,1)} %bitcast.514), channel_id=1, source_target_pairs={{0,2},{1,3},{2,0},{3,1},{4,6},{5,7},{6,4},{7,5},{8,10},{9,11},{10,... | collective-permute-start | bytes 1728008 | tf_op jit(solution)/shard_map/ppermute | solution.py:23
  13.5 11.7 %collective-permute-start.1 = (bf16[96,768]{0,1:T(8,128)(2,1)S(1)}, bf16[96,768]{0,1:T(8,128)(2,1)S(1)}, u32[]{:S(2)}, u32[]{:S(2)}) collective-permute-start(bf16[96,768]{0,1:T(8,128)(2,1)S(1)} %pad_maximum_fusion.36), channel_id=1, source_target_pairs={{0,16},{4,20},{8,24},{12,28},{16,0},{20,4},{24,8},{28,12},{1,17},{... | collective-permute-start | bytes 442376 | tf_op jit(solution)/shard_map/ppermute | solution.py:23
  16.7 8.5 %collective-permute-start.2 = (f32[1,576]{1,0:T(1,128)S(1)}, f32[1,576]{1,0:T(1,128)S(1)}, u32[]{:S(2)}, u32[]{:S(2)}) collective-permute-start(f32[1,576]{1,0:T(1,128)S(1)} %concatenate.128), channel_id=1, source_target_pairs={{0,16},{4,20},{8,24},{12,28},{16,0},{20,4},{24,8},{28,12},{1,17},{... | collective-permute-start | bytes 6920 | tf_op jit(solution)/shard_map/ppermute | solution.py:23
  25.4 10.1 %collective-permute-start.3 = (bf16[192,768]{0,1:T(8,128)(2,1)S(1)}, bf16[192,768]{0,1:T(8,128)(2,1)S(1)}, u32[]{:S(2)}, u32[]{:S(2)}) collective-permute-start(bf16[192,768]{0,1:T(8,128)(2,1)S(1)} %pad_maximum_fusion.33), channel_id=1, source_target_pairs={{0,8},{4,12},{8,0},{12,4},{16,24},{20,28},{24,16},{28,20},{1,9},{5... | collective-permute-start | bytes 884744 | tf_op jit(solution)/shard_map/ppermute | solution.py:23
  26.1 9.4 %collective-permute-start.4 = (f32[2,576]{1,0:T(2,128)S(1)}, f32[2,576]{1,0:T(2,128)S(1)}, u32[]{:S(2)}, u32[]{:S(2)}) collective-permute-start(f32[2,576]{1,0:T(2,128)S(1)} %pad_maximum_fusion.44), channel_id=1, source_target_pairs={{0,8},{4,12},{8,0},{12,4},{16,24},{20,28},{24,16},{28,20},{1,9},{5... | collective-permute-start | bytes 13832 | tf_op jit(solution)/shard_map/ppermute | solution.py:23
  45.1 17.6 %collective-permute-start.5 = (bf16[384,384]{0,1:T(8,128)(2,1)S(1)}, bf16[384,384]{0,1:T(8,128)(2,1)}, u32[]{:S(2)}, u32[]{:S(2)}) collective-permute-start(bf16[384,384]{0,1:T(8,128)(2,1)S(1)} %get-tuple-element.136), channel_id=1, source_target_pairs={{0,4},{4,0},{8,12},{12,8},{16,20},{20,16},{24,28},{28,24},{1,5},{5... | collective-permute-start | bytes 884744 | tf_op jit(solution)/shard_map/ppermute | solution.py:23
  45.7 17.0 %collective-permute-start.6 = (bf16[384,384]{0,1:T(8,128)(2,1)S(1)}, bf16[384,384]{0,1:T(8,128)(2,1)}, u32[]{:S(2)}, u32[]{:S(2)}) collective-permute-start(bf16[384,384]{0,1:T(8,128)(2,1)S(1)} %get-tuple-element.137), channel_id=1, source_target_pairs={{0,2},{1,3},{2,0},{3,1},{4,6},{5,7},{6,4},{7,5},{8,10},{9,11},{10,... | collective-permute-start | bytes 884744 | tf_op jit(solution)/shard_map/ppermute | solution.py:23
  65.4 16.9 %collective-permute-start.7 = (bf16[768,384]{0,1:T(8,128)(2,1)S(1)}, bf16[768,384]{0,1:T(8,128)(2,1)S(1)}, u32[]{:S(2)}, u32[]{:S(2)}) collective-permute-start(bf16[768,384]{0,1:T(8,128)(2,1)S(1)} %pad_maximum_fusion.28), channel_id=1, source_target_pairs={{0,2},{1,3},{2,0},{3,1},{4,6},{5,7},{6,4},{7,5},{8,10},{9,11},{10,... | collective-permute-start | bytes 1769480 | tf_op jit(solution)/shard_map/ppermute | solution.py:23
  65.6 16.8 %collective-permute-start.8 = (bf16[2,384,384]{1,2,0:T(8,128)(2,1)S(1)}, bf16[2,384,384]{1,2,0:T(8,128)(2,1)S(1)}, u32[]{:S(2)}, u32[]{:S(2)}) collective-permute-start(bf16[2,384,384]{1,2,0:T(8,128)(2,1)S(1)} %pad_maximum_fusion.29), channel_id=1, source_target_pairs={{0,4},{4,0},{8,12},{12,8},{16,20},{20,16},{24,28},{28,24},{1,5},{5... | collective-permute-start | bytes 1769480 | tf_op jit(solution)/shard_map/ppermute | solution.py:23
  66.2 15.3 %collective-permute-start.14 = (bf16[96,1536]{1,0:T(8,128)(2,1)S(1)}, bf16[96,1536]{1,0:T(8,128)(2,1)S(1)}, u32[]{:S(2)}, u32[]{:S(2)}) collective-permute-start(bf16[96,1536]{1,0:T(8,128)(2,1)S(1)} %constant_dynamic-update-slice_fusion), channel_id=1, source_target_pairs={{0,16},{4,20},{8,24},{12,28},{16,0},{20,4},{24,8},{28,12},{1,17},{... | collective-permute-start | bytes 884744 | tf_op jit(solution)/shard_map/ppermute | solution.py:23
  70.1 29.0 %collective-permute-start.12 = (bf16[768,768]{1,0:T(8,128)(2,1)S(1)}, bf16[768,768]{1,0:T(8,128)(2,1)S(1)}, u32[]{:S(2)}, u32[]{:S(2)}) collective-permute-start(bf16[768,768]{1,0:T(8,128)(2,1)S(1)} %add_convert_fusion.11), channel_id=1, source_target_pairs={{0,1},{1,0},{2,3},{3,2},{4,5},{5,4},{6,7},{7,6},{8,9},{9,8},{10,11... | collective-permute-start | bytes 3538952 | tf_op jit(solution)/shard_map/ppermute | solution.py:23
  81.5 14.3 %collective-permute-start.15 = (bf16[192,1536]{1,0:T(8,128)(2,1)S(1)}, bf16[192,1536]{1,0:T(8,128)(2,1)S(1)}, u32[]{:S(2)}, u32[]{:S(2)}) collective-permute-start(bf16[192,1536]{1,0:T(8,128)(2,1)S(1)} %pad_maximum_fusion.30), channel_id=1, source_target_pairs={{0,8},{4,12},{8,0},{12,4},{16,24},{20,28},{24,16},{28,20},{1,9},{5... | collective-permute-start | bytes 1769480 | tf_op jit(solution)/shard_map/ppermute | solution.py:23
  96.0 35.8 %collective-permute-start.16 = (bf16[384,768]{1,0:T(8,128)(2,1)S(1)}, bf16[384,768]{1,0:T(8,128)(2,1)S(1)}, u32[]{:S(2)}, u32[]{:S(2)}) collective-permute-start(bf16[384,768]{1,0:T(8,128)(2,1)S(1)} %get-tuple-element.150), channel_id=1, source_target_pairs={{0,4},{4,0},{8,12},{12,8},{16,20},{20,16},{24,28},{28,24},{1,5},{5... | collective-permute-start | bytes 1769480 | tf_op jit(solution)/shard_map/ppermute | solution.py:23
  97.6 34.3 %collective-permute-start.17 = (bf16[384,768]{1,0:T(8,128)(2,1)S(1)}, bf16[384,768]{1,0:T(8,128)(2,1)S(1)}, u32[]{:S(2)}, u32[]{:S(2)}) collective-permute-start(bf16[384,768]{1,0:T(8,128)(2,1)S(1)} %get-tuple-element.151), channel_id=1, source_target_pairs={{0,2},{1,3},{2,0},{3,1},{4,6},{5,7},{6,4},{7,5},{8,10},{9,11},{10,... | collective-permute-start | bytes 1769480 | tf_op jit(solution)/shard_map/ppermute | solution.py:23
  131.2 25.8 %collective-permute-start.13 = (bf16[768,768]{1,0:T(8,128)(2,1)S(1)}, bf16[768,768]{1,0:T(8,128)(2,1)S(1)}, u32[]{:S(2)}, u32[]{:S(2)}) collective-permute-start(bf16[768,768]{1,0:T(8,128)(2,1)S(1)} %add_convert_fusion.10), channel_id=1, source_target_pairs={{0,1},{1,0},{2,3},{3,2},{4,5},{5,4},{6,7},{7,6},{8,9},{9,8},{10,11... | collective-permute-start | bytes 3538952 | tf_op jit(solution)/shard_map/ppermute | solution.py:23
  132.4 23.7 %collective-permute-start.24 = (bf16[96,2304]{1,0:T(8,128)(2,1)S(1)}, bf16[96,2304]{1,0:T(8,128)(2,1)S(1)}, u32[]{:S(2)}, u32[]{:S(2)}) collective-permute-start(bf16[96,2304]{1,0:T(8,128)(2,1)S(1)} %constant_dynamic-update-slice_fusion.2), channel_id=1, source_target_pairs={{0,16},{4,20},{8,24},{12,28},{16,0},{20,4},{24,8},{28,12},{1,17},{... | collective-permute-start | bytes 1327112 | tf_op jit(solution)/shard_map/ppermute | solution.py:23
  136.1 65.1 %collective-permute-start.18 = (bf16[768,768]{1,0:T(8,128)(2,1)S(1)}, bf16[768,768]{1,0:T(8,128)(2,1)S(1)}, u32[]{:S(2)}, u32[]{:S(2)}) collective-permute-start(bf16[768,768]{1,0:T(8,128)(2,1)S(1)} %pad_maximum_fusion.9.refs_0_), channel_id=1, source_target_pairs={{0,1},{1,0},{2,3},{3,2},{4,5},{5,4},{6,7},{7,6},{8,9},{9,8},{10,11... | collective-permute-start | bytes 3538952 | tf_op jit(solution)/shard_map/ppermute | solution.py:23
  137.0 44.5 %collective-permute-start.19 = (bf16[768,768]{1,0:T(8,128)(2,1)S(1)}, bf16[768,768]{1,0:T(8,128)(2,1)S(1)}, u32[]{:S(2)}, u32[]{:S(2)}) collective-permute-start(bf16[768,768]{1,0:T(8,128)(2,1)S(1)} %pad_maximum_fusion.9.refs_0_), channel_id=1, source_target_pairs={{0,2},{1,3},{2,0},{3,1},{4,6},{5,7},{6,4},{7,5},{8,10},{9,11},{10,... | collective-permute-start | bytes 3538952 | tf_op jit(solution)/shard_map/ppermute | solution.py:23
  137.5 44.0 %collective-permute-start.20 = (bf16[2,384,768]{2,1,0:T(8,128)(2,1)S(1)}, bf16[2,384,768]{2,1,0:T(8,128)(2,1)S(1)}, u32[]{:S(2)}, u32[]{:S(2)}) collective-permute-start(bf16[2,384,768]{2,1,0:T(8,128)(2,1)S(1)} %pad_maximum_fusion.10), channel_id=1, source_target_pairs={{0,4},{4,0},{8,12},{12,8},{16,20},{20,16},{24,28},{28,24},{1,5},{5... | collective-permute-start | bytes 3538952 | tf_op jit(solution)/shard_map/ppermute | solution.py:23
  156.2 21.5 %collective-permute-start.25 = (bf16[192,2304]{1,0:T(8,128)(2,1)S(1)}, bf16[192,2304]{1,0:T(8,128)(2,1)S(1)}, u32[]{:S(2)}, u32[]{:S(2)}) collective-permute-start(bf16[192,2304]{1,0:T(8,128)(2,1)S(1)} %pad_maximum_fusion.18), channel_id=1, source_target_pairs={{0,8},{4,12},{8,0},{12,4},{16,24},{20,28},{24,16},{28,20},{1,9},{5... | collective-permute-start | bytes 2654216 | tf_op jit(solution)/shard_map/ppermute | solution.py:23
  178.0 20.7 %collective-permute-start.26 = (bf16[384,1152]{1,0:T(8,128)(2,1)S(1)}, bf16[384,1152]{1,0:T(8,128)(2,1)S(1)}, u32[]{:S(2)}, u32[]{:S(2)}) collective-permute-start(bf16[384,1152]{1,0:T(8,128)(2,1)S(1)} %get-tuple-element.161), channel_id=1, source_target_pairs={{0,4},{4,0},{8,12},{12,8},{16,20},{20,16},{24,28},{28,24},{1,5},{5... | collective-permute-start | bytes 2654216 | tf_op jit(solution)/shard_map/ppermute | solution.py:23
  178.6 20.3 %collective-permute-start.27 = (bf16[384,1152]{1,0:T(8,128)(2,1)S(1)}, bf16[384,1152]{1,0:T(8,128)(2,1)S(1)}, u32[]{:S(2)}, u32[]{:S(2)}) collective-permute-start(bf16[384,1152]{1,0:T(8,128)(2,1)S(1)} %get-tuple-element.162), channel_id=1, source_target_pairs={{0,2},{1,3},{2,0},{3,1},{4,6},{5,7},{6,4},{7,5},{8,10},{9,11},{10,... | collective-permute-start | bytes 2654216 | tf_op jit(solution)/shard_map/ppermute | solution.py:23
  181.4 24.8 %collective-permute-start.21 = (bf16[768,768]{1,0:T(8,128)(2,1)S(1)}, bf16[768,768]{1,0:T(8,128)(2,1)S(1)}, u32[]{:S(2)}, u32[]{:S(2)}) collective-permute-start(bf16[768,768]{1,0:T(8,128)(2,1)S(1)} %collective-permute-done.19.refs_2_), channel_id=1, source_target_pairs={{0,1},{1,0},{2,3},{3,2},{4,5},{5,4},{6,7},{7,6},{8,9},{9,8},{10,11... | collective-permute-start | bytes 3538952 | tf_op jit(solution)/shard_map/ppermute | solution.py:23
  182.6 25.3 %collective-permute-start.22 = (bf16[768,768]{1,0:T(8,128)(2,1)S(1)}, bf16[768,768]{1,0:T(8,128)(2,1)S(1)}, u32[]{:S(2)}, u32[]{:S(2)}) collective-permute-start(bf16[768,768]{1,0:T(8,128)(2,1)S(1)} %pad_maximum_fusion.11.refs_4_), channel_id=1, source_target_pairs={{0,1},{1,0},{2,3},{3,2},{4,5},{5,4},{6,7},{7,6},{8,9},{9,8},{10,11... | collective-permute-start | bytes 3538952 | tf_op jit(solution)/shard_map/ppermute | solution.py:23
  198.7 9.2 %collective-permute-start.23 = (bf16[768,768]{1,0:T(8,128)(2,1)S(1)}, bf16[768,768]{1,0:T(8,128)(2,1)S(1)}, u32[]{:S(2)}, u32[]{:S(2)}) collective-permute-start(bf16[768,768]{1,0:T(8,128)(2,1)S(1)} %pad_maximum_fusion.12.refs_6_), channel_id=1, source_target_pairs={{0,1},{1,0},{2,3},{3,2},{4,5},{5,4},{6,7},{7,6},{8,9},{9,8},{10,11... | collective-permute-start | bytes 3538952 | tf_op jit(solution)/shard_map/ppermute | solution.py:23
  200.6 41.5 %collective-permute-start.28 = (bf16[768,1152]{1,0:T(8,128)(2,1)S(1)}, bf16[768,1152]{1,0:T(8,128)(2,1)}, u32[]{:S(2)}, u32[]{:S(2)}) collective-permute-start(bf16[768,1152]{1,0:T(8,128)(2,1)S(1)} %pad_maximum_fusion.3), channel_id=1, source_target_pairs={{0,2},{1,3},{2,0},{3,1},{4,6},{5,7},{6,4},{7,5},{8,10},{9,11},{10,... | collective-permute-start | bytes 5308424 | tf_op jit(solution)/shard_map/ppermute | solution.py:23
  201.1 41.0 %collective-permute-start.29 = (bf16[2,384,1152]{2,1,0:T(8,128)(2,1)}, bf16[2,384,1152]{2,1,0:T(8,128)(2,1)}, u32[]{:S(2)}, u32[]{:S(2)}) collective-permute-start(bf16[2,384,1152]{2,1,0:T(8,128)(2,1)} %pad_maximum_fusion.4), channel_id=1, source_target_pairs={{0,4},{4,0},{8,12},{12,8},{16,20},{20,16},{24,28},{28,24},{1,5},{5... | collective-permute-start | bytes 5308424 | tf_op jit(solution)/shard_map/ppermute | solution.py:23
  206.3 78.1 %collective-permute-start.37 = (bf16[375,768]{1,0:T(8,128)(2,1)}, bf16[375,768]{1,0:T(8,128)(2,1)}, u32[]{:S(2)}, u32[]{:S(2)}) collective-permute-start(bf16[375,768]{1,0:T(8,128)(2,1)} %bitcast.513), channel_id=1, source_target_pairs={{0,2},{1,3},{2,0},{3,1},{4,6},{5,7},{6,4},{7,5},{8,10},{9,11},{10,... | collective-permute-start | bytes 1728008 | tf_op jit(solution)/shard_map/ppermute | solution.py:23
  231.6 17.2 %collective-permute-start.30 = (bf16[768,768]{1,0:T(8,128)(2,1)S(1)}, bf16[768,768]{1,0:T(8,128)(2,1)S(1)}, u32[]{:S(2)}, u32[]{:S(2)}) collective-permute-start(bf16[768,768]{1,0:T(8,128)(2,1)S(1)} %add_convert_fusion.8), channel_id=1, source_target_pairs={{0,1},{1,0},{2,3},{3,2},{4,5},{5,4},{6,7},{7,6},{8,9},{9,8},{10,11... | collective-permute-start | bytes 3538952 | tf_op jit(solution)/shard_map/ppermute | solution.py:23
  282.8 12.3 %collective-permute-start.31 = (bf16[768,768]{1,0:T(8,128)(2,1)}, bf16[768,768]{1,0:T(8,128)(2,1)}, u32[]{:S(2)}, u32[]{:S(2)}) collective-permute-start(bf16[768,768]{1,0:T(8,128)(2,1)} %add_convert_fusion.7), channel_id=1, source_target_pairs={{0,1},{1,0},{2,3},{3,2},{4,5},{5,4},{6,7},{7,6},{8,9},{9,8},{10,11... | collective-permute-start | bytes 3538952 | tf_op jit(solution)/shard_map/ppermute | solution.py:23
  289.6 12.7 %collective-permute-start.32 = (bf16[768,768]{1,0:T(8,128)(2,1)S(1)}, bf16[768,768]{1,0:T(8,128)(2,1)S(1)}, u32[]{:S(2)}, u32[]{:S(2)}) collective-permute-start(bf16[768,768]{1,0:T(8,128)(2,1)S(1)} %slice.629.refs_0_), channel_id=1, source_target_pairs={{0,1},{1,0},{2,3},{3,2},{4,5},{5,4},{6,7},{7,6},{8,9},{9,8},{10,11... | collective-permute-start | bytes 3538952 | tf_op jit(solution)/shard_map/ppermute | solution.py:23
  291.9 10.4 %collective-permute-start.33 = (bf16[768,768]{1,0:T(8,128)(2,1)S(1)}, bf16[768,768]{1,0:T(8,128)(2,1)S(1)}, u32[]{:S(2)}, u32[]{:S(2)}) collective-permute-start(bf16[768,768]{1,0:T(8,128)(2,1)S(1)} %slice.630.refs_2_), channel_id=1, source_target_pairs={{0,1},{1,0},{2,3},{3,2},{4,5},{5,4},{6,7},{7,6},{8,9},{9,8},{10,11... | collective-permute-start | bytes 3538952 | tf_op jit(solution)/shard_map/ppermute | solution.py:23
  292.9 9.4 %collective-permute-start.34 = (bf16[768,768]{1,0:T(8,128)(2,1)S(1)}, bf16[768,768]{1,0:T(8,128)(2,1)S(1)}, u32[]{:S(2)}, u32[]{:S(2)}) collective-permute-start(bf16[768,768]{1,0:T(8,128)(2,1)S(1)} %pad_maximum_fusion.6.refs_4_), channel_id=1, source_target_pairs={{0,1},{1,0},{2,3},{3,2},{4,5},{5,4},{6,7},{7,6},{8,9},{9,8},{10,11... | collective-permute-start | bytes 3538952 | tf_op jit(solution)/shard_map/ppermute | solution.py:23
  293.9 8.4 collective-permute-start.35
  348.1 42.2 %collective-permute-start.39 = (bf16[4,768,768]{2,1,0:T(8,128)(2,1)}, bf16[4,768,768]{2,1,0:T(8,128)(2,1)}, u32[]{:S(2)}, u32[]{:S(2)}) collective-permute-start(bf16[4,768,768]{2,1,0:T(8,128)(2,1)} %get-tuple-element.182), channel_id=1, source_target_pairs={{0,1},{1,0},{2,3},{3,2},{4,5},{5,4},{6,7},{7,6},{8,9},{9,8},{10,11... | collective-permute-start | bytes 14155784 | tf_op jit(solution)/shard_map/ppermute | solution.py:23
  351.6 20.3 %collective-permute-start.36 = (bf16[384,768]{1,0:T(8,128)(2,1)}, bf16[384,768]{1,0:T(8,128)(2,1)}, u32[]{:S(2)}, u32[]{:S(2)}) collective-permute-start(bf16[384,768]{1,0:T(8,128)(2,1)} %slice.1131), channel_id=1, source_target_pairs={{0,2},{1,3},{2,0},{3,1},{4,6},{5,7},{6,4},{7,5},{8,10},{9,11},{10,... | collective-permute-start | bytes 1769480 | tf_op jit(solution)/shard_map/ppermute | solution.py:23
  360.5 16.1 %collective-permute-start.38 = (bf16[768,768]{1,0:T(8,128)(2,1)}, bf16[768,768]{1,0:T(8,128)(2,1)}, u32[]{:S(2)}, u32[]{:S(2)}) collective-permute-start(bf16[768,768]{1,0:T(8,128)(2,1)} %get-tuple-element.348), channel_id=1, source_target_pairs={{0,1},{1,0},{2,3},{3,2},{4,5},{5,4},{6,7},{7,6},{8,9},{9,8},{10,11... | collective-permute-start | bytes 3538952 | tf_op jit(solution)/shard_map/ppermute | solution.py:23
  430.6 28.5 %collective-permute-start.40 = (bf16[768,768]{1,0:T(8,128)(2,1)}, bf16[768,768]{1,0:T(8,128)(2,1)S(1)}, u32[]{:S(2)}, u32[]{:S(2)}) collective-permute-start(bf16[768,768]{1,0:T(8,128)(2,1)} %slice_bitcast_fusion.2), channel_id=1, source_target_pairs={{0,2},{1,3},{2,0},{3,1},{4,6},{5,7},{6,4},{7,5},{8,10},{9,11},{10,... | collective-permute-start | bytes 3538952 | tf_op jit(solution)/shard_map/ppermute | solution.py:23
  431.4 29.8 %collective-permute-start.41 = (bf16[2,384,768]{2,1,0:T(8,128)(2,1)}, bf16[2,384,768]{2,1,0:T(8,128)(2,1)S(1)}, u32[]{:S(2)}, u32[]{:S(2)}) collective-permute-start(bf16[2,384,768]{2,1,0:T(8,128)(2,1)} %slice.791), channel_id=1, source_target_pairs={{0,4},{4,0},{8,12},{12,8},{16,20},{20,16},{24,28},{28,24},{1,5},{5... | collective-permute-start | bytes 3538952 | tf_op jit(solution)/shard_map/ppermute | solution.py:23
  460.4 39.2 %collective-permute-start.42 = (bf16[384,768]{1,0:T(8,128)(2,1)}, bf16[384,768]{1,0:T(8,128)(2,1)}, u32[]{:S(2)}, u32[]{:S(2)}) collective-permute-start(bf16[384,768]{1,0:T(8,128)(2,1)} %slice.793), channel_id=1, source_target_pairs={{0,4},{4,0},{8,12},{12,8},{16,20},{20,16},{24,28},{28,24},{1,5},{5... | collective-permute-start | bytes 1769480 | tf_op jit(solution)/shard_map/ppermute | solution.py:23
  462.8 38.1 %collective-permute-start.43 = (bf16[384,768]{1,0:T(8,128)(2,1)}, bf16[384,768]{1,0:T(8,128)(2,1)}, u32[]{:S(2)}, u32[]{:S(2)}) collective-permute-start(bf16[384,768]{1,0:T(8,128)(2,1)} %slice_bitcast_fusion.10), channel_id=1, source_target_pairs={{0,2},{1,3},{2,0},{3,1},{4,6},{5,7},{6,4},{7,5},{8,10},{9,11},{10,... | collective-permute-start | bytes 1769480 | tf_op jit(solution)/shard_map/ppermute | solution.py:23
  507.9 46.0 %collective-permute-start.44 = (bf16[768,768]{1,0:T(8,128)(2,1)}, bf16[768,768]{1,0:T(8,128)(2,1)}, u32[]{:S(2)}, u32[]{:S(2)}) collective-permute-start(bf16[768,768]{1,0:T(8,128)(2,1)} %add_convert_fusion.4), channel_id=1, source_target_pairs={{0,1},{1,0},{2,3},{3,2},{4,5},{5,4},{6,7},{7,6},{8,9},{9,8},{10,11... | collective-permute-start | bytes 3538952 | tf_op jit(solution)/shard_map/ppermute | solution.py:23
  513.3 15.5 %collective-permute-start.45 = (bf16[768,384]{0,1:T(8,128)(2,1)S(1)}, bf16[768,384]{0,1:T(8,128)(2,1)S(1)}, u32[]{:S(2)}, u32[]{:S(2)}) collective-permute-start(bf16[768,384]{0,1:T(8,128)(2,1)S(1)} %slice_bitcast_fusion.13), channel_id=1, source_target_pairs={{0,2},{1,3},{2,0},{3,1},{4,6},{5,7},{6,4},{7,5},{8,10},{9,11},{10,... | collective-permute-start | bytes 1769480 | tf_op jit(solution)/shard_map/ppermute | solution.py:23
  513.9 15.2 %collective-permute-start.46 = (bf16[2,384,384]{1,2,0:T(8,128)(2,1)S(1)}, bf16[2,384,384]{1,2,0:T(8,128)(2,1)S(1)}, u32[]{:S(2)}, u32[]{:S(2)}) collective-permute-start(bf16[2,384,384]{1,2,0:T(8,128)(2,1)S(1)} %slice.651), channel_id=1, source_target_pairs={{0,4},{4,0},{8,12},{12,8},{16,20},{20,16},{24,28},{28,24},{1,5},{5... | collective-permute-start | bytes 1769480 | tf_op jit(solution)/shard_map/ppermute | solution.py:23
  515.2 14.8 %collective-permute-start.47 = (bf16[192,1536]{1,0:T(8,128)(2,1)S(1)}, bf16[192,1536]{1,0:T(8,128)(2,1)S(1)}, u32[]{:S(2)}, u32[]{:S(2)}) collective-permute-start(bf16[192,1536]{1,0:T(8,128)(2,1)S(1)} %pad_maximum_fusion.26), channel_id=1, source_target_pairs={{0,8},{4,12},{8,0},{12,4},{16,24},{20,28},{24,16},{28,20},{1,9},{5... | collective-permute-start | bytes 1769480 | tf_op jit(solution)/shard_map/ppermute | solution.py:23
  531.8 8.7 %collective-permute-start.49 = (bf16[384,384]{0,1:T(8,128)(2,1)}, bf16[384,384]{0,1:T(8,128)(2,1)}, u32[]{:S(2)}, u32[]{:S(2)}) collective-permute-start(bf16[384,384]{0,1:T(8,128)(2,1)} %slice.656), channel_id=1, source_target_pairs={{0,4},{4,0},{8,12},{12,8},{16,20},{20,16},{24,28},{28,24},{1,5},{5... | collective-permute-start | bytes 884744 | tf_op jit(solution)/shard_map/ppermute | solution.py:23
  537.4 14.7 %collective-permute-start.51 = (bf16[96,1536]{1,0:T(8,128)(2,1)S(1)}, bf16[96,1536]{1,0:T(8,128)(2,1)S(1)}, u32[]{:S(2)}, u32[]{:S(2)}) collective-permute-start(bf16[96,1536]{1,0:T(8,128)(2,1)S(1)} %slice.660), channel_id=1, source_target_pairs={{0,16},{4,20},{8,24},{12,28},{16,0},{20,4},{24,8},{28,12},{1,17},{... | collective-permute-start | bytes 884744 | tf_op jit(solution)/shard_map/ppermute | solution.py:23
  552.5 35.4 %collective-permute-start.53 = (bf16[192,768]{0,1:T(8,128)(2,1)S(1)}, bf16[192,768]{0,1:T(8,128)(2,1)}, u32[]{:S(2)}, u32[]{:S(2)}) collective-permute-start(bf16[192,768]{0,1:T(8,128)(2,1)S(1)} %slice.801), channel_id=1, source_target_pairs={{0,8},{4,12},{8,0},{12,4},{16,24},{20,28},{24,16},{28,20},{1,9},{5... | collective-permute-start | bytes 884744 | tf_op jit(solution)/shard_map/ppermute | solution.py:23
  587.8 43.5 %collective-permute-start.52 = (bf16[4,768,768]{2,1,0:T(8,128)(2,1)}, bf16[4,768,768]{2,1,0:T(8,128)(2,1)}, u32[]{:S(2)}, u32[]{:S(2)}) collective-permute-start(bf16[4,768,768]{2,1,0:T(8,128)(2,1)} %get-tuple-element.221), channel_id=1, source_target_pairs={{0,1},{1,0},{2,3},{3,2},{4,5},{5,4},{6,7},{7,6},{8,9},{9,8},{10,11... | collective-permute-start | bytes 14155784 | tf_op jit(solution)/shard_map/ppermute | solution.py:23
  589.9 28.0 %collective-permute-start.58 = (bf16[96,768]{0,1:T(8,128)(2,1)}, bf16[96,768]{0,1:T(8,128)(2,1)}, u32[]{:S(2)}, u32[]{:S(2)}) collective-permute-start(bf16[96,768]{0,1:T(8,128)(2,1)} %slice.811), channel_id=1, source_target_pairs={{0,16},{4,20},{8,24},{12,28},{16,0},{20,4},{24,8},{28,12},{1,17},{... | collective-permute-start | bytes 442376 | tf_op jit(solution)/shard_map/ppermute | solution.py:23
  601.7 18.8 %collective-permute-start.48 = (bf16[768,768]{1,0:T(8,128)(2,1)S(1)}, bf16[768,768]{1,0:T(8,128)(2,1)}, u32[]{:S(2)}, u32[]{:S(2)}) collective-permute-start(bf16[768,768]{1,0:T(8,128)(2,1)S(1)} %get-tuple-element.342), channel_id=1, source_target_pairs={{0,1},{1,0},{2,3},{3,2},{4,5},{5,4},{6,7},{7,6},{8,9},{9,8},{10,11... | collective-permute-start | bytes 3538952 | tf_op jit(solution)/shard_map/ppermute | solution.py:23
  672.0 28.2 %collective-permute-start.54 = (bf16[768,768]{1,0:T(8,128)(2,1)S(1)}, bf16[768,768]{1,0:T(8,128)(2,1)S(1)}, u32[]{:S(2)}, u32[]{:S(2)}) collective-permute-start(bf16[768,768]{1,0:T(8,128)(2,1)S(1)} %copy-done.131), channel_id=1, source_target_pairs={{0,2},{1,3},{2,0},{3,1},{4,6},{5,7},{6,4},{7,5},{8,10},{9,11},{10,... | collective-permute-start | bytes 3538952 | tf_op jit(solution)/shard_map/ppermute | solution.py:23
  672.6 29.7 %collective-permute-start.55 = (bf16[2,384,768]{2,1,0:T(8,128)(2,1)S(1)}, bf16[2,384,768]{2,1,0:T(8,128)(2,1)S(1)}, u32[]{:S(2)}, u32[]{:S(2)}) collective-permute-start(bf16[2,384,768]{2,1,0:T(8,128)(2,1)S(1)} %copy-done.130), channel_id=1, source_target_pairs={{0,4},{4,0},{8,12},{12,8},{16,20},{20,16},{24,28},{28,24},{1,5},{5... | collective-permute-start | bytes 3538952 | tf_op jit(solution)/shard_map/ppermute | solution.py:23
  701.5 37.2 %collective-permute-start.56 = (bf16[384,768]{1,0:T(8,128)(2,1)}, bf16[384,768]{1,0:T(8,128)(2,1)}, u32[]{:S(2)}, u32[]{:S(2)}) collective-permute-start(bf16[384,768]{1,0:T(8,128)(2,1)} %slice.807), channel_id=1, source_target_pairs={{0,4},{4,0},{8,12},{12,8},{16,20},{20,16},{24,28},{28,24},{1,5},{5... | collective-permute-start | bytes 1769480 | tf_op jit(solution)/shard_map/ppermute | solution.py:23
  703.5 36.6 %collective-permute-start.57 = (bf16[384,768]{1,0:T(8,128)(2,1)}, bf16[384,768]{1,0:T(8,128)(2,1)}, u32[]{:S(2)}, u32[]{:S(2)}) collective-permute-start(bf16[384,768]{1,0:T(8,128)(2,1)} %slice_bitcast_fusion.8), channel_id=1, source_target_pairs={{0,2},{1,3},{2,0},{3,1},{4,6},{5,7},{6,4},{7,5},{8,10},{9,11},{10,... | collective-permute-start | bytes 1769480 | tf_op jit(solution)/shard_map/ppermute | solution.py:23
  747.3 45.1 %collective-permute-start.59 = (bf16[768,768]{1,0:T(8,128)(2,1)}, bf16[768,768]{1,0:T(8,128)(2,1)}, u32[]{:S(2)}, u32[]{:S(2)}) collective-permute-start(bf16[768,768]{1,0:T(8,128)(2,1)} %add_convert_fusion.2), channel_id=1, source_target_pairs={{0,1},{1,0},{2,3},{3,2},{4,5},{5,4},{6,7},{7,6},{8,9},{9,8},{10,11... | collective-permute-start | bytes 3538952 | tf_op jit(solution)/shard_map/ppermute | solution.py:23
  752.2 16.1 %collective-permute-start.61 = (bf16[768,384]{0,1:T(8,128)(2,1)}, bf16[768,384]{0,1:T(8,128)(2,1)}, u32[]{:S(2)}, u32[]{:S(2)}) collective-permute-start(bf16[768,384]{0,1:T(8,128)(2,1)} %slice_bitcast_fusion.12), channel_id=1, source_target_pairs={{0,2},{1,3},{2,0},{3,1},{4,6},{5,7},{6,4},{7,5},{8,10},{9,11},{10,... | collective-permute-start | bytes 1769480 | tf_op jit(solution)/shard_map/ppermute | solution.py:23
  754.2 15.8 %collective-permute-start.62 = (bf16[2,384,384]{1,2,0:T(8,128)(2,1)}, bf16[2,384,384]{1,2,0:T(8,128)(2,1)}, u32[]{:S(2)}, u32[]{:S(2)}) collective-permute-start(bf16[2,384,384]{1,2,0:T(8,128)(2,1)} %slice.682), channel_id=1, source_target_pairs={{0,4},{4,0},{8,12},{12,8},{16,20},{20,16},{24,28},{28,24},{1,5},{5... | collective-permute-start | bytes 1769480 | tf_op jit(solution)/shard_map/ppermute | solution.py:23
  755.4 15.9 %collective-permute-start.63 = (bf16[192,1536]{1,0:T(8,128)(2,1)}, bf16[192,1536]{1,0:T(8,128)(2,1)}, u32[]{:S(2)}, u32[]{:S(2)}) collective-permute-start(bf16[192,1536]{1,0:T(8,128)(2,1)} %pad_maximum_fusion.24), channel_id=1, source_target_pairs={{0,8},{4,12},{8,0},{12,4},{16,24},{20,28},{24,16},{28,20},{1,9},{5... | collective-permute-start | bytes 1769480 | tf_op jit(solution)/shard_map/ppermute | solution.py:23
  772.8 8.4 collective-permute-start.64
  775.0 15.4 %collective-permute-start.66 = (bf16[96,1536]{1,0:T(8,128)(2,1)S(1)}, bf16[96,1536]{1,0:T(8,128)(2,1)S(1)}, u32[]{:S(2)}, u32[]{:S(2)}) collective-permute-start(bf16[96,1536]{1,0:T(8,128)(2,1)S(1)} %slice.690), channel_id=1, source_target_pairs={{0,16},{4,20},{8,24},{12,28},{16,0},{20,4},{24,8},{28,12},{1,17},{... | collective-permute-start | bytes 884744 | tf_op jit(solution)/shard_map/ppermute | solution.py:23
  809.5 11.0 %collective-permute-start.67 = (bf16[192,768]{0,1:T(8,128)(2,1)S(1)}, bf16[192,768]{0,1:T(8,128)(2,1)S(1)}, u32[]{:S(2)}, u32[]{:S(2)}) collective-permute-start(bf16[192,768]{0,1:T(8,128)(2,1)S(1)} %slice.692), channel_id=1, source_target_pairs={{0,8},{4,12},{8,0},{12,4},{16,24},{20,28},{24,16},{28,20},{1,9},{5... | collective-permute-start | bytes 884744 | tf_op jit(solution)/shard_map/ppermute | solution.py:23
  814.1 21.3 %collective-permute-start.60 = (bf16[384,768]{1,0:T(8,128)(2,1)S(1)}, bf16[384,768]{1,0:T(8,128)(2,1)}, u32[]{:S(2)}, u32[]{:S(2)}) collective-permute-start(bf16[384,768]{1,0:T(8,128)(2,1)S(1)} %slice.1130), channel_id=1, source_target_pairs={{0,2},{1,3},{2,0},{3,1},{4,6},{5,7},{6,4},{7,5},{8,10},{9,11},{10,... | collective-permute-start | bytes 1769480 | tf_op jit(solution)/shard_map/ppermute | solution.py:23
  820.7 11.1 %collective-permute-start.68 = (bf16[96,768]{0,1:T(8,128)(2,1)S(1)}, bf16[96,768]{0,1:T(8,128)(2,1)S(1)}, u32[]{:S(2)}, u32[]{:S(2)}) collective-permute-start(bf16[96,768]{0,1:T(8,128)(2,1)S(1)} %slice.821), channel_id=1, source_target_pairs={{0,16},{4,20},{8,24},{12,28},{16,0},{20,4},{24,8},{28,12},{1,17},{... | collective-permute-start | bytes 442376 | tf_op jit(solution)/shard_map/ppermute | solution.py:23
  (190 other events, 2415.0 us)

commit v3 on v2

v3 whole, which is shorter than its diff:
```python
import functools
import math

import jax
import jax.numpy as jnp
from jax import lax
from jax.experimental import pallas as pl
from jax.experimental.pallas import tpu as pltpu
from jax.sharding import PartitionSpec as P

HD = 64
WIDE = 128
eps = 1e-05
LOG2E = 1.0 / math.log(2.0)
LN2 = math.log(2.0)
MASKED = -1e30
bf16 = jnp.bfloat16
f32 = jnp.float32


def exchange(value, axis, mask):
    count = lax.axis_size(axis)
    return lax.ppermute(value, axis, [(i, i ^ mask) for i in range(count)])


def dp_masks():
    count = lax.axis_size("dp")
    masks = []
    while count > 1:
        count //= 2
        masks.append(count)
    return masks


def relative_mask(position):
    result = 0
    for at, mask in enumerate(dp_masks()):
        result = result + ((position >> at) & 1) * mask
    return result


def together(*values):
    return lax.optimization_barrier(values)


def gather_steps(first, second):
    masks = dp_masks()
    cut = first.shape[1]

    def z_step(mask):
        def step(state):
            return (jnp.concatenate([state[0], exchange(state[0], "dp", mask)], axis=0),)

        return step

    def near(state):
        first, second = state[0][:, :cut], state[0][:, cut:]
        first, second = together(first, second)
        first_more, other = exchange(first, "dp", masks[-1]), exchange(second, "tensor", 2)
        return jnp.concatenate([first, first_more], axis=0), jnp.stack([second, other])

    def last(state):
        first, second = state
        other, more = exchange(first, "tensor", 2), exchange(second, "dp", masks[-1])
        second = [jnp.concatenate([second[i], more[i]], axis=0) for i in range(2)]
        return first, other, *second

    start = (jnp.concatenate([first, second], axis=1),)
    return start, [z_step(mask) for mask in masks[:-1]], [near, last]


class Gathering:
    def __init__(self, groups):
        made = [gather_steps(*group) for group in groups]
        self.states = [start for start, _, _ in made]
        self.plan = [[(0, step)] for step in made[0][1]]
        for at, (_, _, near) in enumerate(made):
            ahead = made[at + 1][1] if at + 1 < len(made) else []
            count = max(len(near), len(ahead))
            for i in range(count):
                stage = [(at, near[i])] if i < len(near) else []
                self.plan.append(stage + ([(at + 1, ahead[i])] if i < len(ahead) else []))
        self.ends = []
        for at in range(len(made)):
            self.ends.append(max(i for i, stage in enumerate(self.plan) for g, _ in stage if g == at))
        self.done = 0

    def advance(self, *others):
        stage = self.plan[self.done]
        self.done += 1
        results = [step(self.states[g]) for g, step in stage]
        flat = [part for result in results for part in result]
        flat = together(*flat, *others)
        at = 0
        for (g, _), result in zip(stage, results):
            self.states[g] = flat[at : at + len(result)]
            at += len(result)
        self.token = flat[0]
        return flat[at:]

    def until(self, group):
        while self.done <= self.ends[group]:
            self.advance()
        return self.states[group]


def behind(values, *tokens):
    return together(*values, *tokens)[: len(values)]


def add_low(kept, received):
    return (kept.astype(f32) + received.astype(f32)).astype(bf16)


def near_one(first, second):
    mask = dp_masks()[-1]
    half = first.shape[1] // 2
    return (
        add_low(first[0], exchange(first[1], "tensor", 2)),
        add_low(second[:, :half], exchange(second[:, half:], "dp", mask)),
    )


def near_core(own, received):
    mask = dp_masks()[-1]
    half = own.shape[1] // 2
    sent = together(add_low(own[1], received[1]), add_low(own[2:, half:], received[2:, half:]))

    def finish():
        first, second = exchange(sent[0], "tensor", 2), exchange(sent[1], "dp", mask)
        first = own[0].astype(f32) + received[0].astype(f32) + first.astype(f32)
        kept = own[2:, :half].astype(f32) + received[2:, :half].astype(f32)
        return first.astype(bf16), (kept + second.astype(f32)).astype(bf16)

    return sent, finish


def near_two(first, second):
    mask = dp_masks()[-1]
    half = first.shape[0] // 2
    return (
        add_low(first[:half], exchange(first[half:], "dp", mask)),
        add_low(second[0], exchange(second[1], "tensor", 2)),
    )


def far(value, masks):
    for mask in masks:
        half = value.shape[0] // 2
        value = add_low(value[:half], exchange(value[half:], "dp", mask))
    return value


class Folding:
    def __init__(self, qk, vo, up, down):
        masks = dp_masks()[-2::-1]
        self.masks = masks[:-1], masks[-1:]
        self.attn = together(qk, vo)
        self.feed = jnp.concatenate([up, down], axis=1)
        self.step = 0

    def advance(self):
        step = self.step
        self.step += 1
        if step < 2:
            attn = (near_one, near_two)[step](*self.attn)
            *attn, self.feed = together(*attn, far(self.feed, self.masks[step]))
            self.attn = attn if step == 0 else jnp.concatenate(attn, axis=1)
        else:
            (self.attn,) = together(far(self.attn, self.masks[step - 2]))

    def token(self):
        return (self.feed, self.attn) if self.step > 1 else (self.feed, *self.attn)

    def result(self):
        half, low = self.attn.shape[1] // 2, self.feed.shape[1] // 2
        parts = self.attn[:, :half], self.attn[:, half:], self.feed[:, :low], self.feed[:, low:]
        return [part.astype(f32) for part in parts]


def split_low(value):
    high = value.astype(bf16)
    rest = value - high.astype(f32)
    mid = rest.astype(bf16)
    return high, mid, (rest - mid.astype(f32)).astype(bf16)


def lane_at(rows):
    return lax.broadcasted_iota(jnp.int32, (rows, WIDE - HD), 1)


def key_extra(rows, row_count, quarter, ones):
    lane = lane_at(rows)
    row = lax.broadcasted_iota(jnp.int32, (rows, WIDE - HD), 0)
    masked = lax.rem(row, quarter) >= row_count
    bias = jnp.where(masked, MASKED, 0.0).astype(f32)
    value = jnp.where(lane == 0, bias, jnp.where(lane <= ones, 1.0, 0.0))
    return value.astype(bf16)


def ones_extra(rows, ones):
    return jnp.where(lane_at(rows) < ones, 1.0, 0.0).astype(bf16)


def widen(part, extra):
    return jnp.concatenate([part, extra], axis=1)


def nt_dot(left, right):
    return lax.dot_general(left, right, (((1,), (1,)), ((), ())), preferred_element_type=f32)


def nn_dot(left, right):
    return lax.dot_general(left, right, (((1,), (0,)), ((), ())), preferred_element_type=f32)


def tn_dot(left, right):
    return lax.dot_general(left, right, (((0,), (0,)), ((), ())), preferred_element_type=f32)


def whole(shape):
    return pl.BlockSpec(shape, lambda j: (0,) * len(shape))


def attend_kernel(row_count, quarter, step, first, *refs):
    normed_a, normed_b, w_qk, w_vo, bias = refs[:5]
    before = () if first else refs[5:7]
    share_a, share_b, qkv, o, lse, q_s, k_s, v_s = refs[5 + len(before) :]
    rows = normed_a.shape[0]
    wide = o.shape[1]
    heads = wide // HD
    k_more = key_extra(rows, row_count, quarter, 0)
    one = ones_extra(rows, 1)
    lane = lax.broadcasted_iota(jnp.int32, (1, 2 * wide), 1)
    scale = jnp.where(lane < wide, HD**-0.5 * LOG2E, 1.0)
    for half, normed in enumerate((normed_a, normed_b)):
        at = pl.ds(half * rows, rows)
        qk = ((nn_dot(normed[...], w_qk[...]) + bias[0:1, :]) * scale).astype(bf16)
        v = (nn_dot(normed[...], w_vo[:, :wide]) + bias[1:2, :wide]).astype(bf16)
        qkv[at, : 2 * wide] = qk
        qkv[at, 2 * wide :] = v
        for h in range(heads):
            low, high = h * HD, (h + 1) * HD
            q_s[h, at, :] = widen(qk[:, low:high], one)
            k_s[h, at, :] = widen(qk[:, wide + low : wide + high], k_more)
            v_s[h, at, :] = widen(v[:, low:high], one)

    for h in range(heads):

        def work(i, carry, h=h):
            for part in range(2):
                at = pl.ds(pl.multiple_of((2 * i + part) * step, step), step)
                scores = nt_dot(q_s[h, at, :], k_s[h])
                top = jnp.max(scores, axis=-1, keepdims=True)
                weights = jnp.exp2(scores - top).astype(bf16)
                summed = nn_dot(weights, v_s[h])
                total = summed[:, HD : HD + 1]
                o[at, h * HD : (h + 1) * HD] = (summed[:, :HD] / total).astype(bf16)
                lse[at, h : h + 1] = top + jnp.log2(total)
            return carry

        lax.fori_loop(0, rows // step, work, 0)
    w_o = w_vo[:, wide:]
    part_a = nt_dot(o[pl.ds(0, rows), :], w_o)
    part_b = nt_dot(o[pl.ds(rows, rows), :], w_o)
    if not first:
        part_a = part_a + before[0][...]
        part_b = part_b + before[1][...]
    share_a[...] = part_a
    share_b[...] = part_b.astype(share_b.dtype)


def attend(row_count, quarter, normed_a, normed_b, w_qk, w_vo, bias, before):
    rows, width = normed_a.shape
    wide = w_qk.shape[1] // 2
    heads = wide // HD
    operands = (normed_a, normed_b, w_qk, w_vo, bias, *before)
    outs = [
        jax.ShapeDtypeStruct((rows, width), f32),
        jax.ShapeDtypeStruct((rows, width), bf16 if before else f32),
        jax.ShapeDtypeStruct((2 * rows, 3 * wide), bf16),
        jax.ShapeDtypeStruct((2 * rows, wide), bf16),
        jax.ShapeDtypeStruct((2 * rows, 8), f32),
    ]
    return pl.pallas_call(
        functools.partial(attend_kernel, row_count, quarter, min(256, rows), not before),
        grid=(1,),
        in_specs=[whole(part.shape) for part in operands],
        out_specs=[whole(part.shape) for part in outs],
        out_shape=outs,
        scratch_shapes=[pltpu.VMEM((heads, 2 * rows, WIDE), bf16)] * 3,
        compiler_params=pltpu.CompilerParams(vmem_limit_bytes=56 * 2**20),
    )(*operands)


def attend_back_kernel(row_count, quarter, step, first, *refs):
    branch_a, branch_b, w_qk, w_vo, qkv, o, lse = refs[:7]
    before = () if first else refs[7:9]
    dn_a, dn_b, dqkv, q_s, k_s, kt_s, v_s, do_s, dq_s, dk_s, dv_s = refs[7 + len(before) :]
    rows = branch_a.shape[0]
    wide = o.shape[1]
    heads = wide // HD
    k_more = key_extra(rows, row_count, quarter, 3)
    three = ones_extra(rows, 3)
    lane = lane_at(rows)

    def spread_lanes(first, parts):
        value = jnp.where(lane < first, 1.0, 0.0).astype(f32)
        for at, part in enumerate(parts):
            value = jnp.where(lane == first + at, part.astype(f32), value)
        return value.astype(bf16)

    for half, branch in enumerate((branch_a, branch_b)):
        at = pl.ds(half * rows, rows)
        grad_all = nn_dot(branch[...], w_vo[:, wide:]).astype(bf16)
        for h in range(heads):
            low, high = h * HD, (h + 1) * HD
            minus_lse = split_low(-lse[at, h : h + 1])
            q_s[h, at, :] = widen(qkv[at, low:high], spread_lanes(1, minus_lse))
            keys = widen(qkv[at, wide + low : wide + high], k_more)
            k_s[h, at, :] = keys
            kt_s[h, :, at] = jnp.transpose(keys.astype(f32)).astype(bf16)
            v_s[h, at, :] = widen(qkv[at, 2 * wide + low : 2 * wide + high], three)
            grad = grad_all[:, low:high]
            inner = jnp.sum(grad.astype(f32) * o[at, low:high].astype(f32), axis=1, keepdims=True)
            do_s[h, at, :] = widen(grad, spread_lanes(0, split_low(-inner)))

    dk_s[...] = jnp.zeros_like(dk_s)
    dv_s[...] = jnp.zeros_like(dv_s)
    chunks = 2 * rows // step

    def work(i, carry):
        h = i // chunks
        at = pl.ds(pl.multiple_of(lax.rem(i, chunks) * step, step), step)
        queries = q_s[h, at, :]
        grad_out = do_s[h, at, :]
        probs = jnp.exp2(nt_dot(k_s[h], queries))
        grad_scores = (probs * nt_dot(v_s[h], grad_out)).astype(bf16)
        dv_s[h] += nn_dot(probs.astype(bf16), grad_out)
        dk_s[h] += nn_dot(grad_scores, queries)
        dq_s[h, at, :] = jnp.transpose(nn_dot(kt_s[h], grad_scores))
        return carry

    lax.fori_loop(0, heads * chunks, work, 0)
    for h in range(heads):
        low, high = h * HD, (h + 1) * HD
        dqkv[:, low:high] = (dq_s[h][:, :HD] * HD**-0.5).astype(bf16)
        dqkv[:, wide + low : wide + high] = (dk_s[h][:, :HD] * LN2).astype(bf16)
        dqkv[:, 2 * wide + low : 2 * wide + high] = dv_s[h][:, :HD].astype(bf16)
    for half, dest in enumerate((dn_a, dn_b)):
        at = pl.ds(half * rows, rows)
        part = nt_dot(dqkv[at, : 2 * wide], w_qk[...])
        part = part + nt_dot(dqkv[at, 2 * wide :], w_vo[:, :wide])
        if not first:
            part = part + before[half][...]
        dest[...] = part.astype(dest.dtype)


def attend_back(row_count, quarter, branch_a, branch_b, w_qk, w_vo, qkv, o, lse, before):
    rows, width = branch_a.shape
    wide = o.shape[1]
    heads = wide // HD
    operands = (branch_a, branch_b, w_qk, w_vo, qkv, o, lse, *before)
    outs = [
        jax.ShapeDtypeStruct((rows, width), f32),
        jax.ShapeDtypeStruct((rows, width), bf16 if before else f32),
        jax.ShapeDtypeStruct((2 * rows, 3 * wide), bf16),
    ]
    return pl.pallas_call(
        functools.partial(attend_back_kernel, row_count, quarter, min(256, rows), not before),
        grid=(1,),
        in_specs=[whole(part.shape) for part in operands],
        out_specs=[whole(part.shape) for part in outs],
        out_shape=outs,
        scratch_shapes=[
            pltpu.VMEM((heads, 2 * rows, WIDE), bf16),
            pltpu.VMEM((heads, 2 * rows, WIDE), bf16),
            pltpu.VMEM((heads, WIDE, 2 * rows), bf16),
            pltpu.VMEM((heads, 2 * rows, WIDE), bf16),
            pltpu.VMEM((heads, 2 * rows, WIDE), bf16),
            pltpu.VMEM((heads, 2 * rows, WIDE), f32),
            pltpu.VMEM((heads, 2 * rows, WIDE), f32),
            pltpu.VMEM((heads, 2 * rows, WIDE), f32),
        ],
        compiler_params=pltpu.CompilerParams(vmem_limit_bytes=60 * 2**20),
    )(*operands)


def normalized(value):
    centred = value - jnp.mean(value, axis=-1, keepdims=True)
    scale = lax.rsqrt(jnp.mean(centred * centred, axis=-1, keepdims=True) + eps)
    return centred * scale, scale


def norm_back(value, gain, grad):
    unit, scale = normalized(value)
    scaled = grad * gain
    result = scale * (
        scaled
        - jnp.mean(scaled, axis=-1, keepdims=True)
        - unit * jnp.mean(scaled * unit, axis=-1, keepdims=True)
    )
    sums = [jnp.sum(part, axis=0, keepdims=True) for part in (grad * unit, grad)]
    return result, *sums


def gelu_both(value):
    share = 0.5 * (1.0 + lax.erf(value * math.sqrt(0.5)))
    density = jnp.exp(-0.5 * value * value) * (1.0 / math.sqrt(2.0 * math.pi))
    return (value * share).astype(bf16), (share + value * density).astype(bf16)


def feed_kernel(final, *refs):
    current, share_a, share_b, vectors, bias = refs[:5]
    ups, downs, activated, slopes = [refs[5 + 4 * i : 9 + 4 * i] for i in range(4)]
    middle, normed, total = refs[21:24]
    j = pl.program_id(0)

    @pl.when(j == 0)
    def _():
        value = current[...] + (share_a[...] + share_b[...].astype(f32) + vectors[0:1, :])
        middle[...] = value
        normed[...] = (normalized(value)[0] * vectors[1:2, :] + vectors[2:3, :]).astype(bf16)
        total[...] = value + vectors[3:4, :]

    rows_in = normed[...]
    for t in range(4):
        upward = nn_dot(rows_in, ups[t][...]) + bias[t : t + 1, :]
        activated[t][...], slopes[t][...] = gelu_both(upward)
    joined = jnp.concatenate([ref[...] for ref in activated], axis=1)
    down = jnp.concatenate([ref[...] for ref in downs], axis=1)
    total[...] += nt_dot(joined, down)
    if not final:
        following = refs[24]

        @pl.when(j == pl.num_programs(0) - 1)
        def _():
            unit, _ = normalized(total[...])
            following[...] = (unit * vectors[4:5, :] + vectors[5:6, :]).astype(bf16)


def single(shape):
    return pl.BlockSpec(shape, lambda j: (0,) * len(shape), pipeline_mode=pl.Buffered(1))


def column_block(rows, step):
    return pl.BlockSpec((rows, step), lambda j: (0, j))


def feed(final, current, share_a, share_b, vectors, bias, ups, downs):
    rows, width = current.shape
    hidden = bias.shape[1]
    step = min(256, hidden)
    rest = [f32, bf16, f32] if final else [f32, bf16, f32, bf16]
    fronts = (current, share_a, share_b, vectors)
    return pl.pallas_call(
        functools.partial(feed_kernel, final),
        grid=(hidden // step,),
        in_specs=[single(part.shape) for part in fronts]
        + [column_block(4, step)]
        + [column_block(width, step)] * 8,
        out_specs=[column_block(rows, step)] * 8 + [whole((rows, width))] * len(rest),
        out_shape=[jax.ShapeDtypeStruct((rows, hidden), bf16)] * 8
        + [jax.ShapeDtypeStruct((rows, width), kind) for kind in rest],
        compiler_params=pltpu.CompilerParams(vmem_limit_bytes=60 * 2**20),
    )(*fronts, bias, *ups, *downs)


def feed_back_kernel(final, *refs):
    count = 1 if final else 4
    fronts, refs = refs[:count], refs[count:]
    middle, normed, vectors = refs[:3]
    ups, downs, activated, slopes = [refs[3 + 4 * i : 7 + 4 * i] for i in range(4)]
    own, other, bias_grad, grad_out, branch, sums = refs[19:25]
    total, grad, grad_low, normed_t, grad_t = refs[25:]
    j = pl.program_id(0)

    @pl.when(j == 0)
    def _():
        sums[...] = jnp.zeros_like(sums)
        if final:
            value = fronts[0][...].astype(f32)
        else:
            above, layer_out, share_a, share_b = fronts
            grad_normed = share_a[...] + share_b[...].astype(f32)
            value, gain_one, shift_one = norm_back(layer_out[...], vectors[1:2, :], grad_normed)
            value = value + above[...]
            sums[4:5, :], sums[5:6, :] = gain_one, shift_one
        grad[...] = value
        low = value.astype(bf16)
        grad_low[...] = low
        sums[0:1, :] = jnp.sum(low.astype(f32), axis=0, keepdims=True)
        normed_t[...] = jnp.transpose(normed[...].astype(f32)).astype(bf16)
        grad_t[...] = jnp.transpose(low.astype(f32)).astype(bf16)
        total[...] = jnp.zeros_like(total)

    grad_rows = grad_low[...]
    grad_ups = []
    for t in range(4):
        grad_act = nn_dot(grad_rows, downs[t][...])
        scaled = grad_act * slopes[t][...].astype(f32)
        grad_ups.append(scaled.astype(bf16))
        bias_grad[t : t + 1, :] = jnp.sum(scaled, axis=0, keepdims=True)
        dest = (own, other)[t % 2]
        dest[t // 2] = nn_dot(normed_t[...], grad_ups[t]).astype(bf16)
        dest[2 + t // 2] = nn_dot(grad_t[...], activated[t][...]).astype(bf16)
    joined = jnp.concatenate(grad_ups, axis=1)
    up = jnp.concatenate([ref[...] for ref in ups], axis=1)
    total[...] += nt_dot(joined, up)

    @pl.when(j == pl.num_programs(0) - 1)
    def _():
        value, gain_two, shift_two = norm_back(middle[...], vectors[0:1, :], total[...])
        value = value + grad[...]
        grad_out[...] = value
        low = value.astype(bf16)
        branch[...] = low
        sums[1:2, :], sums[2:3, :] = gain_two, shift_two
        sums[3:4, :] = jnp.sum(low.astype(f32), axis=0, keepdims=True)


def feed_back(final, fronts, middle, normed, vectors, ups, downs, activated, slopes):
    rows, width = normed.shape
    hidden = activated[0].shape[1]
    step = min(256, hidden)
    stack = pl.BlockSpec((4, width, step), lambda j: (0, 0, j))
    singles = (*fronts, middle, normed, vectors)
    return pl.pallas_call(
        functools.partial(feed_back_kernel, final),
        grid=(hidden // step,),
        in_specs=[single(part.shape) for part in singles]
        + [column_block(width, step)] * 8
        + [column_block(rows, step)] * 8,
        out_specs=[stack] * 2
        + [column_block(4, step)]
        + [whole((rows, width))] * 2
        + [whole((8, width))],
        out_shape=[jax.ShapeDtypeStruct((4, width, hidden), bf16)] * 2
        + [
            jax.ShapeDtypeStruct((4, hidden), f32),
            jax.ShapeDtypeStruct((rows, width), f32),
            jax.ShapeDtypeStruct((rows, width), bf16),
            jax.ShapeDtypeStruct((8, width), f32),
        ],
        scratch_shapes=[pltpu.VMEM((rows, width), f32)] * 2
        + [pltpu.VMEM((rows, width), bf16)]
        + [pltpu.VMEM((width, rows), bf16)] * 2,
        compiler_params=pltpu.CompilerParams(vmem_limit_bytes=62 * 2**20),
    )(*singles, *ups, *downs, *activated, *slopes)


def local(
    frames,
    cotangent,
    qkv_weight,
    out_weight,
    up_weight,
    down_weight,
    qv_bias,
    up_bias,
    norm_gains,
    norm_shifts,
    out_biases,
):
    layers, block = qkv_weight.shape[:2]
    wide = qkv_weight.shape[3]
    row_count, width = frames.shape[1:]
    hidden = up_weight.shape[2]
    quarter = -(-row_count // 128) * 128
    rows = 2 * quarter
    count_dp = lax.axis_size("dp")
    me = lax.axis_index("dp")
    t_me = lax.axis_index("tensor")
    y_me = t_me // 2
    t_order = jnp.arange(4) ^ t_me
    positions = jnp.arange(count_dp)
    block_at = relative_mask(positions) ^ me
    place_of = jnp.argmax(block_at[None, :] == positions[:, None], axis=1)

    small_parts = (norm_gains, norm_shifts, out_biases, qv_bias, up_bias)
    small_sizes = [part.size for part in small_parts]
    small = jnp.concatenate([part.reshape(1, -1) for part in small_parts], axis=1)

    source = jnp.repeat(block_at, block) * block + jnp.tile(jnp.arange(block), count_dp)
    to_relative = (jnp.arange(width)[:, None] == source[None, :]).astype(bf16)

    def take_clip(value):
        mine = lax.dynamic_index_in_dim(value, y_me, 0, keepdims=False)
        theirs = exchange(lax.dynamic_index_in_dim(value, 1 - y_me, 0, keepdims=False), "tensor", 2)
        padding = ((0, 0), (0, quarter - row_count), (0, 0))
        both = jnp.pad(jnp.stack([mine, theirs]), padding).reshape(rows, width)
        return nn_dot(both, to_relative)

    def give_clip(value):
        mine, theirs = value[:quarter], value[quarter:].astype(bf16)
        theirs = nt_dot(exchange(theirs, "tensor", 2), to_relative)[:row_count]
        high = mine.astype(bf16)
        low = (mine - high.astype(f32)).astype(bf16)
        mine = (nt_dot(high, to_relative) + nt_dot(low, to_relative))[:row_count]
        first = y_me == 0
        return jnp.stack([jnp.where(first, mine, theirs), jnp.where(first, theirs, mine)])

    current = take_clip(frames)
    gradient = take_clip(cotangent)

    groups = []
    for at in range(layers):
        qk = jnp.concatenate([qkv_weight[at, :, 0], qkv_weight[at, :, 1]], axis=1)
        vo = jnp.concatenate([qkv_weight[at, :, 2], out_weight[at].T], axis=1)
        groups += [(qk, vo), (up_weight[at], down_weight[at].T)]
    gathering = Gathering(groups)
    for mask in dp_masks():
        more = exchange(small, "dp", mask)
        if mask > 1:
            (more,) = gathering.advance(more)
        small = jnp.concatenate([small, more], axis=0)
    small = jnp.stack([small, exchange(small, "tensor", 1)])
    small = jnp.stack([small, exchange(small, "tensor", 2)])
    small = small.reshape(4, count_dp, -1)
    by_part = jnp.split(small, [sum(small_sizes[: i + 1]) for i in range(4)], axis=2)

    def by_width(part):
        part = jnp.take(part, t_order, axis=0).reshape(4, count_dp, layers, 2, -1)
        return part.transpose(2, 3, 1, 0, 4).reshape(layers, 2, width)

    gain_all, shift_all, obias_all = [by_width(part) for part in by_part[:3]]
    qv_all = jnp.take(by_part[3][0::2], place_of, axis=1).reshape(2, count_dp, layers, 2, -1)
    qv_all = qv_all.transpose(2, 3, 0, 1, 4).reshape(layers, 2, 2, wide)
    up_all = jnp.take(by_part[4], place_of, axis=1).reshape(4, count_dp, layers, -1)
    up_all = up_all.transpose(2, 0, 1, 3).reshape(layers, 4, hidden)

    def feed_weights(group):
        parts = gathering.until(group)
        return [
            [parts[2 * i], exchange(parts[2 * i], "tensor", 1), parts[2 * i + 1], exchange(parts[2 * i + 1], "tensor", 1)]
            for i in range(2)
        ]

    weights = []
    saved = []
    unit, _ = normalized(current)
    normed_a = (unit * gain_all[0, 0] + shift_all[0, 0]).astype(bf16)
    normed_b = exchange(normed_a, "tensor", 1)
    for at in range(layers):
        final = at == layers - 1
        w_qk, w_qk_other, w_vo, w_vo_other = gathering.until(2 * at)
        w_attn = ((w_qk, w_vo), (w_qk_other, w_vo_other))
        bias = jnp.pad(qv_all[at].transpose(1, 0, 2), ((0, 0), (0, 0), (0, wide)))
        shares = ()
        heads = []
        for t in range(2):
            ready = (normed_a, normed_b)
            if t == 1:
                gathering.advance()
                ready = behind(ready, gathering.token, *shares)
            out = attend(row_count, quarter, *ready, *w_attn[t], bias[t], shares)
            shares = tuple(out[:2])
            heads.append(out[2:])
        share_b = exchange(shares[1], "tensor", 1)
        w_up, w_down = feed_weights(2 * at + 1)
        following = 0 if final else at + 1
        vectors = jnp.stack(
            [
                obias_all[at, 0],
                gain_all[at, 1],
                shift_all[at, 1],
                obias_all[at, 1],
                gain_all[following, 0],
                shift_all[following, 0],
            ]
        )
        vectors = jnp.pad(vectors, ((0, 2), (0, 0)))
        fed = feed(final, current, shares[0], share_b, vectors, up_all[at], w_up, w_down)
        weights.append((w_attn, w_up, w_down))
        normed = jnp.concatenate([normed_a, normed_b], axis=0)
        saved.append((current, normed, heads, fed[:4], fed[4:8], fed[8], fed[9]))
        current = fed[10]
        if not final:
            normed_a = fed[11]
            normed_b = exchange(normed_a, "tensor", 1)
    encoded = give_clip(current)

    small_grads = [None] * layers
    weight_grads = [None] * layers
    gains_one = [None] * layers
    folding = None
    fronts = (gradient,)
    for at in reversed(range(layers)):
        final = at == layers - 1
        w_attn, w_up, w_down = weights[at]
        layer_in, normed, heads, activated, slopes, middle, normed_two = saved[at]
        if folding is not None:
            folding.advance()
            fronts = behind(fronts, *folding.token())
        vectors = jnp.stack([gain_all[at, 1], gain_all[0 if final else at + 1, 0]])
        vectors = jnp.pad(vectors, ((0, 6), (0, 0)))
        own, other, bup, gradient, branch_a, sums = feed_back(
            final, fronts, middle, normed_two, vectors, w_up, w_down, activated, slopes
        )
        if not final:
            gains_one[at + 1] = sums[4:6]
        branch_b = exchange(branch_a, "tensor", 1)
        sent, finish = near_core(own, exchange(other, "tensor", 1))
        shares = ()
        dqkv = []
        for t in range(2):
            tokens = list(sent) if t == 0 else list(feed_state) + list(shares)
            if folding is not None:
                folding.advance()
                tokens += folding.token()
            ready = behind((branch_a, branch_b), *tokens)
            *shares, part = attend_back(
                row_count, quarter, *ready, *w_attn[t], *heads[t], tuple(shares)
            )
            dqkv.append(part)
            feed_state = near_two(*feed_state) if t else finish()
        tokens = list(feed_state)
        if folding is not None:
            folding.advance()
            tokens += folding.token()
            weight_grads[at + 1] = folding.result()
        *shares, dqkv[0], dqkv[1] = behind((*shares, *dqkv), *tokens)
        share_b = exchange(shares[1], "tensor", 1)
        branch = jnp.concatenate([branch_a, branch_b], axis=0)
        dw = [tn_dot(normed, dqkv[t]).astype(bf16) for t in range(2)]
        dw_o = [tn_dot(branch, heads[t][1]).astype(bf16) for t in range(2)]
        dw_qk = jnp.stack([dw[t][:, : 2 * wide] for t in range(2)])
        dw_vo = jnp.stack(
            [jnp.concatenate([dw[t][:, 2 * wide :], dw_o[t]], axis=1) for t in range(2)]
        )
        folding = Folding(dw_qk, dw_vo, *feed_state)
        dbias = jnp.stack([jnp.sum(part, axis=0, dtype=f32) for part in dqkv])
        dbias = dbias.reshape(2, 3, wide).transpose(1, 0, 2)
        fronts = (gradient, layer_in, shares[0], share_b)
        small_grads[at] = (sums, dbias[0::2], bup)
    grad_in, *last_sums = norm_back(
        layer_in, gain_all[0, 0], shares[0] + share_b.astype(f32)
    )
    gradient = gradient + grad_in
    gains_one[0] = jnp.concatenate(last_sums, axis=0)
    for step in range(4):
        if step == 2:
            (folding.attn,) = behind((folding.attn,), gradient)
        folding.advance()
    weight_grads[0] = folding.result()
    frames_grad = give_clip(gradient)

    sums, bqv, bups = [jnp.stack([small_grads[at][i] for at in range(layers)]) for i in range(3)]
    one = jnp.stack(gains_one)
    gains = jnp.stack([one[:, 0], sums[:, 1]], axis=1)
    shifts = jnp.stack([one[:, 1], sums[:, 2]], axis=1)
    obiases = jnp.stack([sums[:, 3], sums[:, 0]], axis=1)

    def from_width(part):
        part = part.reshape(layers, 2, count_dp, 4, -1).transpose(3, 2, 0, 1, 4)
        return jnp.take(part.reshape(4, count_dp, -1), t_order, axis=0)

    bqv = bqv.reshape(layers, 2, 2, count_dp, -1).transpose(2, 3, 0, 1, 4)
    bqv = jnp.take(bqv.reshape(2, count_dp, -1), block_at, axis=1)
    bqv = jnp.stack([bqv, jnp.zeros_like(bqv)], axis=1).reshape(4, count_dp, -1)
    bups = bups.reshape(layers, 4, count_dp, -1).transpose(1, 2, 0, 3)
    bups = jnp.take(bups.reshape(4, count_dp, -1), block_at, axis=1)
    small = jnp.concatenate(
        [from_width(gains), from_width(shifts), from_width(obiases), bqv, bups], axis=2
    )
    small = small.reshape(2, 2, count_dp, -1)
    small = small[0] + exchange(small[1], "tensor", 2)
    small = small[0] + exchange(small[1], "tensor", 1)
    for mask in reversed(dp_masks()):
        half = small.shape[0] // 2
        small = small[:half] + exchange(small[half:], "dp", mask)
    pieces = jnp.split(small[0], [sum(small_sizes[: i + 1]) for i in range(4)])
    gains, shifts, obiases, bqv, bups = [
        piece.reshape(part.shape) for piece, part in zip(pieces, small_parts)
    ]

    def stacked(make):
        return jnp.stack([make(*weight_grads[at]) for at in range(layers)])

    return (
        encoded,
        frames_grad,
        stacked(lambda qk, vo, up, down: jnp.stack([qk[:, :wide], qk[:, wide:], vo[:, :wide]], axis=1)),
        stacked(lambda qk, vo, up, down: vo[:, wide:].T),
        stacked(lambda qk, vo, up, down: up),
        stacked(lambda qk, vo, up, down: down.T),
        bqv,
        bups,
        gains,
        shifts,
        obiases,
    )


def solution(mesh):
    in_specs = (
        P("dp", "tensor", None),
        P("dp", "tensor", None),
        P(None, "dp", None, "tensor"),
        P(None, "tensor", "dp"),
        P(None, "dp", "tensor"),
        P(None, "tensor", "dp"),
        P(None, None, ("tensor", "dp")),
        P(None, ("tensor", "dp")),
        P(None, None, ("dp", "tensor")),
        P(None, None, ("dp", "tensor")),
        P(None, None, ("dp", "tensor")),
    )
    out_specs = (
        P("dp", "tensor", None),
        P("dp", "tensor", None),
        P(None, "dp", None, "tensor"),
        P(None, "tensor", "dp"),
        P(None, "dp", "tensor"),
        P(None, "tensor", "dp"),
        P(None, None, ("tensor", "dp")),
        P(None, ("tensor", "dp")),
        P(None, None, ("dp", "tensor")),
        P(None, None, ("dp", "tensor")),
        P(None, None, ("dp", "tensor")),
    )
    return jax.shard_map(local, mesh=mesh, in_specs=in_specs, out_specs=out_specs, check_vma=False)
```

time: 849 us -> 861 us (1.014)
  matrix products: 108 us -> 30.3 us
  Pallas kernels: 265 us -> 329 us
  waiting for transfers between devices: 188 us -> 212 us
  other arithmetic: 89.1 us -> 74.9 us
  starting transfers between devices: 67.8 us -> 76.6 us
    dot_general x30 -> x6, matrix products: 57.4 us -> 6.8 us  [nt_dot(): lax.dot_general(left, right, (((1,), (1,)), ((), ())), preferred_element_...]
    pallas_call x2 -> x4, Pallas kernels: 58.3 us -> 86 us  [attend(): pl.pallas_call(functools.partial(attend_kernel, row_count, quarter, min(2...]
    ppermute x74 -> x80, waiting for transfers between devices: 188 us -> 212 us  [exchange(): return lax.ppermute(value, axis, [(i, i ^ mask) for i in range(count)])]
    reduce_sum x23 -> x5, other arithmetic: 27.5 us -> 4.45 us  [the longest x4 2.67 us: local(): dbias = jnp.stack([jnp.sum(part, axis=0, dtype=f32) for part in dqkv])]
    pallas_call x4, Pallas kernels: 119 us -> 141 us  [attend_back(): pl.pallas_call(functools.partial(attend_back_kernel, row_count, quarter,...]
    unnamed x376 -> x187, local copies, waits for them, and re-layouts: 35.6 us -> 15.8 us
    dot_general x12 -> x0, matrix products: 18.1 us -> none  [project(): return jnp.einsum('fd,tdk->tfk', value, weight, preferred_element_type=f32)]
    pallas_call x4, Pallas kernels: 87.2 us -> 102 us  [the longest x2 64 us: feed_back(): pl.pallas_call(functools.partial(feed_back_kernel, final), grid=(hidden /...]
  transfers between devices with their start and end apart: 74 -> 80, of which waited for: 27 -> 37; matrix products, arithmetic and copies ran while one was open for 28% -> 19% of each run, Pallas kernels for 19% -> 29%
where the time goes in v3:
time: 861 us; the launch traced here: 851 us
  Pallas kernels  329 us (38%)
  waiting for transfers between devices  212 us (25%)
  local copies, waits for them, and re-layouts  126 us (15%)
  starting transfers between devices  76.6 us (9%)
  other arithmetic  74.9 us (9%)
  matrix products  30.3 us (4%)
    ppermute x80, waiting for transfers between devices, exchange(): return lax.ppermute(value, axis, [(i, i ^ mask) for i in range(count)])  212 us
    pallas_call x4, Pallas kernels, attend_back(): pl.pallas_call(functools.partial(attend_back_kernel, row_count, quarter,...  141 us
    pallas_call x4, Pallas kernels, attend(): pl.pallas_call(functools.partial(attend_kernel, row_count, quarter, min(2...  86 us
    ppermute x80, starting transfers between devices, exchange(): return lax.ppermute(value, axis, [(i, i ^ mask) for i in range(count)])  76.6 us
    pallas_call x2, Pallas kernels, feed_back(): pl.pallas_call(functools.partial(feed_back_kernel, final), grid=(hidden /...  64 us
    pallas_call x2, Pallas kernels, feed(): pl.pallas_call(functools.partial(feed_kernel, final), grid=(hidden // ste...  37.8 us
    dot_general x8, matrix products, tn_dot(): lax.dot_general(left, right, (((0,), (0,)), ((), ())), preferred_element_...  18.3 us
    convert_element_type x24, other arithmetic, add_low(): return (kept.astype(f32) + received.astype(f32)).astype(bf16)  18.2 us
  transfers between devices with their start and end apart: 80, of which 37 were waited for; matrix products, arithmetic and copies ran while one was open for 19% of the time, Pallas kernels for 29%

profile of v3, /device:TPU:0, one launch (start us, length us, event | category | flops | bytes accessed | tf_op | source)
XLA Modules:
  0.0 851.3 jit_solution(13095689977483410589)
XLA Ops:
  0.7 7.6 constant_dynamic-slice_fusion.1
  9.2 3.0 collective-permute-start
  13.1 2.6 collective-permute-start.1
  16.7 2.7 collective-permute-start.11
  23.8 9.7 %collective-permute-done.1 = bf16[96,768]{1,0:T(8,128)(2,1)} collective-permute-done((bf16[96,768]{1,0:T(8,128)(2,1)}, bf16[96,768]{1,0:T(8,128)(2,1)}, u32[]{:S(2)}, u32[]{:S(2)}) %collective-permute-start.1) | collective-permute-done | bytes 147488 | tf_op jit(solution)/shard_map/ppermute | solution.py:23
  34.5 3.0 collective-permute-start.3
  38.1 17.4 %collective-permute-done.3 = bf16[192,768]{1,0:T(8,128)(2,1)S(1)} collective-permute-done((bf16[192,768]{1,0:T(8,128)(2,1)S(1)}, bf16[192,768]{1,0:T(8,128)(2,1)S(1)}, u32[]{:S(2)}, u32[]{:S(2)}) %collective-permute-start.3) | collective-permute-done | bytes 294944 | tf_op jit(solution)/shard_map/ppermute | solution.py:23
  55.5 3.6 collective-permute-done.4
  70.6 4.2 collective-permute-done.10
  82.7 6.2 collective-permute-done.13
  89.0 2.0 collective-permute-done.14
  92.2 3.3 collective-permute-done.12.refs_2_
  100.3 2.7 fusion.70
  103.0 6.5 collective-permute-done.16
  112.4 2.2 copy.107.refs_0_
  120.4 2.2 collective-permute-done.21
  122.6 13.3 %collective-permute-done.20 = bf16[2,384,768]{2,1,0:T(8,128)(2,1)} collective-permute-done((bf16[2,384,768]{2,1,0:T(8,128)(2,1)}, bf16[2,384,768]{2,1,0:T(8,128)(2,1)}, u32[]{:S(2)}, u32[]{:S(2)}) %collective-permute-start.20) | collective-permute-done | bytes 1179680 | tf_op jit(solution)/shard_map/ppermute | solution.py:23
  137.4 2.8 collective-permute-done.19.refs_7_.refs_9_
  146.0 2.0 gather_fusion.2
  159.8 20.7 %shard_map.194 = (f32[768,768]{1,0:T(8,128)}, f32[768,768]{1,0:T(8,128)}, bf16[1536,576]{1,0:T(8,128)(2,1)}, bf16[1536,192]{1,0:T(8,128)(2,1)}, f32[1536,8]{1,0:T(8,128)}) custom-call(bf16[768,768]{1,0:T(8,128)(2,1)} %add_convert_fusion.6.refs_0_, bf16[768,768]{1,0:T(8,128)(2,1)} %collective-permute-done.8.refs_1_, bf16[768,384]{1,0:T(8,128)(2,1)} %copy-done.15, ...), custom_call_target="tpu_custom_call" | custom-call | tf_op jit(solution)/shard_map/pallas_call | solution.py:285
  180.6 22.4 %shard_map.195 = (f32[768,768]{1,0:T(8,128)}, bf16[768,768]{1,0:T(8,128)(2,1)}, bf16[1536,576]{1,0:T(8,128)(2,1)}, bf16[1536,192]{1,0:T(8,128)(2,1)}, f32[1536,8]{1,0:T(8,128)}) custom-call(bf16[768,768]{1,0:T(8,128)(2,1)} %add_convert_fusion.6.refs_0_, bf16[768,768]{1,0:T(8,128)(2,1)} %collective-permute-done.8.refs_1_, bf16[768,384]{1,0:T(8,128)(2,1)} %copy-done.24, ...), custom_call_target="tpu_custom_call" | custom-call | tf_op jit(solution)/shard_map/pallas_call | solution.py:285
  209.2 9.6 %collective-permute-done.30.refs_2_ = bf16[768,384]{1,0:T(8,128)(2,1)S(1)} collective-permute-done((bf16[768,384]{1,0:T(8,128)(2,1)S(1)}, bf16[768,384]{1,0:T(8,128)(2,1)S(1)}, u32[]{:S(2)}, u32[]{:S(2)}) %collective-permute-start.30) | collective-permute-done | bytes 589856 | tf_op jit(solution)/shard_map/ppermute | solution.py:23
  224.6 2.1 gather_fusion.4
  232.5 20.0 %shard_map.196 = (bf16[768,768]{1,0:T(8,128)(2,1)}, bf16[768,768]{1,0:T(8,128)(2,1)}, bf16[768,768]{1,0:T(8,128)(2,1)}, bf16[768,768]{1,0:T(8,128)(2,1)}, bf16[7...) custom-call(f32[768,768]{1,0:T(8,128)} %copy-done, ...), custom_call_target="tpu_custom_call" | custom-call | tf_op jit(solution)/shard_map/pallas_call | solution.py:456
  252.6 2.4 pad_maximum_fusion.16
  266.4 20.7 %shard_map.197 = (f32[768,768]{1,0:T(8,128)}, f32[768,768]{1,0:T(8,128)}, bf16[1536,576]{1,0:T(8,128)(2,1)}, bf16[1536,192]{1,0:T(8,128)(2,1)}, f32[1536,8]{1,0:T(8,128)}) custom-call(bf16[768,768]{1,0:T(8,128)(2,1)} %get-tuple-element.215.refs_0_, bf16[768,768]{1,0:T(8,128)(2,1)} %copy-done.9, bf16[768,384]{1,0:T(8,128)(2,1)} %pad_maximum_fusion.32.refs_2_, ...), custom_call_target="tpu_custom_call" | custom-call | tf_op jit(solution)/shard_map/pallas_call | solution.py:285
  287.2 22.1 %shard_map.198 = (f32[768,768]{1,0:T(8,128)}, bf16[768,768]{1,0:T(8,128)(2,1)}, bf16[1536,576]{1,0:T(8,128)(2,1)}, bf16[1536,192]{1,0:T(8,128)(2,1)}, f32[1536,8]{1,0:T(8,128)}) custom-call(bf16[768,768]{1,0:T(8,128)(2,1)} %get-tuple-element.215.refs_0_, bf16[768,768]{1,0:T(8,128)(2,1)} %copy-done.9, bf16[768,384]{1,0:T(8,128)(2,1)} %copy-done.25, ...), custom_call_target="tpu_custom_call" | custom-call | tf_op jit(solution)/shard_map/pallas_call | solution.py:285
  320.5 2.6 fusion.9.refs_0_
  323.2 17.8 %shard_map.199 = (bf16[768,768]{1,0:T(8,128)(2,1)}, bf16[768,768]{1,0:T(8,128)(2,1)}, bf16[768,768]{1,0:T(8,128)(2,1)}, bf16[768,768]{1,0:T(8,128)(2,1)}, bf16[7...) custom-call(f32[768,768]{1,0:T(8,128)} %get-tuple-element.269.refs_0, ...), custom_call_target="tpu_custom_call" | custom-call | tf_op jit(solution)/shard_map/pallas_call | solution.py:456
  340.9 30.2 %shard_map.200 = (bf16[4,768,768]{2,1,0:T(8,128)(2,1)}, bf16[4,768,768]{2,1,0:T(8,128)(2,1)}, f32[4,768]{1,0:T(4,128)}, f32[768,768]{1,0:T(8,128)}, bf16[768,768]{1,0:T(8,128)(2,1)}, /*index=5*/f32[8,768]{1,0:T(8,128)}) custom-call(f32[768,768]{1,0:T(8,128)} %fusion.9.refs_0_, f32[768,768]{1,0:T(8,128)} %get-tuple-element.227.refs_1_, ...), custom_call_target="tpu_custom_call" | custom-call | tf_op jit(solution)/shard_map/pallas_call | solution.py:528
  371.7 7.7 collective-permute-done.45
  388.9 22.1 %collective-permute-done.46 = bf16[768,768]{1,0:T(8,128)(2,1)S(1)} collective-permute-done((bf16[768,768]{1,0:T(8,128)(2,1)S(1)}, bf16[768,768]{1,0:T(8,128)(2,1)S(1)}, u32[]{:S(2)}, u32[]{:S(2)}) %collective-permute-start.46) | collective-permute-done | bytes 1179680 | tf_op jit(solution)/shard_map/ppermute | solution.py:23
  418.1 34.7 %shard_map.201 = (f32[768,768]{1,0:T(8,128)}, f32[768,768]{1,0:T(8,128)}, bf16[1536,576]{1,0:T(8,128)(2,1)}) custom-call(bf16[768,768]{1,0:T(8,128)(2,1)} %get-tuple-element.250.refs_0_, bf16[768,768]{1,0:T(8,128)(2,1)} %copy-done.13, bf16[768,384]{1,0:T(8,128)(2,1)} %pad_maximum_fusion.32.refs_2_, bf16[768,384]{1,0:T(8,128)(2,1)} %pad_maximum_fusion.35.refs_3_, ...), custom_call_target="tpu_custom_call" | custom-call | tf_op jit(solution)/shard_map/pallas_call | solution.py:369
  452.8 35.8 %shard_map.202 = (f32[768,768]{1,0:T(8,128)}, bf16[768,768]{1,0:T(8,128)(2,1)}, bf16[1536,576]{1,0:T(8,128)(2,1)}) custom-call(bf16[768,768]{1,0:T(8,128)(2,1)} %get-tuple-element.250.refs_0_, bf16[768,768]{1,0:T(8,128)(2,1)} %copy-done.13, bf16[768,384]{1,0:T(8,128)(2,1)} %copy-done.25, bf16[768,384]{1,0:T(8,128)(2,1)} %pad_maximum_fusion.36.refs_3_, ...), custom_call_target="tpu_custom_call" | custom-call | tf_op jit(solution)/shard_map/pallas_call | solution.py:369
  491.1 3.4 convolution_convert_fusion
  494.7 3.6 convolution_convert_fusion.1
  504.2 9.8 %collective-permute-done.51 = bf16[768,384]{0,1:T(8,128)(2,1)S(1)} collective-permute-done((bf16[768,384]{0,1:T(8,128)(2,1)S(1)}, bf16[768,384]{0,1:T(8,128)(2,1)S(1)}, u32[]{:S(2)}, u32[]{:S(2)}) %collective-permute-start.51) | collective-permute-done | bytes 589856 | tf_op jit(solution)/shard_map/ppermute | solution.py:23
  514.1 2.6 collective-permute-done.52
  517.5 33.8 %shard_map.203 = (bf16[4,768,768]{2,1,0:T(8,128)(2,1)}, bf16[4,768,768]{2,1,0:T(8,128)(2,1)}, f32[4,768]{1,0:T(4,128)}, f32[768,768]{1,0:T(8,128)}, bf16[768,768]{1,0:T(8,128)(2,1)}, /*index=5*/f32[8,768]{1,0:T(8,128)}) custom-call(f32[768,768]{1,0:T(8,128)} %get-tuple-element.268.refs_0_, f32[768,768]{1,0:T(8,128)} %get-tuple-element.269.refs_0_.refs_1_, ...), custom_call_target="tpu_custom_call" | custom-call | tf_op jit(solution)/shard_map/pallas_call | solution.py:528
  554.0 2.2 fusion.11
  556.9 11.7 %collective-permute-done.42 = bf16[384,768]{1,0:T(8,128)(2,1)S(1)} collective-permute-done((bf16[384,768]{1,0:T(8,128)(2,1)S(1)}, bf16[384,768]{1,0:T(8,128)(2,1)S(1)}, u32[]{:S(2)}, u32[]{:S(2)}) %collective-permute-start.42) | collective-permute-done | bytes 589856 | tf_op jit(solution)/shard_map/ppermute | solution.py:23
  569.5 2.6 copy.126
  575.5 5.9 collective-permute-start.60
  582.3 11.4 %collective-permute-done.60 = bf16[96,1536]{1,0:T(8,128)(2,1)S(1)} collective-permute-done((bf16[96,1536]{1,0:T(8,128)(2,1)S(1)}, bf16[96,1536]{1,0:T(8,128)(2,1)S(1)}, u32[]{:S(2)}, u32[]{:S(2)}) %collective-permute-start.60) | collective-permute-done | bytes 294944 | tf_op jit(solution)/shard_map/ppermute | solution.py:23
  595.6 9.6 %collective-permute-done.61 = bf16[192,768]{0,1:T(8,128)(2,1)S(1)} collective-permute-done((bf16[192,768]{0,1:T(8,128)(2,1)S(1)}, bf16[192,768]{0,1:T(8,128)(2,1)S(1)}, u32[]{:S(2)}, u32[]{:S(2)}) %collective-permute-start.61) | collective-permute-done | bytes 294944 | tf_op jit(solution)/shard_map/ppermute | solution.py:23
  608.6 2.1 fusion.19
  613.8 2.8 collective-permute-done.64
  619.1 22.0 %collective-permute-done.56 = bf16[768,768]{1,0:T(8,128)(2,1)S(1)} collective-permute-done((bf16[768,768]{1,0:T(8,128)(2,1)S(1)}, bf16[768,768]{1,0:T(8,128)(2,1)S(1)}, u32[]{:S(2)}, u32[]{:S(2)}) %collective-permute-start.56) | collective-permute-done | bytes 1179680 | tf_op jit(solution)/shard_map/ppermute | solution.py:23
  650.5 35.0 %shard_map.204 = (f32[768,768]{1,0:T(8,128)}, f32[768,768]{1,0:T(8,128)}, bf16[1536,576]{1,0:T(8,128)(2,1)}) custom-call(bf16[768,768]{1,0:T(8,128)(2,1)} %get-tuple-element.298.refs_0_, bf16[768,768]{1,0:T(8,128)(2,1)} %copy-done.11, bf16[768,384]{1,0:T(8,128)(2,1)} %copy-done.15, bf16[768,384]{1,0:T(8,128)(2,1)} %get-tuple-element.183.refs_3_, ...), custom_call_target="tpu_custom_call" | custom-call | tf_op jit(solution)/shard_map/pallas_call | solution.py:369
  685.4 35.7 %shard_map.205 = (f32[768,768]{1,0:T(8,128)}, bf16[768,768]{1,0:T(8,128)(2,1)}, bf16[1536,576]{1,0:T(8,128)(2,1)}) custom-call(bf16[768,768]{1,0:T(8,128)(2,1)} %get-tuple-element.298.refs_0_, bf16[768,768]{1,0:T(8,128)(2,1)} %copy-done.11, bf16[768,384]{1,0:T(8,128)(2,1)} %copy-done.24, bf16[768,384]{1,0:T(8,128)(2,1)} %get-tuple-element.190.refs_3_, ...), custom_call_target="tpu_custom_call" | custom-call | tf_op jit(solution)/shard_map/pallas_call | solution.py:369
  723.7 3.4 fusion.17
  727.2 3.5 fusion.16
  753.2 2.0 gather_fusion.8
  763.1 5.2 collective-permute-done.70
  769.0 8.4 collective-permute-done.72
  787.3 2.0 gather_fusion.7
  793.9 2.0 gather_fusion.5
  800.4 2.0 gather_fusion.6
  809.3 2.3 collective-permute-done.75
  815.2 3.1 multiply_add_fusion
  824.8 4.8 collective-permute-done.79
  830.8 2.5 collective-permute-start.74
  838.5 3.5 collective-permute-done.74
  848.5 2.6 copy.127
  (596 shorter events, 239.7 us)
Async XLA Ops:
  9.2 89.9 %collective-permute-start = (bf16[375,768]{1,0:T(8,128)(2,1)}, bf16[375,768]{1,0:T(8,128)(2,1)}, u32[]{:S(2)}, u32[]{:S(2)}) collective-permute-start(bf16[375,768]{1,0:T(8,128)(2,1)} %bitcast.303), channel_id=1, source_target_pairs={{0,2},{1,3},{2,0},{3,1},{4,6},{5,7},{6,4},{7,5},{8,10},{9,11},{10,... | collective-permute-start | bytes 1728008 | tf_op jit(solution)/shard_map/ppermute | solution.py:23
  13.1 20.4 %collective-permute-start.1 = (bf16[96,768]{1,0:T(8,128)(2,1)}, bf16[96,768]{1,0:T(8,128)(2,1)}, u32[]{:S(2)}, u32[]{:S(2)}) collective-permute-start(bf16[96,768]{1,0:T(8,128)(2,1)} %pad_maximum_fusion.44), channel_id=1, source_target_pairs={{0,16},{4,20},{8,24},{12,28},{16,0},{20,4},{24,8},{28,12},{1,17},{... | collective-permute-start | bytes 442376 | tf_op jit(solution)/shard_map/ppermute | solution.py:23
  16.2 18.3 %collective-permute-start.2 = (f32[1,576]{1,0:T(1,128)S(1)}, f32[1,576]{1,0:T(1,128)S(1)}, u32[]{:S(2)}, u32[]{:S(2)}) collective-permute-start(f32[1,576]{1,0:T(1,128)S(1)} %concatenate.132), channel_id=1, source_target_pairs={{0,16},{4,20},{8,24},{12,28},{16,0},{20,4},{24,8},{28,12},{1,17},{... | collective-permute-start | bytes 6920 | tf_op jit(solution)/shard_map/ppermute | solution.py:23
  16.7 46.3 %collective-permute-start.11 = (bf16[96,1536]{1,0:T(8,128)(2,1)S(1)}, bf16[96,1536]{1,0:T(8,128)(2,1)S(1)}, u32[]{:S(2)}, u32[]{:S(2)}) collective-permute-start(bf16[96,1536]{1,0:T(8,128)(2,1)S(1)} %pad_maximum_fusion.40), channel_id=1, source_target_pairs={{0,16},{4,20},{8,24},{12,28},{16,0},{20,4},{24,8},{28,12},{1,17},{... | collective-permute-start | bytes 884744 | tf_op jit(solution)/shard_map/ppermute | solution.py:23
  20.2 40.5 %collective-permute-start.17 = (bf16[96,768]{1,0:T(8,128)(2,1)}, bf16[96,768]{1,0:T(8,128)(2,1)S(1)}, u32[]{:S(2)}, u32[]{:S(2)}) collective-permute-start(bf16[96,768]{1,0:T(8,128)(2,1)} %pad_maximum_fusion.45), channel_id=1, source_target_pairs={{0,16},{4,20},{8,24},{12,28},{16,0},{20,4},{24,8},{28,12},{1,17},{... | collective-permute-start | bytes 442376 | tf_op jit(solution)/shard_map/ppermute | solution.py:23
  33.5 110.1 %collective-permute-start.29 = (bf16[96,1536]{1,0:T(8,128)(2,1)}, bf16[96,1536]{1,0:T(8,128)(2,1)}, u32[]{:S(2)}, u32[]{:S(2)}) collective-permute-start(bf16[96,1536]{1,0:T(8,128)(2,1)} %pad_maximum_fusion.42), channel_id=1, source_target_pairs={{0,16},{4,20},{8,24},{12,28},{16,0},{20,4},{24,8},{28,12},{1,17},{... | collective-permute-start | bytes 884744 | tf_op jit(solution)/shard_map/ppermute | solution.py:23
  34.5 21.0 %collective-permute-start.3 = (bf16[192,768]{1,0:T(8,128)(2,1)S(1)}, bf16[192,768]{1,0:T(8,128)(2,1)S(1)}, u32[]{:S(2)}, u32[]{:S(2)}) collective-permute-start(bf16[192,768]{1,0:T(8,128)(2,1)S(1)} %pad_maximum_fusion.39), channel_id=1, source_target_pairs={{0,8},{4,12},{8,0},{12,4},{16,24},{20,28},{24,16},{28,20},{1,9},{5... | collective-permute-start | bytes 884744 | tf_op jit(solution)/shard_map/ppermute | solution.py:23
  64.7 10.2 %collective-permute-start.9 = (bf16[384,384]{1,0:T(8,128)(2,1)S(1)}, bf16[384,384]{1,0:T(8,128)(2,1)S(1)}, u32[]{:S(2)}, u32[]{:S(2)}) collective-permute-start(bf16[384,384]{1,0:T(8,128)(2,1)S(1)} %get-tuple-element.173), channel_id=1, source_target_pairs={{0,4},{4,0},{8,12},{12,8},{16,20},{20,16},{24,28},{28,24},{1,5},{5... | collective-permute-start | bytes 884744 | tf_op jit(solution)/shard_map/ppermute | solution.py:23
  75.0 13.9 %collective-permute-start.13 = (bf16[2,384,384]{2,1,0:T(8,128)(2,1)S(1)}, bf16[2,384,384]{2,1,0:T(8,128)(2,1)S(1)}, u32[]{:S(2)}, u32[]{:S(2)}) collective-permute-start(bf16[2,384,384]{2,1,0:T(8,128)(2,1)S(1)} %pad_maximum_fusion.27), channel_id=1, source_target_pairs={{0,4},{4,0},{8,12},{12,8},{16,20},{20,16},{24,28},{28,24},{1,5},{5... | collective-permute-start | bytes 1769480 | tf_op jit(solution)/shard_map/ppermute | solution.py:23
  76.9 14.1 %collective-permute-start.14 = (bf16[192,1536]{1,0:T(8,128)(2,1)S(1)}, bf16[192,1536]{1,0:T(8,128)(2,1)S(1)}, u32[]{:S(2)}, u32[]{:S(2)}) collective-permute-start(bf16[192,1536]{1,0:T(8,128)(2,1)S(1)} %pad_maximum_fusion.28), channel_id=1, source_target_pairs={{0,8},{4,12},{8,0},{12,4},{16,24},{20,28},{24,16},{28,20},{1,9},{5... | collective-permute-start | bytes 1769480 | tf_op jit(solution)/shard_map/ppermute | solution.py:23
  81.4 14.1 %collective-permute-start.12 = (bf16[768,384]{1,0:T(8,128)(2,1)S(1)}, bf16[768,384]{1,0:T(8,128)(2,1)S(1)}, u32[]{:S(2)}, u32[]{:S(2)}) collective-permute-start(bf16[768,384]{1,0:T(8,128)(2,1)S(1)} %pad_maximum_fusion.26.refs_2_), channel_id=1, source_target_pairs={{0,2},{1,3},{2,0},{3,1},{4,6},{5,7},{6,4},{7,5},{8,10},{9,11},{10,... | collective-permute-start | bytes 1769480 | tf_op jit(solution)/shard_map/ppermute | solution.py:23
  96.3 13.1 %collective-permute-start.16 = (bf16[384,768]{1,0:T(8,128)(2,1)S(1)}, bf16[384,768]{1,0:T(8,128)(2,1)S(1)}, u32[]{:S(2)}, u32[]{:S(2)}) collective-permute-start(bf16[384,768]{1,0:T(8,128)(2,1)S(1)} %get-tuple-element.180), channel_id=1, source_target_pairs={{0,2},{1,3},{2,0},{3,1},{4,6},{5,7},{6,4},{7,5},{8,10},{9,11},{10,... | collective-permute-start | bytes 1769480 | tf_op jit(solution)/shard_map/ppermute | solution.py:23
  97.6 12.9 %collective-permute-start.15 = (bf16[384,768]{1,0:T(8,128)(2,1)S(1)}, bf16[384,768]{1,0:T(8,128)(2,1)S(1)}, u32[]{:S(2)}, u32[]{:S(2)}) collective-permute-start(bf16[384,768]{1,0:T(8,128)(2,1)S(1)} %get-tuple-element.179), channel_id=1, source_target_pairs={{0,4},{4,0},{8,12},{12,8},{16,20},{20,16},{24,28},{28,24},{1,5},{5... | collective-permute-start | bytes 1769480 | tf_op jit(solution)/shard_map/ppermute | solution.py:23
  110.6 25.2 %collective-permute-start.20 = (bf16[2,384,768]{2,1,0:T(8,128)(2,1)}, bf16[2,384,768]{2,1,0:T(8,128)(2,1)}, u32[]{:S(2)}, u32[]{:S(2)}) collective-permute-start(bf16[2,384,768]{2,1,0:T(8,128)(2,1)} %pad_maximum_fusion.11), channel_id=1, source_target_pairs={{0,4},{4,0},{8,12},{12,8},{16,20},{20,16},{24,28},{28,24},{1,5},{5... | collective-permute-start | bytes 3538952 | tf_op jit(solution)/shard_map/ppermute | solution.py:23
  115.1 25.1 %collective-permute-start.19 = (bf16[768,768]{1,0:T(8,128)(2,1)S(1)}, bf16[768,768]{1,0:T(8,128)(2,1)}, u32[]{:S(2)}, u32[]{:S(2)}) collective-permute-start(bf16[768,768]{1,0:T(8,128)(2,1)S(1)} %pad_maximum_fusion.10.refs_5_.refs_7_), channel_id=1, source_target_pairs={{0,2},{1,3},{2,0},{3,1},{4,6},{5,7},{6,4},{7,5},{8,10},{9,11},{10,... | collective-permute-start | bytes 3538952 | tf_op jit(solution)/shard_map/ppermute | solution.py:23
  119.0 40.8 %collective-permute-start.8 = (bf16[768,768]{1,0:T(8,128)(2,1)}, bf16[768,768]{1,0:T(8,128)(2,1)}, u32[]{:S(2)}, u32[]{:S(2)}) collective-permute-start(bf16[768,768]{1,0:T(8,128)(2,1)} %add_convert_fusion.6.refs_0_), channel_id=1, source_target_pairs={{0,1},{1,0},{2,3},{3,2},{4,5},{5,4},{6,7},{7,6},{8,9},{9,8},{10,11... | collective-permute-start | bytes 3538952 | tf_op jit(solution)/shard_map/ppermute | solution.py:23
  152.0 55.1 %collective-permute-start.31 = (bf16[2,384,384]{2,1,0:T(8,128)(2,1)}, bf16[2,384,384]{2,1,0:T(8,128)(2,1)}, u32[]{:S(2)}, u32[]{:S(2)}) collective-permute-start(bf16[2,384,384]{2,1,0:T(8,128)(2,1)} %pad_maximum_fusion.33), channel_id=1, source_target_pairs={{0,4},{4,0},{8,12},{12,8},{16,20},{20,16},{24,28},{28,24},{1,5},{5... | collective-permute-start | bytes 1769480 | tf_op jit(solution)/shard_map/ppermute | solution.py:23
  203.0 18.6 %collective-permute-start.18 = (bf16[768,768]{1,0:T(8,128)(2,1)}, bf16[768,768]{1,0:T(8,128)(2,1)}, u32[]{:S(2)}, u32[]{:S(2)}) collective-permute-start(bf16[768,768]{1,0:T(8,128)(2,1)} %get-tuple-element.192), channel_id=1, source_target_pairs={{0,1},{1,0},{2,3},{3,2},{4,5},{5,4},{6,7},{7,6},{8,9},{9,8},{10,11... | collective-permute-start | bytes 3538952 | tf_op jit(solution)/shard_map/ppermute | solution.py:23
  203.0 23.7 %collective-permute-start.22 = (bf16[768,768]{1,0:T(8,128)(2,1)S(1)}, bf16[768,768]{1,0:T(8,128)(2,1)}, u32[]{:S(2)}, u32[]{:S(2)}) collective-permute-start(bf16[768,768]{1,0:T(8,128)(2,1)S(1)} %pad_maximum_fusion.10.refs_5_.refs_7_), channel_id=1, source_target_pairs={{0,1},{1,0},{2,3},{3,2},{4,5},{5,4},{6,7},{7,6},{8,9},{9,8},{10,11... | collective-permute-start | bytes 3538952 | tf_op jit(solution)/shard_map/ppermute | solution.py:23
  203.5 15.3 %collective-permute-start.30 = (bf16[768,384]{1,0:T(8,128)(2,1)S(1)}, bf16[768,384]{1,0:T(8,128)(2,1)S(1)}, u32[]{:S(2)}, u32[]{:S(2)}) collective-permute-start(bf16[768,384]{1,0:T(8,128)(2,1)S(1)} %copy-done.16), channel_id=1, source_target_pairs={{0,2},{1,3},{2,0},{3,1},{4,6},{5,7},{6,4},{7,5},{8,10},{9,11},{10,... | collective-permute-start | bytes 1769480 | tf_op jit(solution)/shard_map/ppermute | solution.py:23
  204.4 15.0 %collective-permute-start.32 = (bf16[192,1536]{1,0:T(8,128)(2,1)S(1)}, bf16[192,1536]{1,0:T(8,128)(2,1)S(1)}, u32[]{:S(2)}, u32[]{:S(2)}) collective-permute-start(bf16[192,1536]{1,0:T(8,128)(2,1)S(1)} %copy-done.26), channel_id=1, source_target_pairs={{0,8},{4,12},{8,0},{12,4},{16,24},{20,28},{24,16},{28,20},{1,9},{5... | collective-permute-start | bytes 1769480 | tf_op jit(solution)/shard_map/ppermute | solution.py:23
  207.2 25.3 %collective-permute-start.23 = (bf16[768,768]{1,0:T(8,128)(2,1)}, bf16[768,768]{1,0:T(8,128)(2,1)}, u32[]{:S(2)}, u32[]{:S(2)}) collective-permute-start(bf16[768,768]{1,0:T(8,128)(2,1)} %collective-permute-done.19.refs_7_.refs_9_), channel_id=1, source_target_pairs={{0,1},{1,0},{2,3},{3,2},{4,5},{5,4},{6,7},{7,6},{8,9},{9,8},{10,11... | collective-permute-start | bytes 3538952 | tf_op jit(solution)/shard_map/ppermute | solution.py:23
  218.8 13.7 %collective-permute-start.24 = (bf16[768,768]{1,0:T(8,128)(2,1)S(1)}, bf16[768,768]{1,0:T(8,128)(2,1)}, u32[]{:S(2)}, u32[]{:S(2)}) collective-permute-start(bf16[768,768]{1,0:T(8,128)(2,1)S(1)} %pad_maximum_fusion.12.refs_9_.refs_11_), channel_id=1, source_target_pairs={{0,1},{1,0},{2,3},{3,2},{4,5},{5,4},{6,7},{7,6},{8,9},{9,8},{10,11... | collective-permute-start | bytes 3538952 | tf_op jit(solution)/shard_map/ppermute | solution.py:23
  219.5 13.0 %collective-permute-start.25 = (bf16[768,768]{1,0:T(8,128)(2,1)S(1)}, bf16[768,768]{1,0:T(8,128)(2,1)}, u32[]{:S(2)}, u32[]{:S(2)}) collective-permute-start(bf16[768,768]{1,0:T(8,128)(2,1)S(1)} %pad_maximum_fusion.13.refs_11_.refs_13_), channel_id=1, source_target_pairs={{0,1},{1,0},{2,3},{3,2},{4,5},{5,4},{6,7},{7,6},{8,9},{9,8},{10,11... | collective-permute-start | bytes 3538952 | tf_op jit(solution)/shard_map/ppermute | solution.py:23
  221.6 31.0 %collective-permute-start.34 = (bf16[384,768]{1,0:T(8,128)(2,1)}, bf16[384,768]{1,0:T(8,128)(2,1)}, u32[]{:S(2)}, u32[]{:S(2)}) collective-permute-start(bf16[384,768]{1,0:T(8,128)(2,1)} %get-tuple-element.209), channel_id=1, source_target_pairs={{0,2},{1,3},{2,0},{3,1},{4,6},{5,7},{6,4},{7,5},{8,10},{9,11},{10,... | collective-permute-start | bytes 1769480 | tf_op jit(solution)/shard_map/ppermute | solution.py:23
  226.7 28.4 %collective-permute-start.33 = (bf16[384,768]{1,0:T(8,128)(2,1)}, bf16[384,768]{1,0:T(8,128)(2,1)}, u32[]{:S(2)}, u32[]{:S(2)}) collective-permute-start(bf16[384,768]{1,0:T(8,128)(2,1)} %get-tuple-element.208), channel_id=1, source_target_pairs={{0,4},{4,0},{8,12},{12,8},{16,20},{20,16},{24,28},{28,24},{1,5},{5... | collective-permute-start | bytes 1769480 | tf_op jit(solution)/shard_map/ppermute | solution.py:23
  252.5 12.9 %collective-permute-start.26 = (bf16[768,768]{1,0:T(8,128)(2,1)}, bf16[768,768]{1,0:T(8,128)(2,1)S(1)}, u32[]{:S(2)}, u32[]{:S(2)}) collective-permute-start(bf16[768,768]{1,0:T(8,128)(2,1)} %get-tuple-element.215.refs_0_), channel_id=1, source_target_pairs={{0,1},{1,0},{2,3},{3,2},{4,5},{5,4},{6,7},{7,6},{8,9},{9,8},{10,11... | collective-permute-start | bytes 3538952 | tf_op jit(solution)/shard_map/ppermute | solution.py:23
  256.3 52.9 %collective-permute-start.37 = (bf16[2,384,768]{2,1,0:T(8,128)(2,1)}, bf16[2,384,768]{2,1,0:T(8,128)(2,1)}, u32[]{:S(2)}, u32[]{:S(2)}) collective-permute-start(bf16[2,384,768]{2,1,0:T(8,128)(2,1)} %pad_maximum_fusion.16), channel_id=1, source_target_pairs={{0,4},{4,0},{8,12},{12,8},{16,20},{20,16},{24,28},{28,24},{1,5},{5... | collective-permute-start | bytes 3538952 | tf_op jit(solution)/shard_map/ppermute | solution.py:23
  257.9 53.9 %collective-permute-start.36 = (bf16[768,768]{1,0:T(8,128)(2,1)S(1)}, bf16[768,768]{1,0:T(8,128)(2,1)S(1)}, u32[]{:S(2)}, u32[]{:S(2)}) collective-permute-start(bf16[768,768]{1,0:T(8,128)(2,1)S(1)} %pad_maximum_fusion.15.refs_5_.refs_4_), channel_id=1, source_target_pairs={{0,2},{1,3},{2,0},{3,1},{4,6},{5,7},{6,4},{7,5},{8,10},{9,11},{10,... | collective-permute-start | bytes 3538952 | tf_op jit(solution)/shard_map/ppermute | solution.py:23
  259.2 53.7 %collective-permute-start.43 = (bf16[375,768]{1,0:T(8,128)(2,1)}, bf16[375,768]{1,0:T(8,128)(2,1)}, u32[]{:S(2)}, u32[]{:S(2)}) collective-permute-start(bf16[375,768]{1,0:T(8,128)(2,1)} %bitcast.304), channel_id=1, source_target_pairs={{0,2},{1,3},{2,0},{3,1},{4,6},{5,7},{6,4},{7,5},{8,10},{9,11},{10,... | collective-permute-start | bytes 1728008 | tf_op jit(solution)/shard_map/ppermute | solution.py:23
  309.2 13.9 %collective-permute-start.35 = (bf16[768,768]{1,0:T(8,128)(2,1)}, bf16[768,768]{1,0:T(8,128)(2,1)}, u32[]{:S(2)}, u32[]{:S(2)}) collective-permute-start(bf16[768,768]{1,0:T(8,128)(2,1)} %get-tuple-element.220), channel_id=1, source_target_pairs={{0,1},{1,0},{2,3},{3,2},{4,5},{5,4},{6,7},{7,6},{8,9},{9,8},{10,11... | collective-permute-start | bytes 3538952 | tf_op jit(solution)/shard_map/ppermute | solution.py:23
  311.8 11.3 %collective-permute-start.38 = (bf16[768,768]{1,0:T(8,128)(2,1)S(1)}, bf16[768,768]{1,0:T(8,128)(2,1)}, u32[]{:S(2)}, u32[]{:S(2)}) collective-permute-start(bf16[768,768]{1,0:T(8,128)(2,1)S(1)} %pad_maximum_fusion.15.refs_5_.refs_4_), channel_id=1, source_target_pairs={{0,1},{1,0},{2,3},{3,2},{4,5},{5,4},{6,7},{7,6},{8,9},{9,8},{10,11... | collective-permute-start | bytes 3538952 | tf_op jit(solution)/shard_map/ppermute | solution.py:23
  312.4 10.8 %collective-permute-start.39 = (bf16[768,768]{1,0:T(8,128)(2,1)S(1)}, bf16[768,768]{1,0:T(8,128)(2,1)}, u32[]{:S(2)}, u32[]{:S(2)}) collective-permute-start(bf16[768,768]{1,0:T(8,128)(2,1)S(1)} %collective-permute-done.36.refs_7_.refs_6_), channel_id=1, source_target_pairs={{0,1},{1,0},{2,3},{3,2},{4,5},{5,4},{6,7},{7,6},{8,9},{9,8},{10,11... | collective-permute-start | bytes 3538952 | tf_op jit(solution)/shard_map/ppermute | solution.py:23
  312.4 10.7 %collective-permute-start.40 = (bf16[768,768]{1,0:T(8,128)(2,1)S(1)}, bf16[768,768]{1,0:T(8,128)(2,1)}, u32[]{:S(2)}, u32[]{:S(2)}) collective-permute-start(bf16[768,768]{1,0:T(8,128)(2,1)S(1)} %pad_maximum_fusion.17.refs_9_.refs_8_), channel_id=1, source_target_pairs={{0,1},{1,0},{2,3},{3,2},{4,5},{5,4},{6,7},{7,6},{8,9},{9,8},{10,11... | collective-permute-start | bytes 3538952 | tf_op jit(solution)/shard_map/ppermute | solution.py:23
  312.9 10.3 %collective-permute-start.41 = (bf16[768,768]{1,0:T(8,128)(2,1)}, bf16[768,768]{1,0:T(8,128)(2,1)}, u32[]{:S(2)}, u32[]{:S(2)}) collective-permute-start(bf16[768,768]{1,0:T(8,128)(2,1)} %pad_maximum_fusion.18.refs_11_.refs_10_), channel_id=1, source_target_pairs={{0,1},{1,0},{2,3},{3,2},{4,5},{5,4},{6,7},{7,6},{8,9},{9,8},{10,11... | collective-permute-start | bytes 3538952 | tf_op jit(solution)/shard_map/ppermute | solution.py:23
  371.6 16.2 %collective-permute-start.44 = (bf16[768,768]{1,0:T(8,128)(2,1)}, bf16[768,768]{1,0:T(8,128)(2,1)S(1)}, u32[]{:S(2)}, u32[]{:S(2)}) collective-permute-start(bf16[768,768]{1,0:T(8,128)(2,1)} %get-tuple-element.250.refs_0_), channel_id=1, source_target_pairs={{0,1},{1,0},{2,3},{3,2},{4,5},{5,4},{6,7},{7,6},{8,9},{9,8},{10,11... | collective-permute-start | bytes 3538952 | tf_op jit(solution)/shard_map/ppermute | solution.py:23
  382.7 28.3 %collective-permute-start.46 = (bf16[768,768]{1,0:T(8,128)(2,1)S(1)}, bf16[768,768]{1,0:T(8,128)(2,1)S(1)}, u32[]{:S(2)}, u32[]{:S(2)}) collective-permute-start(bf16[768,768]{1,0:T(8,128)(2,1)S(1)} %fusion.18), channel_id=1, source_target_pairs={{0,2},{1,3},{2,0},{3,1},{4,6},{5,7},{6,4},{7,5},{8,10},{9,11},{10,... | collective-permute-start | bytes 3538952 | tf_op jit(solution)/shard_map/ppermute | solution.py:23
  383.2 29.7 %collective-permute-start.47 = (bf16[2,384,768]{2,1,0:T(8,128)(2,1)S(1)}, bf16[2,384,768]{2,1,0:T(8,128)(2,1)S(1)}, u32[]{:S(2)}, u32[]{:S(2)}) collective-permute-start(bf16[2,384,768]{2,1,0:T(8,128)(2,1)S(1)} %add_convert_fusion.4), channel_id=1, source_target_pairs={{0,4},{4,0},{8,12},{12,8},{16,20},{20,16},{24,28},{28,24},{1,5},{5... | collective-permute-start | bytes 3538952 | tf_op jit(solution)/shard_map/ppermute | solution.py:23
  412.4 76.2 %collective-permute-start.48 = (bf16[384,768]{1,0:T(8,128)(2,1)}, bf16[384,768]{1,0:T(8,128)(2,1)}, u32[]{:S(2)}, u32[]{:S(2)}) collective-permute-start(bf16[384,768]{1,0:T(8,128)(2,1)} %slice.731), channel_id=1, source_target_pairs={{0,4},{4,0},{8,12},{12,8},{16,20},{20,16},{24,28},{28,24},{1,5},{5... | collective-permute-start | bytes 1769480 | tf_op jit(solution)/shard_map/ppermute | solution.py:23
  414.2 75.7 %collective-permute-start.49 = (bf16[384,768]{1,0:T(8,128)(2,1)}, bf16[384,768]{1,0:T(8,128)(2,1)}, u32[]{:S(2)}, u32[]{:S(2)}) collective-permute-start(bf16[384,768]{1,0:T(8,128)(2,1)} %slice_bitcast_fusion.6), channel_id=1, source_target_pairs={{0,2},{1,3},{2,0},{3,1},{4,6},{5,7},{6,4},{7,5},{8,10},{9,11},{10,... | collective-permute-start | bytes 1769480 | tf_op jit(solution)/shard_map/ppermute | solution.py:23
  499.7 14.3 %collective-permute-start.51 = (bf16[768,384]{0,1:T(8,128)(2,1)S(1)}, bf16[768,384]{0,1:T(8,128)(2,1)S(1)}, u32[]{:S(2)}, u32[]{:S(2)}) collective-permute-start(bf16[768,384]{0,1:T(8,128)(2,1)S(1)} %slice_bitcast_fusion.13), channel_id=1, source_target_pairs={{0,2},{1,3},{2,0},{3,1},{4,6},{5,7},{6,4},{7,5},{8,10},{9,11},{10,... | collective-permute-start | bytes 1769480 | tf_op jit(solution)/shard_map/ppermute | solution.py:23
  500.8 16.7 %collective-permute-start.50 = (bf16[768,768]{1,0:T(8,128)(2,1)S(1)}, bf16[768,768]{1,0:T(8,128)(2,1)}, u32[]{:S(2)}, u32[]{:S(2)}) collective-permute-start(bf16[768,768]{1,0:T(8,128)(2,1)S(1)} %copy-done.83), channel_id=1, source_target_pairs={{0,1},{1,0},{2,3},{3,2},{4,5},{5,4},{6,7},{7,6},{8,9},{9,8},{10,11... | collective-permute-start | bytes 3538952 | tf_op jit(solution)/shard_map/ppermute | solution.py:23
  500.8 15.8 %collective-permute-start.52 = (bf16[2,384,384]{1,2,0:T(8,128)(2,1)S(1)}, bf16[2,384,384]{1,2,0:T(8,128)(2,1)S(1)}, u32[]{:S(2)}, u32[]{:S(2)}) collective-permute-start(bf16[2,384,384]{1,2,0:T(8,128)(2,1)S(1)} %slice.592), channel_id=1, source_target_pairs={{0,4},{4,0},{8,12},{12,8},{16,20},{20,16},{24,28},{28,24},{1,5},{5... | collective-permute-start | bytes 1769480 | tf_op jit(solution)/shard_map/ppermute | solution.py:23
  501.8 15.5 %collective-permute-start.53 = (bf16[192,1536]{1,0:T(8,128)(2,1)S(1)}, bf16[192,1536]{1,0:T(8,128)(2,1)S(1)}, u32[]{:S(2)}, u32[]{:S(2)}) collective-permute-start(bf16[192,1536]{1,0:T(8,128)(2,1)S(1)} %pad_maximum_fusion.24), channel_id=1, source_target_pairs={{0,8},{4,12},{8,0},{12,4},{16,24},{20,28},{24,16},{28,20},{1,9},{5... | collective-permute-start | bytes 1769480 | tf_op jit(solution)/shard_map/ppermute | solution.py:23
  551.3 57.3 %collective-permute-start.55 = (bf16[4,768,768]{2,1,0:T(8,128)(2,1)}, bf16[4,768,768]{2,1,0:T(8,128)(2,1)}, u32[]{:S(2)}, u32[]{:S(2)}) collective-permute-start(bf16[4,768,768]{2,1,0:T(8,128)(2,1)} %get-tuple-element.285), channel_id=1, source_target_pairs={{0,1},{1,0},{2,3},{3,2},{4,5},{5,4},{6,7},{7,6},{8,9},{9,8},{10,11... | collective-permute-start | bytes 14155784 | tf_op jit(solution)/shard_map/ppermute | solution.py:23
  552.7 15.8 %collective-permute-start.42 = (bf16[384,768]{1,0:T(8,128)(2,1)S(1)}, bf16[384,768]{1,0:T(8,128)(2,1)S(1)}, u32[]{:S(2)}, u32[]{:S(2)}) collective-permute-start(bf16[384,768]{1,0:T(8,128)(2,1)S(1)} %slice.975), channel_id=1, source_target_pairs={{0,2},{1,3},{2,0},{3,1},{4,6},{5,7},{6,4},{7,5},{8,10},{9,11},{10,... | collective-permute-start | bytes 1769480 | tf_op jit(solution)/shard_map/ppermute | solution.py:23
  575.5 18.2 %collective-permute-start.60 = (bf16[96,1536]{1,0:T(8,128)(2,1)S(1)}, bf16[96,1536]{1,0:T(8,128)(2,1)S(1)}, u32[]{:S(2)}, u32[]{:S(2)}) collective-permute-start(bf16[96,1536]{1,0:T(8,128)(2,1)S(1)} %slice.608), channel_id=1, source_target_pairs={{0,16},{4,20},{8,24},{12,28},{16,0},{20,4},{24,8},{28,12},{1,17},{... | collective-permute-start | bytes 884744 | tf_op jit(solution)/shard_map/ppermute | solution.py:23
  594.1 11.1 %collective-permute-start.61 = (bf16[192,768]{0,1:T(8,128)(2,1)S(1)}, bf16[192,768]{0,1:T(8,128)(2,1)S(1)}, u32[]{:S(2)}, u32[]{:S(2)}) collective-permute-start(bf16[192,768]{0,1:T(8,128)(2,1)S(1)} %slice.745), channel_id=1, source_target_pairs={{0,8},{4,12},{8,0},{12,4},{16,24},{20,28},{24,16},{28,20},{1,9},{5... | collective-permute-start | bytes 884744 | tf_op jit(solution)/shard_map/ppermute | solution.py:23
  605.4 11.2 %collective-permute-start.64 = (bf16[96,768]{0,1:T(8,128)(2,1)S(1)}, bf16[96,768]{0,1:T(8,128)(2,1)S(1)}, u32[]{:S(2)}, u32[]{:S(2)}) collective-permute-start(bf16[96,768]{0,1:T(8,128)(2,1)S(1)} %slice.751), channel_id=1, source_target_pairs={{0,16},{4,20},{8,24},{12,28},{16,0},{20,4},{24,8},{28,12},{1,17},{... | collective-permute-start | bytes 442376 | tf_op jit(solution)/shard_map/ppermute | solution.py:23
  605.7 13.3 %collective-permute-start.54 = (bf16[768,768]{1,0:T(8,128)(2,1)S(1)}, bf16[768,768]{1,0:T(8,128)(2,1)S(1)}, u32[]{:S(2)}, u32[]{:S(2)}) collective-permute-start(bf16[768,768]{1,0:T(8,128)(2,1)S(1)} %copy-done.7), channel_id=1, source_target_pairs={{0,1},{1,0},{2,3},{3,2},{4,5},{5,4},{6,7},{7,6},{8,9},{9,8},{10,11... | collective-permute-start | bytes 3538952 | tf_op jit(solution)/shard_map/ppermute | solution.py:23
  612.7 28.4 %collective-permute-start.56 = (bf16[768,768]{1,0:T(8,128)(2,1)S(1)}, bf16[768,768]{1,0:T(8,128)(2,1)S(1)}, u32[]{:S(2)}, u32[]{:S(2)}) collective-permute-start(bf16[768,768]{1,0:T(8,128)(2,1)S(1)} %fusion.19), channel_id=1, source_target_pairs={{0,2},{1,3},{2,0},{3,1},{4,6},{5,7},{6,4},{7,5},{8,10},{9,11},{10,... | collective-permute-start | bytes 3538952 | tf_op jit(solution)/shard_map/ppermute | solution.py:23
  616.6 28.0 %collective-permute-start.57 = (bf16[2,384,768]{2,1,0:T(8,128)(2,1)S(1)}, bf16[2,384,768]{2,1,0:T(8,128)(2,1)S(1)}, u32[]{:S(2)}, u32[]{:S(2)}) collective-permute-start(bf16[2,384,768]{2,1,0:T(8,128)(2,1)S(1)} %add_convert_fusion.1), channel_id=1, source_target_pairs={{0,4},{4,0},{8,12},{12,8},{16,20},{20,16},{24,28},{28,24},{1,5},{5... | collective-permute-start | bytes 3538952 | tf_op jit(solution)/shard_map/ppermute | solution.py:23
  643.8 77.3 %collective-permute-start.62 = (bf16[384,768]{1,0:T(8,128)(2,1)}, bf16[384,768]{1,0:T(8,128)(2,1)}, u32[]{:S(2)}, u32[]{:S(2)}) collective-permute-start(bf16[384,768]{1,0:T(8,128)(2,1)} %slice.747), channel_id=1, source_target_pairs={{0,4},{4,0},{8,12},{12,8},{16,20},{20,16},{24,28},{28,24},{1,5},{5... | collective-permute-start | bytes 1769480 | tf_op jit(solution)/shard_map/ppermute | solution.py:23
  647.3 75.2 %collective-permute-start.63 = (bf16[384,768]{1,0:T(8,128)(2,1)}, bf16[384,768]{1,0:T(8,128)(2,1)}, u32[]{:S(2)}, u32[]{:S(2)}) collective-permute-start(bf16[384,768]{1,0:T(8,128)(2,1)} %slice_bitcast_fusion.2), channel_id=1, source_target_pairs={{0,2},{1,3},{2,0},{3,1},{4,6},{5,7},{6,4},{7,5},{8,10},{9,11},{10,... | collective-permute-start | bytes 1769480 | tf_op jit(solution)/shard_map/ppermute | solution.py:23
  735.0 20.2 %collective-permute-start.67 = (bf16[768,384]{0,1:T(8,128)(2,1)}, bf16[768,384]{0,1:T(8,128)(2,1)}, u32[]{:S(2)}, u32[]{:S(2)}) collective-permute-start(bf16[768,384]{0,1:T(8,128)(2,1)} %slice_bitcast_fusion.12), channel_id=1, source_target_pairs={{0,2},{1,3},{2,0},{3,1},{4,6},{5,7},{6,4},{7,5},{8,10},{9,11},{10,... | collective-permute-start | bytes 1769480 | tf_op jit(solution)/shard_map/ppermute | solution.py:23
  736.9 19.6 %collective-permute-start.68 = (bf16[2,384,384]{1,2,0:T(8,128)(2,1)}, bf16[2,384,384]{1,2,0:T(8,128)(2,1)}, u32[]{:S(2)}, u32[]{:S(2)}) collective-permute-start(bf16[2,384,384]{1,2,0:T(8,128)(2,1)} %slice.628), channel_id=1, source_target_pairs={{0,4},{4,0},{8,12},{12,8},{16,20},{20,16},{24,28},{28,24},{1,5},{5... | collective-permute-start | bytes 1769480 | tf_op jit(solution)/shard_map/ppermute | solution.py:23
  740.0 40.2 %collective-permute-start.65 = (bf16[768,768]{1,0:T(8,128)(2,1)}, bf16[768,768]{1,0:T(8,128)(2,1)S(1)}, u32[]{:S(2)}, u32[]{:S(2)}) collective-permute-start(bf16[768,768]{1,0:T(8,128)(2,1)} %get-tuple-element.308), channel_id=1, source_target_pairs={{0,1},{1,0},{2,3},{3,2},{4,5},{5,4},{6,7},{7,6},{8,9},{9,8},{10,11... | collective-permute-start | bytes 3538952 | tf_op jit(solution)/shard_map/ppermute | solution.py:23
  740.0 17.9 %collective-permute-start.69 = (bf16[192,1536]{1,0:T(8,128)(2,1)}, bf16[192,1536]{1,0:T(8,128)(2,1)}, u32[]{:S(2)}, u32[]{:S(2)}) collective-permute-start(bf16[192,1536]{1,0:T(8,128)(2,1)} %pad_maximum_fusion.23), channel_id=1, source_target_pairs={{0,8},{4,12},{8,0},{12,4},{16,24},{20,28},{24,16},{28,20},{1,9},{5... | collective-permute-start | bytes 1769480 | tf_op jit(solution)/shard_map/ppermute | solution.py:23
  759.1 9.2 %collective-permute-start.70 = (bf16[384,384]{0,1:T(8,128)(2,1)S(1)}, bf16[384,384]{0,1:T(8,128)(2,1)S(1)}, u32[]{:S(2)}, u32[]{:S(2)}) collective-permute-start(bf16[384,384]{0,1:T(8,128)(2,1)S(1)} %slice.632), channel_id=1, source_target_pairs={{0,4},{4,0},{8,12},{12,8},{16,20},{20,16},{24,28},{28,24},{1,5},{5... | collective-permute-start | bytes 884744 | tf_op jit(solution)/shard_map/ppermute | solution.py:23
  760.0 8.9 %collective-permute-start.71 = (bf16[384,384]{0,1:T(8,128)(2,1)S(1)}, bf16[384,384]{0,1:T(8,128)(2,1)S(1)}, u32[]{:S(2)}, u32[]{:S(2)}) collective-permute-start(bf16[384,384]{0,1:T(8,128)(2,1)S(1)} %slice_bitcast_fusion.22), channel_id=1, source_target_pairs={{0,2},{1,3},{2,0},{3,1},{4,6},{5,7},{6,4},{7,5},{8,10},{9,11},{10,... | collective-permute-start | bytes 884744 | tf_op jit(solution)/shard_map/ppermute | solution.py:23
  761.8 15.7 %collective-permute-start.72 = (bf16[96,1536]{1,0:T(8,128)(2,1)S(1)}, bf16[96,1536]{1,0:T(8,128)(2,1)S(1)}, u32[]{:S(2)}, u32[]{:S(2)}) collective-permute-start(bf16[96,1536]{1,0:T(8,128)(2,1)S(1)} %slice.636), channel_id=1, source_target_pairs={{0,16},{4,20},{8,24},{12,28},{16,0},{20,4},{24,8},{28,12},{1,17},{... | collective-permute-start | bytes 884744 | tf_op jit(solution)/shard_map/ppermute | solution.py:23
  819.5 11.0 %collective-permute-start.73 = (bf16[192,768]{0,1:T(8,128)(2,1)S(1)}, bf16[192,768]{0,1:T(8,128)(2,1)S(1)}, u32[]{:S(2)}, u32[]{:S(2)}) collective-permute-start(bf16[192,768]{0,1:T(8,128)(2,1)S(1)} %slice.638), channel_id=1, source_target_pairs={{0,8},{4,12},{8,0},{12,4},{16,24},{20,28},{24,16},{28,20},{1,9},{5... | collective-permute-start | bytes 884744 | tf_op jit(solution)/shard_map/ppermute | solution.py:23
  823.7 22.8 %collective-permute-start.66 = (bf16[384,768]{1,0:T(8,128)(2,1)S(1)}, bf16[384,768]{1,0:T(8,128)(2,1)}, u32[]{:S(2)}, u32[]{:S(2)}) collective-permute-start(bf16[384,768]{1,0:T(8,128)(2,1)S(1)} %slice.974), channel_id=1, source_target_pairs={{0,2},{1,3},{2,0},{3,1},{4,6},{5,7},{6,4},{7,5},{8,10},{9,11},{10,... | collective-permute-start | bytes 1769480 | tf_op jit(solution)/shard_map/ppermute | solution.py:23
  830.8 11.2 %collective-permute-start.74 = (bf16[96,768]{0,1:T(8,128)(2,1)S(1)}, bf16[96,768]{0,1:T(8,128)(2,1)}, u32[]{:S(2)}, u32[]{:S(2)}) collective-permute-start(bf16[96,768]{0,1:T(8,128)(2,1)S(1)} %slice.764), channel_id=1, source_target_pairs={{0,16},{4,20},{8,24},{12,28},{16,0},{20,4},{24,8},{28,12},{1,17},{... | collective-permute-start | bytes 442376 | tf_op jit(solution)/shard_map/ppermute | solution.py:23
  (105 other events, 1102.1 us)

commit v4 on v3

--- a/solution.py
+++ b/solution.py
@@ -48,25 +48,37 @@
     cut = first.shape[1]
 
     def z_step(mask):
-        def step(state):
-            return (jnp.concatenate([state[0], exchange(state[0], "dp", mask)], axis=0),)
-
-        return step
-
-    def near(state):
-        first, second = state[0][:, :cut], state[0][:, cut:]
-        first, second = together(first, second)
-        first_more, other = exchange(first, "dp", masks[-1]), exchange(second, "tensor", 2)
-        return jnp.concatenate([first, first_more], axis=0), jnp.stack([second, other])
-
-    def last(state):
-        first, second = state
-        other, more = exchange(first, "tensor", 2), exchange(second, "dp", masks[-1])
-        second = [jnp.concatenate([second[i], more[i]], axis=0) for i in range(2)]
-        return first, other, *second
-
-    start = (jnp.concatenate([first, second], axis=1),)
-    return start, [z_step(mask) for mask in masks[:-1]], [near, last]
+        return (
+            lambda state: (exchange(state[0], "dp", mask),),
+            lambda state, got: (jnp.concatenate([state[0], got[0]], axis=0),),
+        )
+
+    near = (
+        lambda state: (exchange(state[0], "dp", masks[-1]), exchange(state[1], "tensor", 2)),
+        lambda state, got: (
+            jnp.concatenate([state[0], got[0]], axis=0),
+            jnp.stack([state[1], got[1]]),
+        ),
+    )
+    last = (
+        lambda state: (exchange(state[0], "tensor", 2), exchange(state[1], "dp", masks[-1])),
+        lambda state, got: (
+            state[0],
+            got[0],
+            *[jnp.concatenate([state[1][i], got[1][i]], axis=0) for i in range(2)],
+        ),
+    )
+
+    def split(finish):
+        def cut_last(state, got):
+            block = finish(state, got)[0]
+            return block[:, :cut], block[:, cut:]
+
+        return cut_last
+
+    ahead = [z_step(mask) for mask in masks[:-1]]
+    ahead[-1] = (ahead[-1][0], split(ahead[-1][1]))
+    return (jnp.concatenate([first, second], axis=1),), ahead, [near, last]
 
 
 class Gathering:
@@ -76,26 +88,32 @@
         self.plan = [[(0, step)] for step in made[0][1]]
         for at, (_, _, near) in enumerate(made):
             ahead = made[at + 1][1] if at + 1 < len(made) else []
-            count = max(len(near), len(ahead))
-            for i in range(count):
+            for i in range(max(len(near), len(ahead))):
                 stage = [(at, near[i])] if i < len(near) else []
                 self.plan.append(stage + ([(at + 1, ahead[i])] if i < len(ahead) else []))
-        self.ends = []
-        for at in range(len(made)):
-            self.ends.append(max(i for i, stage in enumerate(self.plan) for g, _ in stage if g == at))
+        self.ends = [
+            max(i for i, stage in enumerate(self.plan) for g, _ in stage if g == at)
+            for at in range(len(made))
+        ]
         self.done = 0
+        self.tokens = ()
 
     def advance(self, *others):
         stage = self.plan[self.done]
         self.done += 1
-        results = [step(self.states[g]) for g, step in stage]
-        flat = [part for result in results for part in result]
-        flat = together(*flat, *others)
+        flat = [part for g, _ in stage for part in self.states[g]]
+        flat = behind(flat, *self.tokens)
+        states, received, at = [], [], 0
+        for g, (send, _) in stage:
+            states.append(flat[at : at + len(self.states[g])])
+            at += len(self.states[g])
+            received.append(send(states[-1]))
+        flat = together(*[part for got in received for part in got], *others)
         at = 0
-        for (g, _), result in zip(stage, results):
-            self.states[g] = flat[at : at + len(result)]
-            at += len(result)
-        self.token = flat[0]
+        for (g, (_, finish)), state, got in zip(stage, states, received):
+            self.states[g] = finish(state, flat[at : at + len(got)])
+            at += len(got)
+        self.tokens = [part for g, _ in stage for part in self.states[g][:1]]
         return flat[at:]
 
     def until(self, group):
@@ -112,43 +130,58 @@
     return (kept.astype(f32) + received.astype(f32)).astype(bf16)
 
 
-def near_one(first, second):
-    mask = dp_masks()[-1]
-    half = first.shape[1] // 2
-    return (
-        add_low(first[0], exchange(first[1], "tensor", 2)),
-        add_low(second[:, :half], exchange(second[:, half:], "dp", mask)),
-    )
-
-
-def near_core(own, received):
-    mask = dp_masks()[-1]
-    half = own.shape[1] // 2
-    sent = together(add_low(own[1], received[1]), add_low(own[2:, half:], received[2:, half:]))
-
-    def finish():
-        first, second = exchange(sent[0], "tensor", 2), exchange(sent[1], "dp", mask)
-        first = own[0].astype(f32) + received[0].astype(f32) + first.astype(f32)
-        kept = own[2:, :half].astype(f32) + received[2:, :half].astype(f32)
-        return first.astype(bf16), (kept + second.astype(f32)).astype(bf16)
-
-    return sent, finish
+def near_one_sent(first, second):
+    return first[1], second[:, second.shape[1] // 2 :]
+
+
+def near_one(sent):
+    return exchange(sent[0], "tensor", 2), exchange(sent[1], "dp", dp_masks()[-1])
+
+
+def near_one_sum(first, second, got):
+    return add_low(first[0], got[0]), add_low(second[:, : second.shape[1] // 2], got[1])
 
 
 def near_two(first, second):
-    mask = dp_masks()[-1]
     half = first.shape[0] // 2
-    return (
-        add_low(first[:half], exchange(first[half:], "dp", mask)),
-        add_low(second[0], exchange(second[1], "tensor", 2)),
-    )
+    return exchange(first[half:], "dp", dp_masks()[-1]), exchange(second[1], "tensor", 2)
+
+
+def near_two_sum(first, second, got):
+    return add_low(first[: first.shape[0] // 2], got[0]), add_low(second[0], got[1])
 
 
 def far(value, masks):
-    for mask in masks:
-        half = value.shape[0] // 2
-        value = add_low(value[:half], exchange(value[half:], "dp", mask))
-    return value
+    for mask in masks[:-1]:
+        value = far_sum(value, exchange(value[value.shape[0] // 2 :], "dp", mask))
+    return value, exchange(value[value.shape[0] // 2 :], "dp", masks[-1])
+
+
+def far_sum(value, got):
+    return add_low(value[: value.shape[0] // 2], got)
+
+
+class CoreFold:
+    def __init__(self, own, received):
+        half = own.shape[1] // 2
+        self.half = half
+        self.kept = (own[0], received[0], own[2:, :half], received[2:, :half])
+        self.state = together(
+            add_low(own[1], received[1]), add_low(own[2:, half:], received[2:, half:])
+        )
+        self.step = 0
+
+    def send(self):
+        return near_two(*self.state) if self.step else near_one(self.state)
+
+    def finish(self, got):
+        if self.step:
+            self.state = near_two_sum(*self.state, got)
+        else:
+            first = self.kept[0].astype(f32) + self.kept[1].astype(f32) + got[0].astype(f32)
+            second = self.kept[2].astype(f32) + self.kept[3].astype(f32) + got[1].astype(f32)
+            self.state = together(first.astype(bf16), second.astype(bf16))
+        self.step += 1
 
 
 class Folding:
@@ -159,23 +192,42 @@
         self.feed = jnp.concatenate([up, down], axis=1)
         self.step = 0
 
-    def advance(self):
-        step = self.step
+    def send(self):
+        if self.step < 2:
+            got = near_two(*self.attn) if self.step else near_one(near_one_sent(*self.attn))
+            self.feed, more = far(self.feed, self.masks[self.step])
+            return *got, more
+        self.attn, more = far(self.attn, self.masks[self.step - 2])
+        return (more,)
+
+    def finish(self, got):
+        if self.step < 2:
+            self.attn = (near_two_sum if self.step else near_one_sum)(*self.attn, got[:2])
+            self.feed = far_sum(self.feed, got[2])
+            *self.attn, self.feed = together(*self.attn, self.feed)
+            if self.step == 1:
+                self.attn = jnp.concatenate(self.attn, axis=1)
+        else:
+            (self.attn,) = together(far_sum(self.attn, got[0]))
         self.step += 1
-        if step < 2:
-            attn = (near_one, near_two)[step](*self.attn)
-            *attn, self.feed = together(*attn, far(self.feed, self.masks[step]))
-            self.attn = attn if step == 0 else jnp.concatenate(attn, axis=1)
-        else:
-            (self.attn,) = together(far(self.attn, self.masks[step - 2]))
-
-    def token(self):
+
+    def tokens(self):
         return (self.feed, self.attn) if self.step > 1 else (self.feed, *self.attn)
 
     def result(self):
         half, low = self.attn.shape[1] // 2, self.feed.shape[1] // 2
         parts = self.attn[:, :half], self.attn[:, half:], self.feed[:, :low], self.feed[:, low:]
         return [part.astype(f32) for part in parts]
+
+
+def advance(folds, *others):
+    received = [fold.send() for fold in folds]
+    flat = together(*[part for got in received for part in got], *others)
+    at = 0
+    for fold, got in zip(folds, received):
+        fold.finish(flat[at : at + len(got)])
+        at += len(got)
+    return flat[at:]
 
 
 def split_low(value):
@@ -572,21 +624,45 @@
     me = lax.axis_index("dp")
     t_me = lax.axis_index("tensor")
     y_me = t_me // 2
-    t_order = jnp.arange(4) ^ t_me
-    positions = jnp.arange(count_dp)
-    block_at = relative_mask(positions) ^ me
-    place_of = jnp.argmax(block_at[None, :] == positions[:, None], axis=1)
-
-    small_parts = (norm_gains, norm_shifts, out_biases, qv_bias, up_bias)
-    small_sizes = [part.size for part in small_parts]
-    small = jnp.concatenate([part.reshape(1, -1) for part in small_parts], axis=1)
+    block_at = relative_mask(jnp.arange(count_dp)) ^ me
+
+    norm_part, up_part, qv_part = norm_gains.shape[2], up_bias.shape[1], qv_bias.shape[2]
+    lanes = max(4 * norm_part, up_part)
+
+    def place(part, size, at):
+        room = jnp.zeros((part.shape[0], size), f32)
+        return lax.dynamic_update_slice(room, part, (0, at))
+
+    def to_lanes(part):
+        return jnp.pad(part, ((0, 0), (0, lanes - part.shape[1])))
+
+    by_width = jnp.stack([norm_gains, norm_shifts, out_biases]).reshape(6 * layers, norm_part)
+    by_width = to_lanes(place(by_width, 4 * norm_part, t_me * norm_part))
+    own = jnp.concatenate(
+        [by_width, to_lanes(qv_bias.reshape(2 * layers, qv_part)), to_lanes(up_bias)]
+    )
+    cut, end = 6 * layers, 8 * layers
+    got = exchange(own, "tensor", 1)
+    own = jnp.concatenate([own[:cut] + got[:cut], own[cut:], got[end:]])
+    got = exchange(own, "tensor", 2)
+    by_width = (own[:cut] + got[:cut])[:, : 4 * norm_part]
+    by_hidden = jnp.concatenate(
+        [
+            place(jnp.concatenate([own[end:], got[end:]])[:, :up_part], hidden, me * up_part),
+            place(
+                jnp.concatenate([own[cut:end], got[cut:end]])[:, :qv_part], hidden, me * qv_part
+            ),
+        ]
+    )
 
     source = jnp.repeat(block_at, block) * block + jnp.tile(jnp.arange(block), count_dp)
     to_relative = (jnp.arange(width)[:, None] == source[None, :]).astype(bf16)
 
+    first = y_me == 0
+
     def take_clip(value):
-        mine = lax.dynamic_index_in_dim(value, y_me, 0, keepdims=False)
-        theirs = exchange(lax.dynamic_index_in_dim(value, 1 - y_me, 0, keepdims=False), "tensor", 2)
+        mine = jnp.where(first, value[0], value[1])
+        theirs = exchange(jnp.where(first, value[1], value[0]), "tensor", 2)
         padding = ((0, 0), (0, quarter - row_count), (0, 0))
         both = jnp.pad(jnp.stack([mine, theirs]), padding).reshape(rows, width)
         return nn_dot(both, to_relative)
@@ -597,7 +673,6 @@
         high = mine.astype(bf16)
         low = (mine - high.astype(f32)).astype(bf16)
         mine = (nt_dot(high, to_relative) + nt_dot(low, to_relative))[:row_count]
-        first = y_me == 0
         return jnp.stack([jnp.where(first, mine, theirs), jnp.where(first, theirs, mine)])
 
     current = take_clip(frames)
@@ -610,24 +685,14 @@
         groups += [(qk, vo), (up_weight[at], down_weight[at].T)]
     gathering = Gathering(groups)
     for mask in dp_masks():
-        more = exchange(small, "dp", mask)
+        got = exchange(by_width, "dp", mask), exchange(by_hidden, "dp", mask)
         if mask > 1:
-            (more,) = gathering.advance(more)
-        small = jnp.concatenate([small, more], axis=0)
-    small = jnp.stack([small, exchange(small, "tensor", 1)])
-    small = jnp.stack([small, exchange(small, "tensor", 2)])
-    small = small.reshape(4, count_dp, -1)
-    by_part = jnp.split(small, [sum(small_sizes[: i + 1]) for i in range(4)], axis=2)
-
-    def by_width(part):
-        part = jnp.take(part, t_order, axis=0).reshape(4, count_dp, layers, 2, -1)
-        return part.transpose(2, 3, 1, 0, 4).reshape(layers, 2, width)
-
-    gain_all, shift_all, obias_all = [by_width(part) for part in by_part[:3]]
-    qv_all = jnp.take(by_part[3][0::2], place_of, axis=1).reshape(2, count_dp, layers, 2, -1)
-    qv_all = qv_all.transpose(2, 3, 0, 1, 4).reshape(layers, 2, 2, wide)
-    up_all = jnp.take(by_part[4], place_of, axis=1).reshape(4, count_dp, layers, -1)
-    up_all = up_all.transpose(2, 0, 1, 3).reshape(layers, 4, hidden)
+            got = gathering.advance(*got)
+        by_width = jnp.concatenate([by_width, got[0]], axis=1)
+        by_hidden = by_hidden + got[1]
+    gain_all, shift_all, obias_all = by_width.reshape(3, layers, 2, width)
+    up_all = by_hidden[: 4 * layers].reshape(4, layers, hidden).transpose(1, 0, 2)
+    qv_all = by_hidden[4 * layers :, :wide].reshape(2, layers, 2, wide).transpose(1, 0, 2, 3)
 
     def feed_weights(group):
         parts = gathering.until(group)
@@ -645,15 +710,13 @@
         final = at == layers - 1
         w_qk, w_qk_other, w_vo, w_vo_other = gathering.until(2 * at)
         w_attn = ((w_qk, w_vo), (w_qk_other, w_vo_other))
-        bias = jnp.pad(qv_all[at].transpose(1, 0, 2), ((0, 0), (0, 0), (0, wide)))
+        bias = jnp.pad(qv_all[at], ((0, 0), (0, 0), (0, wide)))
         shares = ()
         heads = []
         for t in range(2):
-            ready = (normed_a, normed_b)
-            if t == 1:
-                gathering.advance()
-                ready = behind(ready, gathering.token, *shares)
+            ready = behind((normed_a, normed_b), *gathering.tokens, *shares)
             out = attend(row_count, quarter, *ready, *w_attn[t], bias[t], shares)
+            out = gathering.advance(*out)
             shares = tuple(out[:2])
             heads.append(out[2:])
         share_b = exchange(shares[1], "tensor", 1)
@@ -671,6 +734,8 @@
         )
         vectors = jnp.pad(vectors, ((0, 2), (0, 0)))
         fed = feed(final, current, shares[0], share_b, vectors, up_all[at], w_up, w_down)
+        if not final:
+            fed = gathering.advance(*fed)
         weights.append((w_attn, w_up, w_down))
         normed = jnp.concatenate([normed_a, normed_b], axis=0)
         saved.append((current, normed, heads, fed[:4], fed[4:8], fed[8], fed[9]))
@@ -689,37 +754,35 @@
         final = at == layers - 1
         w_attn, w_up, w_down = weights[at]
         layer_in, normed, heads, activated, slopes, middle, normed_two = saved[at]
-        if folding is not None:
-            folding.advance()
-            fronts = behind(fronts, *folding.token())
+        uppers = [] if folding is None else [folding]
         vectors = jnp.stack([gain_all[at, 1], gain_all[0 if final else at + 1, 0]])
         vectors = jnp.pad(vectors, ((0, 6), (0, 0)))
-        own, other, bup, gradient, branch_a, sums = feed_back(
+        if uppers:
+            fronts = behind(fronts, *folding.attn, folding.feed)
+        fed = feed_back(
             final, fronts, middle, normed_two, vectors, w_up, w_down, activated, slopes
         )
+        own, other, bup, gradient, branch_a, sums = advance(uppers, *fed)
         if not final:
             gains_one[at + 1] = sums[4:6]
         branch_b = exchange(branch_a, "tensor", 1)
-        sent, finish = near_core(own, exchange(other, "tensor", 1))
+        core = CoreFold(own, exchange(other, "tensor", 1))
         shares = ()
         dqkv = []
         for t in range(2):
-            tokens = list(sent) if t == 0 else list(feed_state) + list(shares)
-            if folding is not None:
-                folding.advance()
-                tokens += folding.token()
+            tokens = [*core.state, *shares]
+            if uppers:
+                tokens += folding.tokens()
             ready = behind((branch_a, branch_b), *tokens)
-            *shares, part = attend_back(
-                row_count, quarter, *ready, *w_attn[t], *heads[t], tuple(shares)
+            *shares, part = advance(
+                [core, *uppers],
+                *attend_back(row_count, quarter, *ready, *w_attn[t], *heads[t], tuple(shares)),
             )
             dqkv.append(part)
-            feed_state = near_two(*feed_state) if t else finish()
-        tokens = list(feed_state)
-        if folding is not None:
-            folding.advance()
-            tokens += folding.token()
+        *shares, dqkv[0], dqkv[1] = behind((*shares, *dqkv), *core.state)
+        if uppers:
+            advance(uppers)
             weight_grads[at + 1] = folding.result()
-        *shares, dqkv[0], dqkv[1] = behind((*shares, *dqkv), *tokens)
         share_b = exchange(shares[1], "tensor", 1)
         branch = jnp.concatenate([branch_a, branch_b], axis=0)
         dw = [tn_dot(normed, dqkv[t]).astype(bf16) for t in range(2)]
@@ -728,7 +791,7 @@
         dw_vo = jnp.stack(
             [jnp.concatenate([dw[t][:, 2 * wide :], dw_o[t]], axis=1) for t in range(2)]
         )
-        folding = Folding(dw_qk, dw_vo, *feed_state)
+        folding = Folding(dw_qk, dw_vo, *core.state)
         dbias = jnp.stack([jnp.sum(part, axis=0, dtype=f32) for part in dqkv])
         dbias = dbias.reshape(2, 3, wide).transpose(1, 0, 2)
         fronts = (gradient, layer_in, shares[0], share_b)
@@ -738,41 +801,52 @@
     )
     gradient = gradient + grad_in
     gains_one[0] = jnp.concatenate(last_sums, axis=0)
-    for step in range(4):
-        if step == 2:
-            (folding.attn,) = behind((folding.attn,), gradient)
-        folding.advance()
+    sums, bqv, bups = [jnp.stack([small_grads[at][i] for at in range(layers)]) for i in range(3)]
+    one = jnp.stack(gains_one)
+    by_width = jnp.stack(
+        [
+            jnp.stack([one[:, 0], sums[:, 1]], axis=1),
+            jnp.stack([one[:, 1], sums[:, 2]], axis=1),
+            jnp.stack([sums[:, 3], sums[:, 0]], axis=1),
+        ]
+    ).reshape(6 * layers, width)
+    by_hidden = [
+        jnp.concatenate(
+            [
+                bups[:, 2 * i : 2 * i + 2].reshape(2 * layers, hidden),
+                jnp.pad(bqv[:, :, i].reshape(2 * layers, wide), ((0, 0), (0, hidden - wide))),
+            ]
+        )
+        for i in range(2)
+    ]
+    (got,) = advance([folding], exchange(by_hidden[1], "tensor", 2))
+    by_hidden = by_hidden[0] + got
+    parts = by_hidden[: 2 * layers].reshape(layers, 2, hidden)
+    gradient, by_width, *folding.attn, folding.feed = together(
+        gradient, by_width, *folding.attn, folding.feed
+    )
+    got = advance(
+        [folding], exchange(by_width, "tensor", 2), exchange(parts[:, 1], "tensor", 1)
+    )
+    by_width = by_width + got[0]
+    by_hidden = jnp.concatenate([parts[:, 0] + got[1], by_hidden[2 * layers :]])
+    got = exchange(by_width, "tensor", 1)
+    for mask in reversed(dp_masks()):
+        if folding.step < 4:
+            got, more = advance([folding], got, exchange(by_hidden, "dp", mask))
+        else:
+            got, more = together(got, exchange(by_hidden, "dp", mask))
+        by_hidden = by_hidden + more
+        by_width = by_width + got if mask == 1 else by_width[:, : by_width.shape[1] // 2] + got
+        got = exchange(by_width[:, by_width.shape[1] // 2 :], "dp", mask)
+    by_width = by_width[:, : by_width.shape[1] // 2] + got
     weight_grads[0] = folding.result()
     frames_grad = give_clip(gradient)
-
-    sums, bqv, bups = [jnp.stack([small_grads[at][i] for at in range(layers)]) for i in range(3)]
-    one = jnp.stack(gains_one)
-    gains = jnp.stack([one[:, 0], sums[:, 1]], axis=1)
-    shifts = jnp.stack([one[:, 1], sums[:, 2]], axis=1)
-    obiases = jnp.stack([sums[:, 3], sums[:, 0]], axis=1)
-
-    def from_width(part):
-        part = part.reshape(layers, 2, count_dp, 4, -1).transpose(3, 2, 0, 1, 4)
-        return jnp.take(part.reshape(4, count_dp, -1), t_order, axis=0)
-
-    bqv = bqv.reshape(layers, 2, 2, count_dp, -1).transpose(2, 3, 0, 1, 4)
-    bqv = jnp.take(bqv.reshape(2, count_dp, -1), block_at, axis=1)
-    bqv = jnp.stack([bqv, jnp.zeros_like(bqv)], axis=1).reshape(4, count_dp, -1)
-    bups = bups.reshape(layers, 4, count_dp, -1).transpose(1, 2, 0, 3)
-    bups = jnp.take(bups.reshape(4, count_dp, -1), block_at, axis=1)
-    small = jnp.concatenate(
-        [from_width(gains), from_width(shifts), from_width(obiases), bqv, bups], axis=2
-    )
-    small = small.reshape(2, 2, count_dp, -1)
-    small = small[0] + exchange(small[1], "tensor", 2)
-    small = small[0] + exchange(small[1], "tensor", 1)
-    for mask in reversed(dp_masks()):
-        half = small.shape[0] // 2
-        small = small[:half] + exchange(small[half:], "dp", mask)
-    pieces = jnp.split(small[0], [sum(small_sizes[: i + 1]) for i in range(4)])
-    gains, shifts, obiases, bqv, bups = [
-        piece.reshape(part.shape) for piece, part in zip(pieces, small_parts)
-    ]
+    by_width = lax.dynamic_slice(by_width, (0, t_me * norm_part), (6 * layers, norm_part))
+    gains, shifts, obiases = by_width.reshape(3, layers, 2, norm_part)
+    bups = lax.dynamic_slice(by_hidden, (0, me * up_part), (layers, up_part))
+    bqv = lax.dynamic_slice(by_hidden, (layers, me * qv_part), (2 * layers, qv_part))
+    bqv = bqv.reshape(layers, 2, qv_part)
 
     def stacked(make):
         return jnp.stack([make(*weight_grads[at]) for at in range(layers)])

time: 861 us -> 708 us (0.82)
  waiting for transfers between devices: 212 us -> 102 us
  local copies, waits for them, and re-layouts: 126 us -> 77.9 us
    ppermute x80 -> x88, waiting for transfers between devices: 212 us -> 102 us  [exchange(): return lax.ppermute(value, axis, [(i, i ^ mask) for i in range(count)])]
    reshape x36 -> x9, local copies, waits for them, and re-layouts: 28 us -> 2.74 us  [the longest x2 2.64 us: local(): bups[:, 2 * i:2 * i + 2].reshape(2 * layers, hidden)]
    gather x10 -> x0, local copies, waits for them, and re-layouts: 14.2 us -> none  [the longest x3 5.98 us: from_width(): return jnp.take(part.reshape(4, count_dp, -1), t_order, axis=0)]
    unnamed x187 -> x213, local copies, waits for them, and re-layouts: 15.8 us -> 25.4 us
    ppermute x80 -> x88, starting transfers between devices: 76.6 us -> 81.1 us  [exchange(): return lax.ppermute(value, axis, [(i, i ^ mask) for i in range(count)])]
  transfers between devices with their start and end apart: 80 -> 88, of which waited for: 37 -> 25; matrix products, arithmetic and copies ran while one was open for 19% -> 18% of each run, Pallas kernels for 29% -> 40%
where the time goes in v4:
time: 708 us; the launch traced here: 698 us
  Pallas kernels  329 us (46%)
  waiting for transfers between devices  102 us (14%)
  starting transfers between devices  81.1 us (11%)
  local copies, waits for them, and re-layouts  77.9 us (11%)
  other arithmetic  74.6 us (11%)
  matrix products  29.9 us (4%)
    pallas_call x4, Pallas kernels, attend_back(): pl.pallas_call(functools.partial(attend_back_kernel, row_count, quarter,...  141 us
    ppermute x88, waiting for transfers between devices, exchange(): return lax.ppermute(value, axis, [(i, i ^ mask) for i in range(count)])  102 us
    pallas_call x4, Pallas kernels, attend(): pl.pallas_call(functools.partial(attend_kernel, row_count, quarter, min(2...  85.8 us
    ppermute x88, starting transfers between devices, exchange(): return lax.ppermute(value, axis, [(i, i ^ mask) for i in range(count)])  81.1 us
    pallas_call x2, Pallas kernels, feed_back(): pl.pallas_call(functools.partial(feed_back_kernel, final), grid=(hidden /...  63.6 us
    pallas_call x2, Pallas kernels, feed(): pl.pallas_call(functools.partial(feed_kernel, final), grid=(hidden // ste...  38.2 us
    unnamed x213, local copies, waits for them, and re-layouts  25.4 us
    convert_element_type x24, other arithmetic, add_low(): return (kept.astype(f32) + received.astype(f32)).astype(bf16)  25.3 us
  transfers between devices with their start and end apart: 88, of which 25 were waited for; matrix products, arithmetic and copies ran while one was open for 18% of the time, Pallas kernels for 40%

profile of v4, /device:TPU:0, one launch (start us, length us, event | category | flops | bytes accessed | tf_op | source)
XLA Modules:
  0.0 697.7 jit_solution(5209136737172215874)
XLA Ops:
  2.8 4.1 collective-permute-start
  12.8 12.1 %collective-permute-done.2 = f32[20,96]{1,0:T(8,128)S(1)} collective-permute-done((f32[20,96]{1,0:T(8,128)S(1)}, f32[20,96]{1,0:T(8,128)S(1)}, u32[]{:S(2)}, u32[]{:S(2)}) %collective-permute-start.2) | collective-permute-done | bytes 7712 | tf_op jit(solution)/shard_map/ppermute | solution.py:23
  25.7 2.9 collective-permute-start.4
  29.5 1.6 collective-permute-done.4
  35.6 3.9 collective-permute-done.6
  43.8 2.5 collective-permute-start.10
  52.9 2.7 fusion.82
  55.6 2.0 copy.41.refs_0_
  62.7 1.7 collective-permute-start.13
  65.9 7.3 %collective-permute-done.11.refs_2_ = bf16[768,384]{1,0:T(8,128)(2,1)S(1)} collective-permute-done((bf16[768,384]{1,0:T(8,128)(2,1)S(1)}, bf16[768,384]{1,0:T(8,128)(2,1)S(1)}, u32[]{:S(2)}, u32[]{:S(2)}) %collective-permute-start.11) | collective-permute-done | bytes 589856 | tf_op jit(solution)/shard_map/ppermute | solution.py:23
  75.8 2.0 collective-permute-start.15
  82.3 21.2 %shard_map.194 = (f32[768,768]{1,0:T(8,128)}, f32[768,768]{1,0:T(8,128)}, bf16[1536,576]{1,0:T(8,128)(2,1)}, bf16[1536,192]{1,0:T(8,128)(2,1)}, f32[1536,8]{1,0:T(8,128)}) custom-call(bf16[768,768]{1,0:T(8,128)(2,1)} %copy-done.6, bf16[768,768]{1,0:T(8,128)(2,1)} %copy-done.20, bf16[768,384]{1,0:T(8,128)(2,1)} %copy-done.18, ...), custom_call_target="tpu_custom_call" | custom-call | tf_op jit(solution)/shard_map/pallas_call | solution.py:337
  105.8 1.7 collective-permute-start.23
  108.4 21.9 %shard_map.195 = (f32[768,768]{1,0:T(8,128)}, bf16[768,768]{1,0:T(8,128)(2,1)}, bf16[1536,576]{1,0:T(8,128)(2,1)}, bf16[1536,192]{1,0:T(8,128)(2,1)}, f32[1536,8]{1,0:T(8,128)}) custom-call(bf16[768,768]{1,0:T(8,128)(2,1)} %copy-done.6, bf16[768,768]{1,0:T(8,128)(2,1)} %copy-done.20, bf16[768,384]{1,0:T(8,128)(2,1)} %copy-done.28, ...), custom_call_target="tpu_custom_call" | custom-call | tf_op jit(solution)/shard_map/pallas_call | solution.py:337
  143.7 20.0 %shard_map.196 = (bf16[768,768]{1,0:T(8,128)(2,1)}, bf16[768,768]{1,0:T(8,128)(2,1)}, bf16[768,768]{1,0:T(8,128)(2,1)}, bf16[768,768]{1,0:T(8,128)(2,1)}, bf16[7...) custom-call(f32[768,768]{1,0:T(8,128)} %copy-done, ...), custom_call_target="tpu_custom_call" | custom-call | tf_op jit(solution)/shard_map/pallas_call | solution.py:508
  169.6 12.4 %collective-permute-done.32.refs_2_ = bf16[768,384]{1,0:T(8,128)(2,1)S(1)} collective-permute-done((bf16[768,384]{1,0:T(8,128)(2,1)S(1)}, bf16[768,384]{1,0:T(8,128)(2,1)S(1)}, u32[]{:S(2)}, u32[]{:S(2)}) %collective-permute-start.32) | collective-permute-done | bytes 589856 | tf_op jit(solution)/shard_map/ppermute | solution.py:23
  184.0 1.7 collective-permute-start.36
  187.8 20.9 %shard_map.197 = (f32[768,768]{1,0:T(8,128)}, f32[768,768]{1,0:T(8,128)}, bf16[1536,576]{1,0:T(8,128)(2,1)}, bf16[1536,192]{1,0:T(8,128)(2,1)}, f32[1536,8]{1,0:T(8,128)}) custom-call(bf16[768,768]{1,0:T(8,128)(2,1)} %get-tuple-element.355.refs_0_, bf16[768,768]{1,0:T(8,128)(2,1)} %copy-done.10, bf16[768,384]{1,0:T(8,128)(2,1)} %copy-done.19, ...), custom_call_target="tpu_custom_call" | custom-call | tf_op jit(solution)/shard_map/pallas_call | solution.py:337
  215.4 21.8 %shard_map.198 = (f32[768,768]{1,0:T(8,128)}, bf16[768,768]{1,0:T(8,128)(2,1)}, bf16[1536,576]{1,0:T(8,128)(2,1)}, bf16[1536,192]{1,0:T(8,128)(2,1)}, f32[1536,8]{1,0:T(8,128)}) custom-call(bf16[768,768]{1,0:T(8,128)(2,1)} %get-tuple-element.355.refs_0_, bf16[768,768]{1,0:T(8,128)(2,1)} %copy-done.10, bf16[768,384]{1,0:T(8,128)(2,1)} %copy-done.29, ...), custom_call_target="tpu_custom_call" | custom-call | tf_op jit(solution)/shard_map/pallas_call | solution.py:337
  239.8 7.1 %collective-permute-done.46 = bf16[375,768]{1,0:T(8,128)(2,1)S(1)} collective-permute-done((bf16[375,768]{1,0:T(8,128)(2,1)}, bf16[375,768]{1,0:T(8,128)(2,1)S(1)}, u32[]{:S(2)}, u32[]{:S(2)}) %collective-permute-start.46) | collective-permute-done | bytes 576032 | tf_op jit(solution)/shard_map/ppermute | solution.py:23
  253.0 2.6 fusion.9.refs_0_
  255.6 18.3 %shard_map.199 = (bf16[768,768]{1,0:T(8,128)(2,1)}, bf16[768,768]{1,0:T(8,128)(2,1)}, bf16[768,768]{1,0:T(8,128)(2,1)}, bf16[768,768]{1,0:T(8,128)(2,1)}, bf16[7...) custom-call(f32[768,768]{1,0:T(8,128)} %get-tuple-element.419.refs_0, ...), custom_call_target="tpu_custom_call" | custom-call | tf_op jit(solution)/shard_map/pallas_call | solution.py:508
  273.9 29.8 %shard_map.200 = (bf16[4,768,768]{2,1,0:T(8,128)(2,1)}, bf16[4,768,768]{2,1,0:T(8,128)(2,1)}, f32[4,768]{1,0:T(4,128)}, f32[768,768]{1,0:T(8,128)}, bf16[768,768]{1,0:T(8,128)(2,1)}, /*index=5*/f32[8,768]{1,0:T(8,128)}) custom-call(f32[768,768]{1,0:T(8,128)} %fusion.9.refs_0_, f32[768,768]{1,0:T(8,128)} %get-tuple-element.368.refs_1_, ...), custom_call_target="tpu_custom_call" | custom-call | tf_op jit(solution)/shard_map/pallas_call | solution.py:580
  304.3 7.7 %collective-permute-done.47 = bf16[4,768,768]{2,1,0:T(8,128)(2,1)S(1)} collective-permute-done((bf16[4,768,768]{2,1,0:T(8,128)(2,1)}, bf16[4,768,768]{2,1,0:T(8,128)(2,1)S(1)}, u32[]{:S(2)}, u32[]{:S(2)}) %collective-permute-start.47) | collective-permute-done | bytes 4718624 | tf_op jit(solution)/shard_map/ppermute | solution.py:23
  312.0 2.5 fusion.18
  314.5 1.7 add_convert_fusion.4
  322.6 34.6 %shard_map.201 = (f32[768,768]{1,0:T(8,128)}, f32[768,768]{1,0:T(8,128)}, bf16[1536,576]{1,0:T(8,128)(2,1)}) custom-call(bf16[768,768]{1,0:T(8,128)(2,1)} %get-tuple-element.397.refs_0_, bf16[768,768]{1,0:T(8,128)(2,1)} %copy-done.15, bf16[768,384]{1,0:T(8,128)(2,1)} %copy-done.19, bf16[768,384]{1,0:T(8,128)(2,1)} %pad_maximum_fusion.29.refs_3_, ...), custom_call_target="tpu_custom_call" | custom-call | tf_op jit(solution)/shard_map/pallas_call | solution.py:421
  357.2 2.4 fusion.5
  359.6 2.4 add_convert_fusion.3
  366.1 3.1 convolution_convert_fusion.5
  369.2 3.0 convolution_convert_fusion.4
  372.2 35.8 %shard_map.202 = (f32[768,768]{1,0:T(8,128)}, bf16[768,768]{1,0:T(8,128)(2,1)}, bf16[1536,576]{1,0:T(8,128)(2,1)}) custom-call(bf16[768,768]{1,0:T(8,128)(2,1)} %get-tuple-element.397.refs_0_, bf16[768,768]{1,0:T(8,128)(2,1)} %copy-done.15, bf16[768,384]{1,0:T(8,128)(2,1)} %copy-done.29, bf16[768,384]{1,0:T(8,128)(2,1)} %pad_maximum_fusion.30.refs_3_, ...), custom_call_target="tpu_custom_call" | custom-call | tf_op jit(solution)/shard_map/pallas_call | solution.py:421
  409.7 3.5 convolution_convert_fusion
  413.3 1.7 convolution_convert_fusion.1
  423.1 33.8 %shard_map.203 = (bf16[4,768,768]{2,1,0:T(8,128)(2,1)}, bf16[4,768,768]{2,1,0:T(8,128)(2,1)}, f32[4,768]{1,0:T(4,128)}, f32[768,768]{1,0:T(8,128)}, bf16[768,768]{1,0:T(8,128)(2,1)}, /*index=5*/f32[8,768]{1,0:T(8,128)}) custom-call(f32[768,768]{1,0:T(8,128)} %get-tuple-element.418.refs_0_, f32[768,768]{1,0:T(8,128)} %get-tuple-element.419.refs_0_.refs_1_, ...), custom_call_target="tpu_custom_call" | custom-call | tf_op jit(solution)/shard_map/pallas_call | solution.py:580
  459.8 2.0 fusion.11
  462.5 11.6 %collective-permute-done.45 = bf16[384,768]{1,0:T(8,128)(2,1)S(1)} collective-permute-done((bf16[384,768]{1,0:T(8,128)(2,1)S(1)}, bf16[384,768]{1,0:T(8,128)(2,1)S(1)}, u32[]{:S(2)}, u32[]{:S(2)}) %collective-permute-start.45) | collective-permute-done | bytes 589856 | tf_op jit(solution)/shard_map/ppermute | solution.py:23
  475.1 2.6 copy.49
  478.2 2.0 convert_reduce_fusion.1
  483.7 3.1 fusion.19
  486.9 3.0 add_convert_fusion.1
  501.0 2.0 collective-permute-start.62
  505.9 34.6 %shard_map.204 = (f32[768,768]{1,0:T(8,128)}, f32[768,768]{1,0:T(8,128)}, bf16[1536,576]{1,0:T(8,128)(2,1)}) custom-call(bf16[768,768]{1,0:T(8,128)(2,1)} %get-tuple-element.470.refs_0_, bf16[768,768]{1,0:T(8,128)(2,1)} %copy-done.13, bf16[768,384]{1,0:T(8,128)(2,1)} %copy-done.18, bf16[768,384]{1,0:T(8,128)(2,1)} %pad_maximum_fusion.24.refs_3_, ...), custom_call_target="tpu_custom_call" | custom-call | tf_op jit(solution)/shard_map/pallas_call | solution.py:421
  541.4 2.4 fusion.4
  543.8 2.4 add_convert_fusion
  552.3 1.7 collective-permute-start.66
  555.4 36.0 %shard_map.205 = (f32[768,768]{1,0:T(8,128)}, bf16[768,768]{1,0:T(8,128)(2,1)}, bf16[1536,576]{1,0:T(8,128)(2,1)}) custom-call(bf16[768,768]{1,0:T(8,128)(2,1)} %get-tuple-element.470.refs_0_, bf16[768,768]{1,0:T(8,128)(2,1)} %copy-done.13, bf16[768,384]{1,0:T(8,128)(2,1)} %copy-done.28, bf16[768,384]{1,0:T(8,128)(2,1)} %pad_maximum_fusion.25.refs_3_, ...), custom_call_target="tpu_custom_call" | custom-call | tf_op jit(solution)/shard_map/pallas_call | solution.py:421
  594.1 3.3 fusion.17
  597.4 1.7 fusion.16
  621.6 6.4 collective-permute-done.84
  631.8 2.0 fusion.22
  633.8 2.0 add_convert_fusion.8
  635.9 2.2 add_convert_fusion.7
  638.3 3.1 multiply_reduce_fusion
  641.6 3.5 multiply_add_fusion
  651.5 5.5 collective-permute-done.76
  657.0 6.2 collective-permute-done.75
  667.9 7.0 %collective-permute-done.78 = bf16[192,768]{0,1:T(8,128)(2,1)S(1)} collective-permute-done((bf16[192,768]{0,1:T(8,128)(2,1)S(1)}, bf16[192,768]{0,1:T(8,128)(2,1)S(1)}, u32[]{:S(2)}, u32[]{:S(2)}) %collective-permute-start.78) | collective-permute-done | bytes 294944 | tf_op jit(solution)/shard_map/ppermute | solution.py:23
  677.0 1.8 collective-permute-start.83
  679.8 2.6 copy.50
  682.4 3.8 collective-permute-done.81
  686.5 2.1 collective-permute-start.86
  692.3 1.8 collective-permute-start.87
  694.8 2.1 collective-permute-done.87
  (597 shorter events, 179.8 us)
Async XLA Ops:
  2.8 28.3 %collective-permute-start = (bf16[96,768]{1,0:T(8,128)(2,1)S(1)}, bf16[96,768]{1,0:T(8,128)(2,1)S(1)}, u32[]{:S(2)}, u32[]{:S(2)}) collective-permute-start(bf16[96,768]{1,0:T(8,128)(2,1)S(1)} %pad_maximum_fusion.37), channel_id=1, source_target_pairs={{0,16},{4,20},{8,24},{12,28},{16,0},{20,4},{24,8},{28,12},{1,17},{... | collective-permute-start | bytes 442376 | tf_op jit(solution)/shard_map/ppermute | solution.py:23
  9.2 42.6 %collective-permute-start.17 = (bf16[375,768]{1,0:T(8,128)(2,1)S(1)}, bf16[375,768]{1,0:T(8,128)(2,1)}, u32[]{:S(2)}, u32[]{:S(2)}) collective-permute-start(bf16[375,768]{1,0:T(8,128)(2,1)S(1)} %get-tuple-element.556), channel_id=1, source_target_pairs={{0,2},{1,3},{2,0},{3,1},{4,6},{5,7},{6,4},{7,5},{8,10},{9,11},{10,... | collective-permute-start | bytes 1728008 | tf_op jit(solution)/shard_map/ppermute | solution.py:23
  11.9 13.0 %collective-permute-start.2 = (f32[20,96]{1,0:T(8,128)S(1)}, f32[20,96]{1,0:T(8,128)S(1)}, u32[]{:S(2)}, u32[]{:S(2)}) collective-permute-start(f32[20,96]{1,0:T(8,128)S(1)} %pad_maximum_fusion.53), channel_id=1, source_target_pairs={{0,2},{1,3},{2,0},{3,1},{4,6},{5,7},{6,4},{7,5},{8,10},{9,11},{10,... | collective-permute-start | bytes 23048 | tf_op jit(solution)/shard_map/ppermute | solution.py:23
  41.7 16.3 %collective-permute-start.8 = (bf16[384,384]{1,0:T(8,128)(2,1)S(1)}, bf16[384,384]{1,0:T(8,128)(2,1)}, u32[]{:S(2)}, u32[]{:S(2)}) collective-permute-start(bf16[384,384]{1,0:T(8,128)(2,1)S(1)} %get-tuple-element.271), channel_id=1, source_target_pairs={{0,4},{4,0},{8,12},{12,8},{16,20},{20,16},{24,28},{28,24},{1,5},{5... | collective-permute-start | bytes 884744 | tf_op jit(solution)/shard_map/ppermute | solution.py:23
  42.3 15.8 %collective-permute-start.9 = (bf16[384,384]{1,0:T(8,128)(2,1)S(1)}, bf16[384,384]{1,0:T(8,128)(2,1)S(1)}, u32[]{:S(2)}, u32[]{:S(2)}) collective-permute-start(bf16[384,384]{1,0:T(8,128)(2,1)S(1)} %get-tuple-element.272), channel_id=1, source_target_pairs={{0,2},{1,3},{2,0},{3,1},{4,6},{5,7},{6,4},{7,5},{8,10},{9,11},{10,... | collective-permute-start | bytes 884744 | tf_op jit(solution)/shard_map/ppermute | solution.py:23
  43.8 14.3 %collective-permute-start.10 = (bf16[96,1536]{1,0:T(8,128)(2,1)S(1)}, bf16[96,1536]{1,0:T(8,128)(2,1)}, u32[]{:S(2)}, u32[]{:S(2)}) collective-permute-start(bf16[96,1536]{1,0:T(8,128)(2,1)S(1)} %get-tuple-element.273), channel_id=1, source_target_pairs={{0,16},{4,20},{8,24},{12,28},{16,0},{20,4},{24,8},{28,12},{1,17},{... | collective-permute-start | bytes 884744 | tf_op jit(solution)/shard_map/ppermute | solution.py:23
  60.7 12.5 %collective-permute-start.11 = (bf16[768,384]{1,0:T(8,128)(2,1)S(1)}, bf16[768,384]{1,0:T(8,128)(2,1)S(1)}, u32[]{:S(2)}, u32[]{:S(2)}) collective-permute-start(bf16[768,384]{1,0:T(8,128)(2,1)S(1)} %pad_maximum_fusion.21.refs_2_), channel_id=1, source_target_pairs={{0,2},{1,3},{2,0},{3,1},{4,6},{5,7},{6,4},{7,5},{8,10},{9,11},{10,... | collective-permute-start | bytes 1769480 | tf_op jit(solution)/shard_map/ppermute | solution.py:23
  61.2 12.3 %collective-permute-start.12 = (bf16[2,384,384]{2,1,0:T(8,128)(2,1)S(1)}, bf16[2,384,384]{2,1,0:T(8,128)(2,1)S(1)}, u32[]{:S(2)}, u32[]{:S(2)}) collective-permute-start(bf16[2,384,384]{2,1,0:T(8,128)(2,1)S(1)} %pad_maximum_fusion.22), channel_id=1, source_target_pairs={{0,4},{4,0},{8,12},{12,8},{16,20},{20,16},{24,28},{28,24},{1,5},{5... | collective-permute-start | bytes 1769480 | tf_op jit(solution)/shard_map/ppermute | solution.py:23
  62.7 12.2 %collective-permute-start.13 = (bf16[192,1536]{1,0:T(8,128)(2,1)S(1)}, bf16[192,1536]{1,0:T(8,128)(2,1)S(1)}, u32[]{:S(2)}, u32[]{:S(2)}) collective-permute-start(bf16[192,1536]{1,0:T(8,128)(2,1)S(1)} %pad_maximum_fusion.23), channel_id=1, source_target_pairs={{0,8},{4,12},{8,0},{12,4},{16,24},{20,28},{24,16},{28,20},{1,9},{5... | collective-permute-start | bytes 1769480 | tf_op jit(solution)/shard_map/ppermute | solution.py:23
  64.9 16.4 %collective-permute-start.19 = (bf16[768,768]{1,0:T(8,128)(2,1)S(1)}, bf16[768,768]{1,0:T(8,128)(2,1)S(1)}, u32[]{:S(2)}, u32[]{:S(2)}) collective-permute-start(bf16[768,768]{1,0:T(8,128)(2,1)S(1)} %add_convert_fusion.6.refs_0_), channel_id=1, source_target_pairs={{0,1},{1,0},{2,3},{3,2},{4,5},{5,4},{6,7},{7,6},{8,9},{9,8},{10,11... | collective-permute-start | bytes 3538952 | tf_op jit(solution)/shard_map/ppermute | solution.py:23
  75.0 28.5 %collective-permute-start.14 = (bf16[384,768]{1,0:T(8,128)(2,1)S(1)}, bf16[384,768]{1,0:T(8,128)(2,1)S(1)}, u32[]{:S(2)}, u32[]{:S(2)}) collective-permute-start(bf16[384,768]{1,0:T(8,128)(2,1)S(1)} %get-tuple-element.281), channel_id=1, source_target_pairs={{0,4},{4,0},{8,12},{12,8},{16,20},{20,16},{24,28},{28,24},{1,5},{5... | collective-permute-start | bytes 1769480 | tf_op jit(solution)/shard_map/ppermute | solution.py:23
  75.8 27.7 %collective-permute-start.15 = (bf16[384,768]{1,0:T(8,128)(2,1)S(1)}, bf16[384,768]{1,0:T(8,128)(2,1)S(1)}, u32[]{:S(2)}, u32[]{:S(2)}) collective-permute-start(bf16[384,768]{1,0:T(8,128)(2,1)S(1)} %get-tuple-element.282), channel_id=1, source_target_pairs={{0,2},{1,3},{2,0},{3,1},{4,6},{5,7},{6,4},{7,5},{8,10},{9,11},{10,... | collective-permute-start | bytes 1769480 | tf_op jit(solution)/shard_map/ppermute | solution.py:23
  77.8 25.7 %collective-permute-start.16 = (bf16[96,768]{1,0:T(8,128)(2,1)}, bf16[96,768]{1,0:T(8,128)(2,1)S(1)}, u32[]{:S(2)}, u32[]{:S(2)}) collective-permute-start(bf16[96,768]{1,0:T(8,128)(2,1)} %pad_maximum_fusion.38), channel_id=1, source_target_pairs={{0,16},{4,20},{8,24},{12,28},{16,0},{20,4},{24,8},{28,12},{1,17},{... | collective-permute-start | bytes 442376 | tf_op jit(solution)/shard_map/ppermute | solution.py:23
  103.7 26.7 %collective-permute-start.21 = (bf16[768,768]{1,0:T(8,128)(2,1)S(1)}, bf16[768,768]{1,0:T(8,128)(2,1)}, u32[]{:S(2)}, u32[]{:S(2)}) collective-permute-start(bf16[768,768]{1,0:T(8,128)(2,1)S(1)} %constant_dynamic-update-slice_fusion.2.refs_5_.refs_7_), channel_id=1, source_target_pairs={{0,2},{1,3},{2,0},{3,1},{4,6},{5,7},{6,4},{7,5},{8,10},{9,11},{10,... | collective-permute-start | bytes 3538952 | tf_op jit(solution)/shard_map/ppermute | solution.py:23
  104.2 26.2 %collective-permute-start.22 = (bf16[2,384,768]{2,1,0:T(8,128)(2,1)S(1)}, bf16[2,384,768]{2,1,0:T(8,128)(2,1)S(1)}, u32[]{:S(2)}, u32[]{:S(2)}) collective-permute-start(bf16[2,384,768]{2,1,0:T(8,128)(2,1)S(1)} %pad_maximum_fusion.10), channel_id=1, source_target_pairs={{0,4},{4,0},{8,12},{12,8},{16,20},{20,16},{24,28},{28,24},{1,5},{5... | collective-permute-start | bytes 3538952 | tf_op jit(solution)/shard_map/ppermute | solution.py:23
  105.8 24.6 %collective-permute-start.23 = (bf16[192,768]{1,0:T(8,128)(2,1)S(1)}, bf16[192,768]{1,0:T(8,128)(2,1)S(1)}, u32[]{:S(2)}, u32[]{:S(2)}) collective-permute-start(bf16[192,768]{1,0:T(8,128)(2,1)S(1)} %constant_dynamic-update-slice_fusion.4), channel_id=1, source_target_pairs={{0,8},{4,12},{8,0},{12,4},{16,24},{20,28},{24,16},{28,20},{1,9},{5... | collective-permute-start | bytes 884744 | tf_op jit(solution)/shard_map/ppermute | solution.py:23
  108.4 28.7 %collective-permute-start.28 = (bf16[768,768]{1,0:T(8,128)(2,1)S(1)}, bf16[768,768]{1,0:T(8,128)(2,1)}, u32[]{:S(2)}, u32[]{:S(2)}) collective-permute-start(bf16[768,768]{1,0:T(8,128)(2,1)S(1)} %constant_dynamic-update-slice_fusion.2.refs_5_.refs_7_), channel_id=1, source_target_pairs={{0,1},{1,0},{2,3},{3,2},{4,5},{5,4},{6,7},{7,6},{8,9},{9,8},{10,11... | collective-permute-start | bytes 3538952 | tf_op jit(solution)/shard_map/ppermute | solution.py:23
  131.8 11.9 %collective-permute-start.30 = (bf16[768,768]{1,0:T(8,128)(2,1)S(1)}, bf16[768,768]{1,0:T(8,128)(2,1)}, u32[]{:S(2)}, u32[]{:S(2)}) collective-permute-start(bf16[768,768]{1,0:T(8,128)(2,1)S(1)} %pad_maximum_fusion.11.refs_9_.refs_11_), channel_id=1, source_target_pairs={{0,1},{1,0},{2,3},{3,2},{4,5},{5,4},{6,7},{7,6},{8,9},{9,8},{10,11... | collective-permute-start | bytes 3538952 | tf_op jit(solution)/shard_map/ppermute | solution.py:23
  137.1 26.6 %collective-permute-start.24 = (bf16[384,384]{1,0:T(8,128)(2,1)}, bf16[384,384]{1,0:T(8,128)(2,1)S(1)}, u32[]{:S(2)}, u32[]{:S(2)}) collective-permute-start(bf16[384,384]{1,0:T(8,128)(2,1)} %get-tuple-element.311), channel_id=1, source_target_pairs={{0,4},{4,0},{8,12},{12,8},{16,20},{20,16},{24,28},{28,24},{1,5},{5... | collective-permute-start | bytes 884744 | tf_op jit(solution)/shard_map/ppermute | solution.py:23
  137.8 25.9 %collective-permute-start.25 = (bf16[384,384]{1,0:T(8,128)(2,1)}, bf16[384,384]{1,0:T(8,128)(2,1)S(1)}, u32[]{:S(2)}, u32[]{:S(2)}) collective-permute-start(bf16[384,384]{1,0:T(8,128)(2,1)} %get-tuple-element.312), channel_id=1, source_target_pairs={{0,2},{1,3},{2,0},{3,1},{4,6},{5,7},{6,4},{7,5},{8,10},{9,11},{10,... | collective-permute-start | bytes 884744 | tf_op jit(solution)/shard_map/ppermute | solution.py:23
  139.2 24.6 %collective-permute-start.26 = (bf16[96,1536]{1,0:T(8,128)(2,1)}, bf16[96,1536]{1,0:T(8,128)(2,1)S(1)}, u32[]{:S(2)}, u32[]{:S(2)}) collective-permute-start(bf16[96,1536]{1,0:T(8,128)(2,1)} %get-tuple-element.313), channel_id=1, source_target_pairs={{0,16},{4,20},{8,24},{12,28},{16,0},{20,4},{24,8},{28,12},{1,17},{... | collective-permute-start | bytes 884744 | tf_op jit(solution)/shard_map/ppermute | solution.py:23
  167.1 14.9 %collective-permute-start.32 = (bf16[768,384]{1,0:T(8,128)(2,1)S(1)}, bf16[768,384]{1,0:T(8,128)(2,1)S(1)}, u32[]{:S(2)}, u32[]{:S(2)}) collective-permute-start(bf16[768,384]{1,0:T(8,128)(2,1)S(1)} %pad_maximum_fusion.26.refs_2_), channel_id=1, source_target_pairs={{0,2},{1,3},{2,0},{3,1},{4,6},{5,7},{6,4},{7,5},{8,10},{9,11},{10,... | collective-permute-start | bytes 1769480 | tf_op jit(solution)/shard_map/ppermute | solution.py:23
  167.2 14.9 %collective-permute-start.33 = (bf16[2,384,384]{2,1,0:T(8,128)(2,1)S(1)}, bf16[2,384,384]{2,1,0:T(8,128)(2,1)S(1)}, u32[]{:S(2)}, u32[]{:S(2)}) collective-permute-start(bf16[2,384,384]{2,1,0:T(8,128)(2,1)S(1)} %pad_maximum_fusion.27), channel_id=1, source_target_pairs={{0,4},{4,0},{8,12},{12,8},{16,20},{20,16},{24,28},{28,24},{1,5},{5... | collective-permute-start | bytes 1769480 | tf_op jit(solution)/shard_map/ppermute | solution.py:23
  167.9 14.6 %collective-permute-start.34 = (bf16[192,1536]{1,0:T(8,128)(2,1)S(1)}, bf16[192,1536]{1,0:T(8,128)(2,1)S(1)}, u32[]{:S(2)}, u32[]{:S(2)}) collective-permute-start(bf16[192,1536]{1,0:T(8,128)(2,1)S(1)} %pad_maximum_fusion.28), channel_id=1, source_target_pairs={{0,8},{4,12},{8,0},{12,4},{16,24},{20,28},{24,16},{28,20},{1,9},{5... | collective-permute-start | bytes 1769480 | tf_op jit(solution)/shard_map/ppermute | solution.py:23
  169.5 17.3 %collective-permute-start.37 = (bf16[768,768]{1,0:T(8,128)(2,1)S(1)}, bf16[768,768]{1,0:T(8,128)(2,1)S(1)}, u32[]{:S(2)}, u32[]{:S(2)}) collective-permute-start(bf16[768,768]{1,0:T(8,128)(2,1)S(1)} %copy-done.8), channel_id=1, source_target_pairs={{0,1},{1,0},{2,3},{3,2},{4,5},{5,4},{6,7},{7,6},{8,9},{9,8},{10,11... | collective-permute-start | bytes 3538952 | tf_op jit(solution)/shard_map/ppermute | solution.py:23
  182.8 25.9 %collective-permute-start.35 = (bf16[384,768]{1,0:T(8,128)(2,1)S(1)}, bf16[384,768]{1,0:T(8,128)(2,1)S(1)}, u32[]{:S(2)}, u32[]{:S(2)}) collective-permute-start(bf16[384,768]{1,0:T(8,128)(2,1)S(1)} %get-tuple-element.338), channel_id=1, source_target_pairs={{0,4},{4,0},{8,12},{12,8},{16,20},{20,16},{24,28},{28,24},{1,5},{5... | collective-permute-start | bytes 1769480 | tf_op jit(solution)/shard_map/ppermute | solution.py:23
  184.0 24.7 %collective-permute-start.36 = (bf16[384,768]{1,0:T(8,128)(2,1)S(1)}, bf16[384,768]{1,0:T(8,128)(2,1)S(1)}, u32[]{:S(2)}, u32[]{:S(2)}) collective-permute-start(bf16[384,768]{1,0:T(8,128)(2,1)S(1)} %get-tuple-element.339), channel_id=1, source_target_pairs={{0,2},{1,3},{2,0},{3,1},{4,6},{5,7},{6,4},{7,5},{8,10},{9,11},{10,... | collective-permute-start | bytes 1769480 | tf_op jit(solution)/shard_map/ppermute | solution.py:23
  208.9 29.1 %collective-permute-start.38 = (bf16[768,768]{1,0:T(8,128)(2,1)S(1)}, bf16[768,768]{1,0:T(8,128)(2,1)}, u32[]{:S(2)}, u32[]{:S(2)}) collective-permute-start(bf16[768,768]{1,0:T(8,128)(2,1)S(1)} %constant_dynamic-update-slice_fusion.10.refs_5_.refs_4_), channel_id=1, source_target_pairs={{0,2},{1,3},{2,0},{3,1},{4,6},{5,7},{6,4},{7,5},{8,10},{9,11},{10,... | collective-permute-start | bytes 3538952 | tf_op jit(solution)/shard_map/ppermute | solution.py:23
  209.4 28.7 %collective-permute-start.39 = (bf16[2,384,768]{2,1,0:T(8,128)(2,1)S(1)}, bf16[2,384,768]{2,1,0:T(8,128)(2,1)S(1)}, u32[]{:S(2)}, u32[]{:S(2)}) collective-permute-start(bf16[2,384,768]{2,1,0:T(8,128)(2,1)S(1)} %pad_maximum_fusion.13), channel_id=1, source_target_pairs={{0,4},{4,0},{8,12},{12,8},{16,20},{20,16},{24,28},{28,24},{1,5},{5... | collective-permute-start | bytes 3538952 | tf_op jit(solution)/shard_map/ppermute | solution.py:23
  213.3 33.5 %collective-permute-start.46 = (bf16[375,768]{1,0:T(8,128)(2,1)}, bf16[375,768]{1,0:T(8,128)(2,1)S(1)}, u32[]{:S(2)}, u32[]{:S(2)}) collective-permute-start(bf16[375,768]{1,0:T(8,128)(2,1)} %get-tuple-element.554), channel_id=1, source_target_pairs={{0,2},{1,3},{2,0},{3,1},{4,6},{5,7},{6,4},{7,5},{8,10},{9,11},{10,... | collective-permute-start | bytes 1728008 | tf_op jit(solution)/shard_map/ppermute | solution.py:23
  215.3 40.3 %collective-permute-start.41 = (bf16[768,768]{1,0:T(8,128)(2,1)S(1)}, bf16[768,768]{1,0:T(8,128)(2,1)}, u32[]{:S(2)}, u32[]{:S(2)}) collective-permute-start(bf16[768,768]{1,0:T(8,128)(2,1)S(1)} %constant_dynamic-update-slice_fusion.10.refs_5_.refs_4_), channel_id=1, source_target_pairs={{0,1},{1,0},{2,3},{3,2},{4,5},{5,4},{6,7},{7,6},{8,9},{9,8},{10,11... | collective-permute-start | bytes 3538952 | tf_op jit(solution)/shard_map/ppermute | solution.py:23
  238.0 17.5 %collective-permute-start.40 = (bf16[768,768]{1,0:T(8,128)(2,1)}, bf16[768,768]{1,0:T(8,128)(2,1)}, u32[]{:S(2)}, u32[]{:S(2)}) collective-permute-start(bf16[768,768]{1,0:T(8,128)(2,1)} %get-tuple-element.364), channel_id=1, source_target_pairs={{0,1},{1,0},{2,3},{3,2},{4,5},{5,4},{6,7},{7,6},{8,9},{9,8},{10,11... | collective-permute-start | bytes 3538952 | tf_op jit(solution)/shard_map/ppermute | solution.py:23
  238.0 17.5 %collective-permute-start.42 = (bf16[768,768]{1,0:T(8,128)(2,1)}, bf16[768,768]{1,0:T(8,128)(2,1)}, u32[]{:S(2)}, u32[]{:S(2)}) collective-permute-start(bf16[768,768]{1,0:T(8,128)(2,1)} %collective-permute-done.38.refs_7_.refs_6_), channel_id=1, source_target_pairs={{0,1},{1,0},{2,3},{3,2},{4,5},{5,4},{6,7},{7,6},{8,9},{9,8},{10,11... | collective-permute-start | bytes 3538952 | tf_op jit(solution)/shard_map/ppermute | solution.py:23
  238.7 16.9 %collective-permute-start.43 = (bf16[768,768]{1,0:T(8,128)(2,1)S(1)}, bf16[768,768]{1,0:T(8,128)(2,1)}, u32[]{:S(2)}, u32[]{:S(2)}) collective-permute-start(bf16[768,768]{1,0:T(8,128)(2,1)S(1)} %pad_maximum_fusion.14.refs_9_.refs_8_), channel_id=1, source_target_pairs={{0,1},{1,0},{2,3},{3,2},{4,5},{5,4},{6,7},{7,6},{8,9},{9,8},{10,11... | collective-permute-start | bytes 3538952 | tf_op jit(solution)/shard_map/ppermute | solution.py:23
  304.2 16.9 %collective-permute-start.50 = (bf16[768,768]{1,0:T(8,128)(2,1)}, bf16[768,768]{1,0:T(8,128)(2,1)S(1)}, u32[]{:S(2)}, u32[]{:S(2)}) collective-permute-start(bf16[768,768]{1,0:T(8,128)(2,1)} %get-tuple-element.397.refs_0_), channel_id=1, source_target_pairs={{0,1},{1,0},{2,3},{3,2},{4,5},{5,4},{6,7},{7,6},{8,9},{9,8},{10,11... | collective-permute-start | bytes 3538952 | tf_op jit(solution)/shard_map/ppermute | solution.py:23
  316.2 41.1 %collective-permute-start.48 = (bf16[768,768]{1,0:T(8,128)(2,1)S(1)}, bf16[768,768]{1,0:T(8,128)(2,1)}, u32[]{:S(2)}, u32[]{:S(2)}) collective-permute-start(bf16[768,768]{1,0:T(8,128)(2,1)S(1)} %fusion.18), channel_id=1, source_target_pairs={{0,2},{1,3},{2,0},{3,1},{4,6},{5,7},{6,4},{7,5},{8,10},{9,11},{10,... | collective-permute-start | bytes 3538952 | tf_op jit(solution)/shard_map/ppermute | solution.py:23
  316.9 40.3 %collective-permute-start.49 = (bf16[2,384,768]{2,1,0:T(8,128)(2,1)S(1)}, bf16[2,384,768]{2,1,0:T(8,128)(2,1)}, u32[]{:S(2)}, u32[]{:S(2)}) collective-permute-start(bf16[2,384,768]{2,1,0:T(8,128)(2,1)S(1)} %add_convert_fusion.4), channel_id=1, source_target_pairs={{0,4},{4,0},{8,12},{12,8},{16,20},{20,16},{24,28},{28,24},{1,5},{5... | collective-permute-start | bytes 3538952 | tf_op jit(solution)/shard_map/ppermute | solution.py:23
  362.9 45.1 %collective-permute-start.51 = (bf16[384,768]{1,0:T(8,128)(2,1)}, bf16[384,768]{1,0:T(8,128)(2,1)S(1)}, u32[]{:S(2)}, u32[]{:S(2)}) collective-permute-start(bf16[384,768]{1,0:T(8,128)(2,1)} %slice.645), channel_id=1, source_target_pairs={{0,4},{4,0},{8,12},{12,8},{16,20},{20,16},{24,28},{28,24},{1,5},{5... | collective-permute-start | bytes 1769480 | tf_op jit(solution)/shard_map/ppermute | solution.py:23
  364.7 43.3 %collective-permute-start.52 = (bf16[384,768]{1,0:T(8,128)(2,1)}, bf16[384,768]{1,0:T(8,128)(2,1)}, u32[]{:S(2)}, u32[]{:S(2)}) collective-permute-start(bf16[384,768]{1,0:T(8,128)(2,1)} %slice_bitcast_fusion.7), channel_id=1, source_target_pairs={{0,2},{1,3},{2,0},{3,1},{4,6},{5,7},{6,4},{7,5},{8,10},{9,11},{10,... | collective-permute-start | bytes 1769480 | tf_op jit(solution)/shard_map/ppermute | solution.py:23
  418.6 38.2 %collective-permute-start.53 = (bf16[768,384]{0,1:T(8,128)(2,1)}, bf16[768,384]{0,1:T(8,128)(2,1)}, u32[]{:S(2)}, u32[]{:S(2)}) collective-permute-start(bf16[768,384]{0,1:T(8,128)(2,1)} %slice_bitcast_fusion.6), channel_id=1, source_target_pairs={{0,2},{1,3},{2,0},{3,1},{4,6},{5,7},{6,4},{7,5},{8,10},{9,11},{10,... | collective-permute-start | bytes 1769480 | tf_op jit(solution)/shard_map/ppermute | solution.py:23
  421.0 35.9 %collective-permute-start.54 = (bf16[2,384,384]{1,2,0:T(8,128)(2,1)}, bf16[2,384,384]{1,2,0:T(8,128)(2,1)S(1)}, u32[]{:S(2)}, u32[]{:S(2)}) collective-permute-start(bf16[2,384,384]{1,2,0:T(8,128)(2,1)} %slice.654), channel_id=1, source_target_pairs={{0,4},{4,0},{8,12},{12,8},{16,20},{20,16},{24,28},{28,24},{1,5},{5... | collective-permute-start | bytes 1769480 | tf_op jit(solution)/shard_map/ppermute | solution.py:23
  422.1 34.8 %collective-permute-start.55 = (bf16[192,1536]{1,0:T(8,128)(2,1)}, bf16[192,1536]{1,0:T(8,128)(2,1)}, u32[]{:S(2)}, u32[]{:S(2)}) collective-permute-start(bf16[192,1536]{1,0:T(8,128)(2,1)} %fusion.35), channel_id=1, source_target_pairs={{0,8},{4,12},{8,0},{12,4},{16,24},{20,28},{24,16},{28,20},{1,9},{5... | collective-permute-start | bytes 1769480 | tf_op jit(solution)/shard_map/ppermute | solution.py:23
  456.9 26.8 %collective-permute-start.57 = (bf16[4,768,768]{2,1,0:T(8,128)(2,1)}, bf16[4,768,768]{2,1,0:T(8,128)(2,1)}, u32[]{:S(2)}, u32[]{:S(2)}) collective-permute-start(bf16[4,768,768]{2,1,0:T(8,128)(2,1)} %get-tuple-element.440), channel_id=1, source_target_pairs={{0,1},{1,0},{2,3},{3,2},{4,5},{5,4},{6,7},{7,6},{8,9},{9,8},{10,11... | collective-permute-start | bytes 14155784 | tf_op jit(solution)/shard_map/ppermute | solution.py:23
  458.5 15.7 %collective-permute-start.45 = (bf16[384,768]{1,0:T(8,128)(2,1)S(1)}, bf16[384,768]{1,0:T(8,128)(2,1)S(1)}, u32[]{:S(2)}, u32[]{:S(2)}) collective-permute-start(bf16[384,768]{1,0:T(8,128)(2,1)S(1)} %slice.1049), channel_id=1, source_target_pairs={{0,2},{1,3},{2,0},{3,1},{4,6},{5,7},{6,4},{7,5},{8,10},{9,11},{10,... | collective-permute-start | bytes 1769480 | tf_op jit(solution)/shard_map/ppermute | solution.py:23
  480.9 20.2 %collective-permute-start.63 = (bf16[768,768]{1,0:T(8,128)(2,1)S(1)}, bf16[768,768]{1,0:T(8,128)(2,1)S(1)}, u32[]{:S(2)}, u32[]{:S(2)}) collective-permute-start(bf16[768,768]{1,0:T(8,128)(2,1)S(1)} %copy-done.12), channel_id=1, source_target_pairs={{0,1},{1,0},{2,3},{3,2},{4,5},{5,4},{6,7},{7,6},{8,9},{9,8},{10,11... | collective-permute-start | bytes 3538952 | tf_op jit(solution)/shard_map/ppermute | solution.py:23
  489.9 50.7 %collective-permute-start.58 = (bf16[768,768]{1,0:T(8,128)(2,1)}, bf16[768,768]{1,0:T(8,128)(2,1)}, u32[]{:S(2)}, u32[]{:S(2)}) collective-permute-start(bf16[768,768]{1,0:T(8,128)(2,1)} %fusion.19), channel_id=1, source_target_pairs={{0,2},{1,3},{2,0},{3,1},{4,6},{5,7},{6,4},{7,5},{8,10},{9,11},{10,... | collective-permute-start | bytes 3538952 | tf_op jit(solution)/shard_map/ppermute | solution.py:23
  491.1 49.5 %collective-permute-start.59 = (bf16[2,384,768]{2,1,0:T(8,128)(2,1)}, bf16[2,384,768]{2,1,0:T(8,128)(2,1)}, u32[]{:S(2)}, u32[]{:S(2)}) collective-permute-start(bf16[2,384,768]{2,1,0:T(8,128)(2,1)} %add_convert_fusion.1), channel_id=1, source_target_pairs={{0,4},{4,0},{8,12},{12,8},{16,20},{20,16},{24,28},{28,24},{1,5},{5... | collective-permute-start | bytes 3538952 | tf_op jit(solution)/shard_map/ppermute | solution.py:23
  493.1 47.4 %collective-permute-start.60 = (bf16[384,384]{0,1:T(8,128)(2,1)}, bf16[384,384]{0,1:T(8,128)(2,1)S(1)}, u32[]{:S(2)}, u32[]{:S(2)}) collective-permute-start(bf16[384,384]{0,1:T(8,128)(2,1)} %slice.665), channel_id=1, source_target_pairs={{0,4},{4,0},{8,12},{12,8},{16,20},{20,16},{24,28},{28,24},{1,5},{5... | collective-permute-start | bytes 884744 | tf_op jit(solution)/shard_map/ppermute | solution.py:23
  494.8 45.7 %collective-permute-start.61 = (bf16[384,384]{0,1:T(8,128)(2,1)}, bf16[384,384]{0,1:T(8,128)(2,1)S(1)}, u32[]{:S(2)}, u32[]{:S(2)}) collective-permute-start(bf16[384,384]{0,1:T(8,128)(2,1)} %slice_bitcast_fusion.17), channel_id=1, source_target_pairs={{0,2},{1,3},{2,0},{3,1},{4,6},{5,7},{6,4},{7,5},{8,10},{9,11},{10,... | collective-permute-start | bytes 884744 | tf_op jit(solution)/shard_map/ppermute | solution.py:23
  501.0 39.5 %collective-permute-start.62 = (bf16[96,1536]{1,0:T(8,128)(2,1)}, bf16[96,1536]{1,0:T(8,128)(2,1)S(1)}, u32[]{:S(2)}, u32[]{:S(2)}) collective-permute-start(bf16[96,1536]{1,0:T(8,128)(2,1)} %slice.667), channel_id=1, source_target_pairs={{0,16},{4,20},{8,24},{12,28},{16,0},{20,4},{24,8},{28,12},{1,17},{... | collective-permute-start | bytes 884744 | tf_op jit(solution)/shard_map/ppermute | solution.py:23
  547.1 45.1 %collective-permute-start.64 = (bf16[384,768]{1,0:T(8,128)(2,1)}, bf16[384,768]{1,0:T(8,128)(2,1)S(1)}, u32[]{:S(2)}, u32[]{:S(2)}) collective-permute-start(bf16[384,768]{1,0:T(8,128)(2,1)} %slice.670), channel_id=1, source_target_pairs={{0,4},{4,0},{8,12},{12,8},{16,20},{20,16},{24,28},{28,24},{1,5},{5... | collective-permute-start | bytes 1769480 | tf_op jit(solution)/shard_map/ppermute | solution.py:23
  549.2 43.0 %collective-permute-start.65 = (bf16[384,768]{1,0:T(8,128)(2,1)}, bf16[384,768]{1,0:T(8,128)(2,1)}, u32[]{:S(2)}, u32[]{:S(2)}) collective-permute-start(bf16[384,768]{1,0:T(8,128)(2,1)} %slice_bitcast_fusion.5), channel_id=1, source_target_pairs={{0,2},{1,3},{2,0},{3,1},{4,6},{5,7},{6,4},{7,5},{8,10},{9,11},{10,... | collective-permute-start | bytes 1769480 | tf_op jit(solution)/shard_map/ppermute | solution.py:23
  552.3 39.9 %collective-permute-start.66 = (bf16[192,768]{0,1:T(8,128)(2,1)}, bf16[192,768]{0,1:T(8,128)(2,1)}, u32[]{:S(2)}, u32[]{:S(2)}) collective-permute-start(bf16[192,768]{0,1:T(8,128)(2,1)} %slice.797), channel_id=1, source_target_pairs={{0,8},{4,12},{8,0},{12,4},{16,24},{20,28},{24,16},{28,20},{1,9},{5... | collective-permute-start | bytes 884744 | tf_op jit(solution)/shard_map/ppermute | solution.py:23
  603.2 35.1 %collective-permute-start.67 = (bf16[768,768]{1,0:T(8,128)(2,1)}, bf16[768,768]{1,0:T(8,128)(2,1)}, u32[]{:S(2)}, u32[]{:S(2)}) collective-permute-start(bf16[768,768]{1,0:T(8,128)(2,1)} %get-tuple-element.485), channel_id=1, source_target_pairs={{0,1},{1,0},{2,3},{3,2},{4,5},{5,4},{6,7},{7,6},{8,9},{9,8},{10,11... | collective-permute-start | bytes 3538952 | tf_op jit(solution)/shard_map/ppermute | solution.py:23
  605.4 26.4 %collective-permute-start.68 = (bf16[768,384]{0,1:T(8,128)(2,1)}, bf16[768,384]{0,1:T(8,128)(2,1)}, u32[]{:S(2)}, u32[]{:S(2)}) collective-permute-start(bf16[768,384]{0,1:T(8,128)(2,1)} %slice_bitcast_fusion.4), channel_id=1, source_target_pairs={{0,2},{1,3},{2,0},{3,1},{4,6},{5,7},{6,4},{7,5},{8,10},{9,11},{10,... | collective-permute-start | bytes 1769480 | tf_op jit(solution)/shard_map/ppermute | solution.py:23
  607.4 24.4 %collective-permute-start.69 = (bf16[2,384,384]{1,2,0:T(8,128)(2,1)}, bf16[2,384,384]{1,2,0:T(8,128)(2,1)}, u32[]{:S(2)}, u32[]{:S(2)}) collective-permute-start(bf16[2,384,384]{1,2,0:T(8,128)(2,1)} %slice.691), channel_id=1, source_target_pairs={{0,4},{4,0},{8,12},{12,8},{16,20},{20,16},{24,28},{28,24},{1,5},{5... | collective-permute-start | bytes 1769480 | tf_op jit(solution)/shard_map/ppermute | solution.py:23
  608.6 23.2 %collective-permute-start.70 = (bf16[192,1536]{1,0:T(8,128)(2,1)}, bf16[192,1536]{1,0:T(8,128)(2,1)}, u32[]{:S(2)}, u32[]{:S(2)}) collective-permute-start(bf16[192,1536]{1,0:T(8,128)(2,1)} %fusion.34), channel_id=1, source_target_pairs={{0,8},{4,12},{8,0},{12,4},{16,24},{20,28},{24,16},{28,20},{1,9},{5... | collective-permute-start | bytes 1769480 | tf_op jit(solution)/shard_map/ppermute | solution.py:23
  617.0 11.0 %collective-permute-start.84 = (bf16[96,768]{0,1:T(8,128)(2,1)}, bf16[96,768]{0,1:T(8,128)(2,1)}, u32[]{:S(2)}, u32[]{:S(2)}) collective-permute-start(bf16[96,768]{0,1:T(8,128)(2,1)} %slice.830), channel_id=1, source_target_pairs={{0,16},{4,20},{8,24},{12,28},{16,0},{20,4},{24,8},{28,12},{1,17},{... | collective-permute-start | bytes 442376 | tf_op jit(solution)/shard_map/ppermute | solution.py:23
  638.2 12.3 %collective-permute-start.77 = (f32[2,768]{1,0:T(2,128)S(1)}, f32[2,768]{1,0:T(2,128)S(1)}, u32[]{:S(2)}, u32[]{:S(2)}) collective-permute-start(f32[2,768]{1,0:T(2,128)S(1)} %bitcast.303), channel_id=1, source_target_pairs={{0,1},{1,0},{2,3},{3,2},{4,5},{5,4},{6,7},{7,6},{8,9},{9,8},{10,11... | collective-permute-start | bytes 18440 | tf_op jit(solution)/shard_map/ppermute | solution.py:23
  645.1 11.9 %collective-permute-start.73 = (bf16[384,384]{0,1:T(8,128)(2,1)S(1)}, bf16[384,384]{0,1:T(8,128)(2,1)S(1)}, u32[]{:S(2)}, u32[]{:S(2)}) collective-permute-start(bf16[384,384]{0,1:T(8,128)(2,1)S(1)} %slice.704), channel_id=1, source_target_pairs={{0,4},{4,0},{8,12},{12,8},{16,20},{20,16},{24,28},{28,24},{1,5},{5... | collective-permute-start | bytes 884744 | tf_op jit(solution)/shard_map/ppermute | solution.py:23
  647.1 16.1 %collective-permute-start.75 = (bf16[96,1536]{1,0:T(8,128)(2,1)S(1)}, bf16[96,1536]{1,0:T(8,128)(2,1)S(1)}, u32[]{:S(2)}, u32[]{:S(2)}) collective-permute-start(bf16[96,1536]{1,0:T(8,128)(2,1)S(1)} %slice.706), channel_id=1, source_target_pairs={{0,16},{4,20},{8,24},{12,28},{16,0},{20,4},{24,8},{28,12},{1,17},{... | collective-permute-start | bytes 884744 | tf_op jit(solution)/shard_map/ppermute | solution.py:23
  650.5 28.3 %collective-permute-start.72 = (bf16[384,768]{1,0:T(8,128)(2,1)S(1)}, bf16[384,768]{1,0:T(8,128)(2,1)S(1)}, u32[]{:S(2)}, u32[]{:S(2)}) collective-permute-start(bf16[384,768]{1,0:T(8,128)(2,1)S(1)} %slice.1048), channel_id=1, source_target_pairs={{0,2},{1,3},{2,0},{3,1},{4,6},{5,7},{6,4},{7,5},{8,10},{9,11},{10,... | collective-permute-start | bytes 1769480 | tf_op jit(solution)/shard_map/ppermute | solution.py:23
  663.8 11.1 %collective-permute-start.78 = (bf16[192,768]{0,1:T(8,128)(2,1)S(1)}, bf16[192,768]{0,1:T(8,128)(2,1)S(1)}, u32[]{:S(2)}, u32[]{:S(2)}) collective-permute-start(bf16[192,768]{0,1:T(8,128)(2,1)S(1)} %slice.817), channel_id=1, source_target_pairs={{0,8},{4,12},{8,0},{12,4},{16,24},{20,28},{24,16},{28,20},{1,9},{5... | collective-permute-start | bytes 884744 | tf_op jit(solution)/shard_map/ppermute | solution.py:23
  675.1 11.2 %collective-permute-start.81 = (bf16[96,768]{0,1:T(8,128)(2,1)S(1)}, bf16[96,768]{0,1:T(8,128)(2,1)S(1)}, u32[]{:S(2)}, u32[]{:S(2)}) collective-permute-start(bf16[96,768]{0,1:T(8,128)(2,1)S(1)} %slice.821), channel_id=1, source_target_pairs={{0,16},{4,20},{8,24},{12,28},{16,0},{20,4},{24,8},{28,12},{1,17},{... | collective-permute-start | bytes 442376 | tf_op jit(solution)/shard_map/ppermute | solution.py:23
  (125 other events, 500.3 us)

commit v5 on v4

--- a/solution.py
+++ b/solution.py
@@ -220,6 +220,31 @@
         return [part.astype(f32) for part in parts]
 
 
+class LastFolding:
+    def __init__(self, attn, up, down):
+        self.masks = dp_masks()[-2::-1]
+        self.attn = attn
+        self.feed = jnp.concatenate([up, down], axis=1)
+        self.step = 0
+
+    def send(self):
+        first, last = self.masks[:-1], self.masks[-1:]
+        self.attn, *got = far(self.attn, (dp_masks()[-1:], first, last)[self.step])
+        if self.step < 2:
+            self.feed, more = far(self.feed, (first, last)[self.step])
+            got.append(more)
+        return got
+
+    def finish(self, got):
+        self.attn = far_sum(self.attn, got[0])
+        if self.step < 2:
+            self.feed = far_sum(self.feed, got[1])
+        self.attn, self.feed = together(self.attn, self.feed)
+        self.step += 1
+
+    result = Folding.result
+
+
 def advance(folds, *others):
     received = [fold.send() for fold in folds]
     flat = together(*[part for got in received for part in got], *others)
@@ -274,10 +299,16 @@
     return pl.BlockSpec(shape, lambda j: (0,) * len(shape))
 
 
+def single(shape):
+    return pl.BlockSpec(shape, lambda j: (0,) * len(shape), pipeline_mode=pl.Buffered(1))
+
+
 def attend_kernel(row_count, quarter, step, first, *refs):
     normed_a, normed_b, w_qk, w_vo, bias = refs[:5]
-    before = () if first else refs[5:7]
-    share_a, share_b, qkv, o, lse, q_s, k_s, v_s = refs[5 + len(before) :]
+    if first:
+        qkv, o, lse, q_s, k_s, v_s, o_s = refs[5:]
+    else:
+        o_before, w_before, share_a, share_b, qkv, o, lse, q_s, k_s, v_s, o_s = refs[5:]
     rows = normed_a.shape[0]
     wide = o.shape[1]
     heads = wide // HD
@@ -297,29 +328,26 @@
             k_s[h, at, :] = widen(qk[:, wide + low : wide + high], k_more)
             v_s[h, at, :] = widen(v[:, low:high], one)
 
+    def work(h, carry):
+        is_total = lax.broadcasted_iota(jnp.int32, (step, WIDE), 1) == HD
+        for part in range(2 * rows // step):
+            at = pl.ds(part * step, step)
+            scores = nt_dot(q_s[h, at, :], k_s[h])
+            top = jnp.max(scores, axis=-1, keepdims=True)
+            summed = nn_dot(jnp.exp2(scores - top).astype(bf16), v_s[h])
+            total = summed[:, HD : HD + 1]
+            o_s[h, at, :] = jnp.where(is_total, top + jnp.log2(total), summed / total)
+        return carry
+
+    lax.fori_loop(0, heads, work, 0)
     for h in range(heads):
-
-        def work(i, carry, h=h):
-            for part in range(2):
-                at = pl.ds(pl.multiple_of((2 * i + part) * step, step), step)
-                scores = nt_dot(q_s[h, at, :], k_s[h])
-                top = jnp.max(scores, axis=-1, keepdims=True)
-                weights = jnp.exp2(scores - top).astype(bf16)
-                summed = nn_dot(weights, v_s[h])
-                total = summed[:, HD : HD + 1]
-                o[at, h * HD : (h + 1) * HD] = (summed[:, :HD] / total).astype(bf16)
-                lse[at, h : h + 1] = top + jnp.log2(total)
-            return carry
-
-        lax.fori_loop(0, rows // step, work, 0)
-    w_o = w_vo[:, wide:]
-    part_a = nt_dot(o[pl.ds(0, rows), :], w_o)
-    part_b = nt_dot(o[pl.ds(rows, rows), :], w_o)
+        o[:, h * HD : (h + 1) * HD] = o_s[h][:, :HD].astype(bf16)
+        lse[:, h : h + 1] = o_s[h][:, HD : HD + 1]
     if not first:
-        part_a = part_a + before[0][...]
-        part_b = part_b + before[1][...]
-    share_a[...] = part_a
-    share_b[...] = part_b.astype(share_b.dtype)
+        for half, share in enumerate((share_a, share_b)):
+            at = pl.ds(half * rows, rows)
+            value = nt_dot(o_before[at, :], w_before[:, wide:]) + nt_dot(o[at, :], w_vo[:, wide:])
+            share[...] = value.astype(share.dtype)
 
 
 def attend(row_count, quarter, normed_a, normed_b, w_qk, w_vo, bias, before):
@@ -328,27 +356,31 @@
     heads = wide // HD
     operands = (normed_a, normed_b, w_qk, w_vo, bias, *before)
     outs = [
-        jax.ShapeDtypeStruct((rows, width), f32),
-        jax.ShapeDtypeStruct((rows, width), bf16 if before else f32),
         jax.ShapeDtypeStruct((2 * rows, 3 * wide), bf16),
         jax.ShapeDtypeStruct((2 * rows, wide), bf16),
         jax.ShapeDtypeStruct((2 * rows, 8), f32),
     ]
+    if before:
+        outs = [jax.ShapeDtypeStruct((rows, width), kind) for kind in (f32, bf16)] + outs
     return pl.pallas_call(
-        functools.partial(attend_kernel, row_count, quarter, min(256, rows), not before),
+        functools.partial(attend_kernel, row_count, quarter, min(512, 2 * rows), not before),
         grid=(1,),
-        in_specs=[whole(part.shape) for part in operands],
+        in_specs=[single(part.shape) for part in operands],
         out_specs=[whole(part.shape) for part in outs],
         out_shape=outs,
-        scratch_shapes=[pltpu.VMEM((heads, 2 * rows, WIDE), bf16)] * 3,
-        compiler_params=pltpu.CompilerParams(vmem_limit_bytes=56 * 2**20),
+        scratch_shapes=[pltpu.VMEM((heads, 2 * rows, WIDE), bf16)] * 3
+        + [pltpu.VMEM((heads, 2 * rows, WIDE), f32)],
+        compiler_params=pltpu.CompilerParams(vmem_limit_bytes=60 * 2**20),
     )(*operands)
 
 
 def attend_back_kernel(row_count, quarter, step, first, *refs):
     branch_a, branch_b, w_qk, w_vo, qkv, o, lse = refs[:7]
-    before = () if first else refs[7:9]
-    dn_a, dn_b, dqkv, q_s, k_s, kt_s, v_s, do_s, dq_s, dk_s, dv_s = refs[7 + len(before) :]
+    if first:
+        dqkv, q_s, k_s, kt_s, v_s, do_s, dq_s, dk_s, dv_s = refs[7:]
+    else:
+        dqkv_before, w_qk_before, w_vo_before, dn_a, dn_b = refs[7:12]
+        dqkv, q_s, k_s, kt_s, v_s, do_s, dq_s, dk_s, dv_s = refs[12:]
     rows = branch_a.shape[0]
     wide = o.shape[1]
     heads = wide // HD
@@ -377,35 +409,38 @@
             inner = jnp.sum(grad.astype(f32) * o[at, low:high].astype(f32), axis=1, keepdims=True)
             do_s[h, at, :] = widen(grad, spread_lanes(0, split_low(-inner)))
 
-    dk_s[...] = jnp.zeros_like(dk_s)
-    dv_s[...] = jnp.zeros_like(dv_s)
-    chunks = 2 * rows // step
-
-    def work(i, carry):
-        h = i // chunks
-        at = pl.ds(pl.multiple_of(lax.rem(i, chunks) * step, step), step)
-        queries = q_s[h, at, :]
-        grad_out = do_s[h, at, :]
-        probs = jnp.exp2(nt_dot(k_s[h], queries))
-        grad_scores = (probs * nt_dot(v_s[h], grad_out)).astype(bf16)
-        dv_s[h] += nn_dot(probs.astype(bf16), grad_out)
-        dk_s[h] += nn_dot(grad_scores, queries)
-        dq_s[h, at, :] = jnp.transpose(nn_dot(kt_s[h], grad_scores))
+    def work(h, carry):
+        for part in range(2 * rows // step):
+            at = pl.ds(part * step, step)
+            queries = q_s[h, at, :]
+            grad_out = do_s[h, at, :]
+            probs = jnp.exp2(nt_dot(k_s[h], queries))
+            grad_scores = (probs * nt_dot(v_s[h], grad_out)).astype(bf16)
+            grad_values = nn_dot(probs.astype(bf16), grad_out)
+            grad_keys = nn_dot(grad_scores, queries)
+            if part == 0:
+                dv_s[h] = grad_values
+                dk_s[h] = grad_keys
+            else:
+                dv_s[h] += grad_values
+                dk_s[h] += grad_keys
+            dq_s[h, at, :] = jnp.transpose(nn_dot(kt_s[h], grad_scores))
         return carry
 
-    lax.fori_loop(0, heads * chunks, work, 0)
+    lax.fori_loop(0, heads, work, 0)
     for h in range(heads):
         low, high = h * HD, (h + 1) * HD
         dqkv[:, low:high] = (dq_s[h][:, :HD] * HD**-0.5).astype(bf16)
         dqkv[:, wide + low : wide + high] = (dk_s[h][:, :HD] * LN2).astype(bf16)
         dqkv[:, 2 * wide + low : 2 * wide + high] = dv_s[h][:, :HD].astype(bf16)
-    for half, dest in enumerate((dn_a, dn_b)):
-        at = pl.ds(half * rows, rows)
-        part = nt_dot(dqkv[at, : 2 * wide], w_qk[...])
-        part = part + nt_dot(dqkv[at, 2 * wide :], w_vo[:, :wide])
-        if not first:
-            part = part + before[half][...]
-        dest[...] = part.astype(dest.dtype)
+    if not first:
+        for half, dest in enumerate((dn_a, dn_b)):
+            at = pl.ds(half * rows, rows)
+            part = nt_dot(dqkv[at, : 2 * wide], w_qk[...])
+            part = part + nt_dot(dqkv[at, 2 * wide :], w_vo[:, :wide])
+            part = part + nt_dot(dqkv_before[at, : 2 * wide], w_qk_before[...])
+            part = part + nt_dot(dqkv_before[at, 2 * wide :], w_vo_before[:, :wide])
+            dest[...] = part.astype(dest.dtype)
 
 
 def attend_back(row_count, quarter, branch_a, branch_b, w_qk, w_vo, qkv, o, lse, before):
@@ -413,15 +448,13 @@
     wide = o.shape[1]
     heads = wide // HD
     operands = (branch_a, branch_b, w_qk, w_vo, qkv, o, lse, *before)
-    outs = [
-        jax.ShapeDtypeStruct((rows, width), f32),
-        jax.ShapeDtypeStruct((rows, width), bf16 if before else f32),
-        jax.ShapeDtypeStruct((2 * rows, 3 * wide), bf16),
-    ]
+    outs = [jax.ShapeDtypeStruct((2 * rows, 3 * wide), bf16)]
+    if before:
+        outs = [jax.ShapeDtypeStruct((rows, width), kind) for kind in (f32, bf16)] + outs
     return pl.pallas_call(
-        functools.partial(attend_back_kernel, row_count, quarter, min(256, rows), not before),
+        functools.partial(attend_back_kernel, row_count, quarter, min(512, 2 * rows), not before),
         grid=(1,),
-        in_specs=[whole(part.shape) for part in operands],
+        in_specs=[single(part.shape) for part in operands],
         out_specs=[whole(part.shape) for part in outs],
         out_shape=outs,
         scratch_shapes=[
@@ -434,7 +467,7 @@
             pltpu.VMEM((heads, 2 * rows, WIDE), f32),
             pltpu.VMEM((heads, 2 * rows, WIDE), f32),
         ],
-        compiler_params=pltpu.CompilerParams(vmem_limit_bytes=60 * 2**20),
+        compiler_params=pltpu.CompilerParams(vmem_limit_bytes=62 * 2**20),
     )(*operands)
 
 
@@ -489,10 +522,6 @@
         def _():
             unit, _ = normalized(total[...])
             following[...] = (unit * vectors[4:5, :] + vectors[5:6, :]).astype(bf16)
-
-
-def single(shape):
-    return pl.BlockSpec(shape, lambda j: (0,) * len(shape), pipeline_mode=pl.Buffered(1))
 
 
 def column_block(rows, step):
@@ -645,6 +674,7 @@
     got = exchange(own, "tensor", 1)
     own = jnp.concatenate([own[:cut] + got[:cut], own[cut:], got[end:]])
     got = exchange(own, "tensor", 2)
+    frames, got = together(frames, got)
     by_width = (own[:cut] + got[:cut])[:, : 4 * norm_part]
     by_hidden = jnp.concatenate(
         [
@@ -660,23 +690,27 @@
 
     first = y_me == 0
 
-    def take_clip(value):
+    def other_clip(value):
+        return exchange(jnp.where(first, value[1], value[0]), "tensor", 2)
+
+    def take_clip(value, theirs):
         mine = jnp.where(first, value[0], value[1])
-        theirs = exchange(jnp.where(first, value[1], value[0]), "tensor", 2)
         padding = ((0, 0), (0, quarter - row_count), (0, 0))
         both = jnp.pad(jnp.stack([mine, theirs]), padding).reshape(rows, width)
         return nn_dot(both, to_relative)
 
-    def give_clip(value):
-        mine, theirs = value[:quarter], value[quarter:].astype(bf16)
-        theirs = nt_dot(exchange(theirs, "tensor", 2), to_relative)[:row_count]
+    def give_half(value):
+        return exchange(value[quarter:].astype(bf16), "tensor", 2)
+
+    def give_clip(value, theirs):
+        mine = value[:quarter]
+        theirs = nt_dot(theirs, to_relative)[:row_count]
         high = mine.astype(bf16)
         low = (mine - high.astype(f32)).astype(bf16)
         mine = (nt_dot(high, to_relative) + nt_dot(low, to_relative))[:row_count]
         return jnp.stack([jnp.where(first, mine, theirs), jnp.where(first, theirs, mine)])
 
-    current = take_clip(frames)
-    gradient = take_clip(cotangent)
+    current = take_clip(frames, other_clip(frames))
 
     groups = []
     for at in range(layers):
@@ -684,10 +718,13 @@
         vo = jnp.concatenate([qkv_weight[at, :, 2], out_weight[at].T], axis=1)
         groups += [(qk, vo), (up_weight[at], down_weight[at].T)]
     gathering = Gathering(groups)
-    for mask in dp_masks():
+    by_width, by_hidden = gathering.advance(by_width, by_hidden)
+    for at, mask in enumerate(dp_masks()):
         got = exchange(by_width, "dp", mask), exchange(by_hidden, "dp", mask)
-        if mask > 1:
+        if mask <= 2:
             got = gathering.advance(*got)
+        else:
+            got = together(*got)
         by_width = jnp.concatenate([by_width, got[0]], axis=1)
         by_hidden = by_hidden + got[1]
     gain_all, shift_all, obias_all = by_width.reshape(3, layers, 2, width)
@@ -705,20 +742,19 @@
     saved = []
     unit, _ = normalized(current)
     normed_a = (unit * gain_all[0, 0] + shift_all[0, 0]).astype(bf16)
-    normed_b = exchange(normed_a, "tensor", 1)
+    (normed_b,) = gathering.advance(exchange(normed_a, "tensor", 1))
     for at in range(layers):
         final = at == layers - 1
         w_qk, w_qk_other, w_vo, w_vo_other = gathering.until(2 * at)
         w_attn = ((w_qk, w_vo), (w_qk_other, w_vo_other))
         bias = jnp.pad(qv_all[at], ((0, 0), (0, 0), (0, wide)))
-        shares = ()
         heads = []
         for t in range(2):
-            ready = behind((normed_a, normed_b), *gathering.tokens, *shares)
-            out = attend(row_count, quarter, *ready, *w_attn[t], bias[t], shares)
-            out = gathering.advance(*out)
-            shares = tuple(out[:2])
-            heads.append(out[2:])
+            before = (heads[0][1], w_attn[0][1]) if t else ()
+            ready = behind((normed_a, normed_b), *gathering.tokens, *before[:1])
+            out = attend(row_count, quarter, *ready, *w_attn[t], bias[t], before)
+            *shares, qkv, o, lse = gathering.advance(*out)
+            heads.append((qkv, o, lse))
         share_b = exchange(shares[1], "tensor", 1)
         w_up, w_down = feed_weights(2 * at + 1)
         following = 0 if final else at + 1
@@ -735,7 +771,9 @@
         vectors = jnp.pad(vectors, ((0, 2), (0, 0)))
         fed = feed(final, current, shares[0], share_b, vectors, up_all[at], w_up, w_down)
         if not final:
-            fed = gathering.advance(*fed)
+            fed = gathering.advance(*fed, *([other_clip(cotangent)] if at == 0 else []))
+            if at == 0:
+                *fed, clip = fed
         weights.append((w_attn, w_up, w_down))
         normed = jnp.concatenate([normed_a, normed_b], axis=0)
         saved.append((current, normed, heads, fed[:4], fed[4:8], fed[8], fed[9]))
@@ -743,13 +781,13 @@
         if not final:
             normed_a = fed[11]
             normed_b = exchange(normed_a, "tensor", 1)
-    encoded = give_clip(current)
-
+    if layers == 1:
+        clip = other_clip(cotangent)
     small_grads = [None] * layers
     weight_grads = [None] * layers
     gains_one = [None] * layers
     folding = None
-    fronts = (gradient,)
+    fronts = (take_clip(cotangent, clip),)
     for at in reversed(range(layers)):
         final = at == layers - 1
         w_attn, w_up, w_down = weights[at]
@@ -762,46 +800,77 @@
         fed = feed_back(
             final, fronts, middle, normed_two, vectors, w_up, w_down, activated, slopes
         )
+        if final:
+            *fed, half = together(*fed, give_half(current))
+            encoded = give_clip(current, half)
         own, other, bup, gradient, branch_a, sums = advance(uppers, *fed)
         if not final:
             gains_one[at + 1] = sums[4:6]
         branch_b = exchange(branch_a, "tensor", 1)
         core = CoreFold(own, exchange(other, "tensor", 1))
-        shares = ()
-        dqkv = []
-        for t in range(2):
-            tokens = [*core.state, *shares]
-            if uppers:
-                tokens += folding.tokens()
-            ready = behind((branch_a, branch_b), *tokens)
-            *shares, part = advance(
-                [core, *uppers],
-                *attend_back(row_count, quarter, *ready, *w_attn[t], *heads[t], tuple(shares)),
-            )
-            dqkv.append(part)
-        *shares, dqkv[0], dqkv[1] = behind((*shares, *dqkv), *core.state)
+        branch = jnp.concatenate([branch_a, branch_b], axis=0)
+
+        def weight_grad(t, dqkv):
+            dw = tn_dot(normed, dqkv).astype(bf16)
+            dw_o = tn_dot(branch, heads[t][1]).astype(bf16)
+            return dw[:, : 2 * wide], jnp.concatenate([dw[:, 2 * wide :], dw_o], axis=1)
+
+        def state_tokens():
+            return [*core.state, *(folding.tokens() if uppers else ())]
+
+        ready = behind((branch_a, branch_b), *state_tokens())
+        (dqkv_other,) = advance(
+            [core, *uppers],
+            *attend_back(row_count, quarter, *ready, *w_attn[1], *heads[1], ()),
+        )
+        if at == 0:
+            sent = jnp.concatenate(weight_grad(1, dqkv_other), axis=1)
+            got = (exchange(sent, "tensor", 2),)
+        else:
+            sent, got = dqkv_other, ()
+        ready = behind((branch_a, branch_b), sent, *state_tokens())
+        *got, share_a, share_b, dqkv_own = advance(
+            [core, *uppers],
+            *got,
+            *attend_back(
+                row_count, quarter, *ready, *w_attn[0], *heads[0], (dqkv_other, *w_attn[1])
+            ),
+        )
+        share_a, share_b, dqkv_own = behind((share_a, share_b, dqkv_own), *core.state)
         if uppers:
             advance(uppers)
             weight_grads[at + 1] = folding.result()
-        share_b = exchange(shares[1], "tensor", 1)
-        branch = jnp.concatenate([branch_a, branch_b], axis=0)
-        dw = [tn_dot(normed, dqkv[t]).astype(bf16) for t in range(2)]
-        dw_o = [tn_dot(branch, heads[t][1]).astype(bf16) for t in range(2)]
-        dw_qk = jnp.stack([dw[t][:, : 2 * wide] for t in range(2)])
-        dw_vo = jnp.stack(
-            [jnp.concatenate([dw[t][:, 2 * wide :], dw_o[t]], axis=1) for t in range(2)]
-        )
-        folding = Folding(dw_qk, dw_vo, *core.state)
-        dbias = jnp.stack([jnp.sum(part, axis=0, dtype=f32) for part in dqkv])
-        dbias = dbias.reshape(2, 3, wide).transpose(1, 0, 2)
-        fronts = (gradient, layer_in, shares[0], share_b)
-        small_grads[at] = (sums, dbias[0::2], bup)
+        share_b = exchange(share_b, "tensor", 1)
+        dw_own = weight_grad(0, dqkv_own)
+        if at == 0:
+            dw_own = add_low(jnp.concatenate(dw_own, axis=1), got[0])
+            folding = LastFolding(dw_own, *core.state)
+        else:
+            dw_other = weight_grad(1, dqkv_other)
+            stacks = [jnp.stack(pair) for pair in zip(dw_own, dw_other)]
+            folding = Folding(*stacks, *core.state)
+        dbias = jnp.stack([jnp.sum(part, axis=0, dtype=f32) for part in (dqkv_own, dqkv_other)])
+        dbias = dbias.reshape(2, 3, wide)[:, 0::2]
+        fronts = (gradient, layer_in, share_a, share_b)
+        small_grads[at] = (sums, dbias, bup)
     grad_in, *last_sums = norm_back(
-        layer_in, gain_all[0, 0], shares[0] + share_b.astype(f32)
+        layer_in, gain_all[0, 0], share_a + share_b.astype(f32)
     )
     gradient = gradient + grad_in
     gains_one[0] = jnp.concatenate(last_sums, axis=0)
     sums, bqv, bups = [jnp.stack([small_grads[at][i] for at in range(layers)]) for i in range(3)]
+    bqv = bqv.reshape(layers, 2, 2, count_dp, qv_part).transpose(1, 0, 2, 3, 4)
+    bqv = jnp.pad(bqv, ((0, 0),) * 4 + ((0, block - qv_part),)).reshape(2, 2 * layers, width)
+    bups = bups.reshape(layers, 2, 2, count_dp, up_part).transpose(1, 2, 0, 3, 4)
+    bups = jnp.pad(bups, ((0, 0),) * 4 + ((0, block - up_part),)).reshape(2, 2 * layers, width)
+    by_hidden = jnp.concatenate([bups, bqv], axis=1).reshape(8 * layers, width)
+    by_hidden = lax.dot_general(
+        by_hidden,
+        to_relative.astype(f32),
+        (((1,), (0,)), ((), ())),
+        precision=lax.Precision.HIGHEST,
+        preferred_element_type=f32,
+    ).reshape(2, 4 * layers, width)
     one = jnp.stack(gains_one)
     by_width = jnp.stack(
         [
@@ -810,43 +879,32 @@
             jnp.stack([sums[:, 3], sums[:, 0]], axis=1),
         ]
     ).reshape(6 * layers, width)
-    by_hidden = [
-        jnp.concatenate(
-            [
-                bups[:, 2 * i : 2 * i + 2].reshape(2 * layers, hidden),
-                jnp.pad(bqv[:, :, i].reshape(2 * layers, wide), ((0, 0), (0, hidden - wide))),
-            ]
-        )
-        for i in range(2)
-    ]
-    (got,) = advance([folding], exchange(by_hidden[1], "tensor", 2))
-    by_hidden = by_hidden[0] + got
-    parts = by_hidden[: 2 * layers].reshape(layers, 2, hidden)
-    gradient, by_width, *folding.attn, folding.feed = together(
-        gradient, by_width, *folding.attn, folding.feed
-    )
-    got = advance(
-        [folding], exchange(by_width, "tensor", 2), exchange(parts[:, 1], "tensor", 1)
-    )
-    by_width = by_width + got[0]
-    by_hidden = jnp.concatenate([parts[:, 0] + got[1], by_hidden[2 * layers :]])
-    got = exchange(by_width, "tensor", 1)
+    small = [jnp.concatenate([by_width, by_hidden[i]]) for i in range(2)]
+    advance([folding])
+    gradient, *small, folding.attn, folding.feed = together(
+        gradient, *small, folding.attn, folding.feed
+    )
+    half = give_half(gradient)
+    small = small[0] + exchange(small[1], "tensor", 2)
+    cut = 6 * layers
+    got = exchange(
+        jnp.concatenate([small[:cut], small[cut + layers : cut + 2 * layers]]), "tensor", 1
+    )
+    small = jnp.concatenate(
+        [small[: cut + layers] + got[: cut + layers], small[cut + 2 * layers :]]
+    )
+    half, small = advance([folding], half, small)
+    frames_grad = give_clip(gradient, half)
     for mask in reversed(dp_masks()):
-        if folding.step < 4:
-            got, more = advance([folding], got, exchange(by_hidden, "dp", mask))
-        else:
-            got, more = together(got, exchange(by_hidden, "dp", mask))
-        by_hidden = by_hidden + more
-        by_width = by_width + got if mask == 1 else by_width[:, : by_width.shape[1] // 2] + got
-        got = exchange(by_width[:, by_width.shape[1] // 2 :], "dp", mask)
-    by_width = by_width[:, : by_width.shape[1] // 2] + got
+        got = exchange(small[:, small.shape[1] // 2 :], "dp", mask)
+        if folding.step < 3:
+            (got,) = advance([folding], got)
+        small = small[:, : small.shape[1] // 2] + got
     weight_grads[0] = folding.result()
-    frames_grad = give_clip(gradient)
-    by_width = lax.dynamic_slice(by_width, (0, t_me * norm_part), (6 * layers, norm_part))
+    by_width = lax.dynamic_slice(small, (0, t_me * norm_part), (cut, norm_part))
     gains, shifts, obiases = by_width.reshape(3, layers, 2, norm_part)
-    bups = lax.dynamic_slice(by_hidden, (0, me * up_part), (layers, up_part))
-    bqv = lax.dynamic_slice(by_hidden, (layers, me * qv_part), (2 * layers, qv_part))
-    bqv = bqv.reshape(layers, 2, qv_part)
+    bups = small[cut : cut + layers, :up_part]
+    bqv = small[cut + layers :, :qv_part].reshape(layers, 2, qv_part)
 
     def stacked(make):
         return jnp.stack([make(*weight_grads[at]) for at in range(layers)])

time: 708 us -> 657 us (0.928)
  Pallas kernels: 329 us -> 298 us
  waiting for transfers between devices: 102 us -> 78.9 us
  other arithmetic: 74.6 us -> 81.7 us
    ppermute x88 -> x81, waiting for transfers between devices: 102 us -> 78.9 us  [exchange(): return lax.ppermute(value, axis, [(i, i ^ mask) for i in range(count)])]
    pallas_call x4, Pallas kernels: 141 us -> 123 us  [attend_back(): pl.pallas_call(functools.partial(attend_back_kernel, row_count, quarter,...]
    pallas_call x4, Pallas kernels: 85.8 us -> 73.1 us  [attend(): pl.pallas_call(functools.partial(attend_kernel, row_count, quarter, min(5...]
    convert_element_type x24 -> x22, other arithmetic: 25.3 us -> 30 us  [add_low(): return (kept.astype(f32) + received.astype(f32)).astype(bf16)]
    unnamed x213 -> x255, local copies, waits for them, and re-layouts: 25.4 us -> 21.4 us
    ppermute x88 -> x81, starting transfers between devices: 81.1 us -> 80.8 us  [exchange(): return lax.ppermute(value, axis, [(i, i ^ mask) for i in range(count)])]
  transfers between devices with their start and end apart: 88 -> 81, of which waited for: 25 -> 25; matrix products, arithmetic and copies ran while one was open for 18% -> 20% of each run, Pallas kernels for 40% -> 43%
where the time goes in v5:
time: 657 us; the launch traced here: 649 us
  Pallas kernels  298 us (45%)
  other arithmetic  81.7 us (12%)
  starting transfers between devices  80.8 us (12%)
  waiting for transfers between devices  78.9 us (12%)
  local copies, waits for them, and re-layouts  76.3 us (12%)
  matrix products  29.6 us (5%)
    pallas_call x4, Pallas kernels, attend_back(): pl.pallas_call(functools.partial(attend_back_kernel, row_count, quarter,...  123 us
    ppermute x81, starting transfers between devices, exchange(): return lax.ppermute(value, axis, [(i, i ^ mask) for i in range(count)])  80.8 us
    ppermute x81, waiting for transfers between devices, exchange(): return lax.ppermute(value, axis, [(i, i ^ mask) for i in range(count)])  78.9 us
    pallas_call x4, Pallas kernels, attend(): pl.pallas_call(functools.partial(attend_kernel, row_count, quarter, min(5...  73.1 us
    pallas_call x2, Pallas kernels, feed_back(): pl.pallas_call(functools.partial(feed_back_kernel, final), grid=(hidden /...  64.1 us
    pallas_call x2, Pallas kernels, feed(): pl.pallas_call(functools.partial(feed_kernel, final), grid=(hidden // ste...  37.8 us
    convert_element_type x22, other arithmetic, add_low(): return (kept.astype(f32) + received.astype(f32)).astype(bf16)  30 us
    unnamed x255, local copies, waits for them, and re-layouts  21.4 us
  transfers between devices with their start and end apart: 81, of which 25 were waited for; matrix products, arithmetic and copies ran while one was open for 20% of the time, Pallas kernels for 43%

profile of v5, /device:TPU:0, one launch (start us, length us, event | category | flops | bytes accessed | tf_op | source)
XLA Modules:
  0.0 648.8 jit_solution(12653169119719198943)
XLA Ops:
  5.5 3.6 collective-permute-start
  11.9 2.1 collective-permute-done.2
  16.9 2.8 collective-permute-start.5
  22.0 4.5 collective-permute-start.7
  27.4 2.9 collective-permute-done.6
  33.4 2.6 collective-permute-start.10
  40.4 2.7 fusion.76
  43.1 2.0 copy.38.refs_0_
  45.6 2.6 collective-permute-done.10
  53.2 2.1 pad_maximum_fusion.21
  63.4 1.8 slice_bitcast_fusion.19
  65.2 6.3 collective-permute-done.13.refs_2_.refs_8_
  77.0 2.0 collective-permute-start.20
  79.0 1.8 slice_bitcast_fusion.18
  81.7 17.3 %shard_map.194 = (bf16[1536,576]{1,0:T(8,128)(2,1)}, bf16[1536,192]{1,0:T(8,128)(2,1)}, f32[1536,8]{1,0:T(8,128)}) custom-call(bf16[768,768]{1,0:T(8,128)(2,1)} %copy-done.13, bf16[768,768]{1,0:T(8,128)(2,1)} %copy-done.28, bf16[768,384]{1,0:T(8,128)(2,1)} %copy-done.25, bf16[768,384]{1,0:T(8,128)(2,1)} %pad_maximum_fusion.23.refs_3_.refs_6_, ...), custom_call_target="tpu_custom_call" | custom-call | tf_op jit(solution)/shard_map/pallas_call | solution.py:365
  106.6 19.2 %shard_map.195 = (f32[768,768]{1,0:T(8,128)}, bf16[768,768]{1,0:T(8,128)(2,1)}, bf16[1536,576]{1,0:T(8,128)(2,1)}, bf16[1536,192]{1,0:T(8,128)(2,1)}, f32[1536,8]{1,0:T(8,128)}) custom-call(bf16[768,768]{1,0:T(8,128)(2,1)} %copy-done.13, bf16[768,768]{1,0:T(8,128)(2,1)} %copy-done.28, bf16[768,384]{1,0:T(8,128)(2,1)} %copy-done.23, ...), custom_call_target="tpu_custom_call" | custom-call | tf_op jit(solution)/shard_map/pallas_call | solution.py:365
  125.9 2.2 collective-permute-done.21.refs_7_.refs_9_
  132.3 2.1 fusion.70
  145.3 19.8 %shard_map.196 = (bf16[768,768]{1,0:T(8,128)(2,1)}, bf16[768,768]{1,0:T(8,128)(2,1)}, bf16[768,768]{1,0:T(8,128)(2,1)}, bf16[768,768]{1,0:T(8,128)(2,1)}, bf16[7...) custom-call(f32[768,768]{1,0:T(8,128)} %copy-done, ...), custom_call_target="tpu_custom_call" | custom-call | tf_op jit(solution)/shard_map/pallas_call | solution.py:537
  170.2 10.5 %collective-permute-done.33.refs_2_.refs_8_ = bf16[768,384]{1,0:T(8,128)(2,1)S(1)} collective-permute-done((bf16[768,384]{1,0:T(8,128)(2,1)S(1)}, bf16[768,384]{1,0:T(8,128)(2,1)S(1)}, u32[]{:S(2)}, u32[]{:S(2)}) %collective-permute-start.33) | collective-permute-done | bytes 589856 | tf_op jit(solution)/shard_map/ppermute | solution.py:23
  188.0 17.2 %shard_map.197 = (bf16[1536,576]{1,0:T(8,128)(2,1)}, bf16[1536,192]{1,0:T(8,128)(2,1)}, f32[1536,8]{1,0:T(8,128)}) custom-call(bf16[768,768]{1,0:T(8,128)(2,1)} %get-tuple-element.347.refs_0_, bf16[768,768]{1,0:T(8,128)(2,1)} %copy-done.18, bf16[768,384]{1,0:T(8,128)(2,1)} %copy-done.26, bf16[768,384]{1,0:T(8,128)(2,1)} %pad_maximum_fusion.28.refs_3_.refs_6_, ...), custom_call_target="tpu_custom_call" | custom-call | tf_op jit(solution)/shard_map/pallas_call | solution.py:365
  206.4 1.8 pad_maximum_fusion.13
  211.0 19.3 %shard_map.198 = (f32[768,768]{1,0:T(8,128)}, bf16[768,768]{1,0:T(8,128)(2,1)}, bf16[1536,576]{1,0:T(8,128)(2,1)}, bf16[1536,192]{1,0:T(8,128)(2,1)}, f32[1536,8]{1,0:T(8,128)}) custom-call(bf16[768,768]{1,0:T(8,128)(2,1)} %get-tuple-element.347.refs_0_, bf16[768,768]{1,0:T(8,128)(2,1)} %copy-done.18, bf16[768,384]{1,0:T(8,128)(2,1)} %copy-done.24, ...), custom_call_target="tpu_custom_call" | custom-call | tf_op jit(solution)/shard_map/pallas_call | solution.py:365
  230.3 2.7 collective-permute-done.39.refs_7_.refs_6_
  237.7 2.2 collective-permute-done.44.refs_10_.refs_9_
  241.8 17.9 %shard_map.199 = (bf16[768,768]{1,0:T(8,128)(2,1)}, bf16[768,768]{1,0:T(8,128)(2,1)}, bf16[768,768]{1,0:T(8,128)(2,1)}, bf16[768,768]{1,0:T(8,128)(2,1)}, bf16[7...) custom-call(f32[768,768]{1,0:T(8,128)} %get-tuple-element.418.refs_0, ...), custom_call_target="tpu_custom_call" | custom-call | tf_op jit(solution)/shard_map/pallas_call | solution.py:537
  263.4 2.5 fusion.11.refs_0_
  265.9 30.3 %shard_map.200 = (bf16[4,768,768]{2,1,0:T(8,128)(2,1)}, bf16[4,768,768]{2,1,0:T(8,128)(2,1)}, f32[4,768]{1,0:T(4,128)}, f32[768,768]{1,0:T(8,128)}, bf16[768,768]{1,0:T(8,128)(2,1)}, /*index=5*/f32[8,768]{1,0:T(8,128)}) custom-call(f32[768,768]{1,0:T(8,128)} %fusion.11.refs_0_, f32[768,768]{1,0:T(8,128)} %get-tuple-element.361.refs_1_, ...), custom_call_target="tpu_custom_call" | custom-call | tf_op jit(solution)/shard_map/pallas_call | solution.py:609
  296.8 7.6 %collective-permute-done.47 = bf16[4,768,768]{2,1,0:T(8,128)(2,1)S(1)} collective-permute-done((bf16[4,768,768]{2,1,0:T(8,128)(2,1)}, bf16[4,768,768]{2,1,0:T(8,128)(2,1)S(1)}, u32[]{:S(2)}, u32[]{:S(2)}) %collective-permute-start.47) | collective-permute-done | bytes 4718624 | tf_op jit(solution)/shard_map/ppermute | solution.py:23
  304.4 2.4 add_convert_fusion.5
  306.8 2.7 fusion.19
  318.7 28.4 %shard_map.201.refs_7_ = bf16[1536,576]{1,0:T(8,128)(2,1)} custom-call(bf16[768,768]{1,0:T(8,128)(2,1)} %get-tuple-element.399.refs_0_, bf16[768,768]{1,0:T(8,128)(2,1)} %copy-done.12, bf16[768,384]{1,0:T(8,128)(2,1)} %copy-done.24, bf16[768,384]{1,0:T(8,128)(2,1)} %pad_maximum_fusion.29.refs_3_.refs_9_, bf16[1536,576]{1,0:T(8,128)(2,1)} %get-tuple-element.391.refs_4_, ...), custom_call_target="tpu_custom_call" | custom-call | tf_op jit(solution)/shard_map/pallas_call | solution.py:454
  347.1 2.4 add_convert_fusion.4
  349.5 2.8 fusion.5
  356.3 3.3 convolution_convert_fusion
  359.7 33.2 %shard_map.202 = (f32[768,768]{1,0:T(8,128)}, bf16[768,768]{1,0:T(8,128)(2,1)}, bf16[1536,576]{1,0:T(8,128)(2,1)}) custom-call(bf16[768,768]{1,0:T(8,128)(2,1)} %get-tuple-element.399.refs_0_, bf16[768,768]{1,0:T(8,128)(2,1)} %copy-done.12, bf16[768,384]{1,0:T(8,128)(2,1)} %copy-done.26, bf16[768,384]{1,0:T(8,128)(2,1)} %pad_maximum_fusion.28.refs_3_.refs_6_, ...), custom_call_target="tpu_custom_call" | custom-call | tf_op jit(solution)/shard_map/pallas_call | solution.py:454
  397.4 3.3 convolution_convert_fusion.1
  408.7 33.8 %shard_map.203 = (bf16[4,768,768]{2,1,0:T(8,128)(2,1)}, bf16[4,768,768]{2,1,0:T(8,128)(2,1)}, f32[4,768]{1,0:T(4,128)}, f32[768,768]{1,0:T(8,128)}, bf16[768,768]{1,0:T(8,128)(2,1)}, /*index=5*/f32[8,768]{1,0:T(8,128)}) custom-call(f32[768,768]{1,0:T(8,128)} %get-tuple-element.417.refs_0_, f32[768,768]{1,0:T(8,128)} %get-tuple-element.418.refs_0_.refs_1_, ...), custom_call_target="tpu_custom_call" | custom-call | tf_op jit(solution)/shard_map/pallas_call | solution.py:609
  443.3 2.1 fusion.13
  447.6 1.8 select_bitcast_fusion.3
  449.7 2.6 copy.49
  453.3 1.9 convert_reduce_fusion.1
  460.0 2.3 add_convert_fusion.11
  465.8 2.9 add_convert_fusion.2
  468.7 3.0 fusion.20
  476.8 2.7 collective-permute-start.62
  481.7 28.6 %shard_map.204.refs_7_ = bf16[1536,576]{1,0:T(8,128)(2,1)} custom-call(bf16[768,768]{1,0:T(8,128)(2,1)} %get-tuple-element.465.refs_0_, bf16[768,768]{1,0:T(8,128)(2,1)} %copy-done.8, bf16[768,384]{1,0:T(8,128)(2,1)} %copy-done.23, bf16[768,384]{1,0:T(8,128)(2,1)} %pad_maximum_fusion.24.refs_3_.refs_9_, bf16[1536,576]{1,0:T(8,128)(2,1)} %get-tuple-element.451.refs_4_, ...), custom_call_target="tpu_custom_call" | custom-call | tf_op jit(solution)/shard_map/pallas_call | solution.py:454
  510.3 3.6 fusion.17
  513.9 1.8 add_convert_fusion.17
  520.2 2.4 add_convert_fusion.1
  522.6 2.8 fusion.4
  531.3 33.3 %shard_map.205 = (f32[768,768]{1,0:T(8,128)}, bf16[768,768]{1,0:T(8,128)(2,1)}, bf16[1536,576]{1,0:T(8,128)(2,1)}) custom-call(bf16[768,768]{1,0:T(8,128)(2,1)} %get-tuple-element.465.refs_0_, bf16[768,768]{1,0:T(8,128)(2,1)} %copy-done.8, bf16[768,384]{1,0:T(8,128)(2,1)} %copy-done.25, bf16[768,384]{1,0:T(8,128)(2,1)} %pad_maximum_fusion.23.refs_3_.refs_6_, ...), custom_call_target="tpu_custom_call" | custom-call | tf_op jit(solution)/shard_map/pallas_call | solution.py:454
  564.6 1.8 slice_bitcast_fusion.22
  582.6 8.0 %collective-permute-done.78 = bf16[96,768]{0,1:T(8,128)(2,1)S(1)} collective-permute-done((bf16[96,768]{0,1:T(8,128)(2,1)S(1)}, bf16[96,768]{0,1:T(8,128)(2,1)S(1)}, u32[]{:S(2)}, u32[]{:S(2)}) %collective-permute-start.78) | collective-permute-done | bytes 147488 | tf_op jit(solution)/shard_map/ppermute | solution.py:23
  592.1 2.1 add_convert_fusion.9
  594.1 2.2 add_convert_fusion.8
  597.9 3.5 multiply_add_fusion
  604.3 2.3 collective-permute-done.74
  607.8 2.9 collective-permute-start.71
  611.5 15.1 %collective-permute-done.71 = bf16[192,768]{0,1:T(8,128)(2,1)S(1)} collective-permute-done((bf16[192,768]{0,1:T(8,128)(2,1)S(1)}, bf16[192,768]{0,1:T(8,128)(2,1)S(1)}, u32[]{:S(2)}, u32[]{:S(2)}) %collective-permute-start.71) | collective-permute-done | bytes 294944 | tf_op jit(solution)/shard_map/ppermute | solution.py:23
  626.9 2.7 collective-permute-start.76
  632.0 2.6 copy.50
  634.6 4.1 collective-permute-done.76
  645.3 1.9 collective-permute-done.80
  (610 shorter events, 179.8 us)
Async XLA Ops:
  5.5 11.3 %collective-permute-start = (bf16[96,768]{1,0:T(8,128)(2,1)S(1)}, bf16[96,768]{1,0:T(8,128)(2,1)S(1)}, u32[]{:S(2)}, u32[]{:S(2)}) collective-permute-start(bf16[96,768]{1,0:T(8,128)(2,1)S(1)} %pad_maximum_fusion.36), channel_id=1, source_target_pairs={{0,16},{4,20},{8,24},{12,28},{16,0},{20,4},{24,8},{28,12},{1,17},{... | collective-permute-start | bytes 442376 | tf_op jit(solution)/shard_map/ppermute | solution.py:23
  14.2 24.6 %collective-permute-start.16 = (bf16[375,768]{1,0:T(8,128)(2,1)S(1)}, bf16[375,768]{1,0:T(8,128)(2,1)S(1)}, u32[]{:S(2)}, u32[]{:S(2)}) collective-permute-start(bf16[375,768]{1,0:T(8,128)(2,1)S(1)} %get-tuple-element.550), channel_id=1, source_target_pairs={{0,2},{1,3},{2,0},{3,1},{4,6},{5,7},{6,4},{7,5},{8,10},{9,11},{10,... | collective-permute-start | bytes 1728008 | tf_op jit(solution)/shard_map/ppermute | solution.py:23
  19.8 10.6 %collective-permute-start.3 = (bf16[192,768]{1,0:T(8,128)(2,1)S(1)}, bf16[192,768]{1,0:T(8,128)(2,1)S(1)}, u32[]{:S(2)}, u32[]{:S(2)}) collective-permute-start(bf16[192,768]{1,0:T(8,128)(2,1)S(1)} %pad_maximum_fusion.32), channel_id=1, source_target_pairs={{0,8},{4,12},{8,0},{12,4},{16,24},{20,28},{24,16},{28,20},{1,9},{5... | collective-permute-start | bytes 884744 | tf_op jit(solution)/shard_map/ppermute | solution.py:23
  22.0 8.3 %collective-permute-start.7 = (f32[16,768]{1,0:T(8,128)S(1)}, f32[16,768]{1,0:T(8,128)S(1)}, u32[]{:S(2)}, u32[]{:S(2)}) collective-permute-start(f32[16,768]{1,0:T(8,128)S(1)} %add.212), channel_id=1, source_target_pairs={{0,8},{4,12},{8,0},{12,4},{16,24},{20,28},{24,16},{28,20},{1,9},{5... | collective-permute-start | bytes 147464 | tf_op jit(solution)/shard_map/ppermute | solution.py:23
  31.0 14.5 %collective-permute-start.11 = (f32[12,384]{1,0:T(8,128)}, f32[12,384]{1,0:T(8,128)}, u32[]{:S(2)}, u32[]{:S(2)}) collective-permute-start(f32[12,384]{1,0:T(8,128)} %pad_maximum_fusion.44), channel_id=1, source_target_pairs={{0,4},{4,0},{8,12},{12,8},{16,20},{20,16},{24,28},{28,24},{1,5},{5... | collective-permute-start | bytes 55304 | tf_op jit(solution)/shard_map/ppermute | solution.py:23
  33.4 14.8 %collective-permute-start.10 = (bf16[96,1536]{1,0:T(8,128)(2,1)S(1)}, bf16[96,1536]{1,0:T(8,128)(2,1)S(1)}, u32[]{:S(2)}, u32[]{:S(2)}) collective-permute-start(bf16[96,1536]{1,0:T(8,128)(2,1)S(1)} %get-tuple-element.267), channel_id=1, source_target_pairs={{0,16},{4,20},{8,24},{12,28},{16,0},{20,4},{24,8},{28,12},{1,17},{... | collective-permute-start | bytes 884744 | tf_op jit(solution)/shard_map/ppermute | solution.py:23
  36.0 12.1 %collective-permute-start.8 = (bf16[384,384]{1,0:T(8,128)(2,1)}, bf16[384,384]{1,0:T(8,128)(2,1)}, u32[]{:S(2)}, u32[]{:S(2)}) collective-permute-start(bf16[384,384]{1,0:T(8,128)(2,1)} %get-tuple-element.265), channel_id=1, source_target_pairs={{0,4},{4,0},{8,12},{12,8},{16,20},{20,16},{24,28},{28,24},{1,5},{5... | collective-permute-start | bytes 884744 | tf_op jit(solution)/shard_map/ppermute | solution.py:23
  36.6 11.6 %collective-permute-start.9 = (bf16[384,384]{1,0:T(8,128)(2,1)}, bf16[384,384]{1,0:T(8,128)(2,1)}, u32[]{:S(2)}, u32[]{:S(2)}) collective-permute-start(bf16[384,384]{1,0:T(8,128)(2,1)} %get-tuple-element.266), channel_id=1, source_target_pairs={{0,2},{1,3},{2,0},{3,1},{4,6},{5,7},{6,4},{7,5},{8,10},{9,11},{10,... | collective-permute-start | bytes 884744 | tf_op jit(solution)/shard_map/ppermute | solution.py:23
  51.6 21.8 %collective-permute-start.17 = (bf16[768,768]{1,0:T(8,128)(2,1)S(1)}, bf16[768,768]{1,0:T(8,128)(2,1)S(1)}, u32[]{:S(2)}, u32[]{:S(2)}) collective-permute-start(bf16[768,768]{1,0:T(8,128)(2,1)S(1)} %add_convert_fusion.7.refs_0_), channel_id=1, source_target_pairs={{0,1},{1,0},{2,3},{3,2},{4,5},{5,4},{6,7},{7,6},{8,9},{9,8},{10,11... | collective-permute-start | bytes 3538952 | tf_op jit(solution)/shard_map/ppermute | solution.py:23
  56.2 15.3 %collective-permute-start.13 = (bf16[768,384]{1,0:T(8,128)(2,1)S(1)}, bf16[768,384]{1,0:T(8,128)(2,1)S(1)}, u32[]{:S(2)}, u32[]{:S(2)}) collective-permute-start(bf16[768,384]{1,0:T(8,128)(2,1)S(1)} %pad_maximum_fusion.20.refs_2_), channel_id=1, source_target_pairs={{0,2},{1,3},{2,0},{3,1},{4,6},{5,7},{6,4},{7,5},{8,10},{9,11},{10,... | collective-permute-start | bytes 1769480 | tf_op jit(solution)/shard_map/ppermute | solution.py:23
  57.8 15.3 %collective-permute-start.14 = (bf16[2,384,384]{2,1,0:T(8,128)(2,1)}, bf16[2,384,384]{2,1,0:T(8,128)(2,1)}, u32[]{:S(2)}, u32[]{:S(2)}) collective-permute-start(bf16[2,384,384]{2,1,0:T(8,128)(2,1)} %pad_maximum_fusion.21), channel_id=1, source_target_pairs={{0,4},{4,0},{8,12},{12,8},{16,20},{20,16},{24,28},{28,24},{1,5},{5... | collective-permute-start | bytes 1769480 | tf_op jit(solution)/shard_map/ppermute | solution.py:23
  58.3 15.1 %collective-permute-start.15 = (bf16[192,1536]{1,0:T(8,128)(2,1)}, bf16[192,1536]{1,0:T(8,128)(2,1)}, u32[]{:S(2)}, u32[]{:S(2)}) collective-permute-start(bf16[192,1536]{1,0:T(8,128)(2,1)} %pad_maximum_fusion.22), channel_id=1, source_target_pairs={{0,8},{4,12},{8,0},{12,4},{16,24},{20,28},{24,16},{28,20},{1,9},{5... | collective-permute-start | bytes 1769480 | tf_op jit(solution)/shard_map/ppermute | solution.py:23
  75.0 24.1 %collective-permute-start.18 = (bf16[384,768]{1,0:T(8,128)(2,1)S(1)}, bf16[384,768]{1,0:T(8,128)(2,1)}, u32[]{:S(2)}, u32[]{:S(2)}) collective-permute-start(bf16[384,768]{1,0:T(8,128)(2,1)S(1)} %get-tuple-element.279), channel_id=1, source_target_pairs={{0,4},{4,0},{8,12},{12,8},{16,20},{20,16},{24,28},{28,24},{1,5},{5... | collective-permute-start | bytes 1769480 | tf_op jit(solution)/shard_map/ppermute | solution.py:23
  76.5 22.6 %collective-permute-start.19 = (bf16[384,768]{1,0:T(8,128)(2,1)S(1)}, bf16[384,768]{1,0:T(8,128)(2,1)}, u32[]{:S(2)}, u32[]{:S(2)}) collective-permute-start(bf16[384,768]{1,0:T(8,128)(2,1)S(1)} %get-tuple-element.280), channel_id=1, source_target_pairs={{0,2},{1,3},{2,0},{3,1},{4,6},{5,7},{6,4},{7,5},{8,10},{9,11},{10,... | collective-permute-start | bytes 1769480 | tf_op jit(solution)/shard_map/ppermute | solution.py:23
  77.0 22.1 %collective-permute-start.20 = (bf16[96,768]{1,0:T(8,128)(2,1)S(1)}, bf16[96,768]{1,0:T(8,128)(2,1)S(1)}, u32[]{:S(2)}, u32[]{:S(2)}) collective-permute-start(bf16[96,768]{1,0:T(8,128)(2,1)S(1)} %copy-done.76), channel_id=1, source_target_pairs={{0,16},{4,20},{8,24},{12,28},{16,0},{20,4},{24,8},{28,12},{1,17},{... | collective-permute-start | bytes 442376 | tf_op jit(solution)/shard_map/ppermute | solution.py:23
  102.1 26.1 %collective-permute-start.21 = (bf16[768,768]{1,0:T(8,128)(2,1)S(1)}, bf16[768,768]{1,0:T(8,128)(2,1)}, u32[]{:S(2)}, u32[]{:S(2)}) collective-permute-start(bf16[768,768]{1,0:T(8,128)(2,1)S(1)} %constant_dynamic-update-slice_fusion.2.refs_5_.refs_7_), channel_id=1, source_target_pairs={{0,2},{1,3},{2,0},{3,1},{4,6},{5,7},{6,4},{7,5},{8,10},{9,11},{10,... | collective-permute-start | bytes 3538952 | tf_op jit(solution)/shard_map/ppermute | solution.py:23
  103.4 25.8 %collective-permute-start.22 = (bf16[2,384,768]{2,1,0:T(8,128)(2,1)S(1)}, bf16[2,384,768]{2,1,0:T(8,128)(2,1)}, u32[]{:S(2)}, u32[]{:S(2)}) collective-permute-start(bf16[2,384,768]{2,1,0:T(8,128)(2,1)S(1)} %pad_maximum_fusion.10), channel_id=1, source_target_pairs={{0,4},{4,0},{8,12},{12,8},{16,20},{20,16},{24,28},{28,24},{1,5},{5... | collective-permute-start | bytes 3538952 | tf_op jit(solution)/shard_map/ppermute | solution.py:23
  103.9 22.0 %collective-permute-start.23 = (bf16[192,768]{1,0:T(8,128)(2,1)S(1)}, bf16[192,768]{1,0:T(8,128)(2,1)S(1)}, u32[]{:S(2)}, u32[]{:S(2)}) collective-permute-start(bf16[192,768]{1,0:T(8,128)(2,1)S(1)} %copy-done.70), channel_id=1, source_target_pairs={{0,8},{4,12},{8,0},{12,4},{16,24},{20,28},{24,16},{28,20},{1,9},{5... | collective-permute-start | bytes 884744 | tf_op jit(solution)/shard_map/ppermute | solution.py:23
  106.6 32.3 %collective-permute-start.28 = (bf16[768,768]{1,0:T(8,128)(2,1)S(1)}, bf16[768,768]{1,0:T(8,128)(2,1)}, u32[]{:S(2)}, u32[]{:S(2)}) collective-permute-start(bf16[768,768]{1,0:T(8,128)(2,1)S(1)} %constant_dynamic-update-slice_fusion.2.refs_5_.refs_7_), channel_id=1, source_target_pairs={{0,1},{1,0},{2,3},{3,2},{4,5},{5,4},{6,7},{7,6},{8,9},{9,8},{10,11... | collective-permute-start | bytes 3538952 | tf_op jit(solution)/shard_map/ppermute | solution.py:23
  130.6 9.2 %collective-permute-start.31 = (bf16[768,768]{1,0:T(8,128)(2,1)S(1)}, bf16[768,768]{1,0:T(8,128)(2,1)}, u32[]{:S(2)}, u32[]{:S(2)}) collective-permute-start(bf16[768,768]{1,0:T(8,128)(2,1)S(1)} %pad_maximum_fusion.12.refs_11_.refs_13_), channel_id=1, source_target_pairs={{0,1},{1,0},{2,3},{3,2},{4,5},{5,4},{6,7},{7,6},{8,9},{9,8},{10,11... | collective-permute-start | bytes 3538952 | tf_op jit(solution)/shard_map/ppermute | solution.py:23
  131.6 8.9 %collective-permute-start.30 = (bf16[768,768]{1,0:T(8,128)(2,1)S(1)}, bf16[768,768]{1,0:T(8,128)(2,1)}, u32[]{:S(2)}, u32[]{:S(2)}) collective-permute-start(bf16[768,768]{1,0:T(8,128)(2,1)S(1)} %pad_maximum_fusion.11.refs_9_.refs_11_), channel_id=1, source_target_pairs={{0,1},{1,0},{2,3},{3,2},{4,5},{5,4},{6,7},{7,6},{8,9},{9,8},{10,11... | collective-permute-start | bytes 3538952 | tf_op jit(solution)/shard_map/ppermute | solution.py:23
  131.6 10.0 %collective-permute-start.27 = (bf16[768,768]{1,0:T(8,128)(2,1)}, bf16[768,768]{1,0:T(8,128)(2,1)}, u32[]{:S(2)}, u32[]{:S(2)}) collective-permute-start(bf16[768,768]{1,0:T(8,128)(2,1)} %get-tuple-element.310), channel_id=1, source_target_pairs={{0,1},{1,0},{2,3},{3,2},{4,5},{5,4},{6,7},{7,6},{8,9},{9,8},{10,11... | collective-permute-start | bytes 3538952 | tf_op jit(solution)/shard_map/ppermute | solution.py:23
  134.4 10.8 %collective-permute-start.29 = (bf16[768,768]{1,0:T(8,128)(2,1)}, bf16[768,768]{1,0:T(8,128)(2,1)}, u32[]{:S(2)}, u32[]{:S(2)}) collective-permute-start(bf16[768,768]{1,0:T(8,128)(2,1)} %collective-permute-done.21.refs_7_.refs_9_), channel_id=1, source_target_pairs={{0,1},{1,0},{2,3},{3,2},{4,5},{5,4},{6,7},{7,6},{8,9},{9,8},{10,11... | collective-permute-start | bytes 3538952 | tf_op jit(solution)/shard_map/ppermute | solution.py:23
  138.9 26.2 %collective-permute-start.32 = (bf16[375,768]{1,0:T(8,128)(2,1)}, bf16[375,768]{1,0:T(8,128)(2,1)S(1)}, u32[]{:S(2)}, u32[]{:S(2)}) collective-permute-start(bf16[375,768]{1,0:T(8,128)(2,1)} %get-tuple-element.536), channel_id=1, source_target_pairs={{0,2},{1,3},{2,0},{3,1},{4,6},{5,7},{6,4},{7,5},{8,10},{9,11},{10,... | collective-permute-start | bytes 1728008 | tf_op jit(solution)/shard_map/ppermute | solution.py:23
  139.8 25.4 %collective-permute-start.24 = (bf16[384,384]{1,0:T(8,128)(2,1)S(1)}, bf16[384,384]{1,0:T(8,128)(2,1)S(1)}, u32[]{:S(2)}, u32[]{:S(2)}) collective-permute-start(bf16[384,384]{1,0:T(8,128)(2,1)S(1)} %get-tuple-element.306), channel_id=1, source_target_pairs={{0,4},{4,0},{8,12},{12,8},{16,20},{20,16},{24,28},{28,24},{1,5},{5... | collective-permute-start | bytes 884744 | tf_op jit(solution)/shard_map/ppermute | solution.py:23
  140.5 24.7 %collective-permute-start.25 = (bf16[384,384]{1,0:T(8,128)(2,1)S(1)}, bf16[384,384]{1,0:T(8,128)(2,1)S(1)}, u32[]{:S(2)}, u32[]{:S(2)}) collective-permute-start(bf16[384,384]{1,0:T(8,128)(2,1)S(1)} %get-tuple-element.307), channel_id=1, source_target_pairs={{0,2},{1,3},{2,0},{3,1},{4,6},{5,7},{6,4},{7,5},{8,10},{9,11},{10,... | collective-permute-start | bytes 884744 | tf_op jit(solution)/shard_map/ppermute | solution.py:23
  141.7 23.5 %collective-permute-start.26 = (bf16[96,1536]{1,0:T(8,128)(2,1)}, bf16[96,1536]{1,0:T(8,128)(2,1)S(1)}, u32[]{:S(2)}, u32[]{:S(2)}) collective-permute-start(bf16[96,1536]{1,0:T(8,128)(2,1)} %get-tuple-element.308), channel_id=1, source_target_pairs={{0,16},{4,20},{8,24},{12,28},{16,0},{20,4},{24,8},{28,12},{1,17},{... | collective-permute-start | bytes 884744 | tf_op jit(solution)/shard_map/ppermute | solution.py:23
  166.6 14.2 %collective-permute-start.33 = (bf16[768,384]{1,0:T(8,128)(2,1)S(1)}, bf16[768,384]{1,0:T(8,128)(2,1)S(1)}, u32[]{:S(2)}, u32[]{:S(2)}) collective-permute-start(bf16[768,384]{1,0:T(8,128)(2,1)S(1)} %pad_maximum_fusion.25.refs_2_), channel_id=1, source_target_pairs={{0,2},{1,3},{2,0},{3,1},{4,6},{5,7},{6,4},{7,5},{8,10},{9,11},{10,... | collective-permute-start | bytes 1769480 | tf_op jit(solution)/shard_map/ppermute | solution.py:23
  167.3 13.9 %collective-permute-start.34 = (bf16[2,384,384]{2,1,0:T(8,128)(2,1)S(1)}, bf16[2,384,384]{2,1,0:T(8,128)(2,1)S(1)}, u32[]{:S(2)}, u32[]{:S(2)}) collective-permute-start(bf16[2,384,384]{2,1,0:T(8,128)(2,1)S(1)} %pad_maximum_fusion.26), channel_id=1, source_target_pairs={{0,4},{4,0},{8,12},{12,8},{16,20},{20,16},{24,28},{28,24},{1,5},{5... | collective-permute-start | bytes 1769480 | tf_op jit(solution)/shard_map/ppermute | solution.py:23
  168.5 13.6 %collective-permute-start.35 = (bf16[192,1536]{1,0:T(8,128)(2,1)S(1)}, bf16[192,1536]{1,0:T(8,128)(2,1)S(1)}, u32[]{:S(2)}, u32[]{:S(2)}) collective-permute-start(bf16[192,1536]{1,0:T(8,128)(2,1)S(1)} %pad_maximum_fusion.27), channel_id=1, source_target_pairs={{0,8},{4,12},{8,0},{12,4},{16,24},{20,28},{24,16},{28,20},{1,9},{5... | collective-permute-start | bytes 1769480 | tf_op jit(solution)/shard_map/ppermute | solution.py:23
  170.2 16.8 %collective-permute-start.38 = (bf16[768,768]{1,0:T(8,128)(2,1)S(1)}, bf16[768,768]{1,0:T(8,128)(2,1)S(1)}, u32[]{:S(2)}, u32[]{:S(2)}) collective-permute-start(bf16[768,768]{1,0:T(8,128)(2,1)S(1)} %copy-done.16), channel_id=1, source_target_pairs={{0,1},{1,0},{2,3},{3,2},{4,5},{5,4},{6,7},{7,6},{8,9},{9,8},{10,11... | collective-permute-start | bytes 3538952 | tf_op jit(solution)/shard_map/ppermute | solution.py:23
  183.0 22.2 %collective-permute-start.36 = (bf16[384,768]{1,0:T(8,128)(2,1)S(1)}, bf16[384,768]{1,0:T(8,128)(2,1)}, u32[]{:S(2)}, u32[]{:S(2)}) collective-permute-start(bf16[384,768]{1,0:T(8,128)(2,1)S(1)} %get-tuple-element.333), channel_id=1, source_target_pairs={{0,4},{4,0},{8,12},{12,8},{16,20},{20,16},{24,28},{28,24},{1,5},{5... | collective-permute-start | bytes 1769480 | tf_op jit(solution)/shard_map/ppermute | solution.py:23
  183.9 21.4 %collective-permute-start.37 = (bf16[384,768]{1,0:T(8,128)(2,1)}, bf16[384,768]{1,0:T(8,128)(2,1)}, u32[]{:S(2)}, u32[]{:S(2)}) collective-permute-start(bf16[384,768]{1,0:T(8,128)(2,1)} %get-tuple-element.334), channel_id=1, source_target_pairs={{0,2},{1,3},{2,0},{3,1},{4,6},{5,7},{6,4},{7,5},{8,10},{9,11},{10,... | collective-permute-start | bytes 1769480 | tf_op jit(solution)/shard_map/ppermute | solution.py:23
  208.1 24.9 %collective-permute-start.39 = (bf16[768,768]{1,0:T(8,128)(2,1)S(1)}, bf16[768,768]{1,0:T(8,128)(2,1)}, u32[]{:S(2)}, u32[]{:S(2)}) collective-permute-start(bf16[768,768]{1,0:T(8,128)(2,1)S(1)} %constant_dynamic-update-slice_fusion.10.refs_5_.refs_4_), channel_id=1, source_target_pairs={{0,2},{1,3},{2,0},{3,1},{4,6},{5,7},{6,4},{7,5},{8,10},{9,11},{10,... | collective-permute-start | bytes 3538952 | tf_op jit(solution)/shard_map/ppermute | solution.py:23
  208.9 24.4 %collective-permute-start.40 = (bf16[2,384,768]{2,1,0:T(8,128)(2,1)S(1)}, bf16[2,384,768]{2,1,0:T(8,128)(2,1)S(1)}, u32[]{:S(2)}, u32[]{:S(2)}) collective-permute-start(bf16[2,384,768]{2,1,0:T(8,128)(2,1)S(1)} %pad_maximum_fusion.13), channel_id=1, source_target_pairs={{0,4},{4,0},{8,12},{12,8},{16,20},{20,16},{24,28},{28,24},{1,5},{5... | collective-permute-start | bytes 3538952 | tf_op jit(solution)/shard_map/ppermute | solution.py:23
  211.0 26.7 %collective-permute-start.42 = (bf16[768,768]{1,0:T(8,128)(2,1)S(1)}, bf16[768,768]{1,0:T(8,128)(2,1)}, u32[]{:S(2)}, u32[]{:S(2)}) collective-permute-start(bf16[768,768]{1,0:T(8,128)(2,1)S(1)} %constant_dynamic-update-slice_fusion.10.refs_5_.refs_4_), channel_id=1, source_target_pairs={{0,1},{1,0},{2,3},{3,2},{4,5},{5,4},{6,7},{7,6},{8,9},{9,8},{10,11... | collective-permute-start | bytes 3538952 | tf_op jit(solution)/shard_map/ppermute | solution.py:23
  261.2 34.9 %collective-permute-start.46 = (bf16[384,768]{1,0:T(8,128)(2,1)S(1)}, bf16[384,768]{1,0:T(8,128)(2,1)S(1)}, u32[]{:S(2)}, u32[]{:S(2)}) collective-permute-start(bf16[384,768]{1,0:T(8,128)(2,1)S(1)} %slice.991), channel_id=1, source_target_pairs={{0,2},{1,3},{2,0},{3,1},{4,6},{5,7},{6,4},{7,5},{8,10},{9,11},{10,... | collective-permute-start | bytes 1769480 | tf_op jit(solution)/shard_map/ppermute | solution.py:23
  296.3 18.1 %collective-permute-start.50 = (bf16[768,768]{1,0:T(8,128)(2,1)}, bf16[768,768]{1,0:T(8,128)(2,1)S(1)}, u32[]{:S(2)}, u32[]{:S(2)}) collective-permute-start(bf16[768,768]{1,0:T(8,128)(2,1)} %get-tuple-element.399.refs_0_), channel_id=1, source_target_pairs={{0,1},{1,0},{2,3},{3,2},{4,5},{5,4},{6,7},{7,6},{8,9},{9,8},{10,11... | collective-permute-start | bytes 3538952 | tf_op jit(solution)/shard_map/ppermute | solution.py:23
  309.5 37.6 %collective-permute-start.48 = (bf16[768,768]{1,0:T(8,128)(2,1)}, bf16[768,768]{1,0:T(8,128)(2,1)}, u32[]{:S(2)}, u32[]{:S(2)}) collective-permute-start(bf16[768,768]{1,0:T(8,128)(2,1)} %fusion.19), channel_id=1, source_target_pairs={{0,2},{1,3},{2,0},{3,1},{4,6},{5,7},{6,4},{7,5},{8,10},{9,11},{10,... | collective-permute-start | bytes 3538952 | tf_op jit(solution)/shard_map/ppermute | solution.py:23
  310.2 36.9 %collective-permute-start.49 = (bf16[2,384,768]{2,1,0:T(8,128)(2,1)S(1)}, bf16[2,384,768]{2,1,0:T(8,128)(2,1)}, u32[]{:S(2)}, u32[]{:S(2)}) collective-permute-start(bf16[2,384,768]{2,1,0:T(8,128)(2,1)S(1)} %add_convert_fusion.5), channel_id=1, source_target_pairs={{0,4},{4,0},{8,12},{12,8},{16,20},{20,16},{24,28},{28,24},{1,5},{5... | collective-permute-start | bytes 3538952 | tf_op jit(solution)/shard_map/ppermute | solution.py:23
  353.3 40.8 %collective-permute-start.51 = (bf16[384,768]{1,0:T(8,128)(2,1)}, bf16[384,768]{1,0:T(8,128)(2,1)S(1)}, u32[]{:S(2)}, u32[]{:S(2)}) collective-permute-start(bf16[384,768]{1,0:T(8,128)(2,1)} %slice.623), channel_id=1, source_target_pairs={{0,4},{4,0},{8,12},{12,8},{16,20},{20,16},{24,28},{28,24},{1,5},{5... | collective-permute-start | bytes 1769480 | tf_op jit(solution)/shard_map/ppermute | solution.py:23
  355.0 39.1 %collective-permute-start.52 = (bf16[384,768]{1,0:T(8,128)(2,1)}, bf16[384,768]{1,0:T(8,128)(2,1)}, u32[]{:S(2)}, u32[]{:S(2)}) collective-permute-start(bf16[384,768]{1,0:T(8,128)(2,1)} %slice_bitcast_fusion.4), channel_id=1, source_target_pairs={{0,2},{1,3},{2,0},{3,1},{4,6},{5,7},{6,4},{7,5},{8,10},{9,11},{10,... | collective-permute-start | bytes 1769480 | tf_op jit(solution)/shard_map/ppermute | solution.py:23
  403.4 39.1 %collective-permute-start.55 = (bf16[192,1536]{1,0:T(8,128)(2,1)}, bf16[192,1536]{1,0:T(8,128)(2,1)}, u32[]{:S(2)}, u32[]{:S(2)}) collective-permute-start(bf16[192,1536]{1,0:T(8,128)(2,1)} %fusion.36), channel_id=1, source_target_pairs={{0,8},{4,12},{8,0},{12,4},{16,24},{20,28},{24,16},{28,20},{1,9},{5... | collective-permute-start | bytes 1769480 | tf_op jit(solution)/shard_map/ppermute | solution.py:23
  405.0 37.5 %collective-permute-start.53 = (bf16[768,384]{0,1:T(8,128)(2,1)}, bf16[768,384]{0,1:T(8,128)(2,1)S(1)}, u32[]{:S(2)}, u32[]{:S(2)}) collective-permute-start(bf16[768,384]{0,1:T(8,128)(2,1)} %slice_bitcast_fusion.3), channel_id=1, source_target_pairs={{0,2},{1,3},{2,0},{3,1},{4,6},{5,7},{6,4},{7,5},{8,10},{9,11},{10,... | collective-permute-start | bytes 1769480 | tf_op jit(solution)/shard_map/ppermute | solution.py:23
  406.6 35.9 %collective-permute-start.54 = (bf16[2,384,384]{1,2,0:T(8,128)(2,1)}, bf16[2,384,384]{1,2,0:T(8,128)(2,1)}, u32[]{:S(2)}, u32[]{:S(2)}) collective-permute-start(bf16[2,384,384]{1,2,0:T(8,128)(2,1)} %slice.632), channel_id=1, source_target_pairs={{0,4},{4,0},{8,12},{12,8},{16,20},{20,16},{24,28},{28,24},{1,5},{5... | collective-permute-start | bytes 1769480 | tf_op jit(solution)/shard_map/ppermute | solution.py:23
  442.5 23.3 %collective-permute-start.57 = (bf16[4,768,768]{2,1,0:T(8,128)(2,1)}, bf16[4,768,768]{2,1,0:T(8,128)(2,1)}, u32[]{:S(2)}, u32[]{:S(2)}) collective-permute-start(bf16[4,768,768]{2,1,0:T(8,128)(2,1)} %get-tuple-element.439), channel_id=1, source_target_pairs={{0,1},{1,0},{2,3},{3,2},{4,5},{5,4},{6,7},{7,6},{8,9},{9,8},{10,11... | collective-permute-start | bytes 14155784 | tf_op jit(solution)/shard_map/ppermute | solution.py:23
  462.3 14.4 %collective-permute-start.63 = (bf16[768,768]{1,0:T(8,128)(2,1)S(1)}, bf16[768,768]{1,0:T(8,128)(2,1)S(1)}, u32[]{:S(2)}, u32[]{:S(2)}) collective-permute-start(bf16[768,768]{1,0:T(8,128)(2,1)S(1)} %copy-done.7), channel_id=1, source_target_pairs={{0,1},{1,0},{2,3},{3,2},{4,5},{5,4},{6,7},{7,6},{8,9},{9,8},{10,11... | collective-permute-start | bytes 3538952 | tf_op jit(solution)/shard_map/ppermute | solution.py:23
  463.1 47.2 %collective-permute-start.60 = (bf16[384,384]{0,1:T(8,128)(2,1)}, bf16[384,384]{0,1:T(8,128)(2,1)}, u32[]{:S(2)}, u32[]{:S(2)}) collective-permute-start(bf16[384,384]{0,1:T(8,128)(2,1)} %slice.643), channel_id=1, source_target_pairs={{0,4},{4,0},{8,12},{12,8},{16,20},{20,16},{24,28},{28,24},{1,5},{5... | collective-permute-start | bytes 884744 | tf_op jit(solution)/shard_map/ppermute | solution.py:23
  464.4 45.8 %collective-permute-start.61 = (bf16[384,384]{0,1:T(8,128)(2,1)}, bf16[384,384]{0,1:T(8,128)(2,1)}, u32[]{:S(2)}, u32[]{:S(2)}) collective-permute-start(bf16[384,384]{0,1:T(8,128)(2,1)} %slice_bitcast_fusion.13), channel_id=1, source_target_pairs={{0,2},{1,3},{2,0},{3,1},{4,6},{5,7},{6,4},{7,5},{8,10},{9,11},{10,... | collective-permute-start | bytes 884744 | tf_op jit(solution)/shard_map/ppermute | solution.py:23
  471.7 38.6 %collective-permute-start.58 = (bf16[768,768]{1,0:T(8,128)(2,1)}, bf16[768,768]{1,0:T(8,128)(2,1)}, u32[]{:S(2)}, u32[]{:S(2)}) collective-permute-start(bf16[768,768]{1,0:T(8,128)(2,1)} %fusion.20), channel_id=1, source_target_pairs={{0,2},{1,3},{2,0},{3,1},{4,6},{5,7},{6,4},{7,5},{8,10},{9,11},{10,... | collective-permute-start | bytes 3538952 | tf_op jit(solution)/shard_map/ppermute | solution.py:23
  472.5 37.8 %collective-permute-start.59 = (bf16[2,384,768]{2,1,0:T(8,128)(2,1)}, bf16[2,384,768]{2,1,0:T(8,128)(2,1)}, u32[]{:S(2)}, u32[]{:S(2)}) collective-permute-start(bf16[2,384,768]{2,1,0:T(8,128)(2,1)} %add_convert_fusion.2), channel_id=1, source_target_pairs={{0,4},{4,0},{8,12},{12,8},{16,20},{20,16},{24,28},{28,24},{1,5},{5... | collective-permute-start | bytes 3538952 | tf_op jit(solution)/shard_map/ppermute | solution.py:23
  476.8 33.5 %collective-permute-start.62 = (bf16[96,1536]{1,0:T(8,128)(2,1)}, bf16[96,1536]{1,0:T(8,128)(2,1)}, u32[]{:S(2)}, u32[]{:S(2)}) collective-permute-start(bf16[96,1536]{1,0:T(8,128)(2,1)} %slice.645), channel_id=1, source_target_pairs={{0,16},{4,20},{8,24},{12,28},{16,0},{20,4},{24,8},{28,12},{1,17},{... | collective-permute-start | bytes 884744 | tf_op jit(solution)/shard_map/ppermute | solution.py:23
  518.9 47.5 %collective-permute-start.67 = (bf16[768,768]{0,1:T(8,128)(2,1)}, bf16[768,768]{0,1:T(8,128)(2,1)S(1)}, u32[]{:S(2)}, u32[]{:S(2)}) collective-permute-start(bf16[768,768]{0,1:T(8,128)(2,1)} %pad_maximum_fusion.18), channel_id=1, source_target_pairs={{0,2},{1,3},{2,0},{3,1},{4,6},{5,7},{6,4},{7,5},{8,10},{9,11},{10,... | collective-permute-start | bytes 3538952 | tf_op jit(solution)/shard_map/ppermute | solution.py:23
  526.4 40.1 %collective-permute-start.64 = (bf16[384,768]{1,0:T(8,128)(2,1)}, bf16[384,768]{1,0:T(8,128)(2,1)}, u32[]{:S(2)}, u32[]{:S(2)}) collective-permute-start(bf16[384,768]{1,0:T(8,128)(2,1)} %slice.648), channel_id=1, source_target_pairs={{0,4},{4,0},{8,12},{12,8},{16,20},{20,16},{24,28},{28,24},{1,5},{5... | collective-permute-start | bytes 1769480 | tf_op jit(solution)/shard_map/ppermute | solution.py:23
  527.9 38.5 %collective-permute-start.65 = (bf16[384,768]{1,0:T(8,128)(2,1)}, bf16[384,768]{1,0:T(8,128)(2,1)}, u32[]{:S(2)}, u32[]{:S(2)}) collective-permute-start(bf16[384,768]{1,0:T(8,128)(2,1)} %slice_bitcast_fusion.2), channel_id=1, source_target_pairs={{0,2},{1,3},{2,0},{3,1},{4,6},{5,7},{6,4},{7,5},{8,10},{9,11},{10,... | collective-permute-start | bytes 1769480 | tf_op jit(solution)/shard_map/ppermute | solution.py:23
  529.7 36.7 %collective-permute-start.66 = (bf16[192,768]{0,1:T(8,128)(2,1)}, bf16[192,768]{0,1:T(8,128)(2,1)}, u32[]{:S(2)}, u32[]{:S(2)}) collective-permute-start(bf16[192,768]{0,1:T(8,128)(2,1)} %slice.763), channel_id=1, source_target_pairs={{0,8},{4,12},{8,0},{12,4},{16,24},{20,28},{24,16},{28,20},{1,9},{5... | collective-permute-start | bytes 884744 | tf_op jit(solution)/shard_map/ppermute | solution.py:23
  573.9 18.1 %collective-permute-start.70 = (bf16[192,1536]{1,0:T(8,128)(2,1)}, bf16[192,1536]{1,0:T(8,128)(2,1)}, u32[]{:S(2)}, u32[]{:S(2)}) collective-permute-start(bf16[192,1536]{1,0:T(8,128)(2,1)} %fusion.35), channel_id=1, source_target_pairs={{0,8},{4,12},{8,0},{12,4},{16,24},{20,28},{24,16},{28,20},{1,9},{5... | collective-permute-start | bytes 1769480 | tf_op jit(solution)/shard_map/ppermute | solution.py:23
  576.6 15.4 %collective-permute-start.69 = (bf16[384,768]{0,1:T(8,128)(2,1)}, bf16[384,768]{0,1:T(8,128)(2,1)}, u32[]{:S(2)}, u32[]{:S(2)}) collective-permute-start(bf16[384,768]{0,1:T(8,128)(2,1)} %slice.769), channel_id=1, source_target_pairs={{0,4},{4,0},{8,12},{12,8},{16,20},{20,16},{24,28},{28,24},{1,5},{5... | collective-permute-start | bytes 1769480 | tf_op jit(solution)/shard_map/ppermute | solution.py:23
  578.3 18.0 %collective-permute-start.68 = (bf16[768,768]{1,0:T(8,128)(2,1)}, bf16[768,768]{1,0:T(8,128)(2,1)S(1)}, u32[]{:S(2)}, u32[]{:S(2)}) collective-permute-start(bf16[768,768]{1,0:T(8,128)(2,1)} %get-tuple-element.478), channel_id=1, source_target_pairs={{0,1},{1,0},{2,3},{3,2},{4,5},{5,4},{6,7},{7,6},{8,9},{9,8},{10,11... | collective-permute-start | bytes 3538952 | tf_op jit(solution)/shard_map/ppermute | solution.py:23
  579.6 10.9 %collective-permute-start.78 = (bf16[96,768]{0,1:T(8,128)(2,1)S(1)}, bf16[96,768]{0,1:T(8,128)(2,1)S(1)}, u32[]{:S(2)}, u32[]{:S(2)}) collective-permute-start(bf16[96,768]{0,1:T(8,128)(2,1)S(1)} %slice.784), channel_id=1, source_target_pairs={{0,16},{4,20},{8,24},{12,28},{16,0},{20,4},{24,8},{28,12},{1,17},{... | collective-permute-start | bytes 442376 | tf_op jit(solution)/shard_map/ppermute | solution.py:23
  603.4 23.2 %collective-permute-start.73 = (bf16[384,768]{1,0:T(8,128)(2,1)S(1)}, bf16[384,768]{1,0:T(8,128)(2,1)S(1)}, u32[]{:S(2)}, u32[]{:S(2)}) collective-permute-start(bf16[384,768]{1,0:T(8,128)(2,1)S(1)} %slice.990), channel_id=1, source_target_pairs={{0,2},{1,3},{2,0},{3,1},{4,6},{5,7},{6,4},{7,5},{8,10},{9,11},{10,... | collective-permute-start | bytes 1769480 | tf_op jit(solution)/shard_map/ppermute | solution.py:23
  607.8 18.7 %collective-permute-start.71 = (bf16[192,768]{0,1:T(8,128)(2,1)S(1)}, bf16[192,768]{0,1:T(8,128)(2,1)S(1)}, u32[]{:S(2)}, u32[]{:S(2)}) collective-permute-start(bf16[192,768]{0,1:T(8,128)(2,1)S(1)} %slice.673), channel_id=1, source_target_pairs={{0,8},{4,12},{8,0},{12,4},{16,24},{20,28},{24,16},{28,20},{1,9},{5... | collective-permute-start | bytes 884744 | tf_op jit(solution)/shard_map/ppermute | solution.py:23
  610.7 15.9 %collective-permute-start.72 = (bf16[96,1536]{1,0:T(8,128)(2,1)S(1)}, bf16[96,1536]{1,0:T(8,128)(2,1)S(1)}, u32[]{:S(2)}, u32[]{:S(2)}) collective-permute-start(bf16[96,1536]{1,0:T(8,128)(2,1)S(1)} %slice.674), channel_id=1, source_target_pairs={{0,16},{4,20},{8,24},{12,28},{16,0},{20,4},{24,8},{28,12},{1,17},{... | collective-permute-start | bytes 884744 | tf_op jit(solution)/shard_map/ppermute | solution.py:23
  626.9 11.8 %collective-permute-start.76 = (bf16[96,768]{0,1:T(8,128)(2,1)S(1)}, bf16[96,768]{0,1:T(8,128)(2,1)S(1)}, u32[]{:S(2)}, u32[]{:S(2)}) collective-permute-start(bf16[96,768]{0,1:T(8,128)(2,1)S(1)} %slice.684), channel_id=1, source_target_pairs={{0,16},{4,20},{8,24},{12,28},{16,0},{20,4},{24,8},{28,12},{1,17},{... | collective-permute-start | bytes 442376 | tf_op jit(solution)/shard_map/ppermute | solution.py:23
  (138 other events, 567.5 us)

commit v6 on v5

--- a/solution.py
+++ b/solution.py
@@ -57,15 +57,20 @@
         lambda state: (exchange(state[0], "dp", masks[-1]), exchange(state[1], "tensor", 2)),
         lambda state, got: (
             jnp.concatenate([state[0], got[0]], axis=0),
-            jnp.stack([state[1], got[1]]),
+            state[1],
+            got[1],
         ),
     )
     last = (
-        lambda state: (exchange(state[0], "tensor", 2), exchange(state[1], "dp", masks[-1])),
+        lambda state: (
+            exchange(state[0], "tensor", 2),
+            exchange(state[1], "dp", masks[-1]),
+            exchange(state[2], "dp", masks[-1]),
+        ),
         lambda state, got: (
             state[0],
             got[0],
-            *[jnp.concatenate([state[1][i], got[1][i]], axis=0) for i in range(2)],
+            *[jnp.concatenate([state[1 + i], got[1 + i]], axis=0) for i in range(2)],
         ),
     )
 
@@ -88,9 +93,11 @@
         self.plan = [[(0, step)] for step in made[0][1]]
         for at, (_, _, near) in enumerate(made):
             ahead = made[at + 1][1] if at + 1 < len(made) else []
-            for i in range(max(len(near), len(ahead))):
+            late = 1 if at % 2 == 0 and at > 0 else 0
+            for i in range(max(len(near), len(ahead) + late)):
                 stage = [(at, near[i])] if i < len(near) else []
-                self.plan.append(stage + ([(at + 1, ahead[i])] if i < len(ahead) else []))
+                j = i - late
+                self.plan.append(stage + ([(at + 1, ahead[j])] if 0 <= j < len(ahead) else []))
         self.ends = [
             max(i for i, stage in enumerate(self.plan) for g, _ in stage if g == at)
             for at in range(len(made))
@@ -161,58 +168,69 @@
     return add_low(value[: value.shape[0] // 2], got)
 
 
-class CoreFold:
-    def __init__(self, own, received):
-        half = own.shape[1] // 2
-        self.half = half
-        self.kept = (own[0], received[0], own[2:, :half], received[2:, :half])
-        self.state = together(
-            add_low(own[1], received[1]), add_low(own[2:, half:], received[2:, half:])
-        )
+class Folding:
+    def __init__(self, own, other):
+        masks = dp_masks()[-2::-1]
+        self.masks = masks[:-1], masks[-1:]
+        self.own, self.other = own, other
+        self.half = own.shape[1] // 2
+        self.attn = None
         self.step = 0
 
     def send(self):
-        return near_two(*self.state) if self.step else near_one(self.state)
+        step = self.step
+        if step == 0:
+            return (exchange(self.other, "tensor", 1),)
+        if step == 1:
+            return near_one(self.feed)
+        if step == 2:
+            got = near_two(*self.feed)
+            return got if self.attn is None else got + near_one(near_one_sent(*self.attn))
+        if step == 3:
+            self.feed, more = far(self.feed, self.masks[0])
+            return *near_two(*self.attn), more
+        self.attn, *got = far(self.attn, self.masks[step - 4])
+        if step == 4:
+            self.feed, more = far(self.feed, self.masks[1])
+            got.append(more)
+        return got
 
     def finish(self, got):
-        if self.step:
-            self.state = near_two_sum(*self.state, got)
-        else:
+        step, half = self.step, self.half
+        self.step += 1
+        if step == 0:
+            own, other = self.own, got[0]
+            self.kept = (own[0], other[0], own[2:, :half], other[2:, :half])
+            self.feed = together(
+                add_low(own[1], other[1]), add_low(own[2:, half:], other[2:, half:])
+            )
+        elif step == 1:
             first = self.kept[0].astype(f32) + self.kept[1].astype(f32) + got[0].astype(f32)
             second = self.kept[2].astype(f32) + self.kept[3].astype(f32) + got[1].astype(f32)
-            self.state = together(first.astype(bf16), second.astype(bf16))
-        self.step += 1
-
-
-class Folding:
-    def __init__(self, qk, vo, up, down):
-        masks = dp_masks()[-2::-1]
-        self.masks = masks[:-1], masks[-1:]
-        self.attn = together(qk, vo)
-        self.feed = jnp.concatenate([up, down], axis=1)
-        self.step = 0
-
-    def send(self):
-        if self.step < 2:
-            got = near_two(*self.attn) if self.step else near_one(near_one_sent(*self.attn))
-            self.feed, more = far(self.feed, self.masks[self.step])
-            return *got, more
-        self.attn, more = far(self.attn, self.masks[self.step - 2])
-        return (more,)
-
-    def finish(self, got):
-        if self.step < 2:
-            self.attn = (near_two_sum if self.step else near_one_sum)(*self.attn, got[:2])
+            self.feed = together(first.astype(bf16), second.astype(bf16))
+        elif step == 2:
+            self.feed = together(*near_two_sum(*self.feed, got[:2]))
+            if self.attn is not None:
+                self.feed = jnp.concatenate(self.feed, axis=1)
+                self.attn = near_one_sum(*self.attn, got[2:])
+                self.feed, *self.attn = together(self.feed, *self.attn)
+        elif step == 3:
+            self.attn = jnp.concatenate(near_two_sum(*self.attn, got[:2]), axis=1)
             self.feed = far_sum(self.feed, got[2])
-            *self.attn, self.feed = together(*self.attn, self.feed)
-            if self.step == 1:
-                self.attn = jnp.concatenate(self.attn, axis=1)
+            self.attn, self.feed = together(self.attn, self.feed)
         else:
-            (self.attn,) = together(far_sum(self.attn, got[0]))
-        self.step += 1
+            self.attn = far_sum(self.attn, got[0])
+            if step == 4:
+                self.feed = far_sum(self.feed, got[1])
+            self.attn, self.feed = together(self.attn, self.feed)
 
     def tokens(self):
-        return (self.feed, self.attn) if self.step > 1 else (self.feed, *self.attn)
+        if self.step == 0:
+            return []
+        parts = self.feed if self.step < 3 and isinstance(self.feed, (list, tuple)) else (self.feed,)
+        if self.attn is None:
+            return list(parts)
+        return [*parts, *(self.attn if isinstance(self.attn, (list, tuple)) else (self.attn,))]
 
     def result(self):
         half, low = self.attn.shape[1] // 2, self.feed.shape[1] // 2
@@ -691,7 +709,7 @@
     first = y_me == 0
 
     def other_clip(value):
-        return exchange(jnp.where(first, value[1], value[0]), "tensor", 2)
+        return jnp.where(first, value[1], value[0])
 
     def take_clip(value, theirs):
         mine = jnp.where(first, value[0], value[1])
@@ -710,7 +728,8 @@
         mine = (nt_dot(high, to_relative) + nt_dot(low, to_relative))[:row_count]
         return jnp.stack([jnp.where(first, mine, theirs), jnp.where(first, theirs, mine)])
 
-    current = take_clip(frames, other_clip(frames))
+    current = take_clip(frames, exchange(other_clip(frames), "tensor", 2))
+    clip = other_clip(cotangent)
 
     groups = []
     for at in range(layers):
@@ -721,10 +740,12 @@
     by_width, by_hidden = gathering.advance(by_width, by_hidden)
     for at, mask in enumerate(dp_masks()):
         got = exchange(by_width, "dp", mask), exchange(by_hidden, "dp", mask)
-        if mask <= 2:
-            got = gathering.advance(*got)
+        if mask > 2:
+            got = together(*got)
+        elif mask == 2:
+            *got, clip = gathering.advance(*got, clip)
         else:
-            got = together(*got)
+            got = got[0], *gathering.advance(got[1])
         by_width = jnp.concatenate([by_width, got[0]], axis=1)
         by_hidden = by_hidden + got[1]
     gain_all, shift_all, obias_all = by_width.reshape(3, layers, 2, width)
@@ -756,6 +777,8 @@
             *shares, qkv, o, lse = gathering.advance(*out)
             heads.append((qkv, o, lse))
         share_b = exchange(shares[1], "tensor", 1)
+        if not final:
+            (share_b,) = gathering.advance(share_b)
         w_up, w_down = feed_weights(2 * at + 1)
         following = 0 if final else at + 1
         vectors = jnp.stack(
@@ -771,7 +794,7 @@
         vectors = jnp.pad(vectors, ((0, 2), (0, 0)))
         fed = feed(final, current, shares[0], share_b, vectors, up_all[at], w_up, w_down)
         if not final:
-            fed = gathering.advance(*fed, *([other_clip(cotangent)] if at == 0 else []))
+            fed = gathering.advance(*fed, *([exchange(clip, "tensor", 2)] if at == 0 else []))
             if at == 0:
                 *fed, clip = fed
         weights.append((w_attn, w_up, w_down))
@@ -780,9 +803,9 @@
         current = fed[10]
         if not final:
             normed_a = fed[11]
-            normed_b = exchange(normed_a, "tensor", 1)
+            (normed_b,) = gathering.advance(exchange(normed_a, "tensor", 1))
     if layers == 1:
-        clip = other_clip(cotangent)
+        clip = exchange(clip, "tensor", 2)
     small_grads = [None] * layers
     weight_grads = [None] * layers
     gains_one = [None] * layers
@@ -796,18 +819,17 @@
         vectors = jnp.stack([gain_all[at, 1], gain_all[0 if final else at + 1, 0]])
         vectors = jnp.pad(vectors, ((0, 6), (0, 0)))
         if uppers:
-            fronts = behind(fronts, *folding.attn, folding.feed)
+            fronts = behind(fronts, *folding.tokens())
         fed = feed_back(
             final, fronts, middle, normed_two, vectors, w_up, w_down, activated, slopes
         )
         if final:
-            *fed, half = together(*fed, give_half(current))
-            encoded = give_clip(current, half)
+            *fed, encoded_half = together(*fed, give_half(current))
         own, other, bup, gradient, branch_a, sums = advance(uppers, *fed)
         if not final:
             gains_one[at + 1] = sums[4:6]
         branch_b = exchange(branch_a, "tensor", 1)
-        core = CoreFold(own, exchange(other, "tensor", 1))
+        core = Folding(own, other)
         branch = jnp.concatenate([branch_a, branch_b], axis=0)
 
         def weight_grad(t, dqkv):
@@ -816,8 +838,12 @@
             return dw[:, : 2 * wide], jnp.concatenate([dw[:, 2 * wide :], dw_o], axis=1)
 
         def state_tokens():
-            return [*core.state, *(folding.tokens() if uppers else ())]
-
+            return [part for fold in (core, *uppers) for part in fold.tokens()]
+
+        if at == 0:
+            advance([core, *uppers])
+        elif uppers:
+            advance(uppers)
         ready = behind((branch_a, branch_b), *state_tokens())
         (dqkv_other,) = advance(
             [core, *uppers],
@@ -836,41 +862,42 @@
                 row_count, quarter, *ready, *w_attn[0], *heads[0], (dqkv_other, *w_attn[1])
             ),
         )
-        share_a, share_b, dqkv_own = behind((share_a, share_b, dqkv_own), *core.state)
         if uppers:
-            advance(uppers)
             weight_grads[at + 1] = folding.result()
         share_b = exchange(share_b, "tensor", 1)
         dw_own = weight_grad(0, dqkv_own)
         if at == 0:
             dw_own = add_low(jnp.concatenate(dw_own, axis=1), got[0])
-            folding = LastFolding(dw_own, *core.state)
+            folding = LastFolding(dw_own, *core.feed)
         else:
             dw_other = weight_grad(1, dqkv_other)
-            stacks = [jnp.stack(pair) for pair in zip(dw_own, dw_other)]
-            folding = Folding(*stacks, *core.state)
-        dbias = jnp.stack([jnp.sum(part, axis=0, dtype=f32) for part in (dqkv_own, dqkv_other)])
-        dbias = dbias.reshape(2, 3, wide)[:, 0::2]
+            core.attn = together(*[jnp.stack(pair) for pair in zip(dw_own, dw_other)])
+            folding = core
         fronts = (gradient, layer_in, share_a, share_b)
-        small_grads[at] = (sums, dbias, bup)
+        small_grads[at] = (sums, (dqkv_own, dqkv_other), bup)
     grad_in, *last_sums = norm_back(
         layer_in, gain_all[0, 0], share_a + share_b.astype(f32)
     )
     gradient = gradient + grad_in
     gains_one[0] = jnp.concatenate(last_sums, axis=0)
-    sums, bqv, bups = [jnp.stack([small_grads[at][i] for at in range(layers)]) for i in range(3)]
-    bqv = bqv.reshape(layers, 2, 2, count_dp, qv_part).transpose(1, 0, 2, 3, 4)
-    bqv = jnp.pad(bqv, ((0, 0),) * 4 + ((0, block - qv_part),)).reshape(2, 2 * layers, width)
-    bups = bups.reshape(layers, 2, 2, count_dp, up_part).transpose(1, 2, 0, 3, 4)
-    bups = jnp.pad(bups, ((0, 0),) * 4 + ((0, block - up_part),)).reshape(2, 2 * layers, width)
-    by_hidden = jnp.concatenate([bups, bqv], axis=1).reshape(8 * layers, width)
+    pairs = behind(
+        [part for at in range(1, layers) for part in small_grads[at][1]], *small_grads[0][1]
+    )
+    pairs = [*small_grads[0][1], *pairs]
+    bqv = jnp.stack([jnp.sum(part, axis=0, dtype=f32) for part in pairs])
+    bqv = bqv.reshape(layers, 2, 3, count_dp, qv_part)[:, :, 0::2].transpose(1, 0, 2, 3, 4)
+    bqv = jnp.pad(bqv, ((0, 0),) * 4 + ((0, block - qv_part),)).reshape(4 * layers, width)
+    sums, bups = [jnp.stack([small_grads[at][i] for at in range(layers)]) for i in (0, 2)]
+    bups = bups.reshape(layers, 4, count_dp, up_part).transpose(1, 0, 2, 3)
+    bups = jnp.pad(bups, ((0, 0),) * 3 + ((0, block - up_part),)).reshape(4 * layers, width)
     by_hidden = lax.dot_general(
-        by_hidden,
+        jnp.concatenate([bups, bqv]),
         to_relative.astype(f32),
         (((1,), (0,)), ((), ())),
         precision=lax.Precision.HIGHEST,
         preferred_element_type=f32,
-    ).reshape(2, 4 * layers, width)
+    )
+    bups, bqv = by_hidden[: 4 * layers], by_hidden[4 * layers :]
     one = jnp.stack(gains_one)
     by_width = jnp.stack(
         [
@@ -879,21 +906,26 @@
             jnp.stack([sums[:, 3], sums[:, 0]], axis=1),
         ]
     ).reshape(6 * layers, width)
-    small = [jnp.concatenate([by_width, by_hidden[i]]) for i in range(2)]
+    small = [
+        jnp.concatenate(
+            [by_width, bups[t * layers : (t + 1) * layers]]
+            + ([bqv[t * layers : (t + 2) * layers]] if t % 2 == 0 else [])
+        )
+        for t in range(4)
+    ]
     advance([folding])
     gradient, *small, folding.attn, folding.feed = together(
         gradient, *small, folding.attn, folding.feed
     )
-    half = give_half(gradient)
-    small = small[0] + exchange(small[1], "tensor", 2)
+    half, *got = advance(
+        [folding],
+        give_half(gradient),
+        *[exchange(small[t], "tensor", t) for t in range(1, 4)],
+    )
     cut = 6 * layers
-    got = exchange(
-        jnp.concatenate([small[:cut], small[cut + layers : cut + 2 * layers]]), "tensor", 1
-    )
-    small = jnp.concatenate(
-        [small[: cut + layers] + got[: cut + layers], small[cut + 2 * layers :]]
-    )
-    half, small = advance([folding], half, small)
+    small, more = small[0] + got[1], got[0] + got[2]
+    small = jnp.concatenate([small[: cut + layers] + more, small[cut + layers :]])
+    encoded = give_clip(*behind((current, encoded_half), *small_grads[0][1]))
     frames_grad = give_clip(gradient, half)
     for mask in reversed(dp_masks()):
         got = exchange(small[:, small.shape[1] // 2 :], "dp", mask)

time: 657 us -> 662 us (level)
  local copies, waits for them, and re-layouts: 76.3 us -> 93.9 us
  other arithmetic: 81.7 us -> 67.7 us
    unnamed x255 -> x278, local copies, waits for them, and re-layouts: 21.4 us -> 31.6 us
    another operation x10 -> x5, other arithmetic: 7.66 us -> 0.92 us  [the longest x1 0.62 us: local(): bqv = jnp.stack([jnp.sum(part, axis=0, dtype=f32) for part in pairs])]
    ppermute x81 -> x86, starting transfers between devices: 80.8 us -> 80.2 us  [exchange(): return lax.ppermute(value, axis, [(i, i ^ mask) for i in range(count)])]
    ppermute x81 -> x86, waiting for transfers between devices: 78.9 us -> 78.8 us  [exchange(): return lax.ppermute(value, axis, [(i, i ^ mask) for i in range(count)])]
  transfers between devices with their start and end apart: 81 -> 86, of which waited for: 25 -> 24; matrix products, arithmetic and copies ran while one was open for 20% -> 19% of each run, Pallas kernels for 43% -> 43%
where the time goes in v6:
time: 662 us; the launch traced here: 652 us
  Pallas kernels  298 us (45%)
  local copies, waits for them, and re-layouts  93.9 us (14%)
  starting transfers between devices  80.2 us (12%)
  waiting for transfers between devices  78.8 us (12%)
  other arithmetic  67.7 us (10%)
  matrix products  29.8 us (5%)
    pallas_call x4, Pallas kernels, attend_back(): pl.pallas_call(functools.partial(attend_back_kernel, row_count, quarter,...  123 us
    ppermute x86, starting transfers between devices, exchange(): return lax.ppermute(value, axis, [(i, i ^ mask) for i in range(count)])  80.2 us
    ppermute x86, waiting for transfers between devices, exchange(): return lax.ppermute(value, axis, [(i, i ^ mask) for i in range(count)])  78.8 us
    pallas_call x4, Pallas kernels, attend(): pl.pallas_call(functools.partial(attend_kernel, row_count, quarter, min(5...  73.4 us
    pallas_call x2, Pallas kernels, feed_back(): pl.pallas_call(functools.partial(feed_back_kernel, final), grid=(hidden /...  64.1 us
    pallas_call x2, Pallas kernels, feed(): pl.pallas_call(functools.partial(feed_kernel, final), grid=(hidden // ste...  37.8 us
    unnamed x278, local copies, waits for them, and re-layouts  31.6 us
    convert_element_type x22, other arithmetic, add_low(): return (kept.astype(f32) + received.astype(f32)).astype(bf16)  26.9 us
  transfers between devices with their start and end apart: 86, of which 24 were waited for; matrix products, arithmetic and copies ran while one was open for 19% of the time, Pallas kernels for 43%

profile of v6, /device:TPU:0, one launch (start us, length us, event | category | flops | bytes accessed | tf_op | source)
XLA Modules:
  0.0 652.0 jit_solution(12131928989618007618)
XLA Ops:
  4.0 4.1 collective-permute-start
  14.6 1.9 collective-permute-done.2
  17.4 2.8 collective-permute-start.5
  20.2 1.7 collective-permute-start.3
  23.0 1.9 collective-permute-start.6
  25.2 1.7 collective-permute-start.16
  26.9 2.6 collective-permute-done.6
  38.8 2.3 collective-permute-done.16
  41.2 2.7 fusion.79
  43.9 2.0 copy.40.refs_0_
  49.6 2.7 collective-permute-done.11
  53.5 2.1 pad_maximum_fusion.14
  57.1 1.7 collective-permute-start.15
  69.7 2.5 collective-permute-done.13
  72.2 3.8 collective-permute-done.14
  81.3 2.5 collective-permute-start.21
  85.9 17.3 %shard_map.194 = (bf16[1536,576]{1,0:T(8,128)(2,1)}, bf16[1536,192]{1,0:T(8,128)(2,1)}, f32[1536,8]{1,0:T(8,128)}) custom-call(bf16[768,768]{1,0:T(8,128)(2,1)} %copy-done.8, bf16[768,768]{1,0:T(8,128)(2,1)} %copy-done.28, bf16[768,384]{1,0:T(8,128)(2,1)} %copy-done.27, bf16[768,384]{1,0:T(8,128)(2,1)} %copy-done.24, f32[2,384]{1,0:T(2,128)} %get-tuple-element.664.refs_4_), custom_call_target="tpu_custom_call" | custom-call | tf_op jit(solution)/shard_map/pallas_call | solution.py:383
  111.5 19.6 %shard_map.195 = (f32[768,768]{1,0:T(8,128)}, bf16[768,768]{1,0:T(8,128)(2,1)}, bf16[1536,576]{1,0:T(8,128)(2,1)}, bf16[1536,192]{1,0:T(8,128)(2,1)}, f32[1536,8]{1,0:T(8,128)}) custom-call(bf16[768,768]{1,0:T(8,128)(2,1)} %copy-done.8, bf16[768,768]{1,0:T(8,128)(2,1)} %copy-done.28, bf16[768,384]{1,0:T(8,128)(2,1)} %copy-done.26, ...), custom_call_target="tpu_custom_call" | custom-call | tf_op jit(solution)/shard_map/pallas_call | solution.py:383
  135.5 5.7 collective-permute-done.26
  151.6 19.8 %shard_map.196 = (bf16[768,768]{1,0:T(8,128)(2,1)}, bf16[768,768]{1,0:T(8,128)(2,1)}, bf16[768,768]{1,0:T(8,128)(2,1)}, bf16[768,768]{1,0:T(8,128)(2,1)}, bf16[7...) custom-call(f32[768,768]{1,0:T(8,128)} %copy-done, ...), custom_call_target="tpu_custom_call" | custom-call | tf_op jit(solution)/shard_map/pallas_call | solution.py:555
  171.6 1.8 collective-permute-start.38
  173.4 13.9 %collective-permute-done.38 = bf16[192,1536]{1,0:T(8,128)(2,1)S(1)} collective-permute-done((bf16[192,1536]{1,0:T(8,128)(2,1)S(1)}, bf16[192,1536]{1,0:T(8,128)(2,1)S(1)}, u32[]{:S(2)}, u32[]{:S(2)}) %collective-permute-start.38) | collective-permute-done | bytes 589856 | tf_op jit(solution)/shard_map/ppermute | solution.py:23
  191.8 17.2 %shard_map.197 = (bf16[1536,576]{1,0:T(8,128)(2,1)}, bf16[1536,192]{1,0:T(8,128)(2,1)}, f32[1536,8]{1,0:T(8,128)}) custom-call(bf16[768,768]{1,0:T(8,128)(2,1)} %get-tuple-element.377.refs_0_, bf16[768,768]{1,0:T(8,128)(2,1)} %copy-done.12, bf16[768,384]{1,0:T(8,128)(2,1)} %pad_maximum_fusion.15.refs_2_, bf16[768,384]{1,0:T(8,128)(2,1)} %copy-done.25, ...), custom_call_target="tpu_custom_call" | custom-call | tf_op jit(solution)/shard_map/pallas_call | solution.py:383
  213.7 19.2 %shard_map.198 = (f32[768,768]{1,0:T(8,128)}, bf16[768,768]{1,0:T(8,128)(2,1)}, bf16[1536,576]{1,0:T(8,128)(2,1)}, bf16[1536,192]{1,0:T(8,128)(2,1)}, f32[1536,8]{1,0:T(8,128)}) custom-call(bf16[768,768]{1,0:T(8,128)(2,1)} %get-tuple-element.377.refs_0_, bf16[768,768]{1,0:T(8,128)(2,1)} %copy-done.12, ...), custom_call_target="tpu_custom_call" | custom-call | tf_op jit(solution)/shard_map/pallas_call | solution.py:383
  235.2 2.6 collective-permute-done.44
  245.9 18.0 %shard_map.199 = (bf16[768,768]{1,0:T(8,128)(2,1)}, bf16[768,768]{1,0:T(8,128)(2,1)}, bf16[768,768]{1,0:T(8,128)(2,1)}, bf16[768,768]{1,0:T(8,128)(2,1)}, bf16[7...) custom-call(f32[768,768]{1,0:T(8,128)} %get-tuple-element.446.refs_0, ...), custom_call_target="tpu_custom_call" | custom-call | tf_op jit(solution)/shard_map/pallas_call | solution.py:555
  266.6 2.6 fusion.13.refs_0_
  269.2 30.2 %shard_map.200 = (bf16[4,768,768]{2,1,0:T(8,128)(2,1)}, bf16[4,768,768]{2,1,0:T(8,128)(2,1)}, f32[4,768]{1,0:T(4,128)}, f32[768,768]{1,0:T(8,128)}, bf16[768,768]{1,0:T(8,128)(2,1)}, /*index=5*/f32[8,768]{1,0:T(8,128)}) custom-call(f32[768,768]{1,0:T(8,128)} %fusion.13.refs_0_, f32[768,768]{1,0:T(8,128)} %get-tuple-element.393.refs_1_, ...), custom_call_target="tpu_custom_call" | custom-call | tf_op jit(solution)/shard_map/pallas_call | solution.py:627
  303.9 5.6 collective-permute-done.52.refs_1_
  309.5 28.2 %shard_map.201.refs_7_ = bf16[1536,576]{1,0:T(8,128)(2,1)} custom-call(bf16[768,768]{1,0:T(8,128)(2,1)} %get-tuple-element.428.refs_0_, bf16[768,768]{1,0:T(8,128)(2,1)} %collective-permute-done.52.refs_1_, bf16[768,384]{1,0:T(8,128)(2,1)} %collective-permute-done.29.refs_2_.refs_8_, bf16[768,384]{1,0:T(8,128)(2,1)} %copy-done.23, ...), custom_call_target="tpu_custom_call" | custom-call | tf_op jit(solution)/shard_map/pallas_call | solution.py:472
  337.7 2.4 constant_dynamic-update-slice_fusion.30
  340.1 2.9 fusion.19
  343.0 2.1 add_convert_fusion.5
  350.5 1.7 convolution_convert_fusion
  353.1 33.1 %shard_map.202 = (f32[768,768]{1,0:T(8,128)}, bf16[768,768]{1,0:T(8,128)(2,1)}, bf16[1536,576]{1,0:T(8,128)(2,1)}) custom-call(bf16[768,768]{1,0:T(8,128)(2,1)} %get-tuple-element.428.refs_0_, bf16[768,768]{1,0:T(8,128)(2,1)} %collective-permute-done.52.refs_1_, bf16[768,384]{1,0:T(8,128)(2,1)} %pad_maximum_fusion.15.refs_2_, bf16[768,384]{1,0:T(8,128)(2,1)} %copy-done.25, ...), custom_call_target="tpu_custom_call" | custom-call | tf_op jit(solution)/shard_map/pallas_call | solution.py:472
  388.0 3.6 convolution_convert_fusion.1
  391.7 2.4 fusion.5
  394.1 2.5 add_convert_fusion.4
  405.3 33.9 %shard_map.203 = (bf16[4,768,768]{2,1,0:T(8,128)(2,1)}, bf16[4,768,768]{2,1,0:T(8,128)(2,1)}, f32[4,768]{1,0:T(4,128)}, f32[768,768]{1,0:T(8,128)}, bf16[768,768]{1,0:T(8,128)(2,1)}, /*index=5*/f32[8,768]{1,0:T(8,128)}) custom-call(f32[768,768]{1,0:T(8,128)} %get-tuple-element.445.refs_0_, f32[768,768]{1,0:T(8,128)} %get-tuple-element.446.refs_0_.refs_1_, ...), custom_call_target="tpu_custom_call" | custom-call | tf_op jit(solution)/shard_map/pallas_call | solution.py:627
  449.6 1.8 collective-permute-start.63
  459.9 4.4 collective-permute-done.63
  465.1 2.9 fusion.20
  468.0 2.0 add_convert_fusion.2
  476.1 1.7 collective-permute-start.66
  478.6 2.4 collective-permute-start.67
  482.4 28.5 %shard_map.204.refs_7_ = bf16[1536,576]{1,0:T(8,128)(2,1)} custom-call(bf16[768,768]{1,0:T(8,128)(2,1)} %get-tuple-element.499.refs_0_, bf16[768,768]{1,0:T(8,128)(2,1)} %copy-done.6, bf16[768,384]{1,0:T(8,128)(2,1)} %copy-done.26, bf16[768,384]{1,0:T(8,128)(2,1)} %copy-done.22, bf16[1536,576]{1,0:T(8,128)(2,1)} %get-tuple-element.487.refs_4_, ...), custom_call_target="tpu_custom_call" | custom-call | tf_op jit(solution)/shard_map/pallas_call | solution.py:472
  510.9 2.4 fusion.4
  513.4 2.9 add_convert_fusion.1
  525.2 1.9 add_convert_fusion.17
  528.7 33.1 %shard_map.205 = (f32[768,768]{1,0:T(8,128)}, bf16[768,768]{1,0:T(8,128)(2,1)}, bf16[1536,576]{1,0:T(8,128)(2,1)}) custom-call(bf16[768,768]{1,0:T(8,128)(2,1)} %get-tuple-element.499.refs_0_, bf16[768,768]{1,0:T(8,128)(2,1)} %copy-done.6, bf16[768,384]{1,0:T(8,128)(2,1)} %copy-done.27, bf16[768,384]{1,0:T(8,128)(2,1)} %copy-done.24, ...), custom_call_target="tpu_custom_call" | custom-call | tf_op jit(solution)/shard_map/pallas_call | solution.py:472
  561.9 2.1 fusion.11
  564.1 1.7 fusion.12
  567.1 2.6 fusion.18
  586.5 1.8 select_bitcast_fusion.3
  591.2 4.0 collective-permute-done.74
  595.2 3.8 collective-permute-done.75
  607.4 3.1 multiply_add_fusion
  611.6 2.6 copy.48
  614.8 2.5 collective-permute-start.77
  620.7 4.6 collective-permute-done.81
  626.8 3.7 collective-permute-done.76
  633.9 2.6 copy.49
  636.5 5.2 collective-permute-done.82
  647.7 2.8 collective-permute-done.85
  (628 shorter events, 196.1 us)
Async XLA Ops:
  4.0 13.2 %collective-permute-start = (bf16[96,768]{1,0:T(8,128)(2,1)S(1)}, bf16[96,768]{1,0:T(8,128)(2,1)S(1)}, u32[]{:S(2)}, u32[]{:S(2)}) collective-permute-start(bf16[96,768]{1,0:T(8,128)(2,1)S(1)} %pad_maximum_fusion.24), channel_id=1, source_target_pairs={{0,16},{4,20},{8,24},{12,28},{16,0},{20,4},{24,8},{28,12},{1,17},{... | collective-permute-start | bytes 442376 | tf_op jit(solution)/shard_map/ppermute | solution.py:23
  20.2 9.8 %collective-permute-start.3 = (bf16[192,768]{1,0:T(8,128)(2,1)S(1)}, bf16[192,768]{1,0:T(8,128)(2,1)S(1)}, u32[]{:S(2)}, u32[]{:S(2)}) collective-permute-start(bf16[192,768]{1,0:T(8,128)(2,1)S(1)} %pad_maximum_fusion.20), channel_id=1, source_target_pairs={{0,8},{4,12},{8,0},{12,4},{16,24},{20,28},{24,16},{28,20},{1,9},{5... | collective-permute-start | bytes 884744 | tf_op jit(solution)/shard_map/ppermute | solution.py:23
  25.2 15.9 %collective-permute-start.16 = (bf16[375,768]{1,0:T(8,128)(2,1)S(1)}, bf16[375,768]{1,0:T(8,128)(2,1)S(1)}, u32[]{:S(2)}, u32[]{:S(2)}) collective-permute-start(bf16[375,768]{1,0:T(8,128)(2,1)S(1)} %get-tuple-element.586), channel_id=1, source_target_pairs={{0,2},{1,3},{2,0},{3,1},{4,6},{5,7},{6,4},{7,5},{8,10},{9,11},{10,... | collective-permute-start | bytes 1728008 | tf_op jit(solution)/shard_map/ppermute | solution.py:23
  32.6 19.7 %collective-permute-start.8 = (bf16[384,384]{1,0:T(8,128)(2,1)}, bf16[384,384]{1,0:T(8,128)(2,1)}, u32[]{:S(2)}, u32[]{:S(2)}) collective-permute-start(bf16[384,384]{1,0:T(8,128)(2,1)} %get-tuple-element.287), channel_id=1, source_target_pairs={{0,4},{4,0},{8,12},{12,8},{16,20},{20,16},{24,28},{28,24},{1,5},{5... | collective-permute-start | bytes 884744 | tf_op jit(solution)/shard_map/ppermute | solution.py:23
  33.0 19.3 %collective-permute-start.9 = (bf16[384,384]{1,0:T(8,128)(2,1)}, bf16[384,384]{1,0:T(8,128)(2,1)}, u32[]{:S(2)}, u32[]{:S(2)}) collective-permute-start(bf16[384,384]{1,0:T(8,128)(2,1)} %get-tuple-element.296), channel_id=1, source_target_pairs={{0,2},{1,3},{2,0},{3,1},{4,6},{5,7},{6,4},{7,5},{8,10},{9,11},{10,... | collective-permute-start | bytes 884744 | tf_op jit(solution)/shard_map/ppermute | solution.py:23
  34.6 17.7 %collective-permute-start.10 = (bf16[96,1536]{1,0:T(8,128)(2,1)}, bf16[96,1536]{1,0:T(8,128)(2,1)}, u32[]{:S(2)}, u32[]{:S(2)}) collective-permute-start(bf16[96,1536]{1,0:T(8,128)(2,1)} %get-tuple-element.289), channel_id=1, source_target_pairs={{0,16},{4,20},{8,24},{12,28},{16,0},{20,4},{24,8},{28,12},{1,17},{... | collective-permute-start | bytes 884744 | tf_op jit(solution)/shard_map/ppermute | solution.py:23
  47.8 28.2 %collective-permute-start.18 = (bf16[768,768]{1,0:T(8,128)(2,1)S(1)}, bf16[768,768]{1,0:T(8,128)(2,1)S(1)}, u32[]{:S(2)}, u32[]{:S(2)}) collective-permute-start(bf16[768,768]{1,0:T(8,128)(2,1)S(1)} %add_convert_fusion.7.refs_0_), channel_id=1, source_target_pairs={{0,1},{1,0},{2,3},{3,2},{4,5},{5,4},{6,7},{7,6},{8,9},{9,8},{10,11... | collective-permute-start | bytes 3538952 | tf_op jit(solution)/shard_map/ppermute | solution.py:23
  55.6 20.4 %collective-permute-start.12 = (bf16[768,384]{1,0:T(8,128)(2,1)S(1)}, bf16[768,384]{1,0:T(8,128)(2,1)S(1)}, u32[]{:S(2)}, u32[]{:S(2)}) collective-permute-start(bf16[768,384]{1,0:T(8,128)(2,1)S(1)} %pad_maximum_fusion.13.refs_2_), channel_id=1, source_target_pairs={{0,2},{1,3},{2,0},{3,1},{4,6},{5,7},{6,4},{7,5},{8,10},{9,11},{10,... | collective-permute-start | bytes 1769480 | tf_op jit(solution)/shard_map/ppermute | solution.py:23
  57.1 18.9 %collective-permute-start.15 = (bf16[192,1536]{1,0:T(8,128)(2,1)}, bf16[192,1536]{1,0:T(8,128)(2,1)}, u32[]{:S(2)}, u32[]{:S(2)}) collective-permute-start(bf16[192,1536]{1,0:T(8,128)(2,1)} %pad_maximum_fusion.14), channel_id=1, source_target_pairs={{0,8},{4,12},{8,0},{12,4},{16,24},{20,28},{24,16},{28,20},{1,9},{5... | collective-permute-start | bytes 1769480 | tf_op jit(solution)/shard_map/ppermute | solution.py:23
  61.9 10.3 %collective-permute-start.13 = (bf16[384,384]{1,0:T(8,128)(2,1)}, bf16[384,384]{1,0:T(8,128)(2,1)}, u32[]{:S(2)}, u32[]{:S(2)}) collective-permute-start(bf16[384,384]{1,0:T(8,128)(2,1)} %get-tuple-element.296), channel_id=1, source_target_pairs={{0,4},{4,0},{8,12},{12,8},{16,20},{20,16},{24,28},{28,24},{1,5},{5... | collective-permute-start | bytes 884744 | tf_op jit(solution)/shard_map/ppermute | solution.py:23
  63.5 12.5 %collective-permute-start.14 = (bf16[384,384]{1,0:T(8,128)(2,1)}, bf16[384,384]{1,0:T(8,128)(2,1)}, u32[]{:S(2)}, u32[]{:S(2)}) collective-permute-start(bf16[384,384]{1,0:T(8,128)(2,1)} %collective-permute-done.9), channel_id=1, source_target_pairs={{0,4},{4,0},{8,12},{12,8},{16,20},{20,16},{24,28},{28,24},{1,5},{5... | collective-permute-start | bytes 884744 | tf_op jit(solution)/shard_map/ppermute | solution.py:23
  77.7 25.6 %collective-permute-start.19 = (bf16[384,768]{1,0:T(8,128)(2,1)S(1)}, bf16[384,768]{1,0:T(8,128)(2,1)}, u32[]{:S(2)}, u32[]{:S(2)}) collective-permute-start(bf16[384,768]{1,0:T(8,128)(2,1)S(1)} %get-tuple-element.301), channel_id=1, source_target_pairs={{0,4},{4,0},{8,12},{12,8},{16,20},{20,16},{24,28},{28,24},{1,5},{5... | collective-permute-start | bytes 1769480 | tf_op jit(solution)/shard_map/ppermute | solution.py:23
  79.3 24.0 %collective-permute-start.20 = (bf16[384,768]{1,0:T(8,128)(2,1)S(1)}, bf16[384,768]{1,0:T(8,128)(2,1)S(1)}, u32[]{:S(2)}, u32[]{:S(2)}) collective-permute-start(bf16[384,768]{1,0:T(8,128)(2,1)S(1)} %get-tuple-element.317), channel_id=1, source_target_pairs={{0,2},{1,3},{2,0},{3,1},{4,6},{5,7},{6,4},{7,5},{8,10},{9,11},{10,... | collective-permute-start | bytes 1769480 | tf_op jit(solution)/shard_map/ppermute | solution.py:23
  81.3 21.9 %collective-permute-start.21 = (bf16[96,768]{1,0:T(8,128)(2,1)}, bf16[96,768]{1,0:T(8,128)(2,1)S(1)}, u32[]{:S(2)}, u32[]{:S(2)}) collective-permute-start(bf16[96,768]{1,0:T(8,128)(2,1)} %pad_maximum_fusion.25), channel_id=1, source_target_pairs={{0,16},{4,20},{8,24},{12,28},{16,0},{20,4},{24,8},{28,12},{1,17},{... | collective-permute-start | bytes 442376 | tf_op jit(solution)/shard_map/ppermute | solution.py:23
  104.6 26.5 %collective-permute-start.22 = (bf16[768,768]{1,0:T(8,128)(2,1)S(1)}, bf16[768,768]{1,0:T(8,128)(2,1)}, u32[]{:S(2)}, u32[]{:S(2)}) collective-permute-start(bf16[768,768]{1,0:T(8,128)(2,1)S(1)} %constant_dynamic-update-slice_fusion.4.refs_5_.refs_7_), channel_id=1, source_target_pairs={{0,2},{1,3},{2,0},{3,1},{4,6},{5,7},{6,4},{7,5},{8,10},{9,11},{10,... | collective-permute-start | bytes 3538952 | tf_op jit(solution)/shard_map/ppermute | solution.py:23
  106.3 24.9 %collective-permute-start.23 = (bf16[384,768]{1,0:T(8,128)(2,1)S(1)}, bf16[384,768]{1,0:T(8,128)(2,1)}, u32[]{:S(2)}, u32[]{:S(2)}) collective-permute-start(bf16[384,768]{1,0:T(8,128)(2,1)S(1)} %get-tuple-element.317), channel_id=1, source_target_pairs={{0,4},{4,0},{8,12},{12,8},{16,20},{20,16},{24,28},{28,24},{1,5},{5... | collective-permute-start | bytes 1769480 | tf_op jit(solution)/shard_map/ppermute | solution.py:23
  106.7 24.4 %collective-permute-start.24 = (bf16[384,768]{1,0:T(8,128)(2,1)S(1)}, bf16[384,768]{1,0:T(8,128)(2,1)S(1)}, u32[]{:S(2)}, u32[]{:S(2)}) collective-permute-start(bf16[384,768]{1,0:T(8,128)(2,1)S(1)} %collective-permute-done.20), channel_id=1, source_target_pairs={{0,4},{4,0},{8,12},{12,8},{16,20},{20,16},{24,28},{28,24},{1,5},{5... | collective-permute-start | bytes 1769480 | tf_op jit(solution)/shard_map/ppermute | solution.py:23
  108.3 22.8 %collective-permute-start.25 = (bf16[192,768]{1,0:T(8,128)(2,1)S(1)}, bf16[192,768]{1,0:T(8,128)(2,1)}, u32[]{:S(2)}, u32[]{:S(2)}) collective-permute-start(bf16[192,768]{1,0:T(8,128)(2,1)S(1)} %constant_dynamic-update-slice_fusion.6), channel_id=1, source_target_pairs={{0,8},{4,12},{8,0},{12,4},{16,24},{20,28},{24,16},{28,20},{1,9},{5... | collective-permute-start | bytes 884744 | tf_op jit(solution)/shard_map/ppermute | solution.py:23
  110.7 32.7 %collective-permute-start.33 = (bf16[768,768]{1,0:T(8,128)(2,1)S(1)}, bf16[768,768]{1,0:T(8,128)(2,1)}, u32[]{:S(2)}, u32[]{:S(2)}) collective-permute-start(bf16[768,768]{1,0:T(8,128)(2,1)S(1)} %constant_dynamic-update-slice_fusion.4.refs_5_.refs_7_), channel_id=1, source_target_pairs={{0,1},{1,0},{2,3},{3,2},{4,5},{5,4},{6,7},{7,6},{8,9},{9,8},{10,11... | collective-permute-start | bytes 3538952 | tf_op jit(solution)/shard_map/ppermute | solution.py:23
  132.5 8.7 %collective-permute-start.26 = (bf16[384,384]{1,0:T(8,128)(2,1)S(1)}, bf16[384,384]{1,0:T(8,128)(2,1)S(1)}, u32[]{:S(2)}, u32[]{:S(2)}) collective-permute-start(bf16[384,384]{1,0:T(8,128)(2,1)S(1)} %get-tuple-element.330), channel_id=1, source_target_pairs={{0,4},{4,0},{8,12},{12,8},{16,20},{20,16},{24,28},{28,24},{1,5},{5... | collective-permute-start | bytes 884744 | tf_op jit(solution)/shard_map/ppermute | solution.py:23
  134.0 11.7 %collective-permute-start.34 = (bf16[768,768]{1,0:T(8,128)(2,1)}, bf16[768,768]{1,0:T(8,128)(2,1)}, u32[]{:S(2)}, u32[]{:S(2)}) collective-permute-start(bf16[768,768]{1,0:T(8,128)(2,1)} %collective-permute-done.22.refs_7_.refs_9_), channel_id=1, source_target_pairs={{0,1},{1,0},{2,3},{3,2},{4,5},{5,4},{6,7},{7,6},{8,9},{9,8},{10,11... | collective-permute-start | bytes 3538952 | tf_op jit(solution)/shard_map/ppermute | solution.py:23
  142.9 28.5 %collective-permute-start.29 = (bf16[768,384]{1,0:T(8,128)(2,1)}, bf16[768,384]{1,0:T(8,128)(2,1)}, u32[]{:S(2)}, u32[]{:S(2)}) collective-permute-start(bf16[768,384]{1,0:T(8,128)(2,1)} %pad_maximum_fusion.15.refs_2_), channel_id=1, source_target_pairs={{0,2},{1,3},{2,0},{3,1},{4,6},{5,7},{6,4},{7,5},{8,10},{9,11},{10,... | collective-permute-start | bytes 1769480 | tf_op jit(solution)/shard_map/ppermute | solution.py:23
  143.3 28.0 %collective-permute-start.37 = (bf16[375,768]{1,0:T(8,128)(2,1)}, bf16[375,768]{1,0:T(8,128)(2,1)S(1)}, u32[]{:S(2)}, u32[]{:S(2)}) collective-permute-start(bf16[375,768]{1,0:T(8,128)(2,1)} %get-tuple-element.356), channel_id=1, source_target_pairs={{0,2},{1,3},{2,0},{3,1},{4,6},{5,7},{6,4},{7,5},{8,10},{9,11},{10,... | collective-permute-start | bytes 1728008 | tf_op jit(solution)/shard_map/ppermute | solution.py:23
  145.7 25.7 %collective-permute-start.30 = (bf16[384,384]{1,0:T(8,128)(2,1)}, bf16[384,384]{1,0:T(8,128)(2,1)S(1)}, u32[]{:S(2)}, u32[]{:S(2)}) collective-permute-start(bf16[384,384]{1,0:T(8,128)(2,1)} %copy-done.60), channel_id=1, source_target_pairs={{0,4},{4,0},{8,12},{12,8},{16,20},{20,16},{24,28},{28,24},{1,5},{5... | collective-permute-start | bytes 884744 | tf_op jit(solution)/shard_map/ppermute | solution.py:23
  147.0 24.4 %collective-permute-start.31 = (bf16[384,384]{1,0:T(8,128)(2,1)}, bf16[384,384]{1,0:T(8,128)(2,1)S(1)}, u32[]{:S(2)}, u32[]{:S(2)}) collective-permute-start(bf16[384,384]{1,0:T(8,128)(2,1)} %copy-done.91), channel_id=1, source_target_pairs={{0,4},{4,0},{8,12},{12,8},{16,20},{20,16},{24,28},{28,24},{1,5},{5... | collective-permute-start | bytes 884744 | tf_op jit(solution)/shard_map/ppermute | solution.py:23
  147.8 23.7 %collective-permute-start.32 = (bf16[96,1536]{1,0:T(8,128)(2,1)}, bf16[96,1536]{1,0:T(8,128)(2,1)S(1)}, u32[]{:S(2)}, u32[]{:S(2)}) collective-permute-start(bf16[96,1536]{1,0:T(8,128)(2,1)} %get-tuple-element.338), channel_id=1, source_target_pairs={{0,16},{4,20},{8,24},{12,28},{16,0},{20,4},{24,8},{28,12},{1,17},{... | collective-permute-start | bytes 884744 | tf_op jit(solution)/shard_map/ppermute | solution.py:23
  171.4 15.9 %collective-permute-start.39 = (bf16[768,768]{1,0:T(8,128)(2,1)}, bf16[768,768]{1,0:T(8,128)(2,1)S(1)}, u32[]{:S(2)}, u32[]{:S(2)}) collective-permute-start(bf16[768,768]{1,0:T(8,128)(2,1)} %get-tuple-element.377.refs_0_), channel_id=1, source_target_pairs={{0,1},{1,0},{2,3},{3,2},{4,5},{5,4},{6,7},{7,6},{8,9},{9,8},{10,11... | collective-permute-start | bytes 3538952 | tf_op jit(solution)/shard_map/ppermute | solution.py:23
  171.6 15.8 %collective-permute-start.38 = (bf16[192,1536]{1,0:T(8,128)(2,1)S(1)}, bf16[192,1536]{1,0:T(8,128)(2,1)S(1)}, u32[]{:S(2)}, u32[]{:S(2)}) collective-permute-start(bf16[192,1536]{1,0:T(8,128)(2,1)S(1)} %pad_maximum_fusion.16), channel_id=1, source_target_pairs={{0,8},{4,12},{8,0},{12,4},{16,24},{20,28},{24,16},{28,20},{1,9},{5... | collective-permute-start | bytes 1769480 | tf_op jit(solution)/shard_map/ppermute | solution.py:23
  188.6 20.5 %collective-permute-start.40 = (bf16[384,768]{1,0:T(8,128)(2,1)S(1)}, bf16[384,768]{1,0:T(8,128)(2,1)S(1)}, u32[]{:S(2)}, u32[]{:S(2)}) collective-permute-start(bf16[384,768]{1,0:T(8,128)(2,1)S(1)} %get-tuple-element.362), channel_id=1, source_target_pairs={{0,4},{4,0},{8,12},{12,8},{16,20},{20,16},{24,28},{28,24},{1,5},{5... | collective-permute-start | bytes 1769480 | tf_op jit(solution)/shard_map/ppermute | solution.py:23
  189.8 19.3 %collective-permute-start.41 = (bf16[384,768]{1,0:T(8,128)(2,1)}, bf16[384,768]{1,0:T(8,128)(2,1)}, u32[]{:S(2)}, u32[]{:S(2)}) collective-permute-start(bf16[384,768]{1,0:T(8,128)(2,1)} %get-tuple-element.374), channel_id=1, source_target_pairs={{0,2},{1,3},{2,0},{3,1},{4,6},{5,7},{6,4},{7,5},{8,10},{9,11},{10,... | collective-permute-start | bytes 1769480 | tf_op jit(solution)/shard_map/ppermute | solution.py:23
  209.2 28.7 %collective-permute-start.42 = (bf16[768,768]{1,0:T(8,128)(2,1)S(1)}, bf16[768,768]{1,0:T(8,128)(2,1)}, u32[]{:S(2)}, u32[]{:S(2)}) collective-permute-start(bf16[768,768]{1,0:T(8,128)(2,1)S(1)} %constant_dynamic-update-slice_fusion.20.refs_5_.refs_4_), channel_id=1, source_target_pairs={{0,2},{1,3},{2,0},{3,1},{4,6},{5,7},{6,4},{7,5},{8,10},{9,11},{10,... | collective-permute-start | bytes 3538952 | tf_op jit(solution)/shard_map/ppermute | solution.py:23
  210.8 24.4 %collective-permute-start.43 = (bf16[384,768]{1,0:T(8,128)(2,1)}, bf16[384,768]{1,0:T(8,128)(2,1)}, u32[]{:S(2)}, u32[]{:S(2)}) collective-permute-start(bf16[384,768]{1,0:T(8,128)(2,1)} %get-tuple-element.374), channel_id=1, source_target_pairs={{0,4},{4,0},{8,12},{12,8},{16,20},{20,16},{24,28},{28,24},{1,5},{5... | collective-permute-start | bytes 1769480 | tf_op jit(solution)/shard_map/ppermute | solution.py:23
  211.6 26.3 %collective-permute-start.44 = (bf16[384,768]{1,0:T(8,128)(2,1)}, bf16[384,768]{1,0:T(8,128)(2,1)}, u32[]{:S(2)}, u32[]{:S(2)}) collective-permute-start(bf16[384,768]{1,0:T(8,128)(2,1)} %collective-permute-done.41), channel_id=1, source_target_pairs={{0,4},{4,0},{8,12},{12,8},{16,20},{20,16},{24,28},{28,24},{1,5},{5... | collective-permute-start | bytes 1769480 | tf_op jit(solution)/shard_map/ppermute | solution.py:23
  212.9 31.0 %collective-permute-start.46 = (bf16[768,768]{1,0:T(8,128)(2,1)S(1)}, bf16[768,768]{1,0:T(8,128)(2,1)}, u32[]{:S(2)}, u32[]{:S(2)}) collective-permute-start(bf16[768,768]{1,0:T(8,128)(2,1)S(1)} %constant_dynamic-update-slice_fusion.20.refs_5_.refs_4_), channel_id=1, source_target_pairs={{0,1},{1,0},{2,3},{3,2},{4,5},{5,4},{6,7},{7,6},{8,9},{9,8},{10,11... | collective-permute-start | bytes 3538952 | tf_op jit(solution)/shard_map/ppermute | solution.py:23
  265.3 34.1 %collective-permute-start.50 = (bf16[384,768]{1,0:T(8,128)(2,1)S(1)}, bf16[384,768]{1,0:T(8,128)(2,1)}, u32[]{:S(2)}, u32[]{:S(2)}) collective-permute-start(bf16[384,768]{1,0:T(8,128)(2,1)S(1)} %slice.895), channel_id=1, source_target_pairs={{0,2},{1,3},{2,0},{3,1},{4,6},{5,7},{6,4},{7,5},{8,10},{9,11},{10,... | collective-permute-start | bytes 1769480 | tf_op jit(solution)/shard_map/ppermute | solution.py:23
  299.5 40.6 %collective-permute-start.51 = (bf16[4,768,768]{2,1,0:T(8,128)(2,1)}, bf16[4,768,768]{2,1,0:T(8,128)(2,1)}, u32[]{:S(2)}, u32[]{:S(2)}) collective-permute-start(bf16[4,768,768]{2,1,0:T(8,128)(2,1)} %get-tuple-element.417), channel_id=1, source_target_pairs={{0,1},{1,0},{2,3},{3,2},{4,5},{5,4},{6,7},{7,6},{8,9},{9,8},{10,11... | collective-permute-start | bytes 14155784 | tf_op jit(solution)/shard_map/ppermute | solution.py:23
  299.6 9.9 %collective-permute-start.52 = (bf16[768,768]{1,0:T(8,128)(2,1)}, bf16[768,768]{1,0:T(8,128)(2,1)}, u32[]{:S(2)}, u32[]{:S(2)}) collective-permute-start(bf16[768,768]{1,0:T(8,128)(2,1)} %get-tuple-element.428.refs_0_), channel_id=1, source_target_pairs={{0,1},{1,0},{2,3},{3,2},{4,5},{5,4},{6,7},{7,6},{8,9},{9,8},{10,11... | collective-permute-start | bytes 3538952 | tf_op jit(solution)/shard_map/ppermute | solution.py:23
  345.1 42.5 %collective-permute-start.53 = (bf16[768,768]{1,0:T(8,128)(2,1)}, bf16[768,768]{1,0:T(8,128)(2,1)}, u32[]{:S(2)}, u32[]{:S(2)}) collective-permute-start(bf16[768,768]{1,0:T(8,128)(2,1)} %fusion.19), channel_id=1, source_target_pairs={{0,2},{1,3},{2,0},{3,1},{4,6},{5,7},{6,4},{7,5},{8,10},{9,11},{10,... | collective-permute-start | bytes 3538952 | tf_op jit(solution)/shard_map/ppermute | solution.py:23
  346.7 41.0 %collective-permute-start.54 = (bf16[2,384,768]{2,1,0:T(8,128)(2,1)S(1)}, bf16[2,384,768]{2,1,0:T(8,128)(2,1)}, u32[]{:S(2)}, u32[]{:S(2)}) collective-permute-start(bf16[2,384,768]{2,1,0:T(8,128)(2,1)S(1)} %add_convert_fusion.5), channel_id=1, source_target_pairs={{0,4},{4,0},{8,12},{12,8},{16,20},{20,16},{24,28},{28,24},{1,5},{5... | collective-permute-start | bytes 3538952 | tf_op jit(solution)/shard_map/ppermute | solution.py:23
  397.5 41.8 %collective-permute-start.55 = (bf16[384,768]{1,0:T(8,128)(2,1)}, bf16[384,768]{1,0:T(8,128)(2,1)S(1)}, u32[]{:S(2)}, u32[]{:S(2)}) collective-permute-start(bf16[384,768]{1,0:T(8,128)(2,1)} %slice.565), channel_id=1, source_target_pairs={{0,4},{4,0},{8,12},{12,8},{16,20},{20,16},{24,28},{28,24},{1,5},{5... | collective-permute-start | bytes 1769480 | tf_op jit(solution)/shard_map/ppermute | solution.py:23
  399.5 39.7 %collective-permute-start.56 = (bf16[384,768]{1,0:T(8,128)(2,1)}, bf16[384,768]{1,0:T(8,128)(2,1)}, u32[]{:S(2)}, u32[]{:S(2)}) collective-permute-start(bf16[384,768]{1,0:T(8,128)(2,1)} %slice_bitcast_fusion.4), channel_id=1, source_target_pairs={{0,2},{1,3},{2,0},{3,1},{4,6},{5,7},{6,4},{7,5},{8,10},{9,11},{10,... | collective-permute-start | bytes 1769480 | tf_op jit(solution)/shard_map/ppermute | solution.py:23
  401.5 37.8 %collective-permute-start.57 = (bf16[768,384]{0,1:T(8,128)(2,1)}, bf16[768,384]{0,1:T(8,128)(2,1)}, u32[]{:S(2)}, u32[]{:S(2)}) collective-permute-start(bf16[768,384]{0,1:T(8,128)(2,1)} %slice_bitcast_fusion.3), channel_id=1, source_target_pairs={{0,2},{1,3},{2,0},{3,1},{4,6},{5,7},{6,4},{7,5},{8,10},{9,11},{10,... | collective-permute-start | bytes 1769480 | tf_op jit(solution)/shard_map/ppermute | solution.py:23
  403.9 35.4 %collective-permute-start.58 = (bf16[2,384,384]{1,2,0:T(8,128)(2,1)}, bf16[2,384,384]{1,2,0:T(8,128)(2,1)}, u32[]{:S(2)}, u32[]{:S(2)}) collective-permute-start(bf16[2,384,384]{1,2,0:T(8,128)(2,1)} %slice.572), channel_id=1, source_target_pairs={{0,4},{4,0},{8,12},{12,8},{16,20},{20,16},{24,28},{28,24},{1,5},{5... | collective-permute-start | bytes 1769480 | tf_op jit(solution)/shard_map/ppermute | solution.py:23
  439.3 25.1 %collective-permute-start.60 = (bf16[4,768,768]{2,1,0:T(8,128)(2,1)}, bf16[4,768,768]{2,1,0:T(8,128)(2,1)}, u32[]{:S(2)}, u32[]{:S(2)}) collective-permute-start(bf16[4,768,768]{2,1,0:T(8,128)(2,1)} %get-tuple-element.466), channel_id=1, source_target_pairs={{0,1},{1,0},{2,3},{3,2},{4,5},{5,4},{6,7},{7,6},{8,9},{9,8},{10,11... | collective-permute-start | bytes 14155784 | tf_op jit(solution)/shard_map/ppermute | solution.py:23
  442.8 14.1 %collective-permute-start.68 = (bf16[768,768]{1,0:T(8,128)(2,1)S(1)}, bf16[768,768]{1,0:T(8,128)(2,1)S(1)}, u32[]{:S(2)}, u32[]{:S(2)}) collective-permute-start(bf16[768,768]{1,0:T(8,128)(2,1)S(1)} %copy-done.5), channel_id=1, source_target_pairs={{0,1},{1,0},{2,3},{3,2},{4,5},{5,4},{6,7},{7,6},{8,9},{9,8},{10,11... | collective-permute-start | bytes 3538952 | tf_op jit(solution)/shard_map/ppermute | solution.py:23
  447.1 12.8 %collective-permute-start.61 = (bf16[384,384]{0,1:T(8,128)(2,1)}, bf16[384,384]{0,1:T(8,128)(2,1)}, u32[]{:S(2)}, u32[]{:S(2)}) collective-permute-start(bf16[384,384]{0,1:T(8,128)(2,1)} %slice.578), channel_id=1, source_target_pairs={{0,4},{4,0},{8,12},{12,8},{16,20},{20,16},{24,28},{28,24},{1,5},{5... | collective-permute-start | bytes 884744 | tf_op jit(solution)/shard_map/ppermute | solution.py:23
  449.0 10.9 %collective-permute-start.62 = (bf16[384,384]{0,1:T(8,128)(2,1)}, bf16[384,384]{0,1:T(8,128)(2,1)}, u32[]{:S(2)}, u32[]{:S(2)}) collective-permute-start(bf16[384,384]{0,1:T(8,128)(2,1)} %slice_bitcast_fusion.5), channel_id=1, source_target_pairs={{0,2},{1,3},{2,0},{3,1},{4,6},{5,7},{6,4},{7,5},{8,10},{9,11},{10,... | collective-permute-start | bytes 884744 | tf_op jit(solution)/shard_map/ppermute | solution.py:23
  449.6 14.8 %collective-permute-start.63 = (bf16[192,1536]{1,0:T(8,128)(2,1)S(1)}, bf16[192,1536]{1,0:T(8,128)(2,1)S(1)}, u32[]{:S(2)}, u32[]{:S(2)}) collective-permute-start(bf16[192,1536]{1,0:T(8,128)(2,1)S(1)} %slice.580), channel_id=1, source_target_pairs={{0,8},{4,12},{8,0},{12,4},{16,24},{20,28},{24,16},{28,20},{1,9},{5... | collective-permute-start | bytes 1769480 | tf_op jit(solution)/shard_map/ppermute | solution.py:23
  470.0 40.9 %collective-permute-start.64 = (bf16[768,768]{1,0:T(8,128)(2,1)}, bf16[768,768]{1,0:T(8,128)(2,1)}, u32[]{:S(2)}, u32[]{:S(2)}) collective-permute-start(bf16[768,768]{1,0:T(8,128)(2,1)} %fusion.20), channel_id=1, source_target_pairs={{0,2},{1,3},{2,0},{3,1},{4,6},{5,7},{6,4},{7,5},{8,10},{9,11},{10,... | collective-permute-start | bytes 3538952 | tf_op jit(solution)/shard_map/ppermute | solution.py:23
  471.7 39.3 %collective-permute-start.65 = (bf16[2,384,768]{2,1,0:T(8,128)(2,1)S(1)}, bf16[2,384,768]{2,1,0:T(8,128)(2,1)}, u32[]{:S(2)}, u32[]{:S(2)}) collective-permute-start(bf16[2,384,768]{2,1,0:T(8,128)(2,1)S(1)} %add_convert_fusion.2), channel_id=1, source_target_pairs={{0,4},{4,0},{8,12},{12,8},{16,20},{20,16},{24,28},{28,24},{1,5},{5... | collective-permute-start | bytes 3538952 | tf_op jit(solution)/shard_map/ppermute | solution.py:23
  476.1 34.8 %collective-permute-start.66 = (bf16[192,768]{0,1:T(8,128)(2,1)}, bf16[192,768]{0,1:T(8,128)(2,1)}, u32[]{:S(2)}, u32[]{:S(2)}) collective-permute-start(bf16[192,768]{0,1:T(8,128)(2,1)} %slice.589), channel_id=1, source_target_pairs={{0,8},{4,12},{8,0},{12,4},{16,24},{20,28},{24,16},{28,20},{1,9},{5... | collective-permute-start | bytes 884744 | tf_op jit(solution)/shard_map/ppermute | solution.py:23
  478.6 32.3 %collective-permute-start.67 = (bf16[96,1536]{1,0:T(8,128)(2,1)}, bf16[96,1536]{1,0:T(8,128)(2,1)}, u32[]{:S(2)}, u32[]{:S(2)}) collective-permute-start(bf16[96,1536]{1,0:T(8,128)(2,1)} %slice.590), channel_id=1, source_target_pairs={{0,16},{4,20},{8,24},{12,28},{16,0},{20,4},{24,8},{28,12},{1,17},{... | collective-permute-start | bytes 884744 | tf_op jit(solution)/shard_map/ppermute | solution.py:23
  517.2 44.7 %collective-permute-start.69 = (bf16[384,768]{1,0:T(8,128)(2,1)}, bf16[384,768]{1,0:T(8,128)(2,1)}, u32[]{:S(2)}, u32[]{:S(2)}) collective-permute-start(bf16[384,768]{1,0:T(8,128)(2,1)} %slice.593), channel_id=1, source_target_pairs={{0,4},{4,0},{8,12},{12,8},{16,20},{20,16},{24,28},{28,24},{1,5},{5... | collective-permute-start | bytes 1769480 | tf_op jit(solution)/shard_map/ppermute | solution.py:23
  521.2 40.7 %collective-permute-start.72 = (bf16[768,768]{0,1:T(8,128)(2,1)}, bf16[768,768]{0,1:T(8,128)(2,1)}, u32[]{:S(2)}, u32[]{:S(2)}) collective-permute-start(bf16[768,768]{0,1:T(8,128)(2,1)} %pad_maximum_fusion.12), channel_id=1, source_target_pairs={{0,2},{1,3},{2,0},{3,1},{4,6},{5,7},{6,4},{7,5},{8,10},{9,11},{10,... | collective-permute-start | bytes 3538952 | tf_op jit(solution)/shard_map/ppermute | solution.py:23
  522.5 39.3 %collective-permute-start.70 = (bf16[384,768]{1,0:T(8,128)(2,1)}, bf16[384,768]{1,0:T(8,128)(2,1)}, u32[]{:S(2)}, u32[]{:S(2)}) collective-permute-start(bf16[384,768]{1,0:T(8,128)(2,1)} %slice_bitcast_fusion.2), channel_id=1, source_target_pairs={{0,2},{1,3},{2,0},{3,1},{4,6},{5,7},{6,4},{7,5},{8,10},{9,11},{10,... | collective-permute-start | bytes 1769480 | tf_op jit(solution)/shard_map/ppermute | solution.py:23
  527.2 34.6 %collective-permute-start.71 = (bf16[96,768]{0,1:T(8,128)(2,1)S(1)}, bf16[96,768]{0,1:T(8,128)(2,1)S(1)}, u32[]{:S(2)}, u32[]{:S(2)}) collective-permute-start(bf16[96,768]{0,1:T(8,128)(2,1)S(1)} %slice.597), channel_id=1, source_target_pairs={{0,16},{4,20},{8,24},{12,28},{16,0},{20,4},{24,8},{28,12},{1,17},{... | collective-permute-start | bytes 442376 | tf_op jit(solution)/shard_map/ppermute | solution.py:23
  569.6 31.3 %collective-permute-start.73 = (bf16[768,768]{1,0:T(8,128)(2,1)}, bf16[768,768]{1,0:T(8,128)(2,1)S(1)}, u32[]{:S(2)}, u32[]{:S(2)}) collective-permute-start(bf16[768,768]{1,0:T(8,128)(2,1)} %get-tuple-element.511), channel_id=1, source_target_pairs={{0,1},{1,0},{2,3},{3,2},{4,5},{5,4},{6,7},{7,6},{8,9},{9,8},{10,11... | collective-permute-start | bytes 3538952 | tf_op jit(solution)/shard_map/ppermute | solution.py:23
  580.3 14.9 %collective-permute-start.74 = (bf16[384,768]{0,1:T(8,128)(2,1)S(1)}, bf16[384,768]{0,1:T(8,128)(2,1)S(1)}, u32[]{:S(2)}, u32[]{:S(2)}) collective-permute-start(bf16[384,768]{0,1:T(8,128)(2,1)S(1)} %slice.706), channel_id=1, source_target_pairs={{0,4},{4,0},{8,12},{12,8},{16,20},{20,16},{24,28},{28,24},{1,5},{5... | collective-permute-start | bytes 1769480 | tf_op jit(solution)/shard_map/ppermute | solution.py:23
  584.1 14.9 %collective-permute-start.75 = (bf16[192,1536]{1,0:T(8,128)(2,1)S(1)}, bf16[192,1536]{1,0:T(8,128)(2,1)S(1)}, u32[]{:S(2)}, u32[]{:S(2)}) collective-permute-start(bf16[192,1536]{1,0:T(8,128)(2,1)S(1)} %slice.707), channel_id=1, source_target_pairs={{0,8},{4,12},{8,0},{12,4},{16,24},{20,28},{24,16},{28,20},{1,9},{5... | collective-permute-start | bytes 1769480 | tf_op jit(solution)/shard_map/ppermute | solution.py:23
  610.6 19.8 %collective-permute-start.78 = (bf16[384,768]{1,0:T(8,128)(2,1)S(1)}, bf16[384,768]{1,0:T(8,128)(2,1)S(1)}, u32[]{:S(2)}, u32[]{:S(2)}) collective-permute-start(bf16[384,768]{1,0:T(8,128)(2,1)S(1)} %slice.894), channel_id=1, source_target_pairs={{0,2},{1,3},{2,0},{3,1},{4,6},{5,7},{6,4},{7,5},{8,10},{9,11},{10,... | collective-permute-start | bytes 1769480 | tf_op jit(solution)/shard_map/ppermute | solution.py:23
  614.4 16.1 %collective-permute-start.76 = (bf16[192,768]{0,1:T(8,128)(2,1)S(1)}, bf16[192,768]{0,1:T(8,128)(2,1)S(1)}, u32[]{:S(2)}, u32[]{:S(2)}) collective-permute-start(bf16[192,768]{0,1:T(8,128)(2,1)S(1)} %slice.623), channel_id=1, source_target_pairs={{0,8},{4,12},{8,0},{12,4},{16,24},{20,28},{24,16},{28,20},{1,9},{5... | collective-permute-start | bytes 884744 | tf_op jit(solution)/shard_map/ppermute | solution.py:23
  614.8 15.7 %collective-permute-start.77 = (bf16[96,1536]{1,0:T(8,128)(2,1)S(1)}, bf16[96,1536]{1,0:T(8,128)(2,1)S(1)}, u32[]{:S(2)}, u32[]{:S(2)}) collective-permute-start(bf16[96,1536]{1,0:T(8,128)(2,1)S(1)} %slice.624), channel_id=1, source_target_pairs={{0,16},{4,20},{8,24},{12,28},{16,0},{20,4},{24,8},{28,12},{1,17},{... | collective-permute-start | bytes 884744 | tf_op jit(solution)/shard_map/ppermute | solution.py:23
  618.0 8.7 %collective-permute-start.80 = (f32[18,768]{1,0:T(8,128)S(1)}, f32[18,768]{1,0:T(8,128)S(1)}, u32[]{:S(2)}, u32[]{:S(2)}) collective-permute-start(f32[18,768]{1,0:T(8,128)S(1)} %get-tuple-element.531), channel_id=1, source_target_pairs={{0,2},{1,3},{2,0},{3,1},{4,6},{5,7},{6,4},{7,5},{8,10},{9,11},{10,... | collective-permute-start | bytes 165896 | tf_op jit(solution)/shard_map/ppermute | solution.py:23
  630.8 10.9 %collective-permute-start.82 = (bf16[96,768]{0,1:T(8,128)(2,1)S(1)}, bf16[96,768]{0,1:T(8,128)(2,1)S(1)}, u32[]{:S(2)}, u32[]{:S(2)}) collective-permute-start(bf16[96,768]{0,1:T(8,128)(2,1)S(1)} %slice.630), channel_id=1, source_target_pairs={{0,16},{4,20},{8,24},{12,28},{16,0},{20,4},{24,8},{28,12},{1,17},{... | collective-permute-start | bytes 442376 | tf_op jit(solution)/shard_map/ppermute | solution.py:23
  (150 other events, 700.7 us)

commit v7 on v6

--- a/solution.py
+++ b/solution.py
@@ -321,7 +321,7 @@
     return pl.BlockSpec(shape, lambda j: (0,) * len(shape), pipeline_mode=pl.Buffered(1))
 
 
-def attend_kernel(row_count, quarter, step, first, *refs):
+def attend_kernel(row_count, quarter, step, row, first, *refs):
     normed_a, normed_b, w_qk, w_vo, bias = refs[:5]
     if first:
         qkv, o, lse, q_s, k_s, v_s, o_s = refs[5:]
@@ -336,8 +336,10 @@
     scale = jnp.where(lane < wide, HD**-0.5 * LOG2E, 1.0)
     for half, normed in enumerate((normed_a, normed_b)):
         at = pl.ds(half * rows, rows)
-        qk = ((nn_dot(normed[...], w_qk[...]) + bias[0:1, :]) * scale).astype(bf16)
-        v = (nn_dot(normed[...], w_vo[:, :wide]) + bias[1:2, :wide]).astype(bf16)
+        qk = nn_dot(normed[...], w_qk[...]) + bias[row : row + 1, : 2 * wide]
+        qk = (qk * scale).astype(bf16)
+        v = nn_dot(normed[...], w_vo[:, :wide]) + bias[row + 1 : row + 2, :wide]
+        v = v.astype(bf16)
         qkv[at, : 2 * wide] = qk
         qkv[at, 2 * wide :] = v
         for h in range(heads):
@@ -368,7 +370,7 @@
             share[...] = value.astype(share.dtype)
 
 
-def attend(row_count, quarter, normed_a, normed_b, w_qk, w_vo, bias, before):
+def attend(row_count, quarter, row, normed_a, normed_b, w_qk, w_vo, bias, before):
     rows, width = normed_a.shape
     wide = w_qk.shape[1] // 2
     heads = wide // HD
@@ -381,7 +383,7 @@
     if before:
         outs = [jax.ShapeDtypeStruct((rows, width), kind) for kind in (f32, bf16)] + outs
     return pl.pallas_call(
-        functools.partial(attend_kernel, row_count, quarter, min(512, 2 * rows), not before),
+        functools.partial(attend_kernel, row_count, quarter, min(512, 2 * rows), row, not before),
         grid=(1,),
         in_specs=[single(part.shape) for part in operands],
         out_specs=[whole(part.shape) for part in outs],
@@ -395,10 +397,10 @@
 def attend_back_kernel(row_count, quarter, step, first, *refs):
     branch_a, branch_b, w_qk, w_vo, qkv, o, lse = refs[:7]
     if first:
-        dqkv, q_s, k_s, kt_s, v_s, do_s, dq_s, dk_s, dv_s = refs[7:]
+        dqkv, sums, q_s, k_s, kt_s, v_s, do_s, dq_s, dk_s, dv_s = refs[7:]
     else:
         dqkv_before, w_qk_before, w_vo_before, dn_a, dn_b = refs[7:12]
-        dqkv, q_s, k_s, kt_s, v_s, do_s, dq_s, dk_s, dv_s = refs[12:]
+        dqkv, sums, q_s, k_s, kt_s, v_s, do_s, dq_s, dk_s, dv_s = refs[12:]
     rows = branch_a.shape[0]
     wide = o.shape[1]
     heads = wide // HD
@@ -451,6 +453,8 @@
         dqkv[:, low:high] = (dq_s[h][:, :HD] * HD**-0.5).astype(bf16)
         dqkv[:, wide + low : wide + high] = (dk_s[h][:, :HD] * LN2).astype(bf16)
         dqkv[:, 2 * wide + low : 2 * wide + high] = dv_s[h][:, :HD].astype(bf16)
+    sums[...] = jnp.zeros_like(sums)
+    sums[0:1, :] = jnp.sum(dqkv[...].astype(f32), axis=0, keepdims=True)
     if not first:
         for half, dest in enumerate((dn_a, dn_b)):
             at = pl.ds(half * rows, rows)
@@ -466,7 +470,10 @@
     wide = o.shape[1]
     heads = wide // HD
     operands = (branch_a, branch_b, w_qk, w_vo, qkv, o, lse, *before)
-    outs = [jax.ShapeDtypeStruct((2 * rows, 3 * wide), bf16)]
+    outs = [
+        jax.ShapeDtypeStruct((2 * rows, 3 * wide), bf16),
+        jax.ShapeDtypeStruct((8, 3 * wide), f32),
+    ]
     if before:
         outs = [jax.ShapeDtypeStruct((rows, width), kind) for kind in (f32, bf16)] + outs
     return pl.pallas_call(
@@ -513,7 +520,9 @@
     return (value * share).astype(bf16), (share + value * density).astype(bf16)
 
 
-def feed_kernel(final, *refs):
+def feed_kernel(at, layers, *refs):
+    final = at == layers - 1
+    gain, shift, obias = 2 * at, 2 * layers + 2 * at, 4 * layers + 2 * at
     current, share_a, share_b, vectors, bias = refs[:5]
     ups, downs, activated, slopes = [refs[5 + 4 * i : 9 + 4 * i] for i in range(4)]
     middle, normed, total = refs[21:24]
@@ -521,14 +530,16 @@
 
     @pl.when(j == 0)
     def _():
-        value = current[...] + (share_a[...] + share_b[...].astype(f32) + vectors[0:1, :])
+        value = current[...] + (share_a[...] + share_b[...].astype(f32) + vectors[obias : obias + 1, :])
         middle[...] = value
-        normed[...] = (normalized(value)[0] * vectors[1:2, :] + vectors[2:3, :]).astype(bf16)
-        total[...] = value + vectors[3:4, :]
+        unit, _ = normalized(value)
+        unit = unit * vectors[gain + 1 : gain + 2, :] + vectors[shift + 1 : shift + 2, :]
+        normed[...] = unit.astype(bf16)
+        total[...] = value + vectors[obias + 1 : obias + 2, :]
 
     rows_in = normed[...]
     for t in range(4):
-        upward = nn_dot(rows_in, ups[t][...]) + bias[t : t + 1, :]
+        upward = nn_dot(rows_in, ups[t][...]) + bias[t * layers + at : t * layers + at + 1, :]
         activated[t][...], slopes[t][...] = gelu_both(upward)
     joined = jnp.concatenate([ref[...] for ref in activated], axis=1)
     down = jnp.concatenate([ref[...] for ref in downs], axis=1)
@@ -539,24 +550,25 @@
         @pl.when(j == pl.num_programs(0) - 1)
         def _():
             unit, _ = normalized(total[...])
-            following[...] = (unit * vectors[4:5, :] + vectors[5:6, :]).astype(bf16)
+            unit = unit * vectors[gain + 2 : gain + 3, :] + vectors[shift + 2 : shift + 3, :]
+            following[...] = unit.astype(bf16)
 
 
 def column_block(rows, step):
     return pl.BlockSpec((rows, step), lambda j: (0, j))
 
 
-def feed(final, current, share_a, share_b, vectors, bias, ups, downs):
+def feed(at, layers, current, share_a, share_b, vectors, bias, ups, downs):
     rows, width = current.shape
-    hidden = bias.shape[1]
+    hidden = ups[0].shape[1]
     step = min(256, hidden)
-    rest = [f32, bf16, f32] if final else [f32, bf16, f32, bf16]
+    rest = [f32, bf16, f32] if at == layers - 1 else [f32, bf16, f32, bf16]
     fronts = (current, share_a, share_b, vectors)
     return pl.pallas_call(
-        functools.partial(feed_kernel, final),
+        functools.partial(feed_kernel, at, layers),
         grid=(hidden // step,),
         in_specs=[single(part.shape) for part in fronts]
-        + [column_block(4, step)]
+        + [column_block(bias.shape[0], step)]
         + [column_block(width, step)] * 8,
         out_specs=[column_block(rows, step)] * 8 + [whole((rows, width))] * len(rest),
         out_shape=[jax.ShapeDtypeStruct((rows, hidden), bf16)] * 8
@@ -565,7 +577,9 @@
     )(*fronts, bias, *ups, *downs)
 
 
-def feed_back_kernel(final, *refs):
+def feed_back_kernel(at, layers, *refs):
+    final = at == layers - 1
+    gain = 2 * at
     count = 1 if final else 4
     fronts, refs = refs[:count], refs[count:]
     middle, normed, vectors = refs[:3]
@@ -582,7 +596,9 @@
         else:
             above, layer_out, share_a, share_b = fronts
             grad_normed = share_a[...] + share_b[...].astype(f32)
-            value, gain_one, shift_one = norm_back(layer_out[...], vectors[1:2, :], grad_normed)
+            value, gain_one, shift_one = norm_back(
+                layer_out[...], vectors[gain + 2 : gain + 3, :], grad_normed
+            )
             value = value + above[...]
             sums[4:5, :], sums[5:6, :] = gain_one, shift_one
         grad[...] = value
@@ -609,7 +625,9 @@
 
     @pl.when(j == pl.num_programs(0) - 1)
     def _():
-        value, gain_two, shift_two = norm_back(middle[...], vectors[0:1, :], total[...])
+        value, gain_two, shift_two = norm_back(
+            middle[...], vectors[gain + 1 : gain + 2, :], total[...]
+        )
         value = value + grad[...]
         grad_out[...] = value
         low = value.astype(bf16)
@@ -618,14 +636,14 @@
         sums[3:4, :] = jnp.sum(low.astype(f32), axis=0, keepdims=True)
 
 
-def feed_back(final, fronts, middle, normed, vectors, ups, downs, activated, slopes):
+def feed_back(at, layers, fronts, middle, normed, vectors, ups, downs, activated, slopes):
     rows, width = normed.shape
     hidden = activated[0].shape[1]
     step = min(256, hidden)
     stack = pl.BlockSpec((4, width, step), lambda j: (0, 0, j))
     singles = (*fronts, middle, normed, vectors)
     return pl.pallas_call(
-        functools.partial(feed_back_kernel, final),
+        functools.partial(feed_back_kernel, at, layers),
         grid=(hidden // step,),
         in_specs=[single(part.shape) for part in singles]
         + [column_block(width, step)] * 8
@@ -674,32 +692,17 @@
     block_at = relative_mask(jnp.arange(count_dp)) ^ me
 
     norm_part, up_part, qv_part = norm_gains.shape[2], up_bias.shape[1], qv_bias.shape[2]
-    lanes = max(4 * norm_part, up_part)
 
     def place(part, size, at):
         room = jnp.zeros((part.shape[0], size), f32)
         return lax.dynamic_update_slice(room, part, (0, at))
 
-    def to_lanes(part):
-        return jnp.pad(part, ((0, 0), (0, lanes - part.shape[1])))
-
     by_width = jnp.stack([norm_gains, norm_shifts, out_biases]).reshape(6 * layers, norm_part)
-    by_width = to_lanes(place(by_width, 4 * norm_part, t_me * norm_part))
-    own = jnp.concatenate(
-        [by_width, to_lanes(qv_bias.reshape(2 * layers, qv_part)), to_lanes(up_bias)]
-    )
-    cut, end = 6 * layers, 8 * layers
-    got = exchange(own, "tensor", 1)
-    own = jnp.concatenate([own[:cut] + got[:cut], own[cut:], got[end:]])
-    got = exchange(own, "tensor", 2)
-    frames, got = together(frames, got)
-    by_width = (own[:cut] + got[:cut])[:, : 4 * norm_part]
+    by_width = place(by_width, 4 * norm_part, t_me * norm_part)
     by_hidden = jnp.concatenate(
         [
-            place(jnp.concatenate([own[end:], got[end:]])[:, :up_part], hidden, me * up_part),
-            place(
-                jnp.concatenate([own[cut:end], got[cut:end]])[:, :qv_part], hidden, me * qv_part
-            ),
+            place(up_bias, width, me * up_part),
+            place(qv_bias.reshape(2 * layers, qv_part), width, me * qv_part),
         ]
     )
 
@@ -737,20 +740,23 @@
         vo = jnp.concatenate([qkv_weight[at, :, 2], out_weight[at].T], axis=1)
         groups += [(qk, vo), (up_weight[at], down_weight[at].T)]
     gathering = Gathering(groups)
-    by_width, by_hidden = gathering.advance(by_width, by_hidden)
-    for at, mask in enumerate(dp_masks()):
+    for mask in dp_masks():
         got = exchange(by_width, "dp", mask), exchange(by_hidden, "dp", mask)
-        if mask > 2:
+        if mask == 2:
+            got = gathering.advance(*got)
+        else:
             got = together(*got)
-        elif mask == 2:
-            *got, clip = gathering.advance(*got, clip)
-        else:
-            got = got[0], *gathering.advance(got[1])
         by_width = jnp.concatenate([by_width, got[0]], axis=1)
         by_hidden = by_hidden + got[1]
-    gain_all, shift_all, obias_all = by_width.reshape(3, layers, 2, width)
-    up_all = by_hidden[: 4 * layers].reshape(4, layers, hidden).transpose(1, 0, 2)
-    qv_all = by_hidden[4 * layers :, :wide].reshape(2, layers, 2, wide).transpose(1, 0, 2, 3)
+    cut = 6 * layers
+    own = jnp.concatenate([by_width, by_hidden])
+    got, clip = gathering.advance(exchange(own[: cut + layers], "tensor", 1), clip)
+    own = jnp.concatenate([own[:cut] + got[:cut], own[cut : cut + layers], got[cut:], own[cut + layers :]])
+    (got,) = gathering.advance(exchange(own, "tensor", 2))
+    vectors = own[:cut] + got[:cut]
+    end = cut + 2 * layers
+    biases = jnp.concatenate([own[cut:end], got[cut:end], own[end:], got[end:]])
+    gain_all, shift_all = vectors[: 2 * layers], vectors[2 * layers : 4 * layers]
 
     def feed_weights(group):
         parts = gathering.until(group)
@@ -762,37 +768,25 @@
     weights = []
     saved = []
     unit, _ = normalized(current)
-    normed_a = (unit * gain_all[0, 0] + shift_all[0, 0]).astype(bf16)
+    normed_a = (unit * gain_all[0] + shift_all[0]).astype(bf16)
     (normed_b,) = gathering.advance(exchange(normed_a, "tensor", 1))
     for at in range(layers):
         final = at == layers - 1
         w_qk, w_qk_other, w_vo, w_vo_other = gathering.until(2 * at)
         w_attn = ((w_qk, w_vo), (w_qk_other, w_vo_other))
-        bias = jnp.pad(qv_all[at], ((0, 0), (0, 0), (0, wide)))
         heads = []
         for t in range(2):
             before = (heads[0][1], w_attn[0][1]) if t else ()
             ready = behind((normed_a, normed_b), *gathering.tokens, *before[:1])
-            out = attend(row_count, quarter, *ready, *w_attn[t], bias[t], before)
+            row = 4 * layers + 2 * (t * layers + at)
+            out = attend(row_count, quarter, row, *ready, *w_attn[t], biases, before)
             *shares, qkv, o, lse = gathering.advance(*out)
             heads.append((qkv, o, lse))
         share_b = exchange(shares[1], "tensor", 1)
         if not final:
             (share_b,) = gathering.advance(share_b)
         w_up, w_down = feed_weights(2 * at + 1)
-        following = 0 if final else at + 1
-        vectors = jnp.stack(
-            [
-                obias_all[at, 0],
-                gain_all[at, 1],
-                shift_all[at, 1],
-                obias_all[at, 1],
-                gain_all[following, 0],
-                shift_all[following, 0],
-            ]
-        )
-        vectors = jnp.pad(vectors, ((0, 2), (0, 0)))
-        fed = feed(final, current, shares[0], share_b, vectors, up_all[at], w_up, w_down)
+        fed = feed(at, layers, current, shares[0], share_b, vectors, biases, w_up, w_down)
         if not final:
             fed = gathering.advance(*fed, *([exchange(clip, "tensor", 2)] if at == 0 else []))
             if at == 0:
@@ -808,7 +802,6 @@
         clip = exchange(clip, "tensor", 2)
     small_grads = [None] * layers
     weight_grads = [None] * layers
-    gains_one = [None] * layers
     folding = None
     fronts = (take_clip(cotangent, clip),)
     for at in reversed(range(layers)):
@@ -816,25 +809,21 @@
         w_attn, w_up, w_down = weights[at]
         layer_in, normed, heads, activated, slopes, middle, normed_two = saved[at]
         uppers = [] if folding is None else [folding]
-        vectors = jnp.stack([gain_all[at, 1], gain_all[0 if final else at + 1, 0]])
-        vectors = jnp.pad(vectors, ((0, 6), (0, 0)))
         if uppers:
             fronts = behind(fronts, *folding.tokens())
         fed = feed_back(
-            final, fronts, middle, normed_two, vectors, w_up, w_down, activated, slopes
+            at, layers, fronts, middle, normed_two, vectors, w_up, w_down, activated, slopes
         )
         if final:
             *fed, encoded_half = together(*fed, give_half(current))
         own, other, bup, gradient, branch_a, sums = advance(uppers, *fed)
-        if not final:
-            gains_one[at + 1] = sums[4:6]
         branch_b = exchange(branch_a, "tensor", 1)
         core = Folding(own, other)
-        branch = jnp.concatenate([branch_a, branch_b], axis=0)
 
         def weight_grad(t, dqkv):
             dw = tn_dot(normed, dqkv).astype(bf16)
-            dw_o = tn_dot(branch, heads[t][1]).astype(bf16)
+            o = heads[t][1]
+            dw_o = (tn_dot(branch_a, o[:rows]) + tn_dot(branch_b, o[rows:])).astype(bf16)
             return dw[:, : 2 * wide], jnp.concatenate([dw[:, 2 * wide :], dw_o], axis=1)
 
         def state_tokens():
@@ -845,7 +834,7 @@
         elif uppers:
             advance(uppers)
         ready = behind((branch_a, branch_b), *state_tokens())
-        (dqkv_other,) = advance(
+        dqkv_other, sums_other = advance(
             [core, *uppers],
             *attend_back(row_count, quarter, *ready, *w_attn[1], *heads[1], ()),
         )
@@ -855,7 +844,7 @@
         else:
             sent, got = dqkv_other, ()
         ready = behind((branch_a, branch_b), sent, *state_tokens())
-        *got, share_a, share_b, dqkv_own = advance(
+        *got, share_a, share_b, dqkv_own, sums_own = advance(
             [core, *uppers],
             *got,
             *attend_back(
@@ -874,38 +863,43 @@
             core.attn = together(*[jnp.stack(pair) for pair in zip(dw_own, dw_other)])
             folding = core
         fronts = (gradient, layer_in, share_a, share_b)
-        small_grads[at] = (sums, (dqkv_own, dqkv_other), bup)
+        small_grads[at] = (sums, (sums_own, sums_other), bup)
     grad_in, *last_sums = norm_back(
-        layer_in, gain_all[0, 0], share_a + share_b.astype(f32)
+        layer_in, gain_all[0], share_a + share_b.astype(f32)
     )
     gradient = gradient + grad_in
-    gains_one[0] = jnp.concatenate(last_sums, axis=0)
-    pairs = behind(
-        [part for at in range(1, layers) for part in small_grads[at][1]], *small_grads[0][1]
-    )
-    pairs = [*small_grads[0][1], *pairs]
-    bqv = jnp.stack([jnp.sum(part, axis=0, dtype=f32) for part in pairs])
-    bqv = bqv.reshape(layers, 2, 3, count_dp, qv_part)[:, :, 0::2].transpose(1, 0, 2, 3, 4)
-    bqv = jnp.pad(bqv, ((0, 0),) * 4 + ((0, block - qv_part),)).reshape(4 * layers, width)
-    sums, bups = [jnp.stack([small_grads[at][i] for at in range(layers)]) for i in (0, 2)]
-    bups = bups.reshape(layers, 4, count_dp, up_part).transpose(1, 0, 2, 3)
-    bups = jnp.pad(bups, ((0, 0),) * 3 + ((0, block - up_part),)).reshape(4 * layers, width)
-    by_hidden = lax.dot_general(
-        jnp.concatenate([bups, bqv]),
-        to_relative.astype(f32),
-        (((1,), (0,)), ((), ())),
-        precision=lax.Precision.HIGHEST,
-        preferred_element_type=f32,
-    )
-    bups, bqv = by_hidden[: 4 * layers], by_hidden[4 * layers :]
-    one = jnp.stack(gains_one)
-    by_width = jnp.stack(
-        [
-            jnp.stack([one[:, 0], sums[:, 1]], axis=1),
-            jnp.stack([one[:, 1], sums[:, 2]], axis=1),
-            jnp.stack([sums[:, 3], sums[:, 0]], axis=1),
-        ]
-    ).reshape(6 * layers, width)
+    lane = jnp.arange(width)
+    head_source = block_at[lane // block] * qv_part + lane % block
+    to_blocks = (jnp.arange(wide)[:, None] == head_source[None, :]) & (lane % block < qv_part)
+    up_source = block_at[lane // block] * up_part + lane % block
+    up_blocks = (jnp.arange(hidden)[:, None] == up_source[None, :]) & (lane % block < up_part)
+
+    def reorder(part, matrix):
+        return lax.dot_general(
+            part,
+            matrix.astype(f32),
+            (((1,), (0,)), ((), ())),
+            precision=lax.Precision.HIGHEST,
+            preferred_element_type=f32,
+        )
+
+    bups = reorder(
+        jnp.concatenate([small_grads[at][2][t : t + 1] for t in range(4) for at in range(layers)]),
+        up_blocks,
+    )
+    bqv = reorder(
+        jnp.concatenate(
+            [
+                small_grads[at][1][t][:1, i * wide : (i + 1) * wide]
+                for t in range(2)
+                for at in range(layers)
+                for i in (0, 2)
+            ]
+        ),
+        to_blocks,
+    )
+    last_sums = jnp.concatenate([*last_sums, jnp.zeros((6, width), f32)])
+    by_width = jnp.concatenate([small_grads[at][0] for at in range(layers)] + [last_sums])
     small = [
         jnp.concatenate(
             [by_width, bups[t * layers : (t + 1) * layers]]
@@ -922,19 +916,30 @@
         give_half(gradient),
         *[exchange(small[t], "tensor", t) for t in range(1, 4)],
     )
-    cut = 6 * layers
+    cut = 8 * layers + 8
     small, more = small[0] + got[1], got[0] + got[2]
     small = jnp.concatenate([small[: cut + layers] + more, small[cut + layers :]])
-    encoded = give_clip(*behind((current, encoded_half), *small_grads[0][1]))
     frames_grad = give_clip(gradient, half)
     for mask in reversed(dp_masks()):
         got = exchange(small[:, small.shape[1] // 2 :], "dp", mask)
         if folding.step < 3:
             (got,) = advance([folding], got)
         small = small[:, : small.shape[1] // 2] + got
+        if folding.step == 3 and mask == 1:
+            small, current, encoded_half = together(small, current, encoded_half)
+    encoded = give_clip(current, encoded_half)
     weight_grads[0] = folding.result()
     by_width = lax.dynamic_slice(small, (0, t_me * norm_part), (cut, norm_part))
-    gains, shifts, obiases = by_width.reshape(3, layers, 2, norm_part)
+    rows_of = [by_width[8 * at : 8 * at + 8] for at in range(layers + 1)]
+    one = [rows_of[at][4:6] for at in range(layers - 1)]
+    one = [rows_of[layers][0:2]] + one
+
+    def pair(make):
+        return jnp.stack([jnp.stack(make(at)) for at in range(layers)])
+
+    gains = pair(lambda at: [one[at][0], rows_of[at][1]])
+    shifts = pair(lambda at: [one[at][1], rows_of[at][2]])
+    obiases = pair(lambda at: [rows_of[at][3], rows_of[at][0]])
     bups = small[cut : cut + layers, :up_part]
     bqv = small[cut + layers :, :qv_part].reshape(layers, 2, qv_part)
 

time: 662 us -> 686 us (1.036)
  local copies, waits for them, and re-layouts: 93.9 us -> 104 us
  waiting for transfers between devices: 78.8 us -> 88.1 us
  other arithmetic: 67.7 us -> 75.6 us
    concatenate x2 -> x7, local copies, waits for them, and re-layouts: 2.44 us -> 22.8 us  [the longest x4 21.5 us: local(): jnp.concatenate([by_width, bups[t * layers:(t + 1) * layers]] + ([bqv[t *...]
    another operation x18 -> x0, local copies, waits for them, and re-layouts: 9.96 us -> none  [the longest x3 2.72 us: local(): jnp.stack([obias_all[at, 0], gain_all[at, 1], shift_all[at, 1], obias_all...]
    ppermute x86, waiting for transfers between devices: 78.8 us -> 88.1 us  [exchange(): return lax.ppermute(value, axis, [(i, i ^ mask) for i in range(count)])]
    reshape x8 -> x0, local copies, waits for them, and re-layouts: 7.72 us -> none  [the longest x2 2 us: local(): by_hidden[4 * layers:, :wide].reshape(2, layers, 2, wide)]
    unnamed x278 -> x277, local copies, waits for them, and re-layouts: 31.6 us -> 37.3 us
    dot_general x8 -> x12, matrix products: 15.1 us -> 18.7 us  [tn_dot(): lax.dot_general(left, right, (((0,), (0,)), ((), ())), preferred_element_...]
  transfers between devices with their start and end apart: 86 -> 86, of which waited for: 24 -> 27; matrix products, arithmetic and copies ran while one was open for 19% -> 17% of each run, Pallas kernels for 43% -> 41%
where the time goes in v7:
time: 686 us; the launch traced here: 676 us
  Pallas kernels  299 us (44%)
  local copies, waits for them, and re-layouts  104 us (15%)
  waiting for transfers between devices  88.1 us (13%)
  starting transfers between devices  76.9 us (11%)
  other arithmetic  75.6 us (11%)
  matrix products  29.5 us (4%)
    pallas_call x4, Pallas kernels, attend_back(): pl.pallas_call(functools.partial(attend_back_kernel, row_count, quarter,...  124 us
    ppermute x86, waiting for transfers between devices, exchange(): return lax.ppermute(value, axis, [(i, i ^ mask) for i in range(count)])  88.1 us
    ppermute x86, starting transfers between devices, exchange(): return lax.ppermute(value, axis, [(i, i ^ mask) for i in range(count)])  76.9 us
    pallas_call x4, Pallas kernels, attend(): pl.pallas_call(functools.partial(attend_kernel, row_count, quarter, min(5...  73.3 us
    pallas_call x2, Pallas kernels, feed_back(): pl.pallas_call(functools.partial(feed_back_kernel, at, layers), grid=(hid...  63.4 us
    pallas_call x2, Pallas kernels, feed(): pl.pallas_call(functools.partial(feed_kernel, at, layers), grid=(hidden /...  38.3 us
    unnamed x277, local copies, waits for them, and re-layouts  37.3 us
    convert_element_type x22, other arithmetic, add_low(): return (kept.astype(f32) + received.astype(f32)).astype(bf16)  30.1 us
  transfers between devices with their start and end apart: 86, of which 27 were waited for; matrix products, arithmetic and copies ran while one was open for 17% of the time, Pallas kernels for 41%

profile of v7, /device:TPU:0, one launch (start us, length us, event | category | flops | bytes accessed | tf_op | source)
XLA Modules:
  0.0 675.7 jit_solution(16256491044810366981)
XLA Ops:
  2.4 4.2 collective-permute-start.2
  10.9 3.0 collective-permute-start
  21.0 1.7 collective-permute-start.4
  23.7 2.9 collective-permute-done.3
  33.4 2.2 collective-permute-done.5
  41.1 2.7 fusion.101
  43.8 2.0 copy.40.refs_0_
  46.3 6.6 collective-permute-done.11
  56.4 2.1 pad_maximum_fusion.14
  65.8 5.3 collective-permute-done.14
  71.1 5.2 collective-permute-done.15
  84.8 17.5 %shard_map.194 = (bf16[1536,576]{1,0:T(8,128)(2,1)}, bf16[1536,192]{1,0:T(8,128)(2,1)}, f32[1536,8]{1,0:T(8,128)}) custom-call(bf16[768,768]{1,0:T(8,128)(2,1)} %copy-done.7, bf16[768,768]{1,0:T(8,128)(2,1)} %copy-done.25, bf16[768,384]{1,0:T(8,128)(2,1)} %copy-done.24, bf16[768,384]{1,0:T(8,128)(2,1)} %copy-done.18, f32[16,768]{1,0:T(8,128)} %concatenate.167.refs_4_), custom_call_target="tpu_custom_call" | custom-call | tf_op jit(solution)/shard_map/pallas_call | solution.py:385
  109.8 19.4 %shard_map.195 = (f32[768,768]{1,0:T(8,128)}, bf16[768,768]{1,0:T(8,128)(2,1)}, bf16[1536,576]{1,0:T(8,128)(2,1)}, bf16[1536,192]{1,0:T(8,128)(2,1)}, f32[1536,8]{1,0:T(8,128)}) custom-call(bf16[768,768]{1,0:T(8,128)(2,1)} %copy-done.7, bf16[768,768]{1,0:T(8,128)(2,1)} %copy-done.25, bf16[768,384]{1,0:T(8,128)(2,1)} %copy-done.22, ...), custom_call_target="tpu_custom_call" | custom-call | tf_op jit(solution)/shard_map/pallas_call | solution.py:385
  138.1 3.7 collective-permute-done.26
  149.6 2.9 collective-permute-start.32
  152.5 19.9 %shard_map.196 = (bf16[768,768]{1,0:T(8,128)(2,1)}, bf16[768,768]{1,0:T(8,128)(2,1)}, bf16[768,768]{1,0:T(8,128)(2,1)}, bf16[768,768]{1,0:T(8,128)(2,1)}, bf16[7...) custom-call(f32[768,768]{1,0:T(8,128)} %copy-done, ...), custom_call_target="tpu_custom_call" | custom-call | tf_op jit(solution)/shard_map/pallas_call | solution.py:567
  175.3 14.3 %collective-permute-done.38 = bf16[192,1536]{1,0:T(8,128)(2,1)S(1)} collective-permute-done((bf16[192,1536]{1,0:T(8,128)(2,1)S(1)}, bf16[192,1536]{1,0:T(8,128)(2,1)S(1)}, u32[]{:S(2)}, u32[]{:S(2)}) %collective-permute-start.38) | collective-permute-done | bytes 589856 | tf_op jit(solution)/shard_map/ppermute | solution.py:23
  194.3 17.2 %shard_map.197 = (bf16[1536,576]{1,0:T(8,128)(2,1)}, bf16[1536,192]{1,0:T(8,128)(2,1)}, f32[1536,8]{1,0:T(8,128)}) custom-call(bf16[768,768]{1,0:T(8,128)(2,1)} %get-tuple-element.385.refs_0_, bf16[768,768]{1,0:T(8,128)(2,1)} %copy-done.9, bf16[768,384]{1,0:T(8,128)(2,1)} %pad_maximum_fusion.15.refs_2_, bf16[768,384]{1,0:T(8,128)(2,1)} %copy-done.19, ...), custom_call_target="tpu_custom_call" | custom-call | tf_op jit(solution)/shard_map/pallas_call | solution.py:385
  218.2 19.2 %shard_map.198 = (f32[768,768]{1,0:T(8,128)}, bf16[768,768]{1,0:T(8,128)(2,1)}, bf16[1536,576]{1,0:T(8,128)(2,1)}, bf16[1536,192]{1,0:T(8,128)(2,1)}, f32[1536,8]{1,0:T(8,128)}) custom-call(bf16[768,768]{1,0:T(8,128)(2,1)} %get-tuple-element.385.refs_0_, bf16[768,768]{1,0:T(8,128)(2,1)} %copy-done.9, bf16[768,384]{1,0:T(8,128)(2,1)} %copy-done.23, ...), custom_call_target="tpu_custom_call" | custom-call | tf_op jit(solution)/shard_map/pallas_call | solution.py:385
  238.6 2.3 collective-permute-done.44
  247.1 3.4 collective-permute-done.45.refs_2_
  251.5 18.4 %shard_map.199 = (bf16[768,768]{1,0:T(8,128)(2,1)}, bf16[768,768]{1,0:T(8,128)(2,1)}, bf16[768,768]{1,0:T(8,128)(2,1)}, bf16[768,768]{1,0:T(8,128)(2,1)}, bf16[7...) custom-call(f32[768,768]{1,0:T(8,128)} %get-tuple-element.455.refs_0, ...), custom_call_target="tpu_custom_call" | custom-call | tf_op jit(solution)/shard_map/pallas_call | solution.py:567
  272.6 2.6 fusion.12.refs_0_
  275.2 29.9 %shard_map.200 = (bf16[4,768,768]{2,1,0:T(8,128)(2,1)}, bf16[4,768,768]{2,1,0:T(8,128)(2,1)}, f32[4,768]{1,0:T(4,128)}, f32[768,768]{1,0:T(8,128)}, bf16[768,768]{1,0:T(8,128)(2,1)}, /*index=5*/f32[8,768]{1,0:T(8,128)}) custom-call(f32[768,768]{1,0:T(8,128)} %fusion.12.refs_0_, f32[768,768]{1,0:T(8,128)} %get-tuple-element.399.refs_1_, ...), custom_call_target="tpu_custom_call" | custom-call | tf_op jit(solution)/shard_map/pallas_call | solution.py:645
  309.0 5.9 collective-permute-done.52.refs_1_
  316.0 28.3 %shard_map.201 = (bf16[1536,576]{1,0:T(8,128)(2,1)}, f32[8,576]{1,0:T(8,128)}) custom-call(bf16[768,768]{1,0:T(8,128)(2,1)} %get-tuple-element.436.refs_0_, bf16[768,768]{1,0:T(8,128)(2,1)} %copy-done.5, bf16[768,384]{1,0:T(8,128)(2,1)} %copy-done.23, bf16[768,384]{1,0:T(8,128)(2,1)} %copy-done.17, bf16[1536,576]{1,0:T(8,128)(2,1)} %get-tuple-element.427.refs_4_, ...), custom_call_target="tpu_custom_call" | custom-call | tf_op jit(solution)/shard_map/pallas_call | solution.py:479
  344.3 1.8 fusion.57
  347.2 3.0 add_convert_fusion.5
  350.2 3.1 fusion.25
  358.1 1.7 convolution_convert_fusion
  360.8 33.4 %shard_map.202 = (f32[768,768]{1,0:T(8,128)}, bf16[768,768]{1,0:T(8,128)(2,1)}, bf16[1536,576]{1,0:T(8,128)(2,1)}, f32[8,576]{1,0:T(8,128)}) custom-call(bf16[768,768]{1,0:T(8,128)(2,1)} %get-tuple-element.436.refs_0_, bf16[768,768]{1,0:T(8,128)(2,1)} %copy-done.5, bf16[768,384]{1,0:T(8,128)(2,1)} %pad_maximum_fusion.15.refs_2_, ...), custom_call_target="tpu_custom_call" | custom-call | tf_op jit(solution)/shard_map/pallas_call | solution.py:479
  395.4 4.0 convolution_convert_fusion.1
  399.5 2.1 add_convert_fusion.4
  401.7 2.5 fusion.5
  412.3 33.5 %shard_map.203 = (bf16[4,768,768]{2,1,0:T(8,128)(2,1)}, bf16[4,768,768]{2,1,0:T(8,128)(2,1)}, f32[4,768]{1,0:T(4,128)}, f32[768,768]{1,0:T(8,128)}, bf16[768,768]{1,0:T(8,128)(2,1)}, /*index=5*/f32[8,768]{1,0:T(8,128)}) custom-call(f32[768,768]{1,0:T(8,128)} %get-tuple-element.454.refs_0_, f32[768,768]{1,0:T(8,128)} %get-tuple-element.455.refs_0_.refs_1_, ...), custom_call_target="tpu_custom_call" | custom-call | tf_op jit(solution)/shard_map/pallas_call | solution.py:645
  446.8 4.3 fusion.71
  467.8 3.3 collective-permute-done.61
  472.0 3.9 collective-permute-done.63
  475.9 2.9 add_convert_fusion.2
  478.9 3.0 fusion.26
  488.7 2.6 collective-permute-start.67
  492.9 28.7 %shard_map.204 = (bf16[1536,576]{1,0:T(8,128)(2,1)}, f32[8,576]{1,0:T(8,128)}) custom-call(bf16[768,768]{1,0:T(8,128)(2,1)} %get-tuple-element.511.refs_0_, bf16[768,768]{1,0:T(8,128)(2,1)} %copy-done.3, bf16[768,384]{1,0:T(8,128)(2,1)} %copy-done.22, bf16[768,384]{1,0:T(8,128)(2,1)} %copy-done.16, bf16[1536,576]{1,0:T(8,128)(2,1)} %get-tuple-element.497.refs_4_, ...), custom_call_target="tpu_custom_call" | custom-call | tf_op jit(solution)/shard_map/pallas_call | solution.py:479
  521.6 3.5 fusion.19
  525.2 2.4 add_convert_fusion.1
  527.6 2.8 fusion.4
  537.1 1.7 add_convert_fusion.17
  541.2 33.2 %shard_map.205 = (f32[768,768]{1,0:T(8,128)}, bf16[768,768]{1,0:T(8,128)(2,1)}, bf16[1536,576]{1,0:T(8,128)(2,1)}, f32[8,576]{1,0:T(8,128)}) custom-call(bf16[768,768]{1,0:T(8,128)(2,1)} %get-tuple-element.511.refs_0_, bf16[768,768]{1,0:T(8,128)(2,1)} %copy-done.3, bf16[768,384]{1,0:T(8,128)(2,1)} %copy-done.24, bf16[768,384]{1,0:T(8,128)(2,1)} %copy-done.18, ...), custom_call_target="tpu_custom_call" | custom-call | tf_op jit(solution)/shard_map/pallas_call | solution.py:479
  588.8 3.4 collective-permute-done.75
  593.0 3.5 collective-permute-done.74
  596.5 2.4 add_convert_fusion.9
  598.9 2.0 add_convert_fusion.8
  600.9 3.4 multiply_reduce_fusion
  604.9 5.4 concatenate.195
  610.3 5.3 concatenate.193
  618.1 5.4 concatenate.194
  623.5 5.4 concatenate.192
  628.9 3.2 multiply_add_fusion
  634.4 2.7 collective-permute-start.77
  640.5 5.8 collective-permute-done.81
  647.5 2.6 collective-permute-start.82
  651.1 2.6 copy.44
  653.7 6.4 collective-permute-done.82
  665.6 2.4 collective-permute-start.85
  669.9 2.6 copy.43
  (610 shorter events, 188.0 us)
Async XLA Ops:
  2.4 18.7 %collective-permute-start.2 = (f32[6,768]{1,0:T(8,128)S(1)}, f32[6,768]{1,0:T(8,128)S(1)}, u32[]{:S(2)}, u32[]{:S(2)}) collective-permute-start(f32[6,768]{1,0:T(8,128)S(1)} %pad_maximum_fusion.32), channel_id=1, source_target_pairs={{0,16},{4,20},{8,24},{12,28},{16,0},{20,4},{24,8},{28,12},{1,17},{... | collective-permute-start | bytes 55304 | tf_op jit(solution)/shard_map/ppermute | solution.py:23
  7.6 13.5 %collective-permute-start.1 = (f32[12,96]{1,0:T(8,128)S(1)}, f32[12,96]{1,0:T(8,128)S(1)}, u32[]{:S(2)}, u32[]{:S(2)}) collective-permute-start(f32[12,96]{1,0:T(8,128)S(1)} %dynamic_update_slice.9), channel_id=1, source_target_pairs={{0,16},{4,20},{8,24},{12,28},{16,0},{20,4},{24,8},{28,12},{1,17},{... | collective-permute-start | bytes 13832 | tf_op jit(solution)/shard_map/ppermute | solution.py:23
  10.9 15.7 %collective-permute-start = (bf16[96,768]{1,0:T(8,128)(2,1)S(1)}, bf16[96,768]{1,0:T(8,128)(2,1)S(1)}, u32[]{:S(2)}, u32[]{:S(2)}) collective-permute-start(bf16[96,768]{1,0:T(8,128)(2,1)S(1)} %pad_maximum_fusion.24), channel_id=1, source_target_pairs={{0,16},{4,20},{8,24},{12,28},{16,0},{20,4},{24,8},{28,12},{1,17},{... | collective-permute-start | bytes 442376 | tf_op jit(solution)/shard_map/ppermute | solution.py:23
  15.7 25.3 %collective-permute-start.17 = (bf16[375,768]{1,0:T(8,128)(2,1)S(1)}, bf16[375,768]{1,0:T(8,128)(2,1)S(1)}, u32[]{:S(2)}, u32[]{:S(2)}) collective-permute-start(bf16[375,768]{1,0:T(8,128)(2,1)S(1)} %get-tuple-element.600), channel_id=1, source_target_pairs={{0,2},{1,3},{2,0},{3,1},{4,6},{5,7},{6,4},{7,5},{8,10},{9,11},{10,... | collective-permute-start | bytes 1728008 | tf_op jit(solution)/shard_map/ppermute | solution.py:23
  36.4 9.9 %collective-permute-start.12 = (f32[20,768]{1,0:T(8,128)}, f32[20,768]{1,0:T(8,128)}, u32[]{:S(2)}, u32[]{:S(2)}) collective-permute-start(f32[20,768]{1,0:T(8,128)} %pad_maximum_fusion.26), channel_id=1, source_target_pairs={{0,2},{1,3},{2,0},{3,1},{4,6},{5,7},{6,4},{7,5},{8,10},{9,11},{10,... | collective-permute-start | bytes 184328 | tf_op jit(solution)/shard_map/ppermute | solution.py:23
  39.2 13.8 %collective-permute-start.11 = (bf16[96,1536]{1,0:T(8,128)(2,1)}, bf16[96,1536]{1,0:T(8,128)(2,1)}, u32[]{:S(2)}, u32[]{:S(2)}) collective-permute-start(bf16[96,1536]{1,0:T(8,128)(2,1)} %get-tuple-element.298), channel_id=1, source_target_pairs={{0,16},{4,20},{8,24},{12,28},{16,0},{20,4},{24,8},{28,12},{1,17},{... | collective-permute-start | bytes 884744 | tf_op jit(solution)/shard_map/ppermute | solution.py:23
  39.5 13.4 %collective-permute-start.9 = (bf16[384,384]{1,0:T(8,128)(2,1)}, bf16[384,384]{1,0:T(8,128)(2,1)}, u32[]{:S(2)}, u32[]{:S(2)}) collective-permute-start(bf16[384,384]{1,0:T(8,128)(2,1)} %get-tuple-element.296), channel_id=1, source_target_pairs={{0,4},{4,0},{8,12},{12,8},{16,20},{20,16},{24,28},{28,24},{1,5},{5... | collective-permute-start | bytes 884744 | tf_op jit(solution)/shard_map/ppermute | solution.py:23
  54.8 21.5 %collective-permute-start.18 = (bf16[768,768]{1,0:T(8,128)(2,1)S(1)}, bf16[768,768]{1,0:T(8,128)(2,1)S(1)}, u32[]{:S(2)}, u32[]{:S(2)}) collective-permute-start(bf16[768,768]{1,0:T(8,128)(2,1)S(1)} %add_convert_fusion.7.refs_0_), channel_id=1, source_target_pairs={{0,1},{1,0},{2,3},{3,2},{4,5},{5,4},{6,7},{7,6},{8,9},{9,8},{10,11... | collective-permute-start | bytes 3538952 | tf_op jit(solution)/shard_map/ppermute | solution.py:23
  58.5 17.8 %collective-permute-start.13 = (bf16[768,384]{1,0:T(8,128)(2,1)S(1)}, bf16[768,384]{1,0:T(8,128)(2,1)S(1)}, u32[]{:S(2)}, u32[]{:S(2)}) collective-permute-start(bf16[768,384]{1,0:T(8,128)(2,1)S(1)} %pad_maximum_fusion.13.refs_2_), channel_id=1, source_target_pairs={{0,2},{1,3},{2,0},{3,1},{4,6},{5,7},{6,4},{7,5},{8,10},{9,11},{10,... | collective-permute-start | bytes 1769480 | tf_op jit(solution)/shard_map/ppermute | solution.py:23
  59.5 16.8 %collective-permute-start.16 = (bf16[192,1536]{1,0:T(8,128)(2,1)}, bf16[192,1536]{1,0:T(8,128)(2,1)}, u32[]{:S(2)}, u32[]{:S(2)}) collective-permute-start(bf16[192,1536]{1,0:T(8,128)(2,1)} %pad_maximum_fusion.14), channel_id=1, source_target_pairs={{0,8},{4,12},{8,0},{12,4},{16,24},{20,28},{24,16},{28,20},{1,9},{5... | collective-permute-start | bytes 1769480 | tf_op jit(solution)/shard_map/ppermute | solution.py:23
  61.0 10.1 %collective-permute-start.14 = (bf16[384,384]{1,0:T(8,128)(2,1)}, bf16[384,384]{1,0:T(8,128)(2,1)S(1)}, u32[]{:S(2)}, u32[]{:S(2)}) collective-permute-start(bf16[384,384]{1,0:T(8,128)(2,1)} %copy-done.70), channel_id=1, source_target_pairs={{0,4},{4,0},{8,12},{12,8},{16,20},{20,16},{24,28},{28,24},{1,5},{5... | collective-permute-start | bytes 884744 | tf_op jit(solution)/shard_map/ppermute | solution.py:23
  61.5 14.9 %collective-permute-start.15 = (bf16[384,384]{1,0:T(8,128)(2,1)}, bf16[384,384]{1,0:T(8,128)(2,1)S(1)}, u32[]{:S(2)}, u32[]{:S(2)}) collective-permute-start(bf16[384,384]{1,0:T(8,128)(2,1)} %collective-permute-done.10), channel_id=1, source_target_pairs={{0,4},{4,0},{8,12},{12,8},{16,20},{20,16},{24,28},{28,24},{1,5},{5... | collective-permute-start | bytes 884744 | tf_op jit(solution)/shard_map/ppermute | solution.py:23
  79.5 23.9 %collective-permute-start.19 = (bf16[384,768]{1,0:T(8,128)(2,1)}, bf16[384,768]{1,0:T(8,128)(2,1)S(1)}, u32[]{:S(2)}, u32[]{:S(2)}) collective-permute-start(bf16[384,768]{1,0:T(8,128)(2,1)} %get-tuple-element.309), channel_id=1, source_target_pairs={{0,4},{4,0},{8,12},{12,8},{16,20},{20,16},{24,28},{28,24},{1,5},{5... | collective-permute-start | bytes 1769480 | tf_op jit(solution)/shard_map/ppermute | solution.py:23
  79.9 23.5 %collective-permute-start.20 = (bf16[384,768]{1,0:T(8,128)(2,1)S(1)}, bf16[384,768]{1,0:T(8,128)(2,1)}, u32[]{:S(2)}, u32[]{:S(2)}) collective-permute-start(bf16[384,768]{1,0:T(8,128)(2,1)S(1)} %get-tuple-element.324), channel_id=1, source_target_pairs={{0,2},{1,3},{2,0},{3,1},{4,6},{5,7},{6,4},{7,5},{8,10},{9,11},{10,... | collective-permute-start | bytes 1769480 | tf_op jit(solution)/shard_map/ppermute | solution.py:23
  83.0 20.4 %collective-permute-start.21 = (bf16[96,768]{1,0:T(8,128)(2,1)}, bf16[96,768]{1,0:T(8,128)(2,1)S(1)}, u32[]{:S(2)}, u32[]{:S(2)}) collective-permute-start(bf16[96,768]{1,0:T(8,128)(2,1)} %pad_maximum_fusion.25), channel_id=1, source_target_pairs={{0,16},{4,20},{8,24},{12,28},{16,0},{20,4},{24,8},{28,12},{1,17},{... | collective-permute-start | bytes 442376 | tf_op jit(solution)/shard_map/ppermute | solution.py:23
  103.5 26.9 %collective-permute-start.22 = (bf16[768,768]{1,0:T(8,128)(2,1)S(1)}, bf16[768,768]{1,0:T(8,128)(2,1)S(1)}, u32[]{:S(2)}, u32[]{:S(2)}) collective-permute-start(bf16[768,768]{1,0:T(8,128)(2,1)S(1)} %constant_dynamic-update-slice_fusion.4.refs_5_.refs_7_), channel_id=1, source_target_pairs={{0,2},{1,3},{2,0},{3,1},{4,6},{5,7},{6,4},{7,5},{8,10},{9,11},{10,... | collective-permute-start | bytes 3538952 | tf_op jit(solution)/shard_map/ppermute | solution.py:23
  104.6 25.8 %collective-permute-start.23 = (bf16[384,768]{1,0:T(8,128)(2,1)S(1)}, bf16[384,768]{1,0:T(8,128)(2,1)}, u32[]{:S(2)}, u32[]{:S(2)}) collective-permute-start(bf16[384,768]{1,0:T(8,128)(2,1)S(1)} %get-tuple-element.324), channel_id=1, source_target_pairs={{0,4},{4,0},{8,12},{12,8},{16,20},{20,16},{24,28},{28,24},{1,5},{5... | collective-permute-start | bytes 1769480 | tf_op jit(solution)/shard_map/ppermute | solution.py:23
  106.3 24.2 %collective-permute-start.24 = (bf16[384,768]{1,0:T(8,128)(2,1)}, bf16[384,768]{1,0:T(8,128)(2,1)}, u32[]{:S(2)}, u32[]{:S(2)}) collective-permute-start(bf16[384,768]{1,0:T(8,128)(2,1)} %collective-permute-done.20), channel_id=1, source_target_pairs={{0,4},{4,0},{8,12},{12,8},{16,20},{20,16},{24,28},{28,24},{1,5},{5... | collective-permute-start | bytes 1769480 | tf_op jit(solution)/shard_map/ppermute | solution.py:23
  107.6 22.8 %collective-permute-start.25 = (bf16[192,768]{1,0:T(8,128)(2,1)S(1)}, bf16[192,768]{1,0:T(8,128)(2,1)}, u32[]{:S(2)}, u32[]{:S(2)}) collective-permute-start(bf16[192,768]{1,0:T(8,128)(2,1)S(1)} %constant_dynamic-update-slice_fusion.6), channel_id=1, source_target_pairs={{0,8},{4,12},{8,0},{12,4},{16,24},{20,28},{24,16},{28,20},{1,9},{5... | collective-permute-start | bytes 884744 | tf_op jit(solution)/shard_map/ppermute | solution.py:23
  109.0 36.5 %collective-permute-start.33 = (bf16[768,768]{1,0:T(8,128)(2,1)S(1)}, bf16[768,768]{1,0:T(8,128)(2,1)}, u32[]{:S(2)}, u32[]{:S(2)}) collective-permute-start(bf16[768,768]{1,0:T(8,128)(2,1)S(1)} %constant_dynamic-update-slice_fusion.4.refs_5_.refs_7_), channel_id=1, source_target_pairs={{0,1},{1,0},{2,3},{3,2},{4,5},{5,4},{6,7},{7,6},{8,9},{9,8},{10,11... | collective-permute-start | bytes 3538952 | tf_op jit(solution)/shard_map/ppermute | solution.py:23
  130.6 12.8 %collective-permute-start.28 = (bf16[768,768]{1,0:T(8,128)(2,1)S(1)}, bf16[768,768]{1,0:T(8,128)(2,1)S(1)}, u32[]{:S(2)}, u32[]{:S(2)}) collective-permute-start(bf16[768,768]{1,0:T(8,128)(2,1)S(1)} %copy-done.124), channel_id=1, source_target_pairs={{0,1},{1,0},{2,3},{3,2},{4,5},{5,4},{6,7},{7,6},{8,9},{9,8},{10,11... | collective-permute-start | bytes 3538952 | tf_op jit(solution)/shard_map/ppermute | solution.py:23
  132.8 9.0 %collective-permute-start.26 = (bf16[384,384]{1,0:T(8,128)(2,1)S(1)}, bf16[384,384]{1,0:T(8,128)(2,1)S(1)}, u32[]{:S(2)}, u32[]{:S(2)}) collective-permute-start(bf16[384,384]{1,0:T(8,128)(2,1)S(1)} %get-tuple-element.337), channel_id=1, source_target_pairs={{0,4},{4,0},{8,12},{12,8},{16,20},{20,16},{24,28},{28,24},{1,5},{5... | collective-permute-start | bytes 884744 | tf_op jit(solution)/shard_map/ppermute | solution.py:23
  134.4 9.1 %collective-permute-start.27 = (bf16[384,384]{1,0:T(8,128)(2,1)}, bf16[384,384]{1,0:T(8,128)(2,1)}, u32[]{:S(2)}, u32[]{:S(2)}) collective-permute-start(bf16[384,384]{1,0:T(8,128)(2,1)} %get-tuple-element.343), channel_id=1, source_target_pairs={{0,2},{1,3},{2,0},{3,1},{4,6},{5,7},{6,4},{7,5},{8,10},{9,11},{10,... | collective-permute-start | bytes 884744 | tf_op jit(solution)/shard_map/ppermute | solution.py:23
  136.6 9.9 %collective-permute-start.36 = (bf16[768,768]{1,0:T(8,128)(2,1)S(1)}, bf16[768,768]{1,0:T(8,128)(2,1)S(1)}, u32[]{:S(2)}, u32[]{:S(2)}) collective-permute-start(bf16[768,768]{1,0:T(8,128)(2,1)S(1)} %constant_dynamic-update-slice_fusion.14.refs_11_.refs_13_), channel_id=1, source_target_pairs={{0,1},{1,0},{2,3},{3,2},{4,5},{5,4},{6,7},{7,6},{8,9},{9,8},{10,11... | collective-permute-start | bytes 3538952 | tf_op jit(solution)/shard_map/ppermute | solution.py:23
  144.4 28.4 %collective-permute-start.29 = (bf16[768,384]{1,0:T(8,128)(2,1)}, bf16[768,384]{1,0:T(8,128)(2,1)S(1)}, u32[]{:S(2)}, u32[]{:S(2)}) collective-permute-start(bf16[768,384]{1,0:T(8,128)(2,1)} %pad_maximum_fusion.15.refs_2_), channel_id=1, source_target_pairs={{0,2},{1,3},{2,0},{3,1},{4,6},{5,7},{6,4},{7,5},{8,10},{9,11},{10,... | collective-permute-start | bytes 1769480 | tf_op jit(solution)/shard_map/ppermute | solution.py:23
  145.5 27.3 %collective-permute-start.37 = (bf16[375,768]{1,0:T(8,128)(2,1)}, bf16[375,768]{1,0:T(8,128)(2,1)S(1)}, u32[]{:S(2)}, u32[]{:S(2)}) collective-permute-start(bf16[375,768]{1,0:T(8,128)(2,1)} %get-tuple-element.363), channel_id=1, source_target_pairs={{0,2},{1,3},{2,0},{3,1},{4,6},{5,7},{6,4},{7,5},{8,10},{9,11},{10,... | collective-permute-start | bytes 1728008 | tf_op jit(solution)/shard_map/ppermute | solution.py:23
  146.5 26.3 %collective-permute-start.30 = (bf16[384,384]{1,0:T(8,128)(2,1)}, bf16[384,384]{1,0:T(8,128)(2,1)S(1)}, u32[]{:S(2)}, u32[]{:S(2)}) collective-permute-start(bf16[384,384]{1,0:T(8,128)(2,1)} %get-tuple-element.343), channel_id=1, source_target_pairs={{0,4},{4,0},{8,12},{12,8},{16,20},{20,16},{24,28},{28,24},{1,5},{5... | collective-permute-start | bytes 884744 | tf_op jit(solution)/shard_map/ppermute | solution.py:23
  147.0 25.8 %collective-permute-start.31 = (bf16[384,384]{1,0:T(8,128)(2,1)}, bf16[384,384]{1,0:T(8,128)(2,1)S(1)}, u32[]{:S(2)}, u32[]{:S(2)}) collective-permute-start(bf16[384,384]{1,0:T(8,128)(2,1)} %collective-permute-done.27), channel_id=1, source_target_pairs={{0,4},{4,0},{8,12},{12,8},{16,20},{20,16},{24,28},{28,24},{1,5},{5... | collective-permute-start | bytes 884744 | tf_op jit(solution)/shard_map/ppermute | solution.py:23
  149.6 23.2 %collective-permute-start.32 = (bf16[96,1536]{1,0:T(8,128)(2,1)}, bf16[96,1536]{1,0:T(8,128)(2,1)S(1)}, u32[]{:S(2)}, u32[]{:S(2)}) collective-permute-start(bf16[96,1536]{1,0:T(8,128)(2,1)} %get-tuple-element.345), channel_id=1, source_target_pairs={{0,16},{4,20},{8,24},{12,28},{16,0},{20,4},{24,8},{28,12},{1,17},{... | collective-permute-start | bytes 884744 | tf_op jit(solution)/shard_map/ppermute | solution.py:23
  172.8 16.9 %collective-permute-start.39 = (bf16[768,768]{1,0:T(8,128)(2,1)}, bf16[768,768]{1,0:T(8,128)(2,1)S(1)}, u32[]{:S(2)}, u32[]{:S(2)}) collective-permute-start(bf16[768,768]{1,0:T(8,128)(2,1)} %get-tuple-element.385.refs_0_), channel_id=1, source_target_pairs={{0,1},{1,0},{2,3},{3,2},{4,5},{5,4},{6,7},{7,6},{8,9},{9,8},{10,11... | collective-permute-start | bytes 3538952 | tf_op jit(solution)/shard_map/ppermute | solution.py:23
  174.1 15.6 %collective-permute-start.38 = (bf16[192,1536]{1,0:T(8,128)(2,1)S(1)}, bf16[192,1536]{1,0:T(8,128)(2,1)S(1)}, u32[]{:S(2)}, u32[]{:S(2)}) collective-permute-start(bf16[192,1536]{1,0:T(8,128)(2,1)S(1)} %pad_maximum_fusion.16), channel_id=1, source_target_pairs={{0,8},{4,12},{8,0},{12,4},{16,24},{20,28},{24,16},{28,20},{1,9},{5... | collective-permute-start | bytes 1769480 | tf_op jit(solution)/shard_map/ppermute | solution.py:23
  190.7 21.7 %collective-permute-start.40 = (bf16[384,768]{1,0:T(8,128)(2,1)S(1)}, bf16[384,768]{1,0:T(8,128)(2,1)S(1)}, u32[]{:S(2)}, u32[]{:S(2)}) collective-permute-start(bf16[384,768]{1,0:T(8,128)(2,1)S(1)} %get-tuple-element.370), channel_id=1, source_target_pairs={{0,4},{4,0},{8,12},{12,8},{16,20},{20,16},{24,28},{28,24},{1,5},{5... | collective-permute-start | bytes 1769480 | tf_op jit(solution)/shard_map/ppermute | solution.py:23
  191.4 21.0 %collective-permute-start.41 = (bf16[384,768]{1,0:T(8,128)(2,1)S(1)}, bf16[384,768]{1,0:T(8,128)(2,1)}, u32[]{:S(2)}, u32[]{:S(2)}) collective-permute-start(bf16[384,768]{1,0:T(8,128)(2,1)S(1)} %get-tuple-element.382), channel_id=1, source_target_pairs={{0,2},{1,3},{2,0},{3,1},{4,6},{5,7},{6,4},{7,5},{8,10},{9,11},{10,... | collective-permute-start | bytes 1769480 | tf_op jit(solution)/shard_map/ppermute | solution.py:23
  213.3 27.6 %collective-permute-start.42 = (bf16[768,768]{1,0:T(8,128)(2,1)}, bf16[768,768]{1,0:T(8,128)(2,1)S(1)}, u32[]{:S(2)}, u32[]{:S(2)}) collective-permute-start(bf16[768,768]{1,0:T(8,128)(2,1)} %constant_dynamic-update-slice_fusion.20.refs_5_.refs_4_), channel_id=1, source_target_pairs={{0,2},{1,3},{2,0},{3,1},{4,6},{5,7},{6,4},{7,5},{8,10},{9,11},{10,... | collective-permute-start | bytes 3538952 | tf_op jit(solution)/shard_map/ppermute | solution.py:23
  214.3 24.3 %collective-permute-start.43 = (bf16[384,768]{1,0:T(8,128)(2,1)S(1)}, bf16[384,768]{1,0:T(8,128)(2,1)}, u32[]{:S(2)}, u32[]{:S(2)}) collective-permute-start(bf16[384,768]{1,0:T(8,128)(2,1)S(1)} %get-tuple-element.382), channel_id=1, source_target_pairs={{0,4},{4,0},{8,12},{12,8},{16,20},{20,16},{24,28},{28,24},{1,5},{5... | collective-permute-start | bytes 1769480 | tf_op jit(solution)/shard_map/ppermute | solution.py:23
  215.7 25.2 %collective-permute-start.44 = (bf16[384,768]{1,0:T(8,128)(2,1)}, bf16[384,768]{1,0:T(8,128)(2,1)}, u32[]{:S(2)}, u32[]{:S(2)}) collective-permute-start(bf16[384,768]{1,0:T(8,128)(2,1)} %collective-permute-done.41), channel_id=1, source_target_pairs={{0,4},{4,0},{8,12},{12,8},{16,20},{20,16},{24,28},{28,24},{1,5},{5... | collective-permute-start | bytes 1769480 | tf_op jit(solution)/shard_map/ppermute | solution.py:23
  217.4 27.4 %collective-permute-start.46 = (bf16[768,768]{1,0:T(8,128)(2,1)}, bf16[768,768]{1,0:T(8,128)(2,1)}, u32[]{:S(2)}, u32[]{:S(2)}) collective-permute-start(bf16[768,768]{1,0:T(8,128)(2,1)} %constant_dynamic-update-slice_fusion.20.refs_5_.refs_4_), channel_id=1, source_target_pairs={{0,1},{1,0},{2,3},{3,2},{4,5},{5,4},{6,7},{7,6},{8,9},{9,8},{10,11... | collective-permute-start | bytes 3538952 | tf_op jit(solution)/shard_map/ppermute | solution.py:23
  271.4 33.7 %collective-permute-start.50 = (bf16[384,768]{1,0:T(8,128)(2,1)S(1)}, bf16[384,768]{1,0:T(8,128)(2,1)S(1)}, u32[]{:S(2)}, u32[]{:S(2)}) collective-permute-start(bf16[384,768]{1,0:T(8,128)(2,1)S(1)} %slice.896), channel_id=1, source_target_pairs={{0,2},{1,3},{2,0},{3,1},{4,6},{5,7},{6,4},{7,5},{8,10},{9,11},{10,... | collective-permute-start | bytes 1769480 | tf_op jit(solution)/shard_map/ppermute | solution.py:23
  305.1 42.2 %collective-permute-start.51 = (bf16[4,768,768]{2,1,0:T(8,128)(2,1)}, bf16[4,768,768]{2,1,0:T(8,128)(2,1)}, u32[]{:S(2)}, u32[]{:S(2)}) collective-permute-start(bf16[4,768,768]{2,1,0:T(8,128)(2,1)} %get-tuple-element.423), channel_id=1, source_target_pairs={{0,1},{1,0},{2,3},{3,2},{4,5},{5,4},{6,7},{7,6},{8,9},{9,8},{10,11... | collective-permute-start | bytes 14155784 | tf_op jit(solution)/shard_map/ppermute | solution.py:23
  305.9 9.1 %collective-permute-start.52 = (bf16[768,768]{1,0:T(8,128)(2,1)}, bf16[768,768]{1,0:T(8,128)(2,1)S(1)}, u32[]{:S(2)}, u32[]{:S(2)}) collective-permute-start(bf16[768,768]{1,0:T(8,128)(2,1)} %get-tuple-element.436.refs_0_), channel_id=1, source_target_pairs={{0,1},{1,0},{2,3},{3,2},{4,5},{5,4},{6,7},{7,6},{8,9},{9,8},{10,11... | collective-permute-start | bytes 3538952 | tf_op jit(solution)/shard_map/ppermute | solution.py:23
  353.3 42.1 %collective-permute-start.53 = (bf16[768,768]{1,0:T(8,128)(2,1)}, bf16[768,768]{1,0:T(8,128)(2,1)}, u32[]{:S(2)}, u32[]{:S(2)}) collective-permute-start(bf16[768,768]{1,0:T(8,128)(2,1)} %fusion.25), channel_id=1, source_target_pairs={{0,2},{1,3},{2,0},{3,1},{4,6},{5,7},{6,4},{7,5},{8,10},{9,11},{10,... | collective-permute-start | bytes 3538952 | tf_op jit(solution)/shard_map/ppermute | solution.py:23
  354.3 41.1 %collective-permute-start.54 = (bf16[2,384,768]{2,1,0:T(8,128)(2,1)}, bf16[2,384,768]{2,1,0:T(8,128)(2,1)}, u32[]{:S(2)}, u32[]{:S(2)}) collective-permute-start(bf16[2,384,768]{2,1,0:T(8,128)(2,1)} %add_convert_fusion.5), channel_id=1, source_target_pairs={{0,4},{4,0},{8,12},{12,8},{16,20},{20,16},{24,28},{28,24},{1,5},{5... | collective-permute-start | bytes 3538952 | tf_op jit(solution)/shard_map/ppermute | solution.py:23
  405.6 40.2 %collective-permute-start.57 = (bf16[768,384]{0,1:T(8,128)(2,1)}, bf16[768,384]{0,1:T(8,128)(2,1)S(1)}, u32[]{:S(2)}, u32[]{:S(2)}) collective-permute-start(bf16[768,384]{0,1:T(8,128)(2,1)} %slice_bitcast_fusion.3), channel_id=1, source_target_pairs={{0,2},{1,3},{2,0},{3,1},{4,6},{5,7},{6,4},{7,5},{8,10},{9,11},{10,... | collective-permute-start | bytes 1769480 | tf_op jit(solution)/shard_map/ppermute | solution.py:23
  407.5 38.3 %collective-permute-start.58 = (bf16[2,384,384]{1,2,0:T(8,128)(2,1)}, bf16[2,384,384]{1,2,0:T(8,128)(2,1)}, u32[]{:S(2)}, u32[]{:S(2)}) collective-permute-start(bf16[2,384,384]{1,2,0:T(8,128)(2,1)} %slice.584), channel_id=1, source_target_pairs={{0,4},{4,0},{8,12},{12,8},{16,20},{20,16},{24,28},{28,24},{1,5},{5... | collective-permute-start | bytes 1769480 | tf_op jit(solution)/shard_map/ppermute | solution.py:23
  409.0 36.8 %collective-permute-start.55 = (bf16[384,768]{1,0:T(8,128)(2,1)}, bf16[384,768]{1,0:T(8,128)(2,1)}, u32[]{:S(2)}, u32[]{:S(2)}) collective-permute-start(bf16[384,768]{1,0:T(8,128)(2,1)} %slice.573), channel_id=1, source_target_pairs={{0,4},{4,0},{8,12},{12,8},{16,20},{20,16},{24,28},{28,24},{1,5},{5... | collective-permute-start | bytes 1769480 | tf_op jit(solution)/shard_map/ppermute | solution.py:23
  411.2 34.6 %collective-permute-start.56 = (bf16[384,768]{1,0:T(8,128)(2,1)}, bf16[384,768]{1,0:T(8,128)(2,1)}, u32[]{:S(2)}, u32[]{:S(2)}) collective-permute-start(bf16[384,768]{1,0:T(8,128)(2,1)} %slice_bitcast_fusion.4), channel_id=1, source_target_pairs={{0,2},{1,3},{2,0},{3,1},{4,6},{5,7},{6,4},{7,5},{8,10},{9,11},{10,... | collective-permute-start | bytes 1769480 | tf_op jit(solution)/shard_map/ppermute | solution.py:23
  445.8 30.1 %collective-permute-start.60 = (bf16[4,768,768]{2,1,0:T(8,128)(2,1)}, bf16[4,768,768]{2,1,0:T(8,128)(2,1)}, u32[]{:S(2)}, u32[]{:S(2)}) collective-permute-start(bf16[4,768,768]{2,1,0:T(8,128)(2,1)} %get-tuple-element.476), channel_id=1, source_target_pairs={{0,1},{1,0},{2,3},{3,2},{4,5},{5,4},{6,7},{7,6},{8,9},{9,8},{10,11... | collective-permute-start | bytes 14155784 | tf_op jit(solution)/shard_map/ppermute | solution.py:23
  453.3 12.7 %collective-permute-start.68 = (bf16[768,768]{1,0:T(8,128)(2,1)}, bf16[768,768]{1,0:T(8,128)(2,1)S(1)}, u32[]{:S(2)}, u32[]{:S(2)}) collective-permute-start(bf16[768,768]{1,0:T(8,128)(2,1)} %get-tuple-element.511.refs_0_), channel_id=1, source_target_pairs={{0,1},{1,0},{2,3},{3,2},{4,5},{5,4},{6,7},{7,6},{8,9},{9,8},{10,11... | collective-permute-start | bytes 3538952 | tf_op jit(solution)/shard_map/ppermute | solution.py:23
  460.3 15.6 %collective-permute-start.63 = (bf16[192,1536]{1,0:T(8,128)(2,1)}, bf16[192,1536]{1,0:T(8,128)(2,1)}, u32[]{:S(2)}, u32[]{:S(2)}) collective-permute-start(bf16[192,1536]{1,0:T(8,128)(2,1)} %slice.592), channel_id=1, source_target_pairs={{0,8},{4,12},{8,0},{12,4},{16,24},{20,28},{24,16},{28,20},{1,9},{5... | collective-permute-start | bytes 1769480 | tf_op jit(solution)/shard_map/ppermute | solution.py:23
  483.1 38.6 %collective-permute-start.64 = (bf16[768,768]{1,0:T(8,128)(2,1)}, bf16[768,768]{1,0:T(8,128)(2,1)}, u32[]{:S(2)}, u32[]{:S(2)}) collective-permute-start(bf16[768,768]{1,0:T(8,128)(2,1)} %fusion.26), channel_id=1, source_target_pairs={{0,2},{1,3},{2,0},{3,1},{4,6},{5,7},{6,4},{7,5},{8,10},{9,11},{10,... | collective-permute-start | bytes 3538952 | tf_op jit(solution)/shard_map/ppermute | solution.py:23
  484.1 37.5 %collective-permute-start.65 = (bf16[2,384,768]{2,1,0:T(8,128)(2,1)}, bf16[2,384,768]{2,1,0:T(8,128)(2,1)}, u32[]{:S(2)}, u32[]{:S(2)}) collective-permute-start(bf16[2,384,768]{2,1,0:T(8,128)(2,1)} %add_convert_fusion.2), channel_id=1, source_target_pairs={{0,4},{4,0},{8,12},{12,8},{16,20},{20,16},{24,28},{28,24},{1,5},{5... | collective-permute-start | bytes 3538952 | tf_op jit(solution)/shard_map/ppermute | solution.py:23
  487.1 34.5 %collective-permute-start.66 = (bf16[192,768]{0,1:T(8,128)(2,1)}, bf16[192,768]{0,1:T(8,128)(2,1)}, u32[]{:S(2)}, u32[]{:S(2)}) collective-permute-start(bf16[192,768]{0,1:T(8,128)(2,1)} %slice.601), channel_id=1, source_target_pairs={{0,8},{4,12},{8,0},{12,4},{16,24},{20,28},{24,16},{28,20},{1,9},{5... | collective-permute-start | bytes 884744 | tf_op jit(solution)/shard_map/ppermute | solution.py:23
  488.7 32.9 %collective-permute-start.67 = (bf16[96,1536]{1,0:T(8,128)(2,1)}, bf16[96,1536]{1,0:T(8,128)(2,1)}, u32[]{:S(2)}, u32[]{:S(2)}) collective-permute-start(bf16[96,1536]{1,0:T(8,128)(2,1)} %slice.602), channel_id=1, source_target_pairs={{0,16},{4,20},{8,24},{12,28},{16,0},{20,4},{24,8},{28,12},{1,17},{... | collective-permute-start | bytes 884744 | tf_op jit(solution)/shard_map/ppermute | solution.py:23
  531.7 43.5 %collective-permute-start.72 = (bf16[768,768]{0,1:T(8,128)(2,1)}, bf16[768,768]{0,1:T(8,128)(2,1)}, u32[]{:S(2)}, u32[]{:S(2)}) collective-permute-start(bf16[768,768]{0,1:T(8,128)(2,1)} %pad_maximum_fusion.12), channel_id=1, source_target_pairs={{0,2},{1,3},{2,0},{3,1},{4,6},{5,7},{6,4},{7,5},{8,10},{9,11},{10,... | collective-permute-start | bytes 3538952 | tf_op jit(solution)/shard_map/ppermute | solution.py:23
  533.6 41.6 %collective-permute-start.69 = (bf16[384,768]{1,0:T(8,128)(2,1)}, bf16[384,768]{1,0:T(8,128)(2,1)}, u32[]{:S(2)}, u32[]{:S(2)}) collective-permute-start(bf16[384,768]{1,0:T(8,128)(2,1)} %slice.605), channel_id=1, source_target_pairs={{0,4},{4,0},{8,12},{12,8},{16,20},{20,16},{24,28},{28,24},{1,5},{5... | collective-permute-start | bytes 1769480 | tf_op jit(solution)/shard_map/ppermute | solution.py:23
  536.0 39.1 %collective-permute-start.70 = (bf16[384,768]{1,0:T(8,128)(2,1)}, bf16[384,768]{1,0:T(8,128)(2,1)}, u32[]{:S(2)}, u32[]{:S(2)}) collective-permute-start(bf16[384,768]{1,0:T(8,128)(2,1)} %slice_bitcast_fusion.2), channel_id=1, source_target_pairs={{0,2},{1,3},{2,0},{3,1},{4,6},{5,7},{6,4},{7,5},{8,10},{9,11},{10,... | collective-permute-start | bytes 1769480 | tf_op jit(solution)/shard_map/ppermute | solution.py:23
  540.8 34.4 %collective-permute-start.71 = (bf16[96,768]{0,1:T(8,128)(2,1)S(1)}, bf16[96,768]{0,1:T(8,128)(2,1)S(1)}, u32[]{:S(2)}, u32[]{:S(2)}) collective-permute-start(bf16[96,768]{0,1:T(8,128)(2,1)S(1)} %slice.609), channel_id=1, source_target_pairs={{0,16},{4,20},{8,24},{12,28},{16,0},{20,4},{24,8},{28,12},{1,17},{... | collective-permute-start | bytes 442376 | tf_op jit(solution)/shard_map/ppermute | solution.py:23
  579.8 12.4 %collective-permute-start.75 = (bf16[192,1536]{1,0:T(8,128)(2,1)}, bf16[192,1536]{1,0:T(8,128)(2,1)S(1)}, u32[]{:S(2)}, u32[]{:S(2)}) collective-permute-start(bf16[192,1536]{1,0:T(8,128)(2,1)} %slice.730), channel_id=1, source_target_pairs={{0,8},{4,12},{8,0},{12,4},{16,24},{20,28},{24,16},{28,20},{1,9},{5... | collective-permute-start | bytes 1769480 | tf_op jit(solution)/shard_map/ppermute | solution.py:23
  584.1 12.3 %collective-permute-start.74 = (bf16[384,768]{0,1:T(8,128)(2,1)S(1)}, bf16[384,768]{0,1:T(8,128)(2,1)}, u32[]{:S(2)}, u32[]{:S(2)}) collective-permute-start(bf16[384,768]{0,1:T(8,128)(2,1)S(1)} %slice.729), channel_id=1, source_target_pairs={{0,4},{4,0},{8,12},{12,8},{16,20},{20,16},{24,28},{28,24},{1,5},{5... | collective-permute-start | bytes 1769480 | tf_op jit(solution)/shard_map/ppermute | solution.py:23
  584.9 16.0 %collective-permute-start.73 = (bf16[768,768]{1,0:T(8,128)(2,1)}, bf16[768,768]{1,0:T(8,128)(2,1)S(1)}, u32[]{:S(2)}, u32[]{:S(2)}) collective-permute-start(bf16[768,768]{1,0:T(8,128)(2,1)} %get-tuple-element.520), channel_id=1, source_target_pairs={{0,1},{1,0},{2,3},{3,2},{4,5},{5,4},{6,7},{7,6},{8,9},{9,8},{10,11... | collective-permute-start | bytes 3538952 | tf_op jit(solution)/shard_map/ppermute | solution.py:23
  632.2 14.6 %collective-permute-start.78 = (bf16[384,768]{1,0:T(8,128)(2,1)S(1)}, bf16[384,768]{1,0:T(8,128)(2,1)S(1)}, u32[]{:S(2)}, u32[]{:S(2)}) collective-permute-start(bf16[384,768]{1,0:T(8,128)(2,1)S(1)} %slice.895), channel_id=1, source_target_pairs={{0,2},{1,3},{2,0},{3,1},{4,6},{5,7},{6,4},{7,5},{8,10},{9,11},{10,... | collective-permute-start | bytes 1769480 | tf_op jit(solution)/shard_map/ppermute | solution.py:23
  633.5 13.3 %collective-permute-start.76 = (bf16[192,768]{0,1:T(8,128)(2,1)S(1)}, bf16[192,768]{0,1:T(8,128)(2,1)S(1)}, u32[]{:S(2)}, u32[]{:S(2)}) collective-permute-start(bf16[192,768]{0,1:T(8,128)(2,1)S(1)} %slice.642), channel_id=1, source_target_pairs={{0,8},{4,12},{8,0},{12,4},{16,24},{20,28},{24,16},{28,20},{1,9},{5... | collective-permute-start | bytes 884744 | tf_op jit(solution)/shard_map/ppermute | solution.py:23
  634.4 12.3 %collective-permute-start.77 = (bf16[96,1536]{1,0:T(8,128)(2,1)S(1)}, bf16[96,1536]{1,0:T(8,128)(2,1)S(1)}, u32[]{:S(2)}, u32[]{:S(2)}) collective-permute-start(bf16[96,1536]{1,0:T(8,128)(2,1)S(1)} %slice.643), channel_id=1, source_target_pairs={{0,16},{4,20},{8,24},{12,28},{16,0},{20,4},{24,8},{28,12},{1,17},{... | collective-permute-start | bytes 884744 | tf_op jit(solution)/shard_map/ppermute | solution.py:23
  647.5 12.5 %collective-permute-start.82 = (bf16[96,768]{0,1:T(8,128)(2,1)S(1)}, bf16[96,768]{0,1:T(8,128)(2,1)S(1)}, u32[]{:S(2)}, u32[]{:S(2)}) collective-permute-start(bf16[96,768]{0,1:T(8,128)(2,1)S(1)} %slice.650), channel_id=1, source_target_pairs={{0,16},{4,20},{8,24},{12,28},{16,0},{20,4},{24,8},{28,12},{1,17},{... | collective-permute-start | bytes 442376 | tf_op jit(solution)/shard_map/ppermute | solution.py:23
  (150 other events, 846.8 us)

commit v8 on v7

--- a/solution.py
+++ b/solution.py
@@ -93,11 +93,9 @@
         self.plan = [[(0, step)] for step in made[0][1]]
         for at, (_, _, near) in enumerate(made):
             ahead = made[at + 1][1] if at + 1 < len(made) else []
-            late = 1 if at % 2 == 0 and at > 0 else 0
-            for i in range(max(len(near), len(ahead) + late)):
+            for i in range(max(len(near), len(ahead))):
                 stage = [(at, near[i])] if i < len(near) else []
-                j = i - late
-                self.plan.append(stage + ([(at + 1, ahead[j])] if 0 <= j < len(ahead) else []))
+                self.plan.append(stage + ([(at + 1, ahead[i])] if i < len(ahead) else []))
         self.ends = [
             max(i for i, stage in enumerate(self.plan) for g, _ in stage if g == at)
             for at in range(len(made))
@@ -666,6 +664,57 @@
     )(*singles, *ups, *downs, *activated, *slopes)
 
 
+def finish_kernel(layers, wide, *refs):
+    layer_in, above, share_a, share_b, gain, up_blocks, head_blocks = refs[:7]
+    sums, biases, heads = refs[7 : 7 + layers], refs[7 + layers : 7 + 2 * layers], refs[7 + 2 * layers : 7 + 4 * layers]
+    grad, low, *small = refs[7 + 4 * layers :]
+    grad_normed = share_a[...] + share_b[...].astype(f32)
+    value, gain_one, shift_one = norm_back(layer_in[...], gain[0:1, :], grad_normed)
+    value = value + above[...]
+    grad[...] = value
+    low[...] = value[low.shape[0] :, :].astype(bf16)
+
+    def reorder(part, blocks):
+        return sum(nn_dot(piece, blocks[...]) for piece in split_low(part))
+
+    for t in range(4):
+        small[t][...] = jnp.zeros_like(small[t])
+        small[t][0:1, :] = gain_one
+        small[t][2 * layers : 2 * layers + 1, :] = shift_one
+    for at in range(layers):
+        rows = [(2 * at + 1, 1), (2 * (layers + at) + 1, 2)]
+        rows += [(4 * layers + 2 * at, 3), (4 * layers + 2 * at + 1, 0)]
+        if at + 1 < layers:
+            rows += [(2 * (at + 1), 4), (2 * (layers + at + 1), 5)]
+        bias = reorder(biases[at][...], up_blocks)
+        for t in range(4):
+            for dest, source in rows:
+                small[t][dest : dest + 1, :] = sums[at][source : source + 1, :]
+            small[t][6 * layers + at : 6 * layers + at + 1, :] = bias[t : t + 1, :]
+        for group in range(2):
+            both = heads[2 * at + group]
+            for i, first in enumerate((0, 2 * wide)):
+                dest = 7 * layers + 2 * at + i
+                row = reorder(both[:, first : first + wide], head_blocks)
+                small[2 * group][dest : dest + 1, :] = row[0:1, :]
+
+
+def finish(layers, quarter, wide, fronts, sums, biases, heads):
+    rows, width = fronts[0].shape
+    operands = (*fronts, *sums, *biases, *heads)
+    count = -(-9 * layers // 8) * 8
+    outs = [jax.ShapeDtypeStruct((rows, width), f32), jax.ShapeDtypeStruct((rows - quarter, width), bf16)]
+    outs += [jax.ShapeDtypeStruct((count, width), f32)] * 4
+    return pl.pallas_call(
+        functools.partial(finish_kernel, layers, wide),
+        grid=(1,),
+        in_specs=[single(part.shape) for part in operands],
+        out_specs=[whole(part.shape) for part in outs],
+        out_shape=outs,
+        compiler_params=pltpu.CompilerParams(vmem_limit_bytes=56 * 2**20),
+    )(*operands)
+
+
 def local(
     frames,
     cotangent,
@@ -685,11 +734,16 @@
     hidden = up_weight.shape[2]
     quarter = -(-row_count // 128) * 128
     rows = 2 * quarter
-    count_dp = lax.axis_size("dp")
     me = lax.axis_index("dp")
     t_me = lax.axis_index("tensor")
     y_me = t_me // 2
-    block_at = relative_mask(jnp.arange(count_dp)) ^ me
+
+    def blocks_of(size, part):
+        lane = jnp.arange(width)
+        source = (relative_mask(lane // block) ^ me) * part + lane % block
+        return (
+            (jnp.arange(size)[:, None] == source[None, :]) & (lane % block < part)[None, :]
+        ).astype(bf16)
 
     norm_part, up_part, qv_part = norm_gains.shape[2], up_bias.shape[1], qv_bias.shape[2]
 
@@ -697,6 +751,15 @@
         room = jnp.zeros((part.shape[0], size), f32)
         return lax.dynamic_update_slice(room, part, (0, at))
 
+    groups = []
+    for at in range(layers):
+        qk = jnp.concatenate([qkv_weight[at, :, 0], qkv_weight[at, :, 1]], axis=1)
+        vo = jnp.concatenate([qkv_weight[at, :, 2], out_weight[at].T], axis=1)
+        groups += [(qk, vo), (up_weight[at], down_weight[at].T)]
+    gathering = Gathering(groups)
+    norm_gains, up_bias, frames, cotangent = behind(
+        (norm_gains, up_bias, frames, cotangent), *gathering.states[0]
+    )
     by_width = jnp.stack([norm_gains, norm_shifts, out_biases]).reshape(6 * layers, norm_part)
     by_width = place(by_width, 4 * norm_part, t_me * norm_part)
     by_hidden = jnp.concatenate(
@@ -706,9 +769,7 @@
         ]
     )
 
-    source = jnp.repeat(block_at, block) * block + jnp.tile(jnp.arange(block), count_dp)
-    to_relative = (jnp.arange(width)[:, None] == source[None, :]).astype(bf16)
-
+    to_relative = blocks_of(width, block)
     first = y_me == 0
 
     def other_clip(value):
@@ -734,12 +795,6 @@
     current = take_clip(frames, exchange(other_clip(frames), "tensor", 2))
     clip = other_clip(cotangent)
 
-    groups = []
-    for at in range(layers):
-        qk = jnp.concatenate([qkv_weight[at, :, 0], qkv_weight[at, :, 1]], axis=1)
-        vo = jnp.concatenate([qkv_weight[at, :, 2], out_weight[at].T], axis=1)
-        groups += [(qk, vo), (up_weight[at], down_weight[at].T)]
-    gathering = Gathering(groups)
     for mask in dp_masks():
         got = exchange(by_width, "dp", mask), exchange(by_hidden, "dp", mask)
         if mask == 2:
@@ -797,7 +852,7 @@
         current = fed[10]
         if not final:
             normed_a = fed[11]
-            (normed_b,) = gathering.advance(exchange(normed_a, "tensor", 1))
+            normed_b = exchange(normed_a, "tensor", 1)
     if layers == 1:
         clip = exchange(clip, "tensor", 2)
     small_grads = [None] * layers
@@ -864,61 +919,33 @@
             folding = core
         fronts = (gradient, layer_in, share_a, share_b)
         small_grads[at] = (sums, (sums_own, sums_other), bup)
-    grad_in, *last_sums = norm_back(
-        layer_in, gain_all[0], share_a + share_b.astype(f32)
+    gradient, half, *small = finish(
+        layers,
+        quarter,
+        wide,
+        (
+            layer_in,
+            gradient,
+            share_a,
+            share_b,
+            vectors,
+            blocks_of(hidden, up_part),
+            blocks_of(wide, qv_part),
+        ),
+        [small_grads[at][0] for at in range(layers)],
+        [small_grads[at][2] for at in range(layers)],
+        [part for at in range(layers) for part in small_grads[at][1]],
     )
-    gradient = gradient + grad_in
-    lane = jnp.arange(width)
-    head_source = block_at[lane // block] * qv_part + lane % block
-    to_blocks = (jnp.arange(wide)[:, None] == head_source[None, :]) & (lane % block < qv_part)
-    up_source = block_at[lane // block] * up_part + lane % block
-    up_blocks = (jnp.arange(hidden)[:, None] == up_source[None, :]) & (lane % block < up_part)
-
-    def reorder(part, matrix):
-        return lax.dot_general(
-            part,
-            matrix.astype(f32),
-            (((1,), (0,)), ((), ())),
-            precision=lax.Precision.HIGHEST,
-            preferred_element_type=f32,
-        )
-
-    bups = reorder(
-        jnp.concatenate([small_grads[at][2][t : t + 1] for t in range(4) for at in range(layers)]),
-        up_blocks,
-    )
-    bqv = reorder(
-        jnp.concatenate(
-            [
-                small_grads[at][1][t][:1, i * wide : (i + 1) * wide]
-                for t in range(2)
-                for at in range(layers)
-                for i in (0, 2)
-            ]
-        ),
-        to_blocks,
-    )
-    last_sums = jnp.concatenate([*last_sums, jnp.zeros((6, width), f32)])
-    by_width = jnp.concatenate([small_grads[at][0] for at in range(layers)] + [last_sums])
-    small = [
-        jnp.concatenate(
-            [by_width, bups[t * layers : (t + 1) * layers]]
-            + ([bqv[t * layers : (t + 2) * layers]] if t % 2 == 0 else [])
-        )
-        for t in range(4)
-    ]
     advance([folding])
-    gradient, *small, folding.attn, folding.feed = together(
-        gradient, *small, folding.attn, folding.feed
+    half, *small, folding.attn, folding.feed = together(
+        half, *small, folding.attn, folding.feed
     )
     half, *got = advance(
         [folding],
-        give_half(gradient),
+        exchange(half, "tensor", 2),
         *[exchange(small[t], "tensor", t) for t in range(1, 4)],
     )
-    cut = 8 * layers + 8
-    small, more = small[0] + got[1], got[0] + got[2]
-    small = jnp.concatenate([small[: cut + layers] + more, small[cut + layers :]])
+    small = small[0] + got[0] + got[1] + got[2]
     frames_grad = give_clip(gradient, half)
     for mask in reversed(dp_masks()):
         got = exchange(small[:, small.shape[1] // 2 :], "dp", mask)
@@ -929,19 +956,10 @@
             small, current, encoded_half = together(small, current, encoded_half)
     encoded = give_clip(current, encoded_half)
     weight_grads[0] = folding.result()
-    by_width = lax.dynamic_slice(small, (0, t_me * norm_part), (cut, norm_part))
-    rows_of = [by_width[8 * at : 8 * at + 8] for at in range(layers + 1)]
-    one = [rows_of[at][4:6] for at in range(layers - 1)]
-    one = [rows_of[layers][0:2]] + one
-
-    def pair(make):
-        return jnp.stack([jnp.stack(make(at)) for at in range(layers)])
-
-    gains = pair(lambda at: [one[at][0], rows_of[at][1]])
-    shifts = pair(lambda at: [one[at][1], rows_of[at][2]])
-    obiases = pair(lambda at: [rows_of[at][3], rows_of[at][0]])
-    bups = small[cut : cut + layers, :up_part]
-    bqv = small[cut + layers :, :qv_part].reshape(layers, 2, qv_part)
+    by_width = lax.dynamic_slice(small, (0, t_me * norm_part), (6 * layers, norm_part))
+    gains, shifts, obiases = by_width.reshape(3, layers, 2, norm_part)
+    bups = small[6 * layers : 7 * layers, :up_part]
+    bqv = small[7 * layers : 9 * layers, :qv_part].reshape(layers, 2, qv_part)
 
     def stacked(make):
         return jnp.stack([make(*weight_grads[at]) for at in range(layers)])

time: 686 us -> 643 us (0.937)
  local copies, waits for them, and re-layouts: 104 us -> 71 us
  other arithmetic: 75.6 us -> 50.7 us
  waiting for transfers between devices: 88.1 us -> 100 us
  Pallas kernels: 299 us -> 307 us
    concatenate x6 -> x0, local copies, waits for them, and re-layouts: 21.5 us -> none  [the longest x4 21.5 us: local(): jnp.concatenate([by_width, bups[t * layers:(t + 1) * layers]] + ([bqv[t *...]
    ppermute x86, waiting for transfers between devices: 88.1 us -> 100 us  [exchange(): return lax.ppermute(value, axis, [(i, i ^ mask) for i in range(count)])]
    pallas_call x0 -> x1, Pallas kernels: none -> 8.53 us  [finish(): pl.pallas_call(functools.partial(finish_kernel, layers, wide), grid=(1,),...]
    slice x14 -> x1, local copies, waits for them, and re-layouts: 8.74 us -> 0.57 us  [local(): bups = small[6 * layers:7 * layers, :up_part]]
    convert_element_type x22, other arithmetic: 30.1 us -> 22.2 us  [add_low(): return (kept.astype(f32) + received.astype(f32)).astype(bf16)]
    unnamed x277 -> x275, local copies, waits for them, and re-layouts: 37.3 us -> 38.8 us
  transfers between devices with their start and end apart: 86 -> 86, of which waited for: 27 -> 30; matrix products, arithmetic and copies ran while one was open for 17% -> 14% of each run, Pallas kernels for 41% -> 44%
where the time goes in v8:
time: 643 us; the launch traced here: 633 us
  Pallas kernels  307 us (48%)
  waiting for transfers between devices  100 us (16%)
  starting transfers between devices  71.3 us (11%)
  local copies, waits for them, and re-layouts  71 us (11%)
  other arithmetic  50.7 us (8%)
  matrix products  29.5 us (5%)
    pallas_call x4, Pallas kernels, attend_back(): pl.pallas_call(functools.partial(attend_back_kernel, row_count, quarter,...  123 us
    ppermute x86, waiting for transfers between devices, exchange(): return lax.ppermute(value, axis, [(i, i ^ mask) for i in range(count)])  100 us
    pallas_call x4, Pallas kernels, attend(): pl.pallas_call(functools.partial(attend_kernel, row_count, quarter, min(5...  72.9 us
    ppermute x86, starting transfers between devices, exchange(): return lax.ppermute(value, axis, [(i, i ^ mask) for i in range(count)])  71.3 us
    pallas_call x2, Pallas kernels, feed_back(): pl.pallas_call(functools.partial(feed_back_kernel, at, layers), grid=(hid...  64.2 us
    unnamed x275, local copies, waits for them, and re-layouts  38.8 us
    pallas_call x2, Pallas kernels, feed(): pl.pallas_call(functools.partial(feed_kernel, at, layers), grid=(hidden /...  38.4 us
    convert_element_type x22, other arithmetic, add_low(): return (kept.astype(f32) + received.astype(f32)).astype(bf16)  22.2 us
  transfers between devices with their start and end apart: 86, of which 30 were waited for; matrix products, arithmetic and copies ran while one was open for 14% of the time, Pallas kernels for 44%

profile of v8, /device:TPU:0, one launch (start us, length us, event | category | flops | bytes accessed | tf_op | source)
XLA Modules:
  0.0 633.4 jit_solution(6191317806677335069)
XLA Ops:
  0.7 1.7 slice_bitcast_fusion.24
  4.4 4.2 collective-permute-start.3
  9.0 2.9 collective-permute-start.1
  19.0 2.9 collective-permute-done.4
  28.7 2.2 collective-permute-done.6
  36.3 2.7 fusion.93
  39.0 2.0 copy.44.refs_0_
  41.5 5.7 collective-permute-done.12
  49.8 2.0 pad_maximum_fusion.14
  51.9 1.7 collective-permute-start.14
  56.1 1.7 collective-permute-start.16
  60.5 5.4 collective-permute-done.15
  65.9 4.8 collective-permute-done.16
  77.4 2.8 collective-permute-start.21
  81.4 17.3 %shard_map.194 = (bf16[1536,576]{1,0:T(8,128)(2,1)}, bf16[1536,192]{1,0:T(8,128)(2,1)}, f32[1536,8]{1,0:T(8,128)}) custom-call(bf16[768,768]{1,0:T(8,128)(2,1)} %copy-done.7, bf16[768,768]{1,0:T(8,128)(2,1)} %copy-done.26, bf16[768,384]{1,0:T(8,128)(2,1)} %copy-done.25, bf16[768,384]{1,0:T(8,128)(2,1)} %copy-done.19, f32[16,768]{1,0:T(8,128)} %concatenate.141.refs_4_), custom_call_target="tpu_custom_call" | custom-call | tf_op jit(solution)/shard_map/pallas_call | solution.py:383
  100.0 1.7 collective-permute-start.22
  101.7 1.7 collective-permute-start.23
  106.6 19.2 %shard_map.195 = (f32[768,768]{1,0:T(8,128)}, bf16[768,768]{1,0:T(8,128)(2,1)}, bf16[1536,576]{1,0:T(8,128)(2,1)}, bf16[1536,192]{1,0:T(8,128)(2,1)}, f32[1536,8]{1,0:T(8,128)}) custom-call(bf16[768,768]{1,0:T(8,128)(2,1)} %copy-done.7, bf16[768,768]{1,0:T(8,128)(2,1)} %copy-done.26, bf16[768,384]{1,0:T(8,128)(2,1)} %copy-done.23, ...), custom_call_target="tpu_custom_call" | custom-call | tf_op jit(solution)/shard_map/pallas_call | solution.py:383
  128.0 1.7 collective-permute-start.26
  133.7 3.7 collective-permute-done.26
  138.6 2.0 collective-permute-done.27
  140.6 7.9 %collective-permute-done.28 = bf16[96,1536]{1,0:T(8,128)(2,1)S(1)} collective-permute-done((bf16[96,1536]{1,0:T(8,128)(2,1)S(1)}, bf16[96,1536]{1,0:T(8,128)(2,1)S(1)}, u32[]{:S(2)}, u32[]{:S(2)}) %collective-permute-start.28) | collective-permute-done | bytes 294944 | tf_op jit(solution)/shard_map/ppermute | solution.py:23
  155.6 20.2 %shard_map.196 = (bf16[768,768]{1,0:T(8,128)(2,1)}, bf16[768,768]{1,0:T(8,128)(2,1)}, bf16[768,768]{1,0:T(8,128)(2,1)}, bf16[768,768]{1,0:T(8,128)(2,1)}, bf16[7...) custom-call(f32[768,768]{1,0:T(8,128)} %copy-done, ...), custom_call_target="tpu_custom_call" | custom-call | tf_op jit(solution)/shard_map/pallas_call | solution.py:565
  175.8 2.9 collective-permute-done.38
  186.4 17.2 %shard_map.197 = (bf16[1536,576]{1,0:T(8,128)(2,1)}, bf16[1536,192]{1,0:T(8,128)(2,1)}, f32[1536,8]{1,0:T(8,128)}) custom-call(bf16[768,768]{1,0:T(8,128)(2,1)} %get-tuple-element.397.refs_0_, bf16[768,768]{1,0:T(8,128)(2,1)} %copy-done.9, bf16[768,384]{1,0:T(8,128)(2,1)} %pad_maximum_fusion.15.refs_2_, bf16[768,384]{1,0:T(8,128)(2,1)} %copy-done.20, ...), custom_call_target="tpu_custom_call" | custom-call | tf_op jit(solution)/shard_map/pallas_call | solution.py:383
  206.5 1.7 collective-permute-start.43
  210.4 19.2 %shard_map.198 = (f32[768,768]{1,0:T(8,128)}, bf16[768,768]{1,0:T(8,128)(2,1)}, bf16[1536,576]{1,0:T(8,128)(2,1)}, bf16[1536,192]{1,0:T(8,128)(2,1)}, f32[1536,8]{1,0:T(8,128)}) custom-call(bf16[768,768]{1,0:T(8,128)(2,1)} %get-tuple-element.397.refs_0_, bf16[768,768]{1,0:T(8,128)(2,1)} %copy-done.9, bf16[768,384]{1,0:T(8,128)(2,1)} %copy-done.24, ...), custom_call_target="tpu_custom_call" | custom-call | tf_op jit(solution)/shard_map/pallas_call | solution.py:383
  229.7 4.4 collective-permute-done.44
  238.6 1.7 collective-permute-done.48.refs_10_.refs_9_
  240.3 3.4 collective-permute-done.45.refs_2_
  244.7 18.2 %shard_map.199 = (bf16[768,768]{1,0:T(8,128)(2,1)}, bf16[768,768]{1,0:T(8,128)(2,1)}, bf16[768,768]{1,0:T(8,128)(2,1)}, bf16[768,768]{1,0:T(8,128)(2,1)}, bf16[7...) custom-call(f32[768,768]{1,0:T(8,128)} %get-tuple-element.467.refs_0, ...), custom_call_target="tpu_custom_call" | custom-call | tf_op jit(solution)/shard_map/pallas_call | solution.py:565
  265.3 2.6 fusion.20.refs_0_
  267.9 30.5 %shard_map.200 = (bf16[4,768,768]{2,1,0:T(8,128)(2,1)}, bf16[4,768,768]{2,1,0:T(8,128)(2,1)}, f32[4,768]{1,0:T(4,128)}, f32[768,768]{1,0:T(8,128)}, bf16[768,768]{1,0:T(8,128)(2,1)}, /*index=5*/f32[8,768]{1,0:T(8,128)}) custom-call(f32[768,768]{1,0:T(8,128)} %fusion.20.refs_0_, f32[768,768]{1,0:T(8,128)} %get-tuple-element.411.refs_1_, ...), custom_call_target="tpu_custom_call" | custom-call | tf_op jit(solution)/shard_map/pallas_call | solution.py:643
  302.4 5.9 collective-permute-done.52.refs_1_
  309.4 28.2 %shard_map.201 = (bf16[1536,576]{1,0:T(8,128)(2,1)}, f32[8,576]{1,0:T(8,128)}) custom-call(bf16[768,768]{1,0:T(8,128)(2,1)} %get-tuple-element.448.refs_0_, bf16[768,768]{1,0:T(8,128)(2,1)} %copy-done.5, bf16[768,384]{1,0:T(8,128)(2,1)} %copy-done.24, bf16[768,384]{1,0:T(8,128)(2,1)} %copy-done.18, bf16[1536,576]{1,0:T(8,128)(2,1)} %get-tuple-element.439.refs_4_, ...), custom_call_target="tpu_custom_call" | custom-call | tf_op jit(solution)/shard_map/pallas_call | solution.py:477
  337.6 1.8 fusion.69
  340.7 2.9 add_convert_fusion.5
  343.6 3.1 fusion.32
  347.9 1.7 collective-permute-start.54
  352.1 1.7 convolution_convert_fusion
  354.7 33.2 %shard_map.202 = (f32[768,768]{1,0:T(8,128)}, bf16[768,768]{1,0:T(8,128)(2,1)}, bf16[1536,576]{1,0:T(8,128)(2,1)}, f32[8,576]{1,0:T(8,128)}) custom-call(bf16[768,768]{1,0:T(8,128)(2,1)} %get-tuple-element.448.refs_0_, bf16[768,768]{1,0:T(8,128)(2,1)} %copy-done.5, bf16[768,384]{1,0:T(8,128)(2,1)} %pad_maximum_fusion.15.refs_2_, ...), custom_call_target="tpu_custom_call" | custom-call | tf_op jit(solution)/shard_map/pallas_call | solution.py:477
  389.2 4.0 convolution_convert_fusion.1
  393.3 2.1 add_convert_fusion.4
  395.4 2.5 fusion.5
  406.1 33.7 %shard_map.203 = (bf16[4,768,768]{2,1,0:T(8,128)(2,1)}, bf16[4,768,768]{2,1,0:T(8,128)(2,1)}, f32[4,768]{1,0:T(4,128)}, f32[768,768]{1,0:T(8,128)}, bf16[768,768]{1,0:T(8,128)(2,1)}, /*index=5*/f32[8,768]{1,0:T(8,128)}) custom-call(f32[768,768]{1,0:T(8,128)} %get-tuple-element.466.refs_0_, f32[768,768]{1,0:T(8,128)} %get-tuple-element.467.refs_0_.refs_1_, ...), custom_call_target="tpu_custom_call" | custom-call | tf_op jit(solution)/shard_map/pallas_call | solution.py:643
  450.8 5.3 collective-permute-done.61
  456.3 6.0 collective-permute-done.63
  471.7 28.5 %shard_map.204 = (bf16[1536,576]{1,0:T(8,128)(2,1)}, f32[8,576]{1,0:T(8,128)}) custom-call(bf16[768,768]{1,0:T(8,128)(2,1)} %get-tuple-element.523.refs_0_, bf16[768,768]{1,0:T(8,128)(2,1)} %copy-done.3, bf16[768,384]{1,0:T(8,128)(2,1)} %copy-done.23, bf16[768,384]{1,0:T(8,128)(2,1)} %copy-done.17, bf16[1536,576]{1,0:T(8,128)(2,1)} %get-tuple-element.509.refs_4_, ...), custom_call_target="tpu_custom_call" | custom-call | tf_op jit(solution)/shard_map/pallas_call | solution.py:477
  500.2 3.5 fusion.26
  503.8 2.4 add_convert_fusion.1
  506.2 2.8 fusion.4
  515.1 1.7 add_convert_fusion.17
  519.5 2.3 collective-permute-start.71
  523.0 33.2 %shard_map.205 = (f32[768,768]{1,0:T(8,128)}, bf16[768,768]{1,0:T(8,128)(2,1)}, bf16[1536,576]{1,0:T(8,128)(2,1)}, f32[8,576]{1,0:T(8,128)}) custom-call(bf16[768,768]{1,0:T(8,128)(2,1)} %get-tuple-element.523.refs_0_, bf16[768,768]{1,0:T(8,128)(2,1)} %copy-done.3, bf16[768,384]{1,0:T(8,128)(2,1)} %copy-done.25, bf16[768,384]{1,0:T(8,128)(2,1)} %copy-done.19, ...), custom_call_target="tpu_custom_call" | custom-call | tf_op jit(solution)/shard_map/pallas_call | solution.py:477
  561.0 1.7 collective-permute-start.75
  568.4 5.6 collective-permute-done.75
  574.0 4.4 collective-permute-done.74
  579.8 8.5 %shard_map.206 = (f32[768,768]{1,0:T(8,128)}, bf16[384,768]{1,0:T(8,128)(2,1)}, f32[24,768]{1,0:T(8,128)}, f32[24,768]{1,0:T(8,128)}, f32[24,768]{1,0:T(8,128)}, /*index=5*/f32[24,768]{1,0:T(8,128)}) custom-call(f32[768,768]{1,0:T(8,128)} %copy-done, f32[768,768]{1,0:T(8,128)} %get-tuple-element.486.refs_1_, f32[768,768]{1,0:T(8,128)} %get-tuple-element.531.refs_2_, ...), custom_call_target="tpu_custom_call" | custom-call | tf_op jit(solution)/shard_map/pallas_call | solution.py:708
  593.8 8.5 %collective-permute-done.80 = f32[24,768]{1,0:T(8,128)S(1)} collective-permute-done((f32[24,768]{1,0:T(8,128)S(1)}, f32[24,768]{1,0:T(8,128)S(1)}, u32[]{:S(2)}, u32[]{:S(2)}) %collective-permute-start.80) | collective-permute-done | bytes 73760 | tf_op jit(solution)/shard_map/ppermute | solution.py:23
  604.1 2.0 collective-permute-start.82
  607.1 8.8 %collective-permute-done.82 = bf16[96,768]{0,1:T(8,128)(2,1)S(1)} collective-permute-done((bf16[96,768]{0,1:T(8,128)(2,1)S(1)}, bf16[96,768]{0,1:T(8,128)(2,1)S(1)}, u32[]{:S(2)}, u32[]{:S(2)}) %collective-permute-start.82) | collective-permute-done | bytes 147488 | tf_op jit(solution)/shard_map/ppermute | solution.py:23
  622.5 1.7 pad_maximum_fusion.1
  626.6 2.6 copy.46
  629.2 2.6 copy.45
  (568 shorter events, 157.2 us)
Async XLA Ops:
  4.4 12.4 %collective-permute-start.3 = (f32[6,768]{1,0:T(8,128)S(1)}, f32[6,768]{1,0:T(8,128)S(1)}, u32[]{:S(2)}, u32[]{:S(2)}) collective-permute-start(f32[6,768]{1,0:T(8,128)S(1)} %pad_maximum_fusion.31), channel_id=1, source_target_pairs={{0,16},{4,20},{8,24},{12,28},{16,0},{20,4},{24,8},{28,12},{1,17},{... | collective-permute-start | bytes 55304 | tf_op jit(solution)/shard_map/ppermute | solution.py:23
  9.0 12.9 %collective-permute-start.1 = (bf16[96,768]{1,0:T(8,128)(2,1)S(1)}, bf16[96,768]{1,0:T(8,128)(2,1)S(1)}, u32[]{:S(2)}, u32[]{:S(2)}) collective-permute-start(bf16[96,768]{1,0:T(8,128)(2,1)S(1)} %pad_maximum_fusion.24), channel_id=1, source_target_pairs={{0,16},{4,20},{8,24},{12,28},{16,0},{20,4},{24,8},{28,12},{1,17},{... | collective-permute-start | bytes 442376 | tf_op jit(solution)/shard_map/ppermute | solution.py:23
  12.1 24.1 %collective-permute-start = (bf16[375,768]{1,0:T(8,128)(2,1)S(1)}, bf16[375,768]{1,0:T(8,128)(2,1)S(1)}, u32[]{:S(2)}, u32[]{:S(2)}) collective-permute-start(bf16[375,768]{1,0:T(8,128)(2,1)S(1)} %get-tuple-element.618), channel_id=1, source_target_pairs={{0,2},{1,3},{2,0},{3,1},{4,6},{5,7},{6,4},{7,5},{8,10},{9,11},{10,... | collective-permute-start | bytes 1728008 | tf_op jit(solution)/shard_map/ppermute | solution.py:23
  31.0 10.5 %collective-permute-start.13 = (f32[20,768]{1,0:T(8,128)S(1)}, f32[20,768]{1,0:T(8,128)S(1)}, u32[]{:S(2)}, u32[]{:S(2)}) collective-permute-start(f32[20,768]{1,0:T(8,128)S(1)} %pad_maximum_fusion.26), channel_id=1, source_target_pairs={{0,2},{1,3},{2,0},{3,1},{4,6},{5,7},{6,4},{7,5},{8,10},{9,11},{10,... | collective-permute-start | bytes 184328 | tf_op jit(solution)/shard_map/ppermute | solution.py:23
  32.3 9.2 %collective-permute-start.10 = (bf16[384,384]{1,0:T(8,128)(2,1)S(1)}, bf16[384,384]{1,0:T(8,128)(2,1)}, u32[]{:S(2)}, u32[]{:S(2)}) collective-permute-start(bf16[384,384]{1,0:T(8,128)(2,1)S(1)} %get-tuple-element.309), channel_id=1, source_target_pairs={{0,4},{4,0},{8,12},{12,8},{16,20},{20,16},{24,28},{28,24},{1,5},{5... | collective-permute-start | bytes 884744 | tf_op jit(solution)/shard_map/ppermute | solution.py:23
  34.8 12.4 %collective-permute-start.12 = (bf16[96,1536]{1,0:T(8,128)(2,1)S(1)}, bf16[96,1536]{1,0:T(8,128)(2,1)}, u32[]{:S(2)}, u32[]{:S(2)}) collective-permute-start(bf16[96,1536]{1,0:T(8,128)(2,1)S(1)} %pad_maximum_fusion.21), channel_id=1, source_target_pairs={{0,16},{4,20},{8,24},{12,28},{16,0},{20,4},{24,8},{28,12},{1,17},{... | collective-permute-start | bytes 884744 | tf_op jit(solution)/shard_map/ppermute | solution.py:23
  48.3 22.4 %collective-permute-start.18 = (bf16[768,768]{1,0:T(8,128)(2,1)S(1)}, bf16[768,768]{1,0:T(8,128)(2,1)S(1)}, u32[]{:S(2)}, u32[]{:S(2)}) collective-permute-start(bf16[768,768]{1,0:T(8,128)(2,1)S(1)} %add_convert_fusion.7.refs_0_), channel_id=1, source_target_pairs={{0,1},{1,0},{2,3},{3,2},{4,5},{5,4},{6,7},{7,6},{8,9},{9,8},{10,11... | collective-permute-start | bytes 3538952 | tf_op jit(solution)/shard_map/ppermute | solution.py:23
  51.9 18.8 %collective-permute-start.14 = (bf16[768,384]{1,0:T(8,128)(2,1)S(1)}, bf16[768,384]{1,0:T(8,128)(2,1)S(1)}, u32[]{:S(2)}, u32[]{:S(2)}) collective-permute-start(bf16[768,384]{1,0:T(8,128)(2,1)S(1)} %pad_maximum_fusion.13.refs_2_), channel_id=1, source_target_pairs={{0,2},{1,3},{2,0},{3,1},{4,6},{5,7},{6,4},{7,5},{8,10},{9,11},{10,... | collective-permute-start | bytes 1769480 | tf_op jit(solution)/shard_map/ppermute | solution.py:23
  53.6 17.1 %collective-permute-start.17 = (bf16[192,1536]{1,0:T(8,128)(2,1)}, bf16[192,1536]{1,0:T(8,128)(2,1)}, u32[]{:S(2)}, u32[]{:S(2)}) collective-permute-start(bf16[192,1536]{1,0:T(8,128)(2,1)} %pad_maximum_fusion.14), channel_id=1, source_target_pairs={{0,8},{4,12},{8,0},{12,4},{16,24},{20,28},{24,16},{28,20},{1,9},{5... | collective-permute-start | bytes 1769480 | tf_op jit(solution)/shard_map/ppermute | solution.py:23
  55.7 10.2 %collective-permute-start.15 = (bf16[384,384]{1,0:T(8,128)(2,1)}, bf16[384,384]{1,0:T(8,128)(2,1)S(1)}, u32[]{:S(2)}, u32[]{:S(2)}) collective-permute-start(bf16[384,384]{1,0:T(8,128)(2,1)} %copy-done.70), channel_id=1, source_target_pairs={{0,4},{4,0},{8,12},{12,8},{16,20},{20,16},{24,28},{28,24},{1,5},{5... | collective-permute-start | bytes 884744 | tf_op jit(solution)/shard_map/ppermute | solution.py:23
  56.1 14.6 %collective-permute-start.16 = (bf16[384,384]{1,0:T(8,128)(2,1)}, bf16[384,384]{1,0:T(8,128)(2,1)S(1)}, u32[]{:S(2)}, u32[]{:S(2)}) collective-permute-start(bf16[384,384]{1,0:T(8,128)(2,1)} %collective-permute-done.11), channel_id=1, source_target_pairs={{0,4},{4,0},{8,12},{12,8},{16,20},{20,16},{24,28},{28,24},{1,5},{5... | collective-permute-start | bytes 884744 | tf_op jit(solution)/shard_map/ppermute | solution.py:23
  73.9 26.0 %collective-permute-start.19 = (bf16[384,768]{1,0:T(8,128)(2,1)}, bf16[384,768]{1,0:T(8,128)(2,1)S(1)}, u32[]{:S(2)}, u32[]{:S(2)}) collective-permute-start(bf16[384,768]{1,0:T(8,128)(2,1)} %get-tuple-element.322), channel_id=1, source_target_pairs={{0,4},{4,0},{8,12},{12,8},{16,20},{20,16},{24,28},{28,24},{1,5},{5... | collective-permute-start | bytes 1769480 | tf_op jit(solution)/shard_map/ppermute | solution.py:23
  74.4 25.5 %collective-permute-start.20 = (bf16[384,768]{1,0:T(8,128)(2,1)S(1)}, bf16[384,768]{1,0:T(8,128)(2,1)}, u32[]{:S(2)}, u32[]{:S(2)}) collective-permute-start(bf16[384,768]{1,0:T(8,128)(2,1)S(1)} %get-tuple-element.337), channel_id=1, source_target_pairs={{0,2},{1,3},{2,0},{3,1},{4,6},{5,7},{6,4},{7,5},{8,10},{9,11},{10,... | collective-permute-start | bytes 1769480 | tf_op jit(solution)/shard_map/ppermute | solution.py:23
  77.4 22.5 %collective-permute-start.21 = (bf16[96,768]{1,0:T(8,128)(2,1)}, bf16[96,768]{1,0:T(8,128)(2,1)S(1)}, u32[]{:S(2)}, u32[]{:S(2)}) collective-permute-start(bf16[96,768]{1,0:T(8,128)(2,1)} %pad_maximum_fusion.25), channel_id=1, source_target_pairs={{0,16},{4,20},{8,24},{12,28},{16,0},{20,4},{24,8},{28,12},{1,17},{... | collective-permute-start | bytes 442376 | tf_op jit(solution)/shard_map/ppermute | solution.py:23
  100.0 27.2 %collective-permute-start.22 = (bf16[768,768]{1,0:T(8,128)(2,1)S(1)}, bf16[768,768]{1,0:T(8,128)(2,1)S(1)}, u32[]{:S(2)}, u32[]{:S(2)}) collective-permute-start(bf16[768,768]{1,0:T(8,128)(2,1)S(1)} %constant_dynamic-update-slice_fusion.4.refs_5_.refs_7_), channel_id=1, source_target_pairs={{0,2},{1,3},{2,0},{3,1},{4,6},{5,7},{6,4},{7,5},{8,10},{9,11},{10,... | collective-permute-start | bytes 3538952 | tf_op jit(solution)/shard_map/ppermute | solution.py:23
  101.7 24.2 %collective-permute-start.23 = (bf16[384,768]{1,0:T(8,128)(2,1)S(1)}, bf16[384,768]{1,0:T(8,128)(2,1)}, u32[]{:S(2)}, u32[]{:S(2)}) collective-permute-start(bf16[384,768]{1,0:T(8,128)(2,1)S(1)} %copy-done.55), channel_id=1, source_target_pairs={{0,4},{4,0},{8,12},{12,8},{16,20},{20,16},{24,28},{28,24},{1,5},{5... | collective-permute-start | bytes 1769480 | tf_op jit(solution)/shard_map/ppermute | solution.py:23
  103.4 23.8 %collective-permute-start.24 = (bf16[384,768]{1,0:T(8,128)(2,1)}, bf16[384,768]{1,0:T(8,128)(2,1)}, u32[]{:S(2)}, u32[]{:S(2)}) collective-permute-start(bf16[384,768]{1,0:T(8,128)(2,1)} %collective-permute-done.20), channel_id=1, source_target_pairs={{0,4},{4,0},{8,12},{12,8},{16,20},{20,16},{24,28},{28,24},{1,5},{5... | collective-permute-start | bytes 1769480 | tf_op jit(solution)/shard_map/ppermute | solution.py:23
  104.5 21.4 %collective-permute-start.25 = (bf16[192,768]{1,0:T(8,128)(2,1)S(1)}, bf16[192,768]{1,0:T(8,128)(2,1)S(1)}, u32[]{:S(2)}, u32[]{:S(2)}) collective-permute-start(bf16[192,768]{1,0:T(8,128)(2,1)S(1)} %constant_dynamic-update-slice_fusion.6), channel_id=1, source_target_pairs={{0,8},{4,12},{8,0},{12,4},{16,24},{20,28},{24,16},{28,20},{1,9},{5... | collective-permute-start | bytes 884744 | tf_op jit(solution)/shard_map/ppermute | solution.py:23
  127.2 21.3 %collective-permute-start.29 = (bf16[768,768]{1,0:T(8,128)(2,1)}, bf16[768,768]{1,0:T(8,128)(2,1)S(1)}, u32[]{:S(2)}, u32[]{:S(2)}) collective-permute-start(bf16[768,768]{1,0:T(8,128)(2,1)} %get-tuple-element.353), channel_id=1, source_target_pairs={{0,1},{1,0},{2,3},{3,2},{4,5},{5,4},{6,7},{7,6},{8,9},{9,8},{10,11... | collective-permute-start | bytes 3538952 | tf_op jit(solution)/shard_map/ppermute | solution.py:23
  128.0 9.4 %collective-permute-start.26 = (bf16[384,384]{1,0:T(8,128)(2,1)S(1)}, bf16[384,384]{1,0:T(8,128)(2,1)S(1)}, u32[]{:S(2)}, u32[]{:S(2)}) collective-permute-start(bf16[384,384]{1,0:T(8,128)(2,1)S(1)} %get-tuple-element.350), channel_id=1, source_target_pairs={{0,4},{4,0},{8,12},{12,8},{16,20},{20,16},{24,28},{28,24},{1,5},{5... | collective-permute-start | bytes 884744 | tf_op jit(solution)/shard_map/ppermute | solution.py:23
  129.7 21.5 %collective-permute-start.34 = (bf16[768,768]{1,0:T(8,128)(2,1)S(1)}, bf16[768,768]{1,0:T(8,128)(2,1)S(1)}, u32[]{:S(2)}, u32[]{:S(2)}) collective-permute-start(bf16[768,768]{1,0:T(8,128)(2,1)S(1)} %constant_dynamic-update-slice_fusion.4.refs_5_.refs_7_), channel_id=1, source_target_pairs={{0,1},{1,0},{2,3},{3,2},{4,5},{5,4},{6,7},{7,6},{8,9},{9,8},{10,11... | collective-permute-start | bytes 3538952 | tf_op jit(solution)/shard_map/ppermute | solution.py:23
  131.0 9.6 %collective-permute-start.27 = (bf16[384,384]{1,0:T(8,128)(2,1)}, bf16[384,384]{1,0:T(8,128)(2,1)}, u32[]{:S(2)}, u32[]{:S(2)}) collective-permute-start(bf16[384,384]{1,0:T(8,128)(2,1)} %get-tuple-element.358), channel_id=1, source_target_pairs={{0,2},{1,3},{2,0},{3,1},{4,6},{5,7},{6,4},{7,5},{8,10},{9,11},{10,... | collective-permute-start | bytes 884744 | tf_op jit(solution)/shard_map/ppermute | solution.py:23
  132.3 16.1 %collective-permute-start.28 = (bf16[96,1536]{1,0:T(8,128)(2,1)S(1)}, bf16[96,1536]{1,0:T(8,128)(2,1)S(1)}, u32[]{:S(2)}, u32[]{:S(2)}) collective-permute-start(bf16[96,1536]{1,0:T(8,128)(2,1)S(1)} %copy-done.72), channel_id=1, source_target_pairs={{0,16},{4,20},{8,24},{12,28},{16,0},{20,4},{24,8},{28,12},{1,17},{... | collective-permute-start | bytes 884744 | tf_op jit(solution)/shard_map/ppermute | solution.py:23
  137.4 13.7 %collective-permute-start.37 = (bf16[768,768]{1,0:T(8,128)(2,1)S(1)}, bf16[768,768]{1,0:T(8,128)(2,1)S(1)}, u32[]{:S(2)}, u32[]{:S(2)}) collective-permute-start(bf16[768,768]{1,0:T(8,128)(2,1)S(1)} %constant_dynamic-update-slice_fusion.14.refs_11_.refs_13_), channel_id=1, source_target_pairs={{0,1},{1,0},{2,3},{3,2},{4,5},{5,4},{6,7},{7,6},{8,9},{9,8},{10,11... | collective-permute-start | bytes 3538952 | tf_op jit(solution)/shard_map/ppermute | solution.py:23
  140.6 11.9 %collective-permute-start.36 = (bf16[768,768]{1,0:T(8,128)(2,1)S(1)}, bf16[768,768]{1,0:T(8,128)(2,1)S(1)}, u32[]{:S(2)}, u32[]{:S(2)}) collective-permute-start(bf16[768,768]{1,0:T(8,128)(2,1)S(1)} %constant_dynamic-update-slice_fusion.12.refs_9_.refs_11_), channel_id=1, source_target_pairs={{0,1},{1,0},{2,3},{3,2},{4,5},{5,4},{6,7},{7,6},{8,9},{9,8},{10,11... | collective-permute-start | bytes 3538952 | tf_op jit(solution)/shard_map/ppermute | solution.py:23
  150.4 28.3 %collective-permute-start.30 = (bf16[768,384]{1,0:T(8,128)(2,1)}, bf16[768,384]{1,0:T(8,128)(2,1)S(1)}, u32[]{:S(2)}, u32[]{:S(2)}) collective-permute-start(bf16[768,384]{1,0:T(8,128)(2,1)} %pad_maximum_fusion.15.refs_2_), channel_id=1, source_target_pairs={{0,2},{1,3},{2,0},{3,1},{4,6},{5,7},{6,4},{7,5},{8,10},{9,11},{10,... | collective-permute-start | bytes 1769480 | tf_op jit(solution)/shard_map/ppermute | solution.py:23
  151.2 27.6 %collective-permute-start.33 = (bf16[192,1536]{1,0:T(8,128)(2,1)}, bf16[192,1536]{1,0:T(8,128)(2,1)S(1)}, u32[]{:S(2)}, u32[]{:S(2)}) collective-permute-start(bf16[192,1536]{1,0:T(8,128)(2,1)} %pad_maximum_fusion.16), channel_id=1, source_target_pairs={{0,8},{4,12},{8,0},{12,4},{16,24},{20,28},{24,16},{28,20},{1,9},{5... | collective-permute-start | bytes 1769480 | tf_op jit(solution)/shard_map/ppermute | solution.py:23
  151.2 27.5 %collective-permute-start.38 = (bf16[375,768]{1,0:T(8,128)(2,1)}, bf16[375,768]{1,0:T(8,128)(2,1)S(1)}, u32[]{:S(2)}, u32[]{:S(2)}) collective-permute-start(bf16[375,768]{1,0:T(8,128)(2,1)} %get-tuple-element.378), channel_id=1, source_target_pairs={{0,2},{1,3},{2,0},{3,1},{4,6},{5,7},{6,4},{7,5},{8,10},{9,11},{10,... | collective-permute-start | bytes 1728008 | tf_op jit(solution)/shard_map/ppermute | solution.py:23
  152.5 26.2 %collective-permute-start.31 = (bf16[384,384]{1,0:T(8,128)(2,1)}, bf16[384,384]{1,0:T(8,128)(2,1)}, u32[]{:S(2)}, u32[]{:S(2)}) collective-permute-start(bf16[384,384]{1,0:T(8,128)(2,1)} %get-tuple-element.358), channel_id=1, source_target_pairs={{0,4},{4,0},{8,12},{12,8},{16,20},{20,16},{24,28},{28,24},{1,5},{5... | collective-permute-start | bytes 884744 | tf_op jit(solution)/shard_map/ppermute | solution.py:23
  154.6 24.1 %collective-permute-start.32 = (bf16[384,384]{1,0:T(8,128)(2,1)}, bf16[384,384]{1,0:T(8,128)(2,1)S(1)}, u32[]{:S(2)}, u32[]{:S(2)}) collective-permute-start(bf16[384,384]{1,0:T(8,128)(2,1)} %collective-permute-done.27), channel_id=1, source_target_pairs={{0,4},{4,0},{8,12},{12,8},{16,20},{20,16},{24,28},{28,24},{1,5},{5... | collective-permute-start | bytes 884744 | tf_op jit(solution)/shard_map/ppermute | solution.py:23
  181.1 22.5 %collective-permute-start.39 = (bf16[384,768]{1,0:T(8,128)(2,1)S(1)}, bf16[384,768]{1,0:T(8,128)(2,1)S(1)}, u32[]{:S(2)}, u32[]{:S(2)}) collective-permute-start(bf16[384,768]{1,0:T(8,128)(2,1)S(1)} %get-tuple-element.382), channel_id=1, source_target_pairs={{0,4},{4,0},{8,12},{12,8},{16,20},{20,16},{24,28},{28,24},{1,5},{5... | collective-permute-start | bytes 1769480 | tf_op jit(solution)/shard_map/ppermute | solution.py:23
  181.5 22.1 %collective-permute-start.40 = (bf16[384,768]{1,0:T(8,128)(2,1)S(1)}, bf16[384,768]{1,0:T(8,128)(2,1)S(1)}, u32[]{:S(2)}, u32[]{:S(2)}) collective-permute-start(bf16[384,768]{1,0:T(8,128)(2,1)S(1)} %get-tuple-element.394), channel_id=1, source_target_pairs={{0,2},{1,3},{2,0},{3,1},{4,6},{5,7},{6,4},{7,5},{8,10},{9,11},{10,... | collective-permute-start | bytes 1769480 | tf_op jit(solution)/shard_map/ppermute | solution.py:23
  205.3 28.8 %collective-permute-start.42 = (bf16[768,768]{1,0:T(8,128)(2,1)}, bf16[768,768]{1,0:T(8,128)(2,1)S(1)}, u32[]{:S(2)}, u32[]{:S(2)}) collective-permute-start(bf16[768,768]{1,0:T(8,128)(2,1)} %constant_dynamic-update-slice_fusion.20.refs_5_.refs_4_), channel_id=1, source_target_pairs={{0,2},{1,3},{2,0},{3,1},{4,6},{5,7},{6,4},{7,5},{8,10},{9,11},{10,... | collective-permute-start | bytes 3538952 | tf_op jit(solution)/shard_map/ppermute | solution.py:23
  206.5 23.2 %collective-permute-start.43 = (bf16[384,768]{1,0:T(8,128)(2,1)S(1)}, bf16[384,768]{1,0:T(8,128)(2,1)}, u32[]{:S(2)}, u32[]{:S(2)}) collective-permute-start(bf16[384,768]{1,0:T(8,128)(2,1)S(1)} %get-tuple-element.394), channel_id=1, source_target_pairs={{0,4},{4,0},{8,12},{12,8},{16,20},{20,16},{24,28},{28,24},{1,5},{5... | collective-permute-start | bytes 1769480 | tf_op jit(solution)/shard_map/ppermute | solution.py:23
  208.2 25.9 %collective-permute-start.44 = (bf16[384,768]{1,0:T(8,128)(2,1)}, bf16[384,768]{1,0:T(8,128)(2,1)}, u32[]{:S(2)}, u32[]{:S(2)}) collective-permute-start(bf16[384,768]{1,0:T(8,128)(2,1)} %copy-done.86), channel_id=1, source_target_pairs={{0,4},{4,0},{8,12},{12,8},{16,20},{20,16},{24,28},{28,24},{1,5},{5... | collective-permute-start | bytes 1769480 | tf_op jit(solution)/shard_map/ppermute | solution.py:23
  209.6 28.3 %collective-permute-start.46 = (bf16[768,768]{1,0:T(8,128)(2,1)}, bf16[768,768]{1,0:T(8,128)(2,1)}, u32[]{:S(2)}, u32[]{:S(2)}) collective-permute-start(bf16[768,768]{1,0:T(8,128)(2,1)} %constant_dynamic-update-slice_fusion.20.refs_5_.refs_4_), channel_id=1, source_target_pairs={{0,1},{1,0},{2,3},{3,2},{4,5},{5,4},{6,7},{7,6},{8,9},{9,8},{10,11... | collective-permute-start | bytes 3538952 | tf_op jit(solution)/shard_map/ppermute | solution.py:23
  264.4 34.1 %collective-permute-start.50 = (bf16[384,768]{1,0:T(8,128)(2,1)S(1)}, bf16[384,768]{1,0:T(8,128)(2,1)S(1)}, u32[]{:S(2)}, u32[]{:S(2)}) collective-permute-start(bf16[384,768]{1,0:T(8,128)(2,1)S(1)} %slice.714), channel_id=1, source_target_pairs={{0,2},{1,3},{2,0},{3,1},{4,6},{5,7},{6,4},{7,5},{8,10},{9,11},{10,... | collective-permute-start | bytes 1769480 | tf_op jit(solution)/shard_map/ppermute | solution.py:23
  298.5 42.2 %collective-permute-start.51 = (bf16[4,768,768]{2,1,0:T(8,128)(2,1)}, bf16[4,768,768]{2,1,0:T(8,128)(2,1)}, u32[]{:S(2)}, u32[]{:S(2)}) collective-permute-start(bf16[4,768,768]{2,1,0:T(8,128)(2,1)} %get-tuple-element.435), channel_id=1, source_target_pairs={{0,1},{1,0},{2,3},{3,2},{4,5},{5,4},{6,7},{7,6},{8,9},{9,8},{10,11... | collective-permute-start | bytes 14155784 | tf_op jit(solution)/shard_map/ppermute | solution.py:23
  346.7 42.5 %collective-permute-start.53 = (bf16[768,768]{1,0:T(8,128)(2,1)}, bf16[768,768]{1,0:T(8,128)(2,1)}, u32[]{:S(2)}, u32[]{:S(2)}) collective-permute-start(bf16[768,768]{1,0:T(8,128)(2,1)} %fusion.32), channel_id=1, source_target_pairs={{0,2},{1,3},{2,0},{3,1},{4,6},{5,7},{6,4},{7,5},{8,10},{9,11},{10,... | collective-permute-start | bytes 3538952 | tf_op jit(solution)/shard_map/ppermute | solution.py:23
  347.9 41.2 %collective-permute-start.54 = (bf16[2,384,768]{2,1,0:T(8,128)(2,1)}, bf16[2,384,768]{2,1,0:T(8,128)(2,1)}, u32[]{:S(2)}, u32[]{:S(2)}) collective-permute-start(bf16[2,384,768]{2,1,0:T(8,128)(2,1)} %add_convert_fusion.5), channel_id=1, source_target_pairs={{0,4},{4,0},{8,12},{12,8},{16,20},{20,16},{24,28},{28,24},{1,5},{5... | collective-permute-start | bytes 3538952 | tf_op jit(solution)/shard_map/ppermute | solution.py:23
  399.4 40.5 %collective-permute-start.57 = (bf16[768,384]{0,1:T(8,128)(2,1)}, bf16[768,384]{0,1:T(8,128)(2,1)S(1)}, u32[]{:S(2)}, u32[]{:S(2)}) collective-permute-start(bf16[768,384]{0,1:T(8,128)(2,1)} %slice_bitcast_fusion.3), channel_id=1, source_target_pairs={{0,2},{1,3},{2,0},{3,1},{4,6},{5,7},{6,4},{7,5},{8,10},{9,11},{10,... | collective-permute-start | bytes 1769480 | tf_op jit(solution)/shard_map/ppermute | solution.py:23
  401.0 38.8 %collective-permute-start.58 = (bf16[2,384,384]{1,2,0:T(8,128)(2,1)}, bf16[2,384,384]{1,2,0:T(8,128)(2,1)}, u32[]{:S(2)}, u32[]{:S(2)}) collective-permute-start(bf16[2,384,384]{1,2,0:T(8,128)(2,1)} %slice.455), channel_id=1, source_target_pairs={{0,4},{4,0},{8,12},{12,8},{16,20},{20,16},{24,28},{28,24},{1,5},{5... | collective-permute-start | bytes 1769480 | tf_op jit(solution)/shard_map/ppermute | solution.py:23
  402.3 37.6 %collective-permute-start.55 = (bf16[384,768]{1,0:T(8,128)(2,1)}, bf16[384,768]{1,0:T(8,128)(2,1)}, u32[]{:S(2)}, u32[]{:S(2)}) collective-permute-start(bf16[384,768]{1,0:T(8,128)(2,1)} %slice.444), channel_id=1, source_target_pairs={{0,4},{4,0},{8,12},{12,8},{16,20},{20,16},{24,28},{28,24},{1,5},{5... | collective-permute-start | bytes 1769480 | tf_op jit(solution)/shard_map/ppermute | solution.py:23
  404.8 35.0 %collective-permute-start.56 = (bf16[384,768]{1,0:T(8,128)(2,1)}, bf16[384,768]{1,0:T(8,128)(2,1)}, u32[]{:S(2)}, u32[]{:S(2)}) collective-permute-start(bf16[384,768]{1,0:T(8,128)(2,1)} %slice_bitcast_fusion.4), channel_id=1, source_target_pairs={{0,2},{1,3},{2,0},{3,1},{4,6},{5,7},{6,4},{7,5},{8,10},{9,11},{10,... | collective-permute-start | bytes 1769480 | tf_op jit(solution)/shard_map/ppermute | solution.py:23
  439.9 22.4 %collective-permute-start.60 = (bf16[4,768,768]{2,1,0:T(8,128)(2,1)}, bf16[4,768,768]{2,1,0:T(8,128)(2,1)S(1)}, u32[]{:S(2)}, u32[]{:S(2)}) collective-permute-start(bf16[4,768,768]{2,1,0:T(8,128)(2,1)} %get-tuple-element.488), channel_id=1, source_target_pairs={{0,1},{1,0},{2,3},{3,2},{4,5},{5,4},{6,7},{7,6},{8,9},{9,8},{10,11... | collective-permute-start | bytes 14155784 | tf_op jit(solution)/shard_map/ppermute | solution.py:23
  446.6 15.7 %collective-permute-start.63 = (bf16[192,1536]{1,0:T(8,128)(2,1)S(1)}, bf16[192,1536]{1,0:T(8,128)(2,1)S(1)}, u32[]{:S(2)}, u32[]{:S(2)}) collective-permute-start(bf16[192,1536]{1,0:T(8,128)(2,1)S(1)} %slice.463), channel_id=1, source_target_pairs={{0,8},{4,12},{8,0},{12,4},{16,24},{20,28},{24,16},{28,20},{1,9},{5... | collective-permute-start | bytes 1769480 | tf_op jit(solution)/shard_map/ppermute | solution.py:23
  446.7 9.3 %collective-permute-start.61 = (bf16[384,384]{0,1:T(8,128)(2,1)S(1)}, bf16[384,384]{0,1:T(8,128)(2,1)S(1)}, u32[]{:S(2)}, u32[]{:S(2)}) collective-permute-start(bf16[384,384]{0,1:T(8,128)(2,1)S(1)} %slice.461), channel_id=1, source_target_pairs={{0,4},{4,0},{8,12},{12,8},{16,20},{20,16},{24,28},{28,24},{1,5},{5... | collective-permute-start | bytes 884744 | tf_op jit(solution)/shard_map/ppermute | solution.py:23
  465.4 34.8 %collective-permute-start.64 = (bf16[768,768]{1,0:T(8,128)(2,1)}, bf16[768,768]{1,0:T(8,128)(2,1)}, u32[]{:S(2)}, u32[]{:S(2)}) collective-permute-start(bf16[768,768]{1,0:T(8,128)(2,1)} %fusion.33), channel_id=1, source_target_pairs={{0,2},{1,3},{2,0},{3,1},{4,6},{5,7},{6,4},{7,5},{8,10},{9,11},{10,... | collective-permute-start | bytes 3538952 | tf_op jit(solution)/shard_map/ppermute | solution.py:23
  466.2 34.0 %collective-permute-start.65 = (bf16[2,384,768]{2,1,0:T(8,128)(2,1)}, bf16[2,384,768]{2,1,0:T(8,128)(2,1)}, u32[]{:S(2)}, u32[]{:S(2)}) collective-permute-start(bf16[2,384,768]{2,1,0:T(8,128)(2,1)} %add_convert_fusion.2), channel_id=1, source_target_pairs={{0,4},{4,0},{8,12},{12,8},{16,20},{20,16},{24,28},{28,24},{1,5},{5... | collective-permute-start | bytes 3538952 | tf_op jit(solution)/shard_map/ppermute | solution.py:23
  467.8 32.4 %collective-permute-start.66 = (bf16[192,768]{0,1:T(8,128)(2,1)}, bf16[192,768]{0,1:T(8,128)(2,1)}, u32[]{:S(2)}, u32[]{:S(2)}) collective-permute-start(bf16[192,768]{0,1:T(8,128)(2,1)} %slice.472), channel_id=1, source_target_pairs={{0,8},{4,12},{8,0},{12,4},{16,24},{20,28},{24,16},{28,20},{1,9},{5... | collective-permute-start | bytes 884744 | tf_op jit(solution)/shard_map/ppermute | solution.py:23
  468.8 31.4 %collective-permute-start.67 = (bf16[96,1536]{1,0:T(8,128)(2,1)}, bf16[96,1536]{1,0:T(8,128)(2,1)}, u32[]{:S(2)}, u32[]{:S(2)}) collective-permute-start(bf16[96,1536]{1,0:T(8,128)(2,1)} %slice.473), channel_id=1, source_target_pairs={{0,16},{4,20},{8,24},{12,28},{16,0},{20,4},{24,8},{28,12},{1,17},{... | collective-permute-start | bytes 884744 | tf_op jit(solution)/shard_map/ppermute | solution.py:23
  510.3 45.9 %collective-permute-start.72 = (bf16[768,768]{0,1:T(8,128)(2,1)}, bf16[768,768]{0,1:T(8,128)(2,1)}, u32[]{:S(2)}, u32[]{:S(2)}) collective-permute-start(bf16[768,768]{0,1:T(8,128)(2,1)} %pad_maximum_fusion.12), channel_id=1, source_target_pairs={{0,2},{1,3},{2,0},{3,1},{4,6},{5,7},{6,4},{7,5},{8,10},{9,11},{10,... | collective-permute-start | bytes 3538952 | tf_op jit(solution)/shard_map/ppermute | solution.py:23
  512.3 43.9 %collective-permute-start.69 = (bf16[384,768]{1,0:T(8,128)(2,1)}, bf16[384,768]{1,0:T(8,128)(2,1)}, u32[]{:S(2)}, u32[]{:S(2)}) collective-permute-start(bf16[384,768]{1,0:T(8,128)(2,1)} %slice.476), channel_id=1, source_target_pairs={{0,4},{4,0},{8,12},{12,8},{16,20},{20,16},{24,28},{28,24},{1,5},{5... | collective-permute-start | bytes 1769480 | tf_op jit(solution)/shard_map/ppermute | solution.py:23
  514.4 41.9 %collective-permute-start.70 = (bf16[384,768]{1,0:T(8,128)(2,1)}, bf16[384,768]{1,0:T(8,128)(2,1)}, u32[]{:S(2)}, u32[]{:S(2)}) collective-permute-start(bf16[384,768]{1,0:T(8,128)(2,1)} %slice_bitcast_fusion.2), channel_id=1, source_target_pairs={{0,2},{1,3},{2,0},{3,1},{4,6},{5,7},{6,4},{7,5},{8,10},{9,11},{10,... | collective-permute-start | bytes 1769480 | tf_op jit(solution)/shard_map/ppermute | solution.py:23
  519.5 36.7 %collective-permute-start.71 = (bf16[96,768]{0,1:T(8,128)(2,1)}, bf16[96,768]{0,1:T(8,128)(2,1)}, u32[]{:S(2)}, u32[]{:S(2)}) collective-permute-start(bf16[96,768]{0,1:T(8,128)(2,1)} %slice.480), channel_id=1, source_target_pairs={{0,16},{4,20},{8,24},{12,28},{16,0},{20,4},{24,8},{28,12},{1,17},{... | collective-permute-start | bytes 442376 | tf_op jit(solution)/shard_map/ppermute | solution.py:23
  561.0 13.0 %collective-permute-start.75 = (bf16[192,1536]{1,0:T(8,128)(2,1)}, bf16[192,1536]{1,0:T(8,128)(2,1)S(1)}, u32[]{:S(2)}, u32[]{:S(2)}) collective-permute-start(bf16[192,1536]{1,0:T(8,128)(2,1)} %slice.553), channel_id=1, source_target_pairs={{0,8},{4,12},{8,0},{12,4},{16,24},{20,28},{24,16},{28,20},{1,9},{5... | collective-permute-start | bytes 1769480 | tf_op jit(solution)/shard_map/ppermute | solution.py:23
  566.1 12.4 %collective-permute-start.74 = (bf16[384,768]{0,1:T(8,128)(2,1)S(1)}, bf16[384,768]{0,1:T(8,128)(2,1)S(1)}, u32[]{:S(2)}, u32[]{:S(2)}) collective-permute-start(bf16[384,768]{0,1:T(8,128)(2,1)S(1)} %slice.552), channel_id=1, source_target_pairs={{0,4},{4,0},{8,12},{12,8},{16,20},{20,16},{24,28},{28,24},{1,5},{5... | collective-permute-start | bytes 1769480 | tf_op jit(solution)/shard_map/ppermute | solution.py:23
  567.3 11.4 %collective-permute-start.73 = (bf16[768,768]{1,0:T(8,128)(2,1)}, bf16[768,768]{1,0:T(8,128)(2,1)S(1)}, u32[]{:S(2)}, u32[]{:S(2)}) collective-permute-start(bf16[768,768]{1,0:T(8,128)(2,1)} %get-tuple-element.532), channel_id=1, source_target_pairs={{0,1},{1,0},{2,3},{3,2},{4,5},{5,4},{6,7},{7,6},{8,9},{9,8},{10,11... | collective-permute-start | bytes 3538952 | tf_op jit(solution)/shard_map/ppermute | solution.py:23
  588.3 14.7 %collective-permute-start.78 = (bf16[384,768]{1,0:T(8,128)(2,1)}, bf16[384,768]{1,0:T(8,128)(2,1)S(1)}, u32[]{:S(2)}, u32[]{:S(2)}) collective-permute-start(bf16[384,768]{1,0:T(8,128)(2,1)} %get-tuple-element.559), channel_id=1, source_target_pairs={{0,2},{1,3},{2,0},{3,1},{4,6},{5,7},{6,4},{7,5},{8,10},{9,11},{10,... | collective-permute-start | bytes 1769480 | tf_op jit(solution)/shard_map/ppermute | solution.py:23
  589.8 13.2 %collective-permute-start.76 = (bf16[192,768]{0,1:T(8,128)(2,1)S(1)}, bf16[192,768]{0,1:T(8,128)(2,1)S(1)}, u32[]{:S(2)}, u32[]{:S(2)}) collective-permute-start(bf16[192,768]{0,1:T(8,128)(2,1)S(1)} %slice.491), channel_id=1, source_target_pairs={{0,8},{4,12},{8,0},{12,4},{16,24},{20,28},{24,16},{28,20},{1,9},{5... | collective-permute-start | bytes 884744 | tf_op jit(solution)/shard_map/ppermute | solution.py:23
  590.7 12.3 %collective-permute-start.77 = (bf16[96,1536]{1,0:T(8,128)(2,1)S(1)}, bf16[96,1536]{1,0:T(8,128)(2,1)S(1)}, u32[]{:S(2)}, u32[]{:S(2)}) collective-permute-start(bf16[96,1536]{1,0:T(8,128)(2,1)S(1)} %slice.492), channel_id=1, source_target_pairs={{0,16},{4,20},{8,24},{12,28},{16,0},{20,4},{24,8},{28,12},{1,17},{... | collective-permute-start | bytes 884744 | tf_op jit(solution)/shard_map/ppermute | solution.py:23
  591.1 11.2 %collective-permute-start.80 = (f32[24,768]{1,0:T(8,128)S(1)}, f32[24,768]{1,0:T(8,128)S(1)}, u32[]{:S(2)}, u32[]{:S(2)}) collective-permute-start(f32[24,768]{1,0:T(8,128)S(1)} %copy-done.123), channel_id=1, source_target_pairs={{0,2},{1,3},{2,0},{3,1},{4,6},{5,7},{6,4},{7,5},{8,10},{9,11},{10,... | collective-permute-start | bytes 221192 | tf_op jit(solution)/shard_map/ppermute | solution.py:23
  592.4 10.0 %collective-permute-start.81 = (f32[24,768]{1,0:T(8,128)S(1)}, f32[24,768]{1,0:T(8,128)S(1)}, u32[]{:S(2)}, u32[]{:S(2)}) collective-permute-start(f32[24,768]{1,0:T(8,128)S(1)} %copy-done.122), channel_id=1, source_target_pairs={{0,3},{1,2},{2,1},{3,0},{4,7},{5,6},{6,5},{7,4},{8,11},{9,10},{10,... | collective-permute-start | bytes 221192 | tf_op jit(solution)/shard_map/ppermute | solution.py:23
  604.1 11.8 %collective-permute-start.82 = (bf16[96,768]{0,1:T(8,128)(2,1)S(1)}, bf16[96,768]{0,1:T(8,128)(2,1)S(1)}, u32[]{:S(2)}, u32[]{:S(2)}) collective-permute-start(bf16[96,768]{0,1:T(8,128)(2,1)S(1)} %slice.496), channel_id=1, source_target_pairs={{0,16},{4,20},{8,24},{12,28},{16,0},{20,4},{24,8},{28,12},{1,17},{... | collective-permute-start | bytes 442376 | tf_op jit(solution)/shard_map/ppermute | solution.py:23
  (149 other events, 814.8 us)

commit v9 on v8

--- a/solution.py
+++ b/solution.py
@@ -92,10 +92,11 @@
         self.states = [start for start, _, _ in made]
         self.plan = [[(0, step)] for step in made[0][1]]
         for at, (_, _, near) in enumerate(made):
-            ahead = made[at + 1][1] if at + 1 < len(made) else []
-            for i in range(max(len(near), len(ahead))):
+            ahead = [1] if at == 0 else [at + 1, at + 2] if at % 2 else []
+            ahead = [(g, made[g][1]) for g in ahead if g < len(made)]
+            for i in range(max([len(near)] + [len(steps) for _, steps in ahead])):
                 stage = [(at, near[i])] if i < len(near) else []
-                self.plan.append(stage + ([(at + 1, ahead[i])] if i < len(ahead) else []))
+                self.plan.append(stage + [(g, steps[i]) for g, steps in ahead if i < len(steps)])
         self.ends = [
             max(i for i, stage in enumerate(self.plan) for g, _ in stage if g == at)
             for at in range(len(made))
@@ -106,6 +107,8 @@
     def advance(self, *others):
         stage = self.plan[self.done]
         self.done += 1
+        if stage[0][0] == 0 and len(stage) > 1:
+            return self.start(stage, others)
         flat = [part for g, _ in stage for part in self.states[g]]
         flat = behind(flat, *self.tokens)
         states, received, at = [], [], 0
@@ -120,6 +123,17 @@
             at += len(got)
         self.tokens = [part for g, _ in stage for part in self.states[g][:1]]
         return flat[at:]
+
+    def start(self, stage, others):
+        (first, (send, finish)), (second, (send_more, finish_more)) = stage
+        state = behind(self.states[first], *self.tokens[:1])
+        more = behind(self.states[second], state[0])
+        got, got_more = send(state), send_more(more)
+        flat = together(*got, *others)
+        self.states[first] = finish(state, flat[: len(got)])
+        self.states[second] = finish_more(more, got_more)
+        self.tokens = [self.states[first][0], self.states[second][0]]
+        return flat[len(got) :]
 
     def until(self, group):
         while self.done <= self.ends[group]:
@@ -919,7 +933,7 @@
             folding = core
         fronts = (gradient, layer_in, share_a, share_b)
         small_grads[at] = (sums, (sums_own, sums_other), bup)
-    gradient, half, *small = finish(
+    out = finish(
         layers,
         quarter,
         wide,
@@ -936,16 +950,11 @@
         [small_grads[at][2] for at in range(layers)],
         [part for at in range(layers) for part in small_grads[at][1]],
     )
-    advance([folding])
-    half, *small, folding.attn, folding.feed = together(
-        half, *small, folding.attn, folding.feed
-    )
-    half, *got = advance(
-        [folding],
-        exchange(half, "tensor", 2),
-        *[exchange(small[t], "tensor", t) for t in range(1, 4)],
-    )
+    gradient, half, *small = advance([folding], *out)
+    got = advance([folding], *[exchange(small[t], "tensor", t) for t in range(1, 4)])
     small = small[0] + got[0] + got[1] + got[2]
+    half, small = together(half, small)
+    half = exchange(half, "tensor", 2)
     frames_grad = give_clip(gradient, half)
     for mask in reversed(dp_masks()):
         got = exchange(small[:, small.shape[1] // 2 :], "dp", mask)

time: 643 us -> 644 us (level)
  waiting for transfers between devices: 100 us -> 69.7 us
  starting transfers between devices: 71.3 us -> 81 us
  local copies, waits for them, and re-layouts: 71 us -> 79.5 us
  other arithmetic: 50.7 us -> 57.5 us
    ppermute x86, waiting for transfers between devices: 100 us -> 69.7 us  [exchange(): return lax.ppermute(value, axis, [(i, i ^ mask) for i in range(count)])]
    ppermute x86, starting transfers between devices: 71.3 us -> 81 us  [exchange(): return lax.ppermute(value, axis, [(i, i ^ mask) for i in range(count)])]
    unnamed x275 -> x254, local copies, waits for them, and re-layouts: 38.8 us -> 40.6 us
  transfers between devices with their start and end apart: 86 -> 86, of which waited for: 30 -> 25; matrix products, arithmetic and copies ran while one was open for 14% -> 16% of each run, Pallas kernels for 44% -> 46%
where the time goes in v9:
time: 644 us; the launch traced here: 634 us
  Pallas kernels  307 us (48%)
  starting transfers between devices  81 us (13%)
  local copies, waits for them, and re-layouts  79.5 us (12%)
  waiting for transfers between devices  69.7 us (11%)
  other arithmetic  57.5 us (9%)
  matrix products  35.8 us (6%)
    pallas_call x4, Pallas kernels, attend_back(): pl.pallas_call(functools.partial(attend_back_kernel, row_count, quarter,...  123 us
    ppermute x86, starting transfers between devices, exchange(): return lax.ppermute(value, axis, [(i, i ^ mask) for i in range(count)])  81 us
    pallas_call x4, Pallas kernels, attend(): pl.pallas_call(functools.partial(attend_kernel, row_count, quarter, min(5...  72.9 us
    ppermute x86, waiting for transfers between devices, exchange(): return lax.ppermute(value, axis, [(i, i ^ mask) for i in range(count)])  69.7 us
    pallas_call x2, Pallas kernels, feed_back(): pl.pallas_call(functools.partial(feed_back_kernel, at, layers), grid=(hid...  64 us
    unnamed x254, local copies, waits for them, and re-layouts  40.6 us
    pallas_call x2, Pallas kernels, feed(): pl.pallas_call(functools.partial(feed_kernel, at, layers), grid=(hidden /...  38.4 us
    convert_element_type x22, other arithmetic, add_low(): return (kept.astype(f32) + received.astype(f32)).astype(bf16)  28.5 us
  transfers between devices with their start and end apart: 86, of which 25 were waited for; matrix products, arithmetic and copies ran while one was open for 16% of the time, Pallas kernels for 46%

profile of v9, /device:TPU:0, one launch (start us, length us, event | category | flops | bytes accessed | tf_op | source)
XLA Modules:
  0.0 633.5 jit_solution(15719880281213016726)
XLA Ops:
  3.2 4.2 collective-permute-start.2
  7.8 2.9 collective-permute-start.3
  18.5 1.8 collective-permute-done.4
  27.1 2.2 collective-permute-done.8
  36.0 2.7 fusion.93
  38.7 2.0 copy.39.refs_0_
  41.2 2.1 pad_maximum_fusion.13.refs_2_
  46.8 1.8 pad_maximum_fusion.14
  52.8 1.9 concatenate.143.refs_4_
  56.9 5.7 collective-permute-done.18
  64.6 2.3 collective-permute-start.19
  68.4 2.6 collective-permute-start.22
  75.0 17.3 %shard_map.194 = (bf16[1536,576]{1,0:T(8,128)(2,1)}, bf16[1536,192]{1,0:T(8,128)(2,1)}, f32[1536,8]{1,0:T(8,128)}) custom-call(bf16[768,768]{1,0:T(8,128)(2,1)} %copy-done.7, bf16[768,768]{1,0:T(8,128)(2,1)} %collective-permute-done.16.refs_1_, bf16[768,384]{1,0:T(8,128)(2,1)} %pad_maximum_fusion.13.refs_2_, bf16[768,384]{1,0:T(8,128)(2,1)} %copy-done.18, ...), custom_call_target="tpu_custom_call" | custom-call | tf_op jit(solution)/shard_map/pallas_call | solution.py:397
  92.4 1.8 constant_dynamic-update-slice_fusion.8
  98.9 1.8 collective-permute-start.25
  106.4 19.2 %shard_map.195 = (f32[768,768]{1,0:T(8,128)}, bf16[768,768]{1,0:T(8,128)(2,1)}, bf16[1536,576]{1,0:T(8,128)(2,1)}, bf16[1536,192]{1,0:T(8,128)(2,1)}, f32[1536,8]{1,0:T(8,128)}) custom-call(bf16[768,768]{1,0:T(8,128)(2,1)} %copy-done.7, bf16[768,768]{1,0:T(8,128)(2,1)} %collective-permute-done.16.refs_1_, ...), custom_call_target="tpu_custom_call" | custom-call | tf_op jit(solution)/shard_map/pallas_call | solution.py:397
  135.2 5.2 collective-permute-done.28
  140.4 1.9 collective-permute-done.29
  145.3 1.8 collective-permute-start.32
  148.2 20.2 %shard_map.196 = (bf16[768,768]{1,0:T(8,128)(2,1)}, bf16[768,768]{1,0:T(8,128)(2,1)}, bf16[768,768]{1,0:T(8,128)(2,1)}, bf16[768,768]{1,0:T(8,128)(2,1)}, bf16[7...) custom-call(f32[768,768]{1,0:T(8,128)} %copy-done, ...), custom_call_target="tpu_custom_call" | custom-call | tf_op jit(solution)/shard_map/pallas_call | solution.py:579
  168.5 3.2 collective-permute-done.38
  172.6 1.8 collective-permute-start.39
  175.1 1.9 constant_dynamic-update-slice_fusion.23
  179.0 17.2 %shard_map.197 = (bf16[1536,576]{1,0:T(8,128)(2,1)}, bf16[1536,192]{1,0:T(8,128)(2,1)}, f32[1536,8]{1,0:T(8,128)}) custom-call(bf16[768,768]{1,0:T(8,128)(2,1)} %get-tuple-element.393.refs_0_, bf16[768,768]{1,0:T(8,128)(2,1)} %copy-done.9, bf16[768,384]{1,0:T(8,128)(2,1)} %pad_maximum_fusion.15.refs_2_, bf16[768,384]{1,0:T(8,128)(2,1)} %copy-done.19, ...), custom_call_target="tpu_custom_call" | custom-call | tf_op jit(solution)/shard_map/pallas_call | solution.py:397
  198.6 1.8 collective-permute-start.44
  202.3 19.1 %shard_map.198 = (f32[768,768]{1,0:T(8,128)}, bf16[768,768]{1,0:T(8,128)(2,1)}, bf16[1536,576]{1,0:T(8,128)(2,1)}, bf16[1536,192]{1,0:T(8,128)(2,1)}, f32[1536,8]{1,0:T(8,128)}) custom-call(bf16[768,768]{1,0:T(8,128)(2,1)} %get-tuple-element.393.refs_0_, bf16[768,768]{1,0:T(8,128)(2,1)} %copy-done.9, ...), custom_call_target="tpu_custom_call" | custom-call | tf_op jit(solution)/shard_map/pallas_call | solution.py:397
  222.6 3.3 collective-permute-done.44
  231.6 3.4 collective-permute-done.45.refs_2_
  236.1 18.2 %shard_map.199 = (bf16[768,768]{1,0:T(8,128)(2,1)}, bf16[768,768]{1,0:T(8,128)(2,1)}, bf16[768,768]{1,0:T(8,128)(2,1)}, bf16[768,768]{1,0:T(8,128)(2,1)}, bf16[7...) custom-call(f32[768,768]{1,0:T(8,128)} %get-tuple-element.463.refs_0, ...), custom_call_target="tpu_custom_call" | custom-call | tf_op jit(solution)/shard_map/pallas_call | solution.py:579
  256.6 2.6 fusion.20.refs_0_
  259.2 30.3 %shard_map.200 = (bf16[4,768,768]{2,1,0:T(8,128)(2,1)}, bf16[4,768,768]{2,1,0:T(8,128)(2,1)}, f32[4,768]{1,0:T(4,128)}, f32[768,768]{1,0:T(8,128)}, bf16[768,768]{1,0:T(8,128)(2,1)}, /*index=5*/f32[8,768]{1,0:T(8,128)}) custom-call(f32[768,768]{1,0:T(8,128)} %fusion.20.refs_0_, f32[768,768]{1,0:T(8,128)} %get-tuple-element.407.refs_1_, ...), custom_call_target="tpu_custom_call" | custom-call | tf_op jit(solution)/shard_map/pallas_call | solution.py:657
  293.5 5.9 collective-permute-done.52.refs_1_
  300.4 28.2 %shard_map.201 = (bf16[1536,576]{1,0:T(8,128)(2,1)}, f32[8,576]{1,0:T(8,128)}) custom-call(bf16[768,768]{1,0:T(8,128)(2,1)} %get-tuple-element.444.refs_0_, bf16[768,768]{1,0:T(8,128)(2,1)} %copy-done.5, bf16[768,384]{1,0:T(8,128)(2,1)} %collective-permute-done.31.refs_2_.refs_8_, bf16[768,384]{1,0:T(8,128)(2,1)} %copy-done.17, ...), custom_call_target="tpu_custom_call" | custom-call | tf_op jit(solution)/shard_map/pallas_call | solution.py:491
  328.6 1.8 fusion.69
  331.6 2.9 add_convert_fusion.5
  334.5 3.1 fusion.32
  344.4 33.2 %shard_map.202 = (f32[768,768]{1,0:T(8,128)}, bf16[768,768]{1,0:T(8,128)(2,1)}, bf16[1536,576]{1,0:T(8,128)(2,1)}, f32[8,576]{1,0:T(8,128)}) custom-call(bf16[768,768]{1,0:T(8,128)(2,1)} %get-tuple-element.444.refs_0_, bf16[768,768]{1,0:T(8,128)(2,1)} %copy-done.5, bf16[768,384]{1,0:T(8,128)(2,1)} %pad_maximum_fusion.15.refs_2_, ...), custom_call_target="tpu_custom_call" | custom-call | tf_op jit(solution)/shard_map/pallas_call | solution.py:491
  378.8 4.0 convolution_convert_fusion.1
  383.0 2.1 add_convert_fusion.4
  385.1 2.5 fusion.5
  395.7 33.7 %shard_map.203 = (bf16[4,768,768]{2,1,0:T(8,128)(2,1)}, bf16[4,768,768]{2,1,0:T(8,128)(2,1)}, f32[4,768]{1,0:T(4,128)}, f32[768,768]{1,0:T(8,128)}, bf16[768,768]{1,0:T(8,128)(2,1)}, /*index=5*/f32[8,768]{1,0:T(8,128)}) custom-call(f32[768,768]{1,0:T(8,128)} %get-tuple-element.462.refs_0_, f32[768,768]{1,0:T(8,128)} %get-tuple-element.463.refs_0_.refs_1_, ...), custom_call_target="tpu_custom_call" | custom-call | tf_op jit(solution)/shard_map/pallas_call | solution.py:657
  445.3 4.3 collective-permute-done.61
  451.1 2.9 collective-permute-done.63
  454.0 2.9 add_convert_fusion.2
  456.9 3.0 fusion.33
  469.2 2.9 collective-permute-start.67
  473.8 28.5 %shard_map.204 = (bf16[1536,576]{1,0:T(8,128)(2,1)}, f32[8,576]{1,0:T(8,128)}) custom-call(bf16[768,768]{1,0:T(8,128)(2,1)} %get-tuple-element.518.refs_0_, bf16[768,768]{1,0:T(8,128)(2,1)} %copy-done.3, bf16[768,384]{1,0:T(8,128)(2,1)} %collective-permute-done.13.refs_2_.refs_8_, bf16[768,384]{1,0:T(8,128)(2,1)} %copy-done.16, ...), custom_call_target="tpu_custom_call" | custom-call | tf_op jit(solution)/shard_map/pallas_call | solution.py:491
  502.3 3.5 fusion.26
  505.8 2.4 add_convert_fusion.1
  508.3 2.8 fusion.4
  522.7 33.2 %shard_map.205 = (f32[768,768]{1,0:T(8,128)}, bf16[768,768]{1,0:T(8,128)(2,1)}, bf16[1536,576]{1,0:T(8,128)(2,1)}, f32[8,576]{1,0:T(8,128)}) custom-call(bf16[768,768]{1,0:T(8,128)(2,1)} %get-tuple-element.518.refs_0_, bf16[768,768]{1,0:T(8,128)(2,1)} %copy-done.3, bf16[768,384]{1,0:T(8,128)(2,1)} %pad_maximum_fusion.13.refs_2_, ...), custom_call_target="tpu_custom_call" | custom-call | tf_op jit(solution)/shard_map/pallas_call | solution.py:491
  560.3 2.9 fusion.27
  568.6 8.5 %shard_map.206 = (f32[768,768]{1,0:T(8,128)}, bf16[384,768]{1,0:T(8,128)(2,1)}, f32[24,768]{1,0:T(8,128)}, f32[24,768]{1,0:T(8,128)}, f32[24,768]{1,0:T(8,128)}, /*index=5*/f32[24,768]{1,0:T(8,128)}) custom-call(f32[768,768]{1,0:T(8,128)} %copy-done, f32[768,768]{1,0:T(8,128)} %get-tuple-element.532.refs_1_, f32[768,768]{1,0:T(8,128)} %get-tuple-element.533.refs_2_, ...), custom_call_target="tpu_custom_call" | custom-call | tf_op jit(solution)/shard_map/pallas_call | solution.py:722
  577.2 3.4 collective-permute-done.73
  581.5 3.0 collective-permute-start.77
  587.3 2.5 collective-permute-done.79
  590.4 7.6 %collective-permute-done.76 = bf16[192,768]{0,1:T(8,128)(2,1)S(1)} collective-permute-done((bf16[192,768]{0,1:T(8,128)(2,1)S(1)}, bf16[192,768]{0,1:T(8,128)(2,1)S(1)}, u32[]{:S(2)}, u32[]{:S(2)}) %collective-permute-start.76) | collective-permute-done | bytes 294944 | tf_op jit(solution)/shard_map/ppermute | solution.py:23
  601.2 1.8 fusion.9
  604.3 5.9 collective-permute-done.81
  610.2 1.8 fusion.15
  612.0 1.8 fusion.17
  624.5 3.0 select_bitcast_fusion.1
  627.7 2.6 copy.46
  630.6 2.6 copy.45
  (547 shorter events, 175.2 us)
Async XLA Ops:
  3.2 12.4 %collective-permute-start.2 = (f32[6,768]{1,0:T(8,128)S(1)}, f32[6,768]{1,0:T(8,128)S(1)}, u32[]{:S(2)}, u32[]{:S(2)}) collective-permute-start(f32[6,768]{1,0:T(8,128)S(1)} %pad_maximum_fusion.30), channel_id=1, source_target_pairs={{0,16},{4,20},{8,24},{12,28},{16,0},{20,4},{24,8},{28,12},{1,17},{... | collective-permute-start | bytes 55304 | tf_op jit(solution)/shard_map/ppermute | solution.py:23
  7.8 12.5 %collective-permute-start.3 = (bf16[96,768]{1,0:T(8,128)(2,1)S(1)}, bf16[96,768]{1,0:T(8,128)(2,1)S(1)}, u32[]{:S(2)}, u32[]{:S(2)}) collective-permute-start(bf16[96,768]{1,0:T(8,128)(2,1)S(1)} %pad_maximum_fusion.23), channel_id=1, source_target_pairs={{0,16},{4,20},{8,24},{12,28},{16,0},{20,4},{24,8},{28,12},{1,17},{... | collective-permute-start | bytes 442376 | tf_op jit(solution)/shard_map/ppermute | solution.py:23
  10.9 25.0 %collective-permute-start = (bf16[375,768]{1,0:T(8,128)(2,1)S(1)}, bf16[375,768]{1,0:T(8,128)(2,1)S(1)}, u32[]{:S(2)}, u32[]{:S(2)}) collective-permute-start(bf16[375,768]{1,0:T(8,128)(2,1)S(1)} %get-tuple-element.614), channel_id=1, source_target_pairs={{0,2},{1,3},{2,0},{3,1},{4,6},{5,7},{6,4},{7,5},{8,10},{9,11},{10,... | collective-permute-start | bytes 1728008 | tf_op jit(solution)/shard_map/ppermute | solution.py:23
  30.1 11.1 %collective-permute-start.12 = (f32[20,768]{1,0:T(8,128)}, f32[20,768]{1,0:T(8,128)}, u32[]{:S(2)}, u32[]{:S(2)}) collective-permute-start(f32[20,768]{1,0:T(8,128)} %pad_maximum_fusion.25), channel_id=1, source_target_pairs={{0,2},{1,3},{2,0},{3,1},{4,6},{5,7},{6,4},{7,5},{8,10},{9,11},{10,... | collective-permute-start | bytes 184328 | tf_op jit(solution)/shard_map/ppermute | solution.py:23
  31.9 9.3 %collective-permute-start.10 = (bf16[384,384]{1,0:T(8,128)(2,1)S(1)}, bf16[384,384]{1,0:T(8,128)(2,1)}, u32[]{:S(2)}, u32[]{:S(2)}) collective-permute-start(bf16[384,384]{1,0:T(8,128)(2,1)S(1)} %get-tuple-element.308), channel_id=1, source_target_pairs={{0,4},{4,0},{8,12},{12,8},{16,20},{20,16},{24,28},{28,24},{1,5},{5... | collective-permute-start | bytes 884744 | tf_op jit(solution)/shard_map/ppermute | solution.py:23
  34.3 12.4 %collective-permute-start.17 = (bf16[96,1536]{1,0:T(8,128)(2,1)S(1)}, bf16[96,1536]{1,0:T(8,128)(2,1)}, u32[]{:S(2)}, u32[]{:S(2)}) collective-permute-start(bf16[96,1536]{1,0:T(8,128)(2,1)S(1)} %pad_maximum_fusion.20), channel_id=1, source_target_pairs={{0,16},{4,20},{8,24},{12,28},{16,0},{20,4},{24,8},{28,12},{1,17},{... | collective-permute-start | bytes 884744 | tf_op jit(solution)/shard_map/ppermute | solution.py:23
  43.3 28.8 %collective-permute-start.13 = (bf16[768,384]{1,0:T(8,128)(2,1)}, bf16[768,384]{1,0:T(8,128)(2,1)}, u32[]{:S(2)}, u32[]{:S(2)}) collective-permute-start(bf16[768,384]{1,0:T(8,128)(2,1)} %pad_maximum_fusion.13.refs_2_), channel_id=1, source_target_pairs={{0,2},{1,3},{2,0},{3,1},{4,6},{5,7},{6,4},{7,5},{8,10},{9,11},{10,... | collective-permute-start | bytes 1769480 | tf_op jit(solution)/shard_map/ppermute | solution.py:23
  48.6 14.0 %collective-permute-start.18 = (bf16[192,1536]{1,0:T(8,128)(2,1)}, bf16[192,1536]{1,0:T(8,128)(2,1)}, u32[]{:S(2)}, u32[]{:S(2)}) collective-permute-start(bf16[192,1536]{1,0:T(8,128)(2,1)} %pad_maximum_fusion.14), channel_id=1, source_target_pairs={{0,8},{4,12},{8,0},{12,4},{16,24},{20,28},{24,16},{28,20},{1,9},{5... | collective-permute-start | bytes 1769480 | tf_op jit(solution)/shard_map/ppermute | solution.py:23
  49.9 23.2 %collective-permute-start.16 = (bf16[768,768]{1,0:T(8,128)(2,1)S(1)}, bf16[768,768]{1,0:T(8,128)(2,1)}, u32[]{:S(2)}, u32[]{:S(2)}) collective-permute-start(bf16[768,768]{1,0:T(8,128)(2,1)S(1)} %add_convert_fusion.7.refs_0_), channel_id=1, source_target_pairs={{0,1},{1,0},{2,3},{3,2},{4,5},{5,4},{6,7},{7,6},{8,9},{9,8},{10,11... | collective-permute-start | bytes 3538952 | tf_op jit(solution)/shard_map/ppermute | solution.py:23
  50.0 16.9 %collective-permute-start.14 = (bf16[384,384]{1,0:T(8,128)(2,1)}, bf16[384,384]{1,0:T(8,128)(2,1)}, u32[]{:S(2)}, u32[]{:S(2)}) collective-permute-start(bf16[384,384]{1,0:T(8,128)(2,1)} %get-tuple-element.314), channel_id=1, source_target_pairs={{0,4},{4,0},{8,12},{12,8},{16,20},{20,16},{24,28},{28,24},{1,5},{5... | collective-permute-start | bytes 884744 | tf_op jit(solution)/shard_map/ppermute | solution.py:23
  50.7 17.6 %collective-permute-start.15 = (bf16[384,384]{1,0:T(8,128)(2,1)}, bf16[384,384]{1,0:T(8,128)(2,1)}, u32[]{:S(2)}, u32[]{:S(2)}) collective-permute-start(bf16[384,384]{1,0:T(8,128)(2,1)} %collective-permute-done.11), channel_id=1, source_target_pairs={{0,4},{4,0},{8,12},{12,8},{16,20},{20,16},{24,28},{28,24},{1,5},{5... | collective-permute-start | bytes 884744 | tf_op jit(solution)/shard_map/ppermute | solution.py:23
  64.6 27.7 %collective-permute-start.19 = (bf16[384,768]{1,0:T(8,128)(2,1)}, bf16[384,768]{1,0:T(8,128)(2,1)}, u32[]{:S(2)}, u32[]{:S(2)}) collective-permute-start(bf16[384,768]{1,0:T(8,128)(2,1)} %get-tuple-element.319), channel_id=1, source_target_pairs={{0,4},{4,0},{8,12},{12,8},{16,20},{20,16},{24,28},{28,24},{1,5},{5... | collective-permute-start | bytes 1769480 | tf_op jit(solution)/shard_map/ppermute | solution.py:23
  66.9 25.5 %collective-permute-start.20 = (bf16[384,768]{1,0:T(8,128)(2,1)S(1)}, bf16[384,768]{1,0:T(8,128)(2,1)}, u32[]{:S(2)}, u32[]{:S(2)}) collective-permute-start(bf16[384,768]{1,0:T(8,128)(2,1)S(1)} %get-tuple-element.335), channel_id=1, source_target_pairs={{0,2},{1,3},{2,0},{3,1},{4,6},{5,7},{6,4},{7,5},{8,10},{9,11},{10,... | collective-permute-start | bytes 1769480 | tf_op jit(solution)/shard_map/ppermute | solution.py:23
  68.4 24.0 %collective-permute-start.22 = (bf16[96,1536]{1,0:T(8,128)(2,1)S(1)}, bf16[96,1536]{1,0:T(8,128)(2,1)}, u32[]{:S(2)}, u32[]{:S(2)}) collective-permute-start(bf16[96,1536]{1,0:T(8,128)(2,1)S(1)} %copy-done.63), channel_id=1, source_target_pairs={{0,16},{4,20},{8,24},{12,28},{16,0},{20,4},{24,8},{28,12},{1,17},{... | collective-permute-start | bytes 884744 | tf_op jit(solution)/shard_map/ppermute | solution.py:23
  72.1 20.3 %collective-permute-start.21 = (bf16[96,768]{1,0:T(8,128)(2,1)S(1)}, bf16[96,768]{1,0:T(8,128)(2,1)}, u32[]{:S(2)}, u32[]{:S(2)}) collective-permute-start(bf16[96,768]{1,0:T(8,128)(2,1)S(1)} %copy-done.79), channel_id=1, source_target_pairs={{0,16},{4,20},{8,24},{12,28},{16,0},{20,4},{24,8},{28,12},{1,17},{... | collective-permute-start | bytes 442376 | tf_op jit(solution)/shard_map/ppermute | solution.py:23
  96.2 30.6 %collective-permute-start.23 = (bf16[768,768]{1,0:T(8,128)(2,1)S(1)}, bf16[768,768]{1,0:T(8,128)(2,1)}, u32[]{:S(2)}, u32[]{:S(2)}) collective-permute-start(bf16[768,768]{1,0:T(8,128)(2,1)S(1)} %constant_dynamic-update-slice_fusion.4.refs_5_.refs_7_), channel_id=1, source_target_pairs={{0,2},{1,3},{2,0},{3,1},{4,6},{5,7},{6,4},{7,5},{8,10},{9,11},{10,... | collective-permute-start | bytes 3538952 | tf_op jit(solution)/shard_map/ppermute | solution.py:23
  98.6 28.2 %collective-permute-start.24 = (bf16[384,768]{1,0:T(8,128)(2,1)S(1)}, bf16[384,768]{1,0:T(8,128)(2,1)}, u32[]{:S(2)}, u32[]{:S(2)}) collective-permute-start(bf16[384,768]{1,0:T(8,128)(2,1)S(1)} %copy-done.50), channel_id=1, source_target_pairs={{0,4},{4,0},{8,12},{12,8},{16,20},{20,16},{24,28},{28,24},{1,5},{5... | collective-permute-start | bytes 1769480 | tf_op jit(solution)/shard_map/ppermute | solution.py:23
  98.9 27.9 %collective-permute-start.25 = (bf16[384,768]{1,0:T(8,128)(2,1)}, bf16[384,768]{1,0:T(8,128)(2,1)}, u32[]{:S(2)}, u32[]{:S(2)}) collective-permute-start(bf16[384,768]{1,0:T(8,128)(2,1)} %collective-permute-done.20), channel_id=1, source_target_pairs={{0,4},{4,0},{8,12},{12,8},{16,20},{20,16},{24,28},{28,24},{1,5},{5... | collective-permute-start | bytes 1769480 | tf_op jit(solution)/shard_map/ppermute | solution.py:23
  100.7 26.2 %collective-permute-start.27 = (bf16[192,1536]{1,0:T(8,128)(2,1)}, bf16[192,1536]{1,0:T(8,128)(2,1)}, u32[]{:S(2)}, u32[]{:S(2)}) collective-permute-start(bf16[192,1536]{1,0:T(8,128)(2,1)} %constant_dynamic-update-slice_fusion.8), channel_id=1, source_target_pairs={{0,8},{4,12},{8,0},{12,4},{16,24},{20,28},{24,16},{28,20},{1,9},{5... | collective-permute-start | bytes 1769480 | tf_op jit(solution)/shard_map/ppermute | solution.py:23
  101.5 25.3 %collective-permute-start.26 = (bf16[192,768]{1,0:T(8,128)(2,1)S(1)}, bf16[192,768]{1,0:T(8,128)(2,1)}, u32[]{:S(2)}, u32[]{:S(2)}) collective-permute-start(bf16[192,768]{1,0:T(8,128)(2,1)S(1)} %constant_dynamic-update-slice_fusion.6), channel_id=1, source_target_pairs={{0,8},{4,12},{8,0},{12,4},{16,24},{20,28},{24,16},{28,20},{1,9},{5... | collective-permute-start | bytes 884744 | tf_op jit(solution)/shard_map/ppermute | solution.py:23
  126.7 17.8 %collective-permute-start.34 = (bf16[768,768]{1,0:T(8,128)(2,1)S(1)}, bf16[768,768]{1,0:T(8,128)(2,1)S(1)}, u32[]{:S(2)}, u32[]{:S(2)}) collective-permute-start(bf16[768,768]{1,0:T(8,128)(2,1)S(1)} %constant_dynamic-update-slice_fusion.4.refs_5_.refs_7_), channel_id=1, source_target_pairs={{0,1},{1,0},{2,3},{3,2},{4,5},{5,4},{6,7},{7,6},{8,9},{9,8},{10,11... | collective-permute-start | bytes 3538952 | tf_op jit(solution)/shard_map/ppermute | solution.py:23
  129.6 12.6 %collective-permute-start.30 = (bf16[768,768]{1,0:T(8,128)(2,1)S(1)}, bf16[768,768]{1,0:T(8,128)(2,1)S(1)}, u32[]{:S(2)}, u32[]{:S(2)}) collective-permute-start(bf16[768,768]{1,0:T(8,128)(2,1)S(1)} %copy-done.106), channel_id=1, source_target_pairs={{0,1},{1,0},{2,3},{3,2},{4,5},{5,4},{6,7},{7,6},{8,9},{9,8},{10,11... | collective-permute-start | bytes 3538952 | tf_op jit(solution)/shard_map/ppermute | solution.py:23
  131.2 9.2 %collective-permute-start.28 = (bf16[384,384]{1,0:T(8,128)(2,1)S(1)}, bf16[384,384]{1,0:T(8,128)(2,1)S(1)}, u32[]{:S(2)}, u32[]{:S(2)}) collective-permute-start(bf16[384,384]{1,0:T(8,128)(2,1)S(1)} %get-tuple-element.350), channel_id=1, source_target_pairs={{0,4},{4,0},{8,12},{12,8},{16,20},{20,16},{24,28},{28,24},{1,5},{5... | collective-permute-start | bytes 884744 | tf_op jit(solution)/shard_map/ppermute | solution.py:23
  132.7 12.7 %collective-permute-start.37 = (bf16[768,768]{1,0:T(8,128)(2,1)S(1)}, bf16[768,768]{1,0:T(8,128)(2,1)S(1)}, u32[]{:S(2)}, u32[]{:S(2)}) collective-permute-start(bf16[768,768]{1,0:T(8,128)(2,1)S(1)} %constant_dynamic-update-slice_fusion.18.refs_11_.refs_13_), channel_id=1, source_target_pairs={{0,1},{1,0},{2,3},{3,2},{4,5},{5,4},{6,7},{7,6},{8,9},{9,8},{10,11... | collective-permute-start | bytes 3538952 | tf_op jit(solution)/shard_map/ppermute | solution.py:23
  132.8 9.5 %collective-permute-start.29 = (bf16[384,384]{1,0:T(8,128)(2,1)S(1)}, bf16[384,384]{1,0:T(8,128)(2,1)}, u32[]{:S(2)}, u32[]{:S(2)}) collective-permute-start(bf16[384,384]{1,0:T(8,128)(2,1)S(1)} %get-tuple-element.356), channel_id=1, source_target_pairs={{0,2},{1,3},{2,0},{3,1},{4,6},{5,7},{6,4},{7,5},{8,10},{9,11},{10,... | collective-permute-start | bytes 884744 | tf_op jit(solution)/shard_map/ppermute | solution.py:23
  143.3 28.4 %collective-permute-start.31 = (bf16[768,384]{1,0:T(8,128)(2,1)}, bf16[768,384]{1,0:T(8,128)(2,1)}, u32[]{:S(2)}, u32[]{:S(2)}) collective-permute-start(bf16[768,384]{1,0:T(8,128)(2,1)} %pad_maximum_fusion.15.refs_2_), channel_id=1, source_target_pairs={{0,2},{1,3},{2,0},{3,1},{4,6},{5,7},{6,4},{7,5},{8,10},{9,11},{10,... | collective-permute-start | bytes 1769480 | tf_op jit(solution)/shard_map/ppermute | solution.py:23
  144.5 27.1 %collective-permute-start.38 = (bf16[375,768]{1,0:T(8,128)(2,1)}, bf16[375,768]{1,0:T(8,128)(2,1)S(1)}, u32[]{:S(2)}, u32[]{:S(2)}) collective-permute-start(bf16[375,768]{1,0:T(8,128)(2,1)} %get-tuple-element.375), channel_id=1, source_target_pairs={{0,2},{1,3},{2,0},{3,1},{4,6},{5,7},{6,4},{7,5},{8,10},{9,11},{10,... | collective-permute-start | bytes 1728008 | tf_op jit(solution)/shard_map/ppermute | solution.py:23
  145.3 26.3 %collective-permute-start.32 = (bf16[384,384]{1,0:T(8,128)(2,1)S(1)}, bf16[384,384]{1,0:T(8,128)(2,1)S(1)}, u32[]{:S(2)}, u32[]{:S(2)}) collective-permute-start(bf16[384,384]{1,0:T(8,128)(2,1)S(1)} %get-tuple-element.356), channel_id=1, source_target_pairs={{0,4},{4,0},{8,12},{12,8},{16,20},{20,16},{24,28},{28,24},{1,5},{5... | collective-permute-start | bytes 884744 | tf_op jit(solution)/shard_map/ppermute | solution.py:23
  147.2 24.5 %collective-permute-start.33 = (bf16[384,384]{1,0:T(8,128)(2,1)}, bf16[384,384]{1,0:T(8,128)(2,1)S(1)}, u32[]{:S(2)}, u32[]{:S(2)}) collective-permute-start(bf16[384,384]{1,0:T(8,128)(2,1)} %collective-permute-done.29), channel_id=1, source_target_pairs={{0,4},{4,0},{8,12},{12,8},{16,20},{20,16},{24,28},{28,24},{1,5},{5... | collective-permute-start | bytes 884744 | tf_op jit(solution)/shard_map/ppermute | solution.py:23
  172.6 23.6 %collective-permute-start.39 = (bf16[384,768]{1,0:T(8,128)(2,1)}, bf16[384,768]{1,0:T(8,128)(2,1)S(1)}, u32[]{:S(2)}, u32[]{:S(2)}) collective-permute-start(bf16[384,768]{1,0:T(8,128)(2,1)} %get-tuple-element.378), channel_id=1, source_target_pairs={{0,4},{4,0},{8,12},{12,8},{16,20},{20,16},{24,28},{28,24},{1,5},{5... | collective-permute-start | bytes 1769480 | tf_op jit(solution)/shard_map/ppermute | solution.py:23
  174.4 21.8 %collective-permute-start.40 = (bf16[384,768]{1,0:T(8,128)(2,1)}, bf16[384,768]{1,0:T(8,128)(2,1)}, u32[]{:S(2)}, u32[]{:S(2)}) collective-permute-start(bf16[384,768]{1,0:T(8,128)(2,1)} %get-tuple-element.390), channel_id=1, source_target_pairs={{0,2},{1,3},{2,0},{3,1},{4,6},{5,7},{6,4},{7,5},{8,10},{9,11},{10,... | collective-permute-start | bytes 1769480 | tf_op jit(solution)/shard_map/ppermute | solution.py:23
  197.1 28.8 %collective-permute-start.42 = (bf16[768,768]{1,0:T(8,128)(2,1)}, bf16[768,768]{1,0:T(8,128)(2,1)}, u32[]{:S(2)}, u32[]{:S(2)}) collective-permute-start(bf16[768,768]{1,0:T(8,128)(2,1)} %constant_dynamic-update-slice_fusion.22.refs_5_.refs_4_), channel_id=1, source_target_pairs={{0,2},{1,3},{2,0},{3,1},{4,6},{5,7},{6,4},{7,5},{8,10},{9,11},{10,... | collective-permute-start | bytes 3538952 | tf_op jit(solution)/shard_map/ppermute | solution.py:23
  198.4 24.2 %collective-permute-start.43 = (bf16[384,768]{1,0:T(8,128)(2,1)S(1)}, bf16[384,768]{1,0:T(8,128)(2,1)}, u32[]{:S(2)}, u32[]{:S(2)}) collective-permute-start(bf16[384,768]{1,0:T(8,128)(2,1)S(1)} %copy-done.48), channel_id=1, source_target_pairs={{0,4},{4,0},{8,12},{12,8},{16,20},{20,16},{24,28},{28,24},{1,5},{5... | collective-permute-start | bytes 1769480 | tf_op jit(solution)/shard_map/ppermute | solution.py:23
  198.6 27.2 %collective-permute-start.44 = (bf16[384,768]{1,0:T(8,128)(2,1)}, bf16[384,768]{1,0:T(8,128)(2,1)}, u32[]{:S(2)}, u32[]{:S(2)}) collective-permute-start(bf16[384,768]{1,0:T(8,128)(2,1)} %collective-permute-done.40), channel_id=1, source_target_pairs={{0,4},{4,0},{8,12},{12,8},{16,20},{20,16},{24,28},{28,24},{1,5},{5... | collective-permute-start | bytes 1769480 | tf_op jit(solution)/shard_map/ppermute | solution.py:23
  201.5 27.8 %collective-permute-start.46 = (bf16[768,768]{1,0:T(8,128)(2,1)}, bf16[768,768]{1,0:T(8,128)(2,1)}, u32[]{:S(2)}, u32[]{:S(2)}) collective-permute-start(bf16[768,768]{1,0:T(8,128)(2,1)} %constant_dynamic-update-slice_fusion.22.refs_5_.refs_4_), channel_id=1, source_target_pairs={{0,1},{1,0},{2,3},{3,2},{4,5},{5,4},{6,7},{7,6},{8,9},{9,8},{10,11... | collective-permute-start | bytes 3538952 | tf_op jit(solution)/shard_map/ppermute | solution.py:23
  255.7 33.8 %collective-permute-start.50 = (bf16[384,768]{1,0:T(8,128)(2,1)S(1)}, bf16[384,768]{1,0:T(8,128)(2,1)S(1)}, u32[]{:S(2)}, u32[]{:S(2)}) collective-permute-start(bf16[384,768]{1,0:T(8,128)(2,1)S(1)} %slice.713), channel_id=1, source_target_pairs={{0,2},{1,3},{2,0},{3,1},{4,6},{5,7},{6,4},{7,5},{8,10},{9,11},{10,... | collective-permute-start | bytes 1769480 | tf_op jit(solution)/shard_map/ppermute | solution.py:23
  289.5 42.1 %collective-permute-start.51 = (bf16[4,768,768]{2,1,0:T(8,128)(2,1)}, bf16[4,768,768]{2,1,0:T(8,128)(2,1)}, u32[]{:S(2)}, u32[]{:S(2)}) collective-permute-start(bf16[4,768,768]{2,1,0:T(8,128)(2,1)} %get-tuple-element.431), channel_id=1, source_target_pairs={{0,1},{1,0},{2,3},{3,2},{4,5},{5,4},{6,7},{7,6},{8,9},{9,8},{10,11... | collective-permute-start | bytes 14155784 | tf_op jit(solution)/shard_map/ppermute | solution.py:23
  290.4 9.0 %collective-permute-start.52 = (bf16[768,768]{1,0:T(8,128)(2,1)}, bf16[768,768]{1,0:T(8,128)(2,1)S(1)}, u32[]{:S(2)}, u32[]{:S(2)}) collective-permute-start(bf16[768,768]{1,0:T(8,128)(2,1)} %get-tuple-element.444.refs_0_), channel_id=1, source_target_pairs={{0,1},{1,0},{2,3},{3,2},{4,5},{5,4},{6,7},{7,6},{8,9},{9,8},{10,11... | collective-permute-start | bytes 3538952 | tf_op jit(solution)/shard_map/ppermute | solution.py:23
  337.6 41.2 %collective-permute-start.53 = (bf16[768,768]{1,0:T(8,128)(2,1)}, bf16[768,768]{1,0:T(8,128)(2,1)}, u32[]{:S(2)}, u32[]{:S(2)}) collective-permute-start(bf16[768,768]{1,0:T(8,128)(2,1)} %fusion.32), channel_id=1, source_target_pairs={{0,2},{1,3},{2,0},{3,1},{4,6},{5,7},{6,4},{7,5},{8,10},{9,11},{10,... | collective-permute-start | bytes 3538952 | tf_op jit(solution)/shard_map/ppermute | solution.py:23
  338.9 39.9 %collective-permute-start.54 = (bf16[2,384,768]{2,1,0:T(8,128)(2,1)}, bf16[2,384,768]{2,1,0:T(8,128)(2,1)}, u32[]{:S(2)}, u32[]{:S(2)}) collective-permute-start(bf16[2,384,768]{2,1,0:T(8,128)(2,1)} %add_convert_fusion.5), channel_id=1, source_target_pairs={{0,4},{4,0},{8,12},{12,8},{16,20},{20,16},{24,28},{28,24},{1,5},{5... | collective-permute-start | bytes 3538952 | tf_op jit(solution)/shard_map/ppermute | solution.py:23
  389.0 40.5 %collective-permute-start.57 = (bf16[768,384]{0,1:T(8,128)(2,1)}, bf16[768,384]{0,1:T(8,128)(2,1)S(1)}, u32[]{:S(2)}, u32[]{:S(2)}) collective-permute-start(bf16[768,384]{0,1:T(8,128)(2,1)} %slice_bitcast_fusion.3), channel_id=1, source_target_pairs={{0,2},{1,3},{2,0},{3,1},{4,6},{5,7},{6,4},{7,5},{8,10},{9,11},{10,... | collective-permute-start | bytes 1769480 | tf_op jit(solution)/shard_map/ppermute | solution.py:23
  391.0 38.5 %collective-permute-start.58 = (bf16[2,384,384]{1,2,0:T(8,128)(2,1)}, bf16[2,384,384]{1,2,0:T(8,128)(2,1)}, u32[]{:S(2)}, u32[]{:S(2)}) collective-permute-start(bf16[2,384,384]{1,2,0:T(8,128)(2,1)} %slice.455), channel_id=1, source_target_pairs={{0,4},{4,0},{8,12},{12,8},{16,20},{20,16},{24,28},{28,24},{1,5},{5... | collective-permute-start | bytes 1769480 | tf_op jit(solution)/shard_map/ppermute | solution.py:23
  393.2 36.3 %collective-permute-start.55 = (bf16[384,768]{1,0:T(8,128)(2,1)}, bf16[384,768]{1,0:T(8,128)(2,1)}, u32[]{:S(2)}, u32[]{:S(2)}) collective-permute-start(bf16[384,768]{1,0:T(8,128)(2,1)} %slice.444), channel_id=1, source_target_pairs={{0,4},{4,0},{8,12},{12,8},{16,20},{20,16},{24,28},{28,24},{1,5},{5... | collective-permute-start | bytes 1769480 | tf_op jit(solution)/shard_map/ppermute | solution.py:23
  394.8 34.7 %collective-permute-start.56 = (bf16[384,768]{1,0:T(8,128)(2,1)}, bf16[384,768]{1,0:T(8,128)(2,1)}, u32[]{:S(2)}, u32[]{:S(2)}) collective-permute-start(bf16[384,768]{1,0:T(8,128)(2,1)} %slice_bitcast_fusion.4), channel_id=1, source_target_pairs={{0,2},{1,3},{2,0},{3,1},{4,6},{5,7},{6,4},{7,5},{8,10},{9,11},{10,... | collective-permute-start | bytes 1769480 | tf_op jit(solution)/shard_map/ppermute | solution.py:23
  429.5 24.5 %collective-permute-start.60 = (bf16[4,768,768]{2,1,0:T(8,128)(2,1)}, bf16[4,768,768]{2,1,0:T(8,128)(2,1)}, u32[]{:S(2)}, u32[]{:S(2)}) collective-permute-start(bf16[4,768,768]{2,1,0:T(8,128)(2,1)} %get-tuple-element.483), channel_id=1, source_target_pairs={{0,1},{1,0},{2,3},{3,2},{4,5},{5,4},{6,7},{7,6},{8,9},{9,8},{10,11... | collective-permute-start | bytes 14155784 | tf_op jit(solution)/shard_map/ppermute | solution.py:23
  434.7 9.3 %collective-permute-start.68 = (bf16[768,768]{1,0:T(8,128)(2,1)S(1)}, bf16[768,768]{1,0:T(8,128)(2,1)S(1)}, u32[]{:S(2)}, u32[]{:S(2)}) collective-permute-start(bf16[768,768]{1,0:T(8,128)(2,1)S(1)} %copy-done.1), channel_id=1, source_target_pairs={{0,1},{1,0},{2,3},{3,2},{4,5},{5,4},{6,7},{7,6},{8,9},{9,8},{10,11... | collective-permute-start | bytes 3538952 | tf_op jit(solution)/shard_map/ppermute | solution.py:23
  437.9 16.1 %collective-permute-start.63 = (bf16[192,1536]{1,0:T(8,128)(2,1)}, bf16[192,1536]{1,0:T(8,128)(2,1)}, u32[]{:S(2)}, u32[]{:S(2)}) collective-permute-start(bf16[192,1536]{1,0:T(8,128)(2,1)} %slice.463), channel_id=1, source_target_pairs={{0,8},{4,12},{8,0},{12,4},{16,24},{20,28},{24,16},{28,20},{1,9},{5... | collective-permute-start | bytes 1769480 | tf_op jit(solution)/shard_map/ppermute | solution.py:23
  440.3 9.4 %collective-permute-start.61 = (bf16[384,384]{0,1:T(8,128)(2,1)}, bf16[384,384]{0,1:T(8,128)(2,1)S(1)}, u32[]{:S(2)}, u32[]{:S(2)}) collective-permute-start(bf16[384,384]{0,1:T(8,128)(2,1)} %slice.461), channel_id=1, source_target_pairs={{0,4},{4,0},{8,12},{12,8},{16,20},{20,16},{24,28},{28,24},{1,5},{5... | collective-permute-start | bytes 884744 | tf_op jit(solution)/shard_map/ppermute | solution.py:23
  441.9 9.2 %collective-permute-start.62 = (bf16[384,384]{0,1:T(8,128)(2,1)}, bf16[384,384]{0,1:T(8,128)(2,1)}, u32[]{:S(2)}, u32[]{:S(2)}) collective-permute-start(bf16[384,384]{0,1:T(8,128)(2,1)} %slice_bitcast_fusion.5), channel_id=1, source_target_pairs={{0,2},{1,3},{2,0},{3,1},{4,6},{5,7},{6,4},{7,5},{8,10},{9,11},{10,... | collective-permute-start | bytes 884744 | tf_op jit(solution)/shard_map/ppermute | solution.py:23
  462.1 40.2 %collective-permute-start.64 = (bf16[768,768]{1,0:T(8,128)(2,1)}, bf16[768,768]{1,0:T(8,128)(2,1)}, u32[]{:S(2)}, u32[]{:S(2)}) collective-permute-start(bf16[768,768]{1,0:T(8,128)(2,1)} %fusion.33), channel_id=1, source_target_pairs={{0,2},{1,3},{2,0},{3,1},{4,6},{5,7},{6,4},{7,5},{8,10},{9,11},{10,... | collective-permute-start | bytes 3538952 | tf_op jit(solution)/shard_map/ppermute | solution.py:23
  463.3 39.0 %collective-permute-start.65 = (bf16[2,384,768]{2,1,0:T(8,128)(2,1)}, bf16[2,384,768]{2,1,0:T(8,128)(2,1)}, u32[]{:S(2)}, u32[]{:S(2)}) collective-permute-start(bf16[2,384,768]{2,1,0:T(8,128)(2,1)} %add_convert_fusion.2), channel_id=1, source_target_pairs={{0,4},{4,0},{8,12},{12,8},{16,20},{20,16},{24,28},{28,24},{1,5},{5... | collective-permute-start | bytes 3538952 | tf_op jit(solution)/shard_map/ppermute | solution.py:23
  467.1 35.2 %collective-permute-start.66 = (bf16[192,768]{0,1:T(8,128)(2,1)}, bf16[192,768]{0,1:T(8,128)(2,1)}, u32[]{:S(2)}, u32[]{:S(2)}) collective-permute-start(bf16[192,768]{0,1:T(8,128)(2,1)} %slice.472), channel_id=1, source_target_pairs={{0,8},{4,12},{8,0},{12,4},{16,24},{20,28},{24,16},{28,20},{1,9},{5... | collective-permute-start | bytes 884744 | tf_op jit(solution)/shard_map/ppermute | solution.py:23
  469.2 33.0 %collective-permute-start.67 = (bf16[96,1536]{1,0:T(8,128)(2,1)}, bf16[96,1536]{1,0:T(8,128)(2,1)}, u32[]{:S(2)}, u32[]{:S(2)}) collective-permute-start(bf16[96,1536]{1,0:T(8,128)(2,1)} %slice.473), channel_id=1, source_target_pairs={{0,16},{4,20},{8,24},{12,28},{16,0},{20,4},{24,8},{28,12},{1,17},{... | collective-permute-start | bytes 884744 | tf_op jit(solution)/shard_map/ppermute | solution.py:23
  512.3 43.6 %collective-permute-start.72 = (bf16[768,768]{0,1:T(8,128)(2,1)}, bf16[768,768]{0,1:T(8,128)(2,1)}, u32[]{:S(2)}, u32[]{:S(2)}) collective-permute-start(bf16[768,768]{0,1:T(8,128)(2,1)} %pad_maximum_fusion.12), channel_id=1, source_target_pairs={{0,2},{1,3},{2,0},{3,1},{4,6},{5,7},{6,4},{7,5},{8,10},{9,11},{10,... | collective-permute-start | bytes 3538952 | tf_op jit(solution)/shard_map/ppermute | solution.py:23
  513.8 42.1 %collective-permute-start.69 = (bf16[384,768]{1,0:T(8,128)(2,1)}, bf16[384,768]{1,0:T(8,128)(2,1)}, u32[]{:S(2)}, u32[]{:S(2)}) collective-permute-start(bf16[384,768]{1,0:T(8,128)(2,1)} %slice.476), channel_id=1, source_target_pairs={{0,4},{4,0},{8,12},{12,8},{16,20},{20,16},{24,28},{28,24},{1,5},{5... | collective-permute-start | bytes 1769480 | tf_op jit(solution)/shard_map/ppermute | solution.py:23
  515.9 40.0 %collective-permute-start.70 = (bf16[384,768]{1,0:T(8,128)(2,1)}, bf16[384,768]{1,0:T(8,128)(2,1)}, u32[]{:S(2)}, u32[]{:S(2)}) collective-permute-start(bf16[384,768]{1,0:T(8,128)(2,1)} %slice_bitcast_fusion.2), channel_id=1, source_target_pairs={{0,2},{1,3},{2,0},{3,1},{4,6},{5,7},{6,4},{7,5},{8,10},{9,11},{10,... | collective-permute-start | bytes 1769480 | tf_op jit(solution)/shard_map/ppermute | solution.py:23
  521.5 34.4 %collective-permute-start.71 = (bf16[96,768]{0,1:T(8,128)(2,1)}, bf16[96,768]{0,1:T(8,128)(2,1)}, u32[]{:S(2)}, u32[]{:S(2)}) collective-permute-start(bf16[96,768]{0,1:T(8,128)(2,1)} %slice.480), channel_id=1, source_target_pairs={{0,16},{4,20},{8,24},{12,28},{16,0},{20,4},{24,8},{28,12},{1,17},{... | collective-permute-start | bytes 442376 | tf_op jit(solution)/shard_map/ppermute | solution.py:23
  555.9 11.7 %collective-permute-start.75 = (bf16[768,768]{1,0:T(8,128)(2,1)}, bf16[768,768]{1,0:T(8,128)(2,1)S(1)}, u32[]{:S(2)}, u32[]{:S(2)}) collective-permute-start(bf16[768,768]{1,0:T(8,128)(2,1)} %get-tuple-element.534), channel_id=1, source_target_pairs={{0,1},{1,0},{2,3},{3,2},{4,5},{5,4},{6,7},{7,6},{8,9},{9,8},{10,11... | collective-permute-start | bytes 3538952 | tf_op jit(solution)/shard_map/ppermute | solution.py:23
  558.9 18.3 %collective-permute-start.74 = (bf16[192,1536]{1,0:T(8,128)(2,1)S(1)}, bf16[192,1536]{1,0:T(8,128)(2,1)S(1)}, u32[]{:S(2)}, u32[]{:S(2)}) collective-permute-start(bf16[192,1536]{1,0:T(8,128)(2,1)S(1)} %slice.552), channel_id=1, source_target_pairs={{0,8},{4,12},{8,0},{12,4},{16,24},{20,28},{24,16},{28,20},{1,9},{5... | collective-permute-start | bytes 1769480 | tf_op jit(solution)/shard_map/ppermute | solution.py:23
  564.9 15.7 %collective-permute-start.73 = (bf16[384,768]{0,1:T(8,128)(2,1)S(1)}, bf16[384,768]{0,1:T(8,128)(2,1)S(1)}, u32[]{:S(2)}, u32[]{:S(2)}) collective-permute-start(bf16[384,768]{0,1:T(8,128)(2,1)S(1)} %slice.551), channel_id=1, source_target_pairs={{0,4},{4,0},{8,12},{12,8},{16,20},{20,16},{24,28},{28,24},{1,5},{5... | collective-permute-start | bytes 1769480 | tf_op jit(solution)/shard_map/ppermute | solution.py:23
  581.1 17.0 %collective-permute-start.76 = (bf16[192,768]{0,1:T(8,128)(2,1)S(1)}, bf16[192,768]{0,1:T(8,128)(2,1)S(1)}, u32[]{:S(2)}, u32[]{:S(2)}) collective-permute-start(bf16[192,768]{0,1:T(8,128)(2,1)S(1)} %slice.491), channel_id=1, source_target_pairs={{0,8},{4,12},{8,0},{12,4},{16,24},{20,28},{24,16},{28,20},{1,9},{5... | collective-permute-start | bytes 884744 | tf_op jit(solution)/shard_map/ppermute | solution.py:23
  581.5 16.5 %collective-permute-start.77 = (bf16[96,1536]{1,0:T(8,128)(2,1)S(1)}, bf16[96,1536]{1,0:T(8,128)(2,1)S(1)}, u32[]{:S(2)}, u32[]{:S(2)}) collective-permute-start(bf16[96,1536]{1,0:T(8,128)(2,1)S(1)} %slice.492), channel_id=1, source_target_pairs={{0,16},{4,20},{8,24},{12,28},{16,0},{20,4},{24,8},{28,12},{1,17},{... | collective-permute-start | bytes 884744 | tf_op jit(solution)/shard_map/ppermute | solution.py:23
  599.6 10.6 %collective-permute-start.81 = (bf16[96,768]{0,1:T(8,128)(2,1)S(1)}, bf16[96,768]{0,1:T(8,128)(2,1)S(1)}, u32[]{:S(2)}, u32[]{:S(2)}) collective-permute-start(bf16[96,768]{0,1:T(8,128)(2,1)S(1)} %slice.496), channel_id=1, source_target_pairs={{0,16},{4,20},{8,24},{12,28},{16,0},{20,4},{24,8},{28,12},{1,17},{... | collective-permute-start | bytes 442376 | tf_op jit(solution)/shard_map/ppermute | solution.py:23
  603.0 21.4 %collective-permute-start.83 = (bf16[384,768]{1,0:T(8,128)(2,1)}, bf16[384,768]{1,0:T(8,128)(2,1)S(1)}, u32[]{:S(2)}, u32[]{:S(2)}) collective-permute-start(bf16[384,768]{1,0:T(8,128)(2,1)} %get-tuple-element.570), channel_id=1, source_target_pairs={{0,2},{1,3},{2,0},{3,1},{4,6},{5,7},{6,4},{7,5},{8,10},{9,11},{10,... | collective-permute-start | bytes 1769480 | tf_op jit(solution)/shard_map/ppermute | solution.py:23
  (138 other events, 750.9 us)

commit v10 on v9

--- a/solution.py
+++ b/solution.py
@@ -953,7 +953,7 @@
     gradient, half, *small = advance([folding], *out)
     got = advance([folding], *[exchange(small[t], "tensor", t) for t in range(1, 4)])
     small = small[0] + got[0] + got[1] + got[2]
-    half, small = together(half, small)
+    half, small, current, encoded_half = together(half, small, current, encoded_half)
     half = exchange(half, "tensor", 2)
     frames_grad = give_clip(gradient, half)
     for mask in reversed(dp_masks()):
@@ -961,8 +961,6 @@
         if folding.step < 3:
             (got,) = advance([folding], got)
         small = small[:, : small.shape[1] // 2] + got
-        if folding.step == 3 and mask == 1:
-            small, current, encoded_half = together(small, current, encoded_half)
     encoded = give_clip(current, encoded_half)
     weight_grads[0] = folding.result()
     by_width = lax.dynamic_slice(small, (0, t_me * norm_part), (6 * layers, norm_part))

time: 644 us -> 643 us (level)
  transfers between devices with their start and end apart: 86 -> 86, of which waited for: 25 -> 27; matrix products, arithmetic and copies ran while one was open for 16% -> 16% of each run, Pallas kernels for 46% -> 46%
where the time goes in v10:
time: 643 us; the launch traced here: 633 us
  Pallas kernels  307 us (48%)
  starting transfers between devices  79.7 us (12%)
  local copies, waits for them, and re-layouts  78.2 us (12%)
  waiting for transfers between devices  71.1 us (11%)
  other arithmetic  57.5 us (9%)
  matrix products  36.1 us (6%)
    pallas_call x4, Pallas kernels, attend_back(): pl.pallas_call(functools.partial(attend_back_kernel, row_count, quarter,...  123 us
    ppermute x86, starting transfers between devices, exchange(): return lax.ppermute(value, axis, [(i, i ^ mask) for i in range(count)])  79.7 us
    pallas_call x4, Pallas kernels, attend(): pl.pallas_call(functools.partial(attend_kernel, row_count, quarter, min(5...  72.9 us
    ppermute x86, waiting for transfers between devices, exchange(): return lax.ppermute(value, axis, [(i, i ^ mask) for i in range(count)])  71.1 us
    pallas_call x2, Pallas kernels, feed_back(): pl.pallas_call(functools.partial(feed_back_kernel, at, layers), grid=(hid...  64 us
    unnamed x254, local copies, waits for them, and re-layouts  39.5 us
    pallas_call x2, Pallas kernels, feed(): pl.pallas_call(functools.partial(feed_kernel, at, layers), grid=(hidden /...  38.4 us
    convert_element_type x22, other arithmetic, add_low(): return (kept.astype(f32) + received.astype(f32)).astype(bf16)  28.5 us
  transfers between devices with their start and end apart: 86, of which 27 were waited for; matrix products, arithmetic and copies ran while one was open for 16% of the time, Pallas kernels for 46%

profile of v10, /device:TPU:0, one launch (start us, length us, event | category | flops | bytes accessed | tf_op | source)
XLA Modules:
  0.0 632.5 jit_solution(2916082377770514751)
XLA Ops:
  3.2 4.2 collective-permute-start.2
  7.8 2.9 collective-permute-start.3
  18.5 1.8 collective-permute-done.4
  27.1 2.2 collective-permute-done.8
  36.0 2.7 fusion.93
  38.7 2.0 copy.39.refs_0_
  41.2 2.1 pad_maximum_fusion.13.refs_2_
  46.8 1.8 pad_maximum_fusion.14
  52.8 1.9 concatenate.143.refs_4_
  56.9 5.7 collective-permute-done.18
  64.6 2.3 collective-permute-start.19
  68.4 2.6 collective-permute-start.22
  75.0 17.3 %shard_map.194 = (bf16[1536,576]{1,0:T(8,128)(2,1)}, bf16[1536,192]{1,0:T(8,128)(2,1)}, f32[1536,8]{1,0:T(8,128)}) custom-call(bf16[768,768]{1,0:T(8,128)(2,1)} %copy-done.7, bf16[768,768]{1,0:T(8,128)(2,1)} %collective-permute-done.16.refs_1_, bf16[768,384]{1,0:T(8,128)(2,1)} %pad_maximum_fusion.13.refs_2_, bf16[768,384]{1,0:T(8,128)(2,1)} %copy-done.18, ...), custom_call_target="tpu_custom_call" | custom-call | tf_op jit(solution)/shard_map/pallas_call | solution.py:397
  92.4 1.8 constant_dynamic-update-slice_fusion.8
  106.4 19.2 %shard_map.195 = (f32[768,768]{1,0:T(8,128)}, bf16[768,768]{1,0:T(8,128)(2,1)}, bf16[1536,576]{1,0:T(8,128)(2,1)}, bf16[1536,192]{1,0:T(8,128)(2,1)}, f32[1536,8]{1,0:T(8,128)}) custom-call(bf16[768,768]{1,0:T(8,128)(2,1)} %copy-done.7, bf16[768,768]{1,0:T(8,128)(2,1)} %collective-permute-done.16.refs_1_, ...), custom_call_target="tpu_custom_call" | custom-call | tf_op jit(solution)/shard_map/pallas_call | solution.py:397
  135.2 5.2 collective-permute-done.28
  140.4 1.9 collective-permute-done.29
  145.3 1.8 collective-permute-start.32
  148.2 20.2 %shard_map.196 = (bf16[768,768]{1,0:T(8,128)(2,1)}, bf16[768,768]{1,0:T(8,128)(2,1)}, bf16[768,768]{1,0:T(8,128)(2,1)}, bf16[768,768]{1,0:T(8,128)(2,1)}, bf16[7...) custom-call(f32[768,768]{1,0:T(8,128)} %copy-done, ...), custom_call_target="tpu_custom_call" | custom-call | tf_op jit(solution)/shard_map/pallas_call | solution.py:579
  168.5 3.2 collective-permute-done.38
  172.6 1.8 collective-permute-start.39
  175.1 1.9 constant_dynamic-update-slice_fusion.23
  179.0 17.2 %shard_map.197 = (bf16[1536,576]{1,0:T(8,128)(2,1)}, bf16[1536,192]{1,0:T(8,128)(2,1)}, f32[1536,8]{1,0:T(8,128)}) custom-call(bf16[768,768]{1,0:T(8,128)(2,1)} %get-tuple-element.392.refs_0_, bf16[768,768]{1,0:T(8,128)(2,1)} %copy-done.9, bf16[768,384]{1,0:T(8,128)(2,1)} %pad_maximum_fusion.15.refs_2_, bf16[768,384]{1,0:T(8,128)(2,1)} %copy-done.19, ...), custom_call_target="tpu_custom_call" | custom-call | tf_op jit(solution)/shard_map/pallas_call | solution.py:397
  198.6 1.8 collective-permute-start.44
  202.3 19.1 %shard_map.198 = (f32[768,768]{1,0:T(8,128)}, bf16[768,768]{1,0:T(8,128)(2,1)}, bf16[1536,576]{1,0:T(8,128)(2,1)}, bf16[1536,192]{1,0:T(8,128)(2,1)}, f32[1536,8]{1,0:T(8,128)}) custom-call(bf16[768,768]{1,0:T(8,128)(2,1)} %get-tuple-element.392.refs_0_, bf16[768,768]{1,0:T(8,128)(2,1)} %copy-done.9, ...), custom_call_target="tpu_custom_call" | custom-call | tf_op jit(solution)/shard_map/pallas_call | solution.py:397
  222.6 3.3 collective-permute-done.44
  231.6 3.4 collective-permute-done.45.refs_2_
  236.1 18.2 %shard_map.199 = (bf16[768,768]{1,0:T(8,128)(2,1)}, bf16[768,768]{1,0:T(8,128)(2,1)}, bf16[768,768]{1,0:T(8,128)(2,1)}, bf16[768,768]{1,0:T(8,128)(2,1)}, bf16[7...) custom-call(f32[768,768]{1,0:T(8,128)} %get-tuple-element.462.refs_0, ...), custom_call_target="tpu_custom_call" | custom-call | tf_op jit(solution)/shard_map/pallas_call | solution.py:579
  256.6 2.6 fusion.20.refs_0_
  259.2 30.3 %shard_map.200 = (bf16[4,768,768]{2,1,0:T(8,128)(2,1)}, bf16[4,768,768]{2,1,0:T(8,128)(2,1)}, f32[4,768]{1,0:T(4,128)}, f32[768,768]{1,0:T(8,128)}, bf16[768,768]{1,0:T(8,128)(2,1)}, /*index=5*/f32[8,768]{1,0:T(8,128)}) custom-call(f32[768,768]{1,0:T(8,128)} %fusion.20.refs_0_, f32[768,768]{1,0:T(8,128)} %get-tuple-element.406.refs_1_, ...), custom_call_target="tpu_custom_call" | custom-call | tf_op jit(solution)/shard_map/pallas_call | solution.py:657
  293.5 5.9 collective-permute-done.52.refs_1_
  300.4 28.2 %shard_map.201 = (bf16[1536,576]{1,0:T(8,128)(2,1)}, f32[8,576]{1,0:T(8,128)}) custom-call(bf16[768,768]{1,0:T(8,128)(2,1)} %get-tuple-element.443.refs_0_, bf16[768,768]{1,0:T(8,128)(2,1)} %copy-done.5, bf16[768,384]{1,0:T(8,128)(2,1)} %collective-permute-done.31.refs_2_.refs_8_, bf16[768,384]{1,0:T(8,128)(2,1)} %copy-done.17, ...), custom_call_target="tpu_custom_call" | custom-call | tf_op jit(solution)/shard_map/pallas_call | solution.py:491
  328.6 1.8 fusion.69
  331.6 2.9 add_convert_fusion.5
  334.5 3.1 fusion.32
  344.4 33.2 %shard_map.202 = (f32[768,768]{1,0:T(8,128)}, bf16[768,768]{1,0:T(8,128)(2,1)}, bf16[1536,576]{1,0:T(8,128)(2,1)}, f32[8,576]{1,0:T(8,128)}) custom-call(bf16[768,768]{1,0:T(8,128)(2,1)} %get-tuple-element.443.refs_0_, bf16[768,768]{1,0:T(8,128)(2,1)} %copy-done.5, bf16[768,384]{1,0:T(8,128)(2,1)} %pad_maximum_fusion.15.refs_2_, ...), custom_call_target="tpu_custom_call" | custom-call | tf_op jit(solution)/shard_map/pallas_call | solution.py:491
  378.8 4.0 convolution_convert_fusion.1
  383.0 2.1 add_convert_fusion.4
  385.1 2.5 fusion.5
  395.7 33.7 %shard_map.203 = (bf16[4,768,768]{2,1,0:T(8,128)(2,1)}, bf16[4,768,768]{2,1,0:T(8,128)(2,1)}, f32[4,768]{1,0:T(4,128)}, f32[768,768]{1,0:T(8,128)}, bf16[768,768]{1,0:T(8,128)(2,1)}, /*index=5*/f32[8,768]{1,0:T(8,128)}) custom-call(f32[768,768]{1,0:T(8,128)} %get-tuple-element.461.refs_0_, f32[768,768]{1,0:T(8,128)} %get-tuple-element.462.refs_0_.refs_1_, ...), custom_call_target="tpu_custom_call" | custom-call | tf_op jit(solution)/shard_map/pallas_call | solution.py:657
  445.3 4.3 collective-permute-done.61
  451.1 2.9 collective-permute-done.63
  454.0 2.9 add_convert_fusion.2
  456.9 3.0 fusion.33
  469.2 2.9 collective-permute-start.67
  473.8 28.5 %shard_map.204 = (bf16[1536,576]{1,0:T(8,128)(2,1)}, f32[8,576]{1,0:T(8,128)}) custom-call(bf16[768,768]{1,0:T(8,128)(2,1)} %get-tuple-element.517.refs_0_, bf16[768,768]{1,0:T(8,128)(2,1)} %copy-done.3, bf16[768,384]{1,0:T(8,128)(2,1)} %collective-permute-done.13.refs_2_.refs_8_, bf16[768,384]{1,0:T(8,128)(2,1)} %copy-done.16, ...), custom_call_target="tpu_custom_call" | custom-call | tf_op jit(solution)/shard_map/pallas_call | solution.py:491
  502.3 3.5 fusion.26
  505.8 2.4 add_convert_fusion.1
  508.3 2.8 fusion.4
  522.7 33.2 %shard_map.205 = (f32[768,768]{1,0:T(8,128)}, bf16[768,768]{1,0:T(8,128)(2,1)}, bf16[1536,576]{1,0:T(8,128)(2,1)}, f32[8,576]{1,0:T(8,128)}) custom-call(bf16[768,768]{1,0:T(8,128)(2,1)} %get-tuple-element.517.refs_0_, bf16[768,768]{1,0:T(8,128)(2,1)} %copy-done.3, bf16[768,384]{1,0:T(8,128)(2,1)} %pad_maximum_fusion.13.refs_2_, ...), custom_call_target="tpu_custom_call" | custom-call | tf_op jit(solution)/shard_map/pallas_call | solution.py:491
  560.3 2.9 fusion.27
  568.7 8.5 %shard_map.206 = (f32[768,768]{1,0:T(8,128)}, bf16[384,768]{1,0:T(8,128)(2,1)}, f32[24,768]{1,0:T(8,128)}, f32[24,768]{1,0:T(8,128)}, f32[24,768]{1,0:T(8,128)}, /*index=5*/f32[24,768]{1,0:T(8,128)}) custom-call(f32[768,768]{1,0:T(8,128)} %copy-done, f32[768,768]{1,0:T(8,128)} %get-tuple-element.531.refs_1_, f32[768,768]{1,0:T(8,128)} %get-tuple-element.532.refs_2_, ...), custom_call_target="tpu_custom_call" | custom-call | tf_op jit(solution)/shard_map/pallas_call | solution.py:722
  577.2 3.4 collective-permute-done.73
  581.5 3.0 collective-permute-start.77
  587.2 2.0 fusion.9
  590.3 7.7 %collective-permute-done.76 = bf16[192,768]{0,1:T(8,128)(2,1)S(1)} collective-permute-done((bf16[192,768]{0,1:T(8,128)(2,1)S(1)}, bf16[192,768]{0,1:T(8,128)(2,1)S(1)}, u32[]{:S(2)}, u32[]{:S(2)}) %collective-permute-start.76) | collective-permute-done | bytes 294944 | tf_op jit(solution)/shard_map/ppermute | solution.py:23
  598.1 1.8 fusion.15
  599.9 1.8 fusion.17
  607.3 5.6 collective-permute-done.82
  614.9 1.8 collective-permute-done.84
  619.1 2.4 collective-permute-done.85
  623.5 3.0 select_bitcast_fusion.1
  626.7 2.6 copy.46
  629.6 2.6 copy.45
  (547 shorter events, 174.3 us)
Async XLA Ops:
  3.2 12.4 %collective-permute-start.2 = (f32[6,768]{1,0:T(8,128)S(1)}, f32[6,768]{1,0:T(8,128)S(1)}, u32[]{:S(2)}, u32[]{:S(2)}) collective-permute-start(f32[6,768]{1,0:T(8,128)S(1)} %pad_maximum_fusion.30), channel_id=1, source_target_pairs={{0,16},{4,20},{8,24},{12,28},{16,0},{20,4},{24,8},{28,12},{1,17},{... | collective-permute-start | bytes 55304 | tf_op jit(solution)/shard_map/ppermute | solution.py:23
  7.8 12.5 %collective-permute-start.3 = (bf16[96,768]{1,0:T(8,128)(2,1)S(1)}, bf16[96,768]{1,0:T(8,128)(2,1)S(1)}, u32[]{:S(2)}, u32[]{:S(2)}) collective-permute-start(bf16[96,768]{1,0:T(8,128)(2,1)S(1)} %pad_maximum_fusion.23), channel_id=1, source_target_pairs={{0,16},{4,20},{8,24},{12,28},{16,0},{20,4},{24,8},{28,12},{1,17},{... | collective-permute-start | bytes 442376 | tf_op jit(solution)/shard_map/ppermute | solution.py:23
  10.9 25.0 %collective-permute-start = (bf16[375,768]{1,0:T(8,128)(2,1)S(1)}, bf16[375,768]{1,0:T(8,128)(2,1)S(1)}, u32[]{:S(2)}, u32[]{:S(2)}) collective-permute-start(bf16[375,768]{1,0:T(8,128)(2,1)S(1)} %get-tuple-element.612), channel_id=1, source_target_pairs={{0,2},{1,3},{2,0},{3,1},{4,6},{5,7},{6,4},{7,5},{8,10},{9,11},{10,... | collective-permute-start | bytes 1728008 | tf_op jit(solution)/shard_map/ppermute | solution.py:23
  30.1 11.1 %collective-permute-start.12 = (f32[20,768]{1,0:T(8,128)}, f32[20,768]{1,0:T(8,128)}, u32[]{:S(2)}, u32[]{:S(2)}) collective-permute-start(f32[20,768]{1,0:T(8,128)} %pad_maximum_fusion.25), channel_id=1, source_target_pairs={{0,2},{1,3},{2,0},{3,1},{4,6},{5,7},{6,4},{7,5},{8,10},{9,11},{10,... | collective-permute-start | bytes 184328 | tf_op jit(solution)/shard_map/ppermute | solution.py:23
  31.9 9.3 %collective-permute-start.10 = (bf16[384,384]{1,0:T(8,128)(2,1)S(1)}, bf16[384,384]{1,0:T(8,128)(2,1)}, u32[]{:S(2)}, u32[]{:S(2)}) collective-permute-start(bf16[384,384]{1,0:T(8,128)(2,1)S(1)} %get-tuple-element.307), channel_id=1, source_target_pairs={{0,4},{4,0},{8,12},{12,8},{16,20},{20,16},{24,28},{28,24},{1,5},{5... | collective-permute-start | bytes 884744 | tf_op jit(solution)/shard_map/ppermute | solution.py:23
  34.3 12.4 %collective-permute-start.17 = (bf16[96,1536]{1,0:T(8,128)(2,1)S(1)}, bf16[96,1536]{1,0:T(8,128)(2,1)}, u32[]{:S(2)}, u32[]{:S(2)}) collective-permute-start(bf16[96,1536]{1,0:T(8,128)(2,1)S(1)} %pad_maximum_fusion.20), channel_id=1, source_target_pairs={{0,16},{4,20},{8,24},{12,28},{16,0},{20,4},{24,8},{28,12},{1,17},{... | collective-permute-start | bytes 884744 | tf_op jit(solution)/shard_map/ppermute | solution.py:23
  43.3 28.8 %collective-permute-start.13 = (bf16[768,384]{1,0:T(8,128)(2,1)}, bf16[768,384]{1,0:T(8,128)(2,1)}, u32[]{:S(2)}, u32[]{:S(2)}) collective-permute-start(bf16[768,384]{1,0:T(8,128)(2,1)} %pad_maximum_fusion.13.refs_2_), channel_id=1, source_target_pairs={{0,2},{1,3},{2,0},{3,1},{4,6},{5,7},{6,4},{7,5},{8,10},{9,11},{10,... | collective-permute-start | bytes 1769480 | tf_op jit(solution)/shard_map/ppermute | solution.py:23
  48.6 14.0 %collective-permute-start.18 = (bf16[192,1536]{1,0:T(8,128)(2,1)}, bf16[192,1536]{1,0:T(8,128)(2,1)}, u32[]{:S(2)}, u32[]{:S(2)}) collective-permute-start(bf16[192,1536]{1,0:T(8,128)(2,1)} %pad_maximum_fusion.14), channel_id=1, source_target_pairs={{0,8},{4,12},{8,0},{12,4},{16,24},{20,28},{24,16},{28,20},{1,9},{5... | collective-permute-start | bytes 1769480 | tf_op jit(solution)/shard_map/ppermute | solution.py:23
  49.9 23.2 %collective-permute-start.16 = (bf16[768,768]{1,0:T(8,128)(2,1)S(1)}, bf16[768,768]{1,0:T(8,128)(2,1)}, u32[]{:S(2)}, u32[]{:S(2)}) collective-permute-start(bf16[768,768]{1,0:T(8,128)(2,1)S(1)} %add_convert_fusion.7.refs_0_), channel_id=1, source_target_pairs={{0,1},{1,0},{2,3},{3,2},{4,5},{5,4},{6,7},{7,6},{8,9},{9,8},{10,11... | collective-permute-start | bytes 3538952 | tf_op jit(solution)/shard_map/ppermute | solution.py:23
  50.0 16.9 %collective-permute-start.14 = (bf16[384,384]{1,0:T(8,128)(2,1)}, bf16[384,384]{1,0:T(8,128)(2,1)}, u32[]{:S(2)}, u32[]{:S(2)}) collective-permute-start(bf16[384,384]{1,0:T(8,128)(2,1)} %get-tuple-element.313), channel_id=1, source_target_pairs={{0,4},{4,0},{8,12},{12,8},{16,20},{20,16},{24,28},{28,24},{1,5},{5... | collective-permute-start | bytes 884744 | tf_op jit(solution)/shard_map/ppermute | solution.py:23
  50.7 17.6 %collective-permute-start.15 = (bf16[384,384]{1,0:T(8,128)(2,1)}, bf16[384,384]{1,0:T(8,128)(2,1)}, u32[]{:S(2)}, u32[]{:S(2)}) collective-permute-start(bf16[384,384]{1,0:T(8,128)(2,1)} %collective-permute-done.11), channel_id=1, source_target_pairs={{0,4},{4,0},{8,12},{12,8},{16,20},{20,16},{24,28},{28,24},{1,5},{5... | collective-permute-start | bytes 884744 | tf_op jit(solution)/shard_map/ppermute | solution.py:23
  64.6 27.7 %collective-permute-start.19 = (bf16[384,768]{1,0:T(8,128)(2,1)}, bf16[384,768]{1,0:T(8,128)(2,1)}, u32[]{:S(2)}, u32[]{:S(2)}) collective-permute-start(bf16[384,768]{1,0:T(8,128)(2,1)} %get-tuple-element.318), channel_id=1, source_target_pairs={{0,4},{4,0},{8,12},{12,8},{16,20},{20,16},{24,28},{28,24},{1,5},{5... | collective-permute-start | bytes 1769480 | tf_op jit(solution)/shard_map/ppermute | solution.py:23
  66.9 25.5 %collective-permute-start.20 = (bf16[384,768]{1,0:T(8,128)(2,1)S(1)}, bf16[384,768]{1,0:T(8,128)(2,1)}, u32[]{:S(2)}, u32[]{:S(2)}) collective-permute-start(bf16[384,768]{1,0:T(8,128)(2,1)S(1)} %get-tuple-element.334), channel_id=1, source_target_pairs={{0,2},{1,3},{2,0},{3,1},{4,6},{5,7},{6,4},{7,5},{8,10},{9,11},{10,... | collective-permute-start | bytes 1769480 | tf_op jit(solution)/shard_map/ppermute | solution.py:23
  68.4 24.0 %collective-permute-start.22 = (bf16[96,1536]{1,0:T(8,128)(2,1)S(1)}, bf16[96,1536]{1,0:T(8,128)(2,1)}, u32[]{:S(2)}, u32[]{:S(2)}) collective-permute-start(bf16[96,1536]{1,0:T(8,128)(2,1)S(1)} %copy-done.63), channel_id=1, source_target_pairs={{0,16},{4,20},{8,24},{12,28},{16,0},{20,4},{24,8},{28,12},{1,17},{... | collective-permute-start | bytes 884744 | tf_op jit(solution)/shard_map/ppermute | solution.py:23
  72.1 20.3 %collective-permute-start.21 = (bf16[96,768]{1,0:T(8,128)(2,1)S(1)}, bf16[96,768]{1,0:T(8,128)(2,1)}, u32[]{:S(2)}, u32[]{:S(2)}) collective-permute-start(bf16[96,768]{1,0:T(8,128)(2,1)S(1)} %copy-done.79), channel_id=1, source_target_pairs={{0,16},{4,20},{8,24},{12,28},{16,0},{20,4},{24,8},{28,12},{1,17},{... | collective-permute-start | bytes 442376 | tf_op jit(solution)/shard_map/ppermute | solution.py:23
  96.2 30.6 %collective-permute-start.23 = (bf16[768,768]{1,0:T(8,128)(2,1)S(1)}, bf16[768,768]{1,0:T(8,128)(2,1)}, u32[]{:S(2)}, u32[]{:S(2)}) collective-permute-start(bf16[768,768]{1,0:T(8,128)(2,1)S(1)} %constant_dynamic-update-slice_fusion.4.refs_5_.refs_7_), channel_id=1, source_target_pairs={{0,2},{1,3},{2,0},{3,1},{4,6},{5,7},{6,4},{7,5},{8,10},{9,11},{10,... | collective-permute-start | bytes 3538952 | tf_op jit(solution)/shard_map/ppermute | solution.py:23
  98.6 28.2 %collective-permute-start.24 = (bf16[384,768]{1,0:T(8,128)(2,1)S(1)}, bf16[384,768]{1,0:T(8,128)(2,1)}, u32[]{:S(2)}, u32[]{:S(2)}) collective-permute-start(bf16[384,768]{1,0:T(8,128)(2,1)S(1)} %copy-done.50), channel_id=1, source_target_pairs={{0,4},{4,0},{8,12},{12,8},{16,20},{20,16},{24,28},{28,24},{1,5},{5... | collective-permute-start | bytes 1769480 | tf_op jit(solution)/shard_map/ppermute | solution.py:23
  98.9 27.9 %collective-permute-start.25 = (bf16[384,768]{1,0:T(8,128)(2,1)}, bf16[384,768]{1,0:T(8,128)(2,1)}, u32[]{:S(2)}, u32[]{:S(2)}) collective-permute-start(bf16[384,768]{1,0:T(8,128)(2,1)} %collective-permute-done.20), channel_id=1, source_target_pairs={{0,4},{4,0},{8,12},{12,8},{16,20},{20,16},{24,28},{28,24},{1,5},{5... | collective-permute-start | bytes 1769480 | tf_op jit(solution)/shard_map/ppermute | solution.py:23
  100.7 26.2 %collective-permute-start.27 = (bf16[192,1536]{1,0:T(8,128)(2,1)}, bf16[192,1536]{1,0:T(8,128)(2,1)}, u32[]{:S(2)}, u32[]{:S(2)}) collective-permute-start(bf16[192,1536]{1,0:T(8,128)(2,1)} %constant_dynamic-update-slice_fusion.8), channel_id=1, source_target_pairs={{0,8},{4,12},{8,0},{12,4},{16,24},{20,28},{24,16},{28,20},{1,9},{5... | collective-permute-start | bytes 1769480 | tf_op jit(solution)/shard_map/ppermute | solution.py:23
  101.5 25.3 %collective-permute-start.26 = (bf16[192,768]{1,0:T(8,128)(2,1)S(1)}, bf16[192,768]{1,0:T(8,128)(2,1)}, u32[]{:S(2)}, u32[]{:S(2)}) collective-permute-start(bf16[192,768]{1,0:T(8,128)(2,1)S(1)} %constant_dynamic-update-slice_fusion.6), channel_id=1, source_target_pairs={{0,8},{4,12},{8,0},{12,4},{16,24},{20,28},{24,16},{28,20},{1,9},{5... | collective-permute-start | bytes 884744 | tf_op jit(solution)/shard_map/ppermute | solution.py:23
  126.7 17.8 %collective-permute-start.34 = (bf16[768,768]{1,0:T(8,128)(2,1)S(1)}, bf16[768,768]{1,0:T(8,128)(2,1)S(1)}, u32[]{:S(2)}, u32[]{:S(2)}) collective-permute-start(bf16[768,768]{1,0:T(8,128)(2,1)S(1)} %constant_dynamic-update-slice_fusion.4.refs_5_.refs_7_), channel_id=1, source_target_pairs={{0,1},{1,0},{2,3},{3,2},{4,5},{5,4},{6,7},{7,6},{8,9},{9,8},{10,11... | collective-permute-start | bytes 3538952 | tf_op jit(solution)/shard_map/ppermute | solution.py:23
  129.6 12.6 %collective-permute-start.30 = (bf16[768,768]{1,0:T(8,128)(2,1)S(1)}, bf16[768,768]{1,0:T(8,128)(2,1)S(1)}, u32[]{:S(2)}, u32[]{:S(2)}) collective-permute-start(bf16[768,768]{1,0:T(8,128)(2,1)S(1)} %copy-done.106), channel_id=1, source_target_pairs={{0,1},{1,0},{2,3},{3,2},{4,5},{5,4},{6,7},{7,6},{8,9},{9,8},{10,11... | collective-permute-start | bytes 3538952 | tf_op jit(solution)/shard_map/ppermute | solution.py:23
  131.2 9.2 %collective-permute-start.28 = (bf16[384,384]{1,0:T(8,128)(2,1)S(1)}, bf16[384,384]{1,0:T(8,128)(2,1)S(1)}, u32[]{:S(2)}, u32[]{:S(2)}) collective-permute-start(bf16[384,384]{1,0:T(8,128)(2,1)S(1)} %get-tuple-element.349), channel_id=1, source_target_pairs={{0,4},{4,0},{8,12},{12,8},{16,20},{20,16},{24,28},{28,24},{1,5},{5... | collective-permute-start | bytes 884744 | tf_op jit(solution)/shard_map/ppermute | solution.py:23
  132.7 12.7 %collective-permute-start.37 = (bf16[768,768]{1,0:T(8,128)(2,1)S(1)}, bf16[768,768]{1,0:T(8,128)(2,1)S(1)}, u32[]{:S(2)}, u32[]{:S(2)}) collective-permute-start(bf16[768,768]{1,0:T(8,128)(2,1)S(1)} %constant_dynamic-update-slice_fusion.18.refs_11_.refs_13_), channel_id=1, source_target_pairs={{0,1},{1,0},{2,3},{3,2},{4,5},{5,4},{6,7},{7,6},{8,9},{9,8},{10,11... | collective-permute-start | bytes 3538952 | tf_op jit(solution)/shard_map/ppermute | solution.py:23
  132.8 9.5 %collective-permute-start.29 = (bf16[384,384]{1,0:T(8,128)(2,1)S(1)}, bf16[384,384]{1,0:T(8,128)(2,1)}, u32[]{:S(2)}, u32[]{:S(2)}) collective-permute-start(bf16[384,384]{1,0:T(8,128)(2,1)S(1)} %get-tuple-element.355), channel_id=1, source_target_pairs={{0,2},{1,3},{2,0},{3,1},{4,6},{5,7},{6,4},{7,5},{8,10},{9,11},{10,... | collective-permute-start | bytes 884744 | tf_op jit(solution)/shard_map/ppermute | solution.py:23
  143.3 28.4 %collective-permute-start.31 = (bf16[768,384]{1,0:T(8,128)(2,1)}, bf16[768,384]{1,0:T(8,128)(2,1)}, u32[]{:S(2)}, u32[]{:S(2)}) collective-permute-start(bf16[768,384]{1,0:T(8,128)(2,1)} %pad_maximum_fusion.15.refs_2_), channel_id=1, source_target_pairs={{0,2},{1,3},{2,0},{3,1},{4,6},{5,7},{6,4},{7,5},{8,10},{9,11},{10,... | collective-permute-start | bytes 1769480 | tf_op jit(solution)/shard_map/ppermute | solution.py:23
  144.5 27.1 %collective-permute-start.38 = (bf16[375,768]{1,0:T(8,128)(2,1)}, bf16[375,768]{1,0:T(8,128)(2,1)S(1)}, u32[]{:S(2)}, u32[]{:S(2)}) collective-permute-start(bf16[375,768]{1,0:T(8,128)(2,1)} %get-tuple-element.374), channel_id=1, source_target_pairs={{0,2},{1,3},{2,0},{3,1},{4,6},{5,7},{6,4},{7,5},{8,10},{9,11},{10,... | collective-permute-start | bytes 1728008 | tf_op jit(solution)/shard_map/ppermute | solution.py:23
  145.3 26.3 %collective-permute-start.32 = (bf16[384,384]{1,0:T(8,128)(2,1)S(1)}, bf16[384,384]{1,0:T(8,128)(2,1)S(1)}, u32[]{:S(2)}, u32[]{:S(2)}) collective-permute-start(bf16[384,384]{1,0:T(8,128)(2,1)S(1)} %get-tuple-element.355), channel_id=1, source_target_pairs={{0,4},{4,0},{8,12},{12,8},{16,20},{20,16},{24,28},{28,24},{1,5},{5... | collective-permute-start | bytes 884744 | tf_op jit(solution)/shard_map/ppermute | solution.py:23
  147.2 24.5 %collective-permute-start.33 = (bf16[384,384]{1,0:T(8,128)(2,1)}, bf16[384,384]{1,0:T(8,128)(2,1)S(1)}, u32[]{:S(2)}, u32[]{:S(2)}) collective-permute-start(bf16[384,384]{1,0:T(8,128)(2,1)} %collective-permute-done.29), channel_id=1, source_target_pairs={{0,4},{4,0},{8,12},{12,8},{16,20},{20,16},{24,28},{28,24},{1,5},{5... | collective-permute-start | bytes 884744 | tf_op jit(solution)/shard_map/ppermute | solution.py:23
  172.6 23.6 %collective-permute-start.39 = (bf16[384,768]{1,0:T(8,128)(2,1)}, bf16[384,768]{1,0:T(8,128)(2,1)S(1)}, u32[]{:S(2)}, u32[]{:S(2)}) collective-permute-start(bf16[384,768]{1,0:T(8,128)(2,1)} %get-tuple-element.377), channel_id=1, source_target_pairs={{0,4},{4,0},{8,12},{12,8},{16,20},{20,16},{24,28},{28,24},{1,5},{5... | collective-permute-start | bytes 1769480 | tf_op jit(solution)/shard_map/ppermute | solution.py:23
  174.4 21.8 %collective-permute-start.40 = (bf16[384,768]{1,0:T(8,128)(2,1)}, bf16[384,768]{1,0:T(8,128)(2,1)}, u32[]{:S(2)}, u32[]{:S(2)}) collective-permute-start(bf16[384,768]{1,0:T(8,128)(2,1)} %get-tuple-element.389), channel_id=1, source_target_pairs={{0,2},{1,3},{2,0},{3,1},{4,6},{5,7},{6,4},{7,5},{8,10},{9,11},{10,... | collective-permute-start | bytes 1769480 | tf_op jit(solution)/shard_map/ppermute | solution.py:23
  197.1 28.8 %collective-permute-start.42 = (bf16[768,768]{1,0:T(8,128)(2,1)}, bf16[768,768]{1,0:T(8,128)(2,1)}, u32[]{:S(2)}, u32[]{:S(2)}) collective-permute-start(bf16[768,768]{1,0:T(8,128)(2,1)} %constant_dynamic-update-slice_fusion.22.refs_5_.refs_4_), channel_id=1, source_target_pairs={{0,2},{1,3},{2,0},{3,1},{4,6},{5,7},{6,4},{7,5},{8,10},{9,11},{10,... | collective-permute-start | bytes 3538952 | tf_op jit(solution)/shard_map/ppermute | solution.py:23
  198.4 24.2 %collective-permute-start.43 = (bf16[384,768]{1,0:T(8,128)(2,1)S(1)}, bf16[384,768]{1,0:T(8,128)(2,1)}, u32[]{:S(2)}, u32[]{:S(2)}) collective-permute-start(bf16[384,768]{1,0:T(8,128)(2,1)S(1)} %copy-done.48), channel_id=1, source_target_pairs={{0,4},{4,0},{8,12},{12,8},{16,20},{20,16},{24,28},{28,24},{1,5},{5... | collective-permute-start | bytes 1769480 | tf_op jit(solution)/shard_map/ppermute | solution.py:23
  198.6 27.2 %collective-permute-start.44 = (bf16[384,768]{1,0:T(8,128)(2,1)}, bf16[384,768]{1,0:T(8,128)(2,1)}, u32[]{:S(2)}, u32[]{:S(2)}) collective-permute-start(bf16[384,768]{1,0:T(8,128)(2,1)} %collective-permute-done.40), channel_id=1, source_target_pairs={{0,4},{4,0},{8,12},{12,8},{16,20},{20,16},{24,28},{28,24},{1,5},{5... | collective-permute-start | bytes 1769480 | tf_op jit(solution)/shard_map/ppermute | solution.py:23
  201.5 27.8 %collective-permute-start.46 = (bf16[768,768]{1,0:T(8,128)(2,1)}, bf16[768,768]{1,0:T(8,128)(2,1)}, u32[]{:S(2)}, u32[]{:S(2)}) collective-permute-start(bf16[768,768]{1,0:T(8,128)(2,1)} %constant_dynamic-update-slice_fusion.22.refs_5_.refs_4_), channel_id=1, source_target_pairs={{0,1},{1,0},{2,3},{3,2},{4,5},{5,4},{6,7},{7,6},{8,9},{9,8},{10,11... | collective-permute-start | bytes 3538952 | tf_op jit(solution)/shard_map/ppermute | solution.py:23
  255.7 33.8 %collective-permute-start.50 = (bf16[384,768]{1,0:T(8,128)(2,1)S(1)}, bf16[384,768]{1,0:T(8,128)(2,1)S(1)}, u32[]{:S(2)}, u32[]{:S(2)}) collective-permute-start(bf16[384,768]{1,0:T(8,128)(2,1)S(1)} %slice.715), channel_id=1, source_target_pairs={{0,2},{1,3},{2,0},{3,1},{4,6},{5,7},{6,4},{7,5},{8,10},{9,11},{10,... | collective-permute-start | bytes 1769480 | tf_op jit(solution)/shard_map/ppermute | solution.py:23
  289.5 42.1 %collective-permute-start.51 = (bf16[4,768,768]{2,1,0:T(8,128)(2,1)}, bf16[4,768,768]{2,1,0:T(8,128)(2,1)}, u32[]{:S(2)}, u32[]{:S(2)}) collective-permute-start(bf16[4,768,768]{2,1,0:T(8,128)(2,1)} %get-tuple-element.430), channel_id=1, source_target_pairs={{0,1},{1,0},{2,3},{3,2},{4,5},{5,4},{6,7},{7,6},{8,9},{9,8},{10,11... | collective-permute-start | bytes 14155784 | tf_op jit(solution)/shard_map/ppermute | solution.py:23
  290.4 9.0 %collective-permute-start.52 = (bf16[768,768]{1,0:T(8,128)(2,1)}, bf16[768,768]{1,0:T(8,128)(2,1)S(1)}, u32[]{:S(2)}, u32[]{:S(2)}) collective-permute-start(bf16[768,768]{1,0:T(8,128)(2,1)} %get-tuple-element.443.refs_0_), channel_id=1, source_target_pairs={{0,1},{1,0},{2,3},{3,2},{4,5},{5,4},{6,7},{7,6},{8,9},{9,8},{10,11... | collective-permute-start | bytes 3538952 | tf_op jit(solution)/shard_map/ppermute | solution.py:23
  337.6 41.2 %collective-permute-start.53 = (bf16[768,768]{1,0:T(8,128)(2,1)}, bf16[768,768]{1,0:T(8,128)(2,1)}, u32[]{:S(2)}, u32[]{:S(2)}) collective-permute-start(bf16[768,768]{1,0:T(8,128)(2,1)} %fusion.32), channel_id=1, source_target_pairs={{0,2},{1,3},{2,0},{3,1},{4,6},{5,7},{6,4},{7,5},{8,10},{9,11},{10,... | collective-permute-start | bytes 3538952 | tf_op jit(solution)/shard_map/ppermute | solution.py:23
  338.9 39.9 %collective-permute-start.54 = (bf16[2,384,768]{2,1,0:T(8,128)(2,1)}, bf16[2,384,768]{2,1,0:T(8,128)(2,1)}, u32[]{:S(2)}, u32[]{:S(2)}) collective-permute-start(bf16[2,384,768]{2,1,0:T(8,128)(2,1)} %add_convert_fusion.5), channel_id=1, source_target_pairs={{0,4},{4,0},{8,12},{12,8},{16,20},{20,16},{24,28},{28,24},{1,5},{5... | collective-permute-start | bytes 3538952 | tf_op jit(solution)/shard_map/ppermute | solution.py:23
  389.0 40.5 %collective-permute-start.57 = (bf16[768,384]{0,1:T(8,128)(2,1)}, bf16[768,384]{0,1:T(8,128)(2,1)S(1)}, u32[]{:S(2)}, u32[]{:S(2)}) collective-permute-start(bf16[768,384]{0,1:T(8,128)(2,1)} %slice_bitcast_fusion.3), channel_id=1, source_target_pairs={{0,2},{1,3},{2,0},{3,1},{4,6},{5,7},{6,4},{7,5},{8,10},{9,11},{10,... | collective-permute-start | bytes 1769480 | tf_op jit(solution)/shard_map/ppermute | solution.py:23
  391.0 38.5 %collective-permute-start.58 = (bf16[2,384,384]{1,2,0:T(8,128)(2,1)}, bf16[2,384,384]{1,2,0:T(8,128)(2,1)}, u32[]{:S(2)}, u32[]{:S(2)}) collective-permute-start(bf16[2,384,384]{1,2,0:T(8,128)(2,1)} %slice.455), channel_id=1, source_target_pairs={{0,4},{4,0},{8,12},{12,8},{16,20},{20,16},{24,28},{28,24},{1,5},{5... | collective-permute-start | bytes 1769480 | tf_op jit(solution)/shard_map/ppermute | solution.py:23
  393.2 36.3 %collective-permute-start.55 = (bf16[384,768]{1,0:T(8,128)(2,1)}, bf16[384,768]{1,0:T(8,128)(2,1)}, u32[]{:S(2)}, u32[]{:S(2)}) collective-permute-start(bf16[384,768]{1,0:T(8,128)(2,1)} %slice.444), channel_id=1, source_target_pairs={{0,4},{4,0},{8,12},{12,8},{16,20},{20,16},{24,28},{28,24},{1,5},{5... | collective-permute-start | bytes 1769480 | tf_op jit(solution)/shard_map/ppermute | solution.py:23
  394.8 34.7 %collective-permute-start.56 = (bf16[384,768]{1,0:T(8,128)(2,1)}, bf16[384,768]{1,0:T(8,128)(2,1)}, u32[]{:S(2)}, u32[]{:S(2)}) collective-permute-start(bf16[384,768]{1,0:T(8,128)(2,1)} %slice_bitcast_fusion.4), channel_id=1, source_target_pairs={{0,2},{1,3},{2,0},{3,1},{4,6},{5,7},{6,4},{7,5},{8,10},{9,11},{10,... | collective-permute-start | bytes 1769480 | tf_op jit(solution)/shard_map/ppermute | solution.py:23
  429.5 24.5 %collective-permute-start.60 = (bf16[4,768,768]{2,1,0:T(8,128)(2,1)}, bf16[4,768,768]{2,1,0:T(8,128)(2,1)}, u32[]{:S(2)}, u32[]{:S(2)}) collective-permute-start(bf16[4,768,768]{2,1,0:T(8,128)(2,1)} %get-tuple-element.482), channel_id=1, source_target_pairs={{0,1},{1,0},{2,3},{3,2},{4,5},{5,4},{6,7},{7,6},{8,9},{9,8},{10,11... | collective-permute-start | bytes 14155784 | tf_op jit(solution)/shard_map/ppermute | solution.py:23
  434.7 9.3 %collective-permute-start.68 = (bf16[768,768]{1,0:T(8,128)(2,1)S(1)}, bf16[768,768]{1,0:T(8,128)(2,1)S(1)}, u32[]{:S(2)}, u32[]{:S(2)}) collective-permute-start(bf16[768,768]{1,0:T(8,128)(2,1)S(1)} %copy-done.1), channel_id=1, source_target_pairs={{0,1},{1,0},{2,3},{3,2},{4,5},{5,4},{6,7},{7,6},{8,9},{9,8},{10,11... | collective-permute-start | bytes 3538952 | tf_op jit(solution)/shard_map/ppermute | solution.py:23
  437.9 16.1 %collective-permute-start.63 = (bf16[192,1536]{1,0:T(8,128)(2,1)}, bf16[192,1536]{1,0:T(8,128)(2,1)}, u32[]{:S(2)}, u32[]{:S(2)}) collective-permute-start(bf16[192,1536]{1,0:T(8,128)(2,1)} %slice.463), channel_id=1, source_target_pairs={{0,8},{4,12},{8,0},{12,4},{16,24},{20,28},{24,16},{28,20},{1,9},{5... | collective-permute-start | bytes 1769480 | tf_op jit(solution)/shard_map/ppermute | solution.py:23
  440.3 9.4 %collective-permute-start.61 = (bf16[384,384]{0,1:T(8,128)(2,1)}, bf16[384,384]{0,1:T(8,128)(2,1)S(1)}, u32[]{:S(2)}, u32[]{:S(2)}) collective-permute-start(bf16[384,384]{0,1:T(8,128)(2,1)} %slice.461), channel_id=1, source_target_pairs={{0,4},{4,0},{8,12},{12,8},{16,20},{20,16},{24,28},{28,24},{1,5},{5... | collective-permute-start | bytes 884744 | tf_op jit(solution)/shard_map/ppermute | solution.py:23
  441.9 9.2 %collective-permute-start.62 = (bf16[384,384]{0,1:T(8,128)(2,1)}, bf16[384,384]{0,1:T(8,128)(2,1)}, u32[]{:S(2)}, u32[]{:S(2)}) collective-permute-start(bf16[384,384]{0,1:T(8,128)(2,1)} %slice_bitcast_fusion.5), channel_id=1, source_target_pairs={{0,2},{1,3},{2,0},{3,1},{4,6},{5,7},{6,4},{7,5},{8,10},{9,11},{10,... | collective-permute-start | bytes 884744 | tf_op jit(solution)/shard_map/ppermute | solution.py:23
  462.1 40.2 %collective-permute-start.64 = (bf16[768,768]{1,0:T(8,128)(2,1)}, bf16[768,768]{1,0:T(8,128)(2,1)}, u32[]{:S(2)}, u32[]{:S(2)}) collective-permute-start(bf16[768,768]{1,0:T(8,128)(2,1)} %fusion.33), channel_id=1, source_target_pairs={{0,2},{1,3},{2,0},{3,1},{4,6},{5,7},{6,4},{7,5},{8,10},{9,11},{10,... | collective-permute-start | bytes 3538952 | tf_op jit(solution)/shard_map/ppermute | solution.py:23
  463.3 39.0 %collective-permute-start.65 = (bf16[2,384,768]{2,1,0:T(8,128)(2,1)}, bf16[2,384,768]{2,1,0:T(8,128)(2,1)}, u32[]{:S(2)}, u32[]{:S(2)}) collective-permute-start(bf16[2,384,768]{2,1,0:T(8,128)(2,1)} %add_convert_fusion.2), channel_id=1, source_target_pairs={{0,4},{4,0},{8,12},{12,8},{16,20},{20,16},{24,28},{28,24},{1,5},{5... | collective-permute-start | bytes 3538952 | tf_op jit(solution)/shard_map/ppermute | solution.py:23
  467.1 35.2 %collective-permute-start.66 = (bf16[192,768]{0,1:T(8,128)(2,1)}, bf16[192,768]{0,1:T(8,128)(2,1)}, u32[]{:S(2)}, u32[]{:S(2)}) collective-permute-start(bf16[192,768]{0,1:T(8,128)(2,1)} %slice.472), channel_id=1, source_target_pairs={{0,8},{4,12},{8,0},{12,4},{16,24},{20,28},{24,16},{28,20},{1,9},{5... | collective-permute-start | bytes 884744 | tf_op jit(solution)/shard_map/ppermute | solution.py:23
  469.2 33.0 %collective-permute-start.67 = (bf16[96,1536]{1,0:T(8,128)(2,1)}, bf16[96,1536]{1,0:T(8,128)(2,1)}, u32[]{:S(2)}, u32[]{:S(2)}) collective-permute-start(bf16[96,1536]{1,0:T(8,128)(2,1)} %slice.473), channel_id=1, source_target_pairs={{0,16},{4,20},{8,24},{12,28},{16,0},{20,4},{24,8},{28,12},{1,17},{... | collective-permute-start | bytes 884744 | tf_op jit(solution)/shard_map/ppermute | solution.py:23
  512.3 43.6 %collective-permute-start.72 = (bf16[768,768]{0,1:T(8,128)(2,1)}, bf16[768,768]{0,1:T(8,128)(2,1)}, u32[]{:S(2)}, u32[]{:S(2)}) collective-permute-start(bf16[768,768]{0,1:T(8,128)(2,1)} %pad_maximum_fusion.12), channel_id=1, source_target_pairs={{0,2},{1,3},{2,0},{3,1},{4,6},{5,7},{6,4},{7,5},{8,10},{9,11},{10,... | collective-permute-start | bytes 3538952 | tf_op jit(solution)/shard_map/ppermute | solution.py:23
  513.8 42.1 %collective-permute-start.69 = (bf16[384,768]{1,0:T(8,128)(2,1)}, bf16[384,768]{1,0:T(8,128)(2,1)}, u32[]{:S(2)}, u32[]{:S(2)}) collective-permute-start(bf16[384,768]{1,0:T(8,128)(2,1)} %slice.476), channel_id=1, source_target_pairs={{0,4},{4,0},{8,12},{12,8},{16,20},{20,16},{24,28},{28,24},{1,5},{5... | collective-permute-start | bytes 1769480 | tf_op jit(solution)/shard_map/ppermute | solution.py:23
  515.9 40.0 %collective-permute-start.70 = (bf16[384,768]{1,0:T(8,128)(2,1)}, bf16[384,768]{1,0:T(8,128)(2,1)}, u32[]{:S(2)}, u32[]{:S(2)}) collective-permute-start(bf16[384,768]{1,0:T(8,128)(2,1)} %slice_bitcast_fusion.2), channel_id=1, source_target_pairs={{0,2},{1,3},{2,0},{3,1},{4,6},{5,7},{6,4},{7,5},{8,10},{9,11},{10,... | collective-permute-start | bytes 1769480 | tf_op jit(solution)/shard_map/ppermute | solution.py:23
  521.5 34.4 %collective-permute-start.71 = (bf16[96,768]{0,1:T(8,128)(2,1)}, bf16[96,768]{0,1:T(8,128)(2,1)}, u32[]{:S(2)}, u32[]{:S(2)}) collective-permute-start(bf16[96,768]{0,1:T(8,128)(2,1)} %slice.480), channel_id=1, source_target_pairs={{0,16},{4,20},{8,24},{12,28},{16,0},{20,4},{24,8},{28,12},{1,17},{... | collective-permute-start | bytes 442376 | tf_op jit(solution)/shard_map/ppermute | solution.py:23
  555.9 11.7 %collective-permute-start.75 = (bf16[768,768]{1,0:T(8,128)(2,1)}, bf16[768,768]{1,0:T(8,128)(2,1)S(1)}, u32[]{:S(2)}, u32[]{:S(2)}) collective-permute-start(bf16[768,768]{1,0:T(8,128)(2,1)} %get-tuple-element.533), channel_id=1, source_target_pairs={{0,1},{1,0},{2,3},{3,2},{4,5},{5,4},{6,7},{7,6},{8,9},{9,8},{10,11... | collective-permute-start | bytes 3538952 | tf_op jit(solution)/shard_map/ppermute | solution.py:23
  558.9 18.3 %collective-permute-start.74 = (bf16[192,1536]{1,0:T(8,128)(2,1)S(1)}, bf16[192,1536]{1,0:T(8,128)(2,1)S(1)}, u32[]{:S(2)}, u32[]{:S(2)}) collective-permute-start(bf16[192,1536]{1,0:T(8,128)(2,1)S(1)} %slice.552), channel_id=1, source_target_pairs={{0,8},{4,12},{8,0},{12,4},{16,24},{20,28},{24,16},{28,20},{1,9},{5... | collective-permute-start | bytes 1769480 | tf_op jit(solution)/shard_map/ppermute | solution.py:23
  564.9 15.7 %collective-permute-start.73 = (bf16[384,768]{0,1:T(8,128)(2,1)S(1)}, bf16[384,768]{0,1:T(8,128)(2,1)S(1)}, u32[]{:S(2)}, u32[]{:S(2)}) collective-permute-start(bf16[384,768]{0,1:T(8,128)(2,1)S(1)} %slice.551), channel_id=1, source_target_pairs={{0,4},{4,0},{8,12},{12,8},{16,20},{20,16},{24,28},{28,24},{1,5},{5... | collective-permute-start | bytes 1769480 | tf_op jit(solution)/shard_map/ppermute | solution.py:23
  581.1 17.0 %collective-permute-start.76 = (bf16[192,768]{0,1:T(8,128)(2,1)S(1)}, bf16[192,768]{0,1:T(8,128)(2,1)S(1)}, u32[]{:S(2)}, u32[]{:S(2)}) collective-permute-start(bf16[192,768]{0,1:T(8,128)(2,1)S(1)} %slice.491), channel_id=1, source_target_pairs={{0,8},{4,12},{8,0},{12,4},{16,24},{20,28},{24,16},{28,20},{1,9},{5... | collective-permute-start | bytes 884744 | tf_op jit(solution)/shard_map/ppermute | solution.py:23
  581.5 16.5 %collective-permute-start.77 = (bf16[96,1536]{1,0:T(8,128)(2,1)S(1)}, bf16[96,1536]{1,0:T(8,128)(2,1)S(1)}, u32[]{:S(2)}, u32[]{:S(2)}) collective-permute-start(bf16[96,1536]{1,0:T(8,128)(2,1)S(1)} %slice.492), channel_id=1, source_target_pairs={{0,16},{4,20},{8,24},{12,28},{16,0},{20,4},{24,8},{28,12},{1,17},{... | collective-permute-start | bytes 884744 | tf_op jit(solution)/shard_map/ppermute | solution.py:23
  602.0 10.9 %collective-permute-start.82 = (bf16[96,768]{0,1:T(8,128)(2,1)S(1)}, bf16[96,768]{0,1:T(8,128)(2,1)S(1)}, u32[]{:S(2)}, u32[]{:S(2)}) collective-permute-start(bf16[96,768]{0,1:T(8,128)(2,1)S(1)} %slice.502), channel_id=1, source_target_pairs={{0,16},{4,20},{8,24},{12,28},{16,0},{20,4},{24,8},{28,12},{1,17},{... | collective-permute-start | bytes 442376 | tf_op jit(solution)/shard_map/ppermute | solution.py:23
  605.2 18.3 %collective-permute-start.81 = (bf16[384,768]{1,0:T(8,128)(2,1)}, bf16[384,768]{1,0:T(8,128)(2,1)S(1)}, u32[]{:S(2)}, u32[]{:S(2)}) collective-permute-start(bf16[384,768]{1,0:T(8,128)(2,1)} %get-tuple-element.564), channel_id=1, source_target_pairs={{0,2},{1,3},{2,0},{3,1},{4,6},{5,7},{6,4},{7,5},{8,10},{9,11},{10,... | collective-permute-start | bytes 1769480 | tf_op jit(solution)/shard_map/ppermute | solution.py:23
  (138 other events, 757.3 us)
